TPU v7x, 32 devices: a whole 2x2x4 slice. The times are simulated.
32 devices in a mesh: pairs: 2 (over x), src: 16 (over z, y, core).
Axes of the slice: x: 2, y: 2, z: 4, core: 2. Of those that a mesh axis runs over, the one named last changes fastest.
Arguments:
- src_feat: bfloat16 [32768, 256], P(('pairs', 'src')), parts along dimension 0, may hold values from -6 to 6
- tile_feat: bfloat16 [256, 16, 128, 256], P(('pairs', 'src')), parts along dimension 0, may hold values from -6 to 6
- tile_tgt: int32 [256, 16], P(('pairs', 'src')), parts along dimension 0, may hold values from 0 to 127, as said below
- tile_live: int32 [256], P(('pairs', 'src')), parts along dimension 0, may hold values from 1 to 16, as said below
- src_lin: float32 [32768], P(('pairs', 'src')), parts along dimension 0, may hold values from 0 to 1
- tgt_lin: float32 [32768], P(('pairs', 'src')), parts along dimension 0, may hold values from 0 to 1
- src_mass: float32 [32768], P(('pairs', 'src')), parts along dimension 0, may hold values from 0.5 to 2
- tgt_mass: float32 [32768], P(('pairs', 'src')), parts along dimension 0, may hold values from 0.25 to 6
- tgt_count: int32 [256], P(('pairs', 'src')), parts along dimension 0, may hold values from 1 to 128
Outputs:
- src_scale: float32 [32768], P(('pairs', 'src')), parts along dimension 0
- tgt_scale: float32 [32768], P(('pairs', 'src')), parts along dimension 0
There are 2 independent parts, one for each index of `pairs`. A program takes and returns all parts, laid end to end along the dimension named above; each array names one. Nothing has to cross between parts.
Inputs may be any that keep to these rules, and one draw needn't show every extreme that they name: tile_tgt[s, 0] = s; the slots of one source block name distinct target blocks. `tile_live`: every source block has between 1 and 16 live slots.
All inputs are finite; a program needn't handle non-finite values.
Results may differ from a plain program's by a relative error of at most 0.0003.
Values sent between devices are 32-bit elements; how exact they have to be, the bound alone decides.
No kernel may reach another device: no remote copies, remote signals or barrier semaphores. Data moves between devices by JAX's collectives and lax.ppermute only.
A program may use at most 64 MiB of HBM per device.

v0:
```python
import functools

import jax
import jax.numpy as jnp
from jax import lax
from jax.experimental import pallas as pl
from jax.experimental.pallas import tpu as pltpu
from jax.sharding import PartitionSpec as P

ITERS = 3
EPS = 0.1
RHO = 1.0
ALPHA = 0.5
F = RHO / (RHO + EPS)
STEP = 4
PIECES = 4

VMEM = pltpu.VMEM
SMEM = pltpu.SMEM
NT = (((1,), (1,)), ((), ()))


def diag_mask(block):
    return lax.broadcasted_iota(jnp.int32, (block, block), 0) == lax.broadcasted_iota(
        jnp.int32, (block, block), 1
    )


def to_column(row, mask):
    return jnp.sum(jnp.where(mask, row, 0.0), axis=1, keepdims=True)


def to_row(column, mask):
    return jnp.sum(jnp.where(mask, column, 0.0), axis=0, keepdims=True)


def total_of(x):
    return jnp.sum(jnp.sum(x, axis=0, keepdims=True), axis=1, keepdims=True)


def steps_of(live_s):
    return (live_s + (STEP - 1)) // STEP


def build_tiles(live, first, x_ref, lin_ref, mass_ref, feat, waits, k_ref, la_ref):
    blocks, slots, block, width = feat.shape
    mask = diag_mask(block)
    for s in range(blocks):
        at = first + s
        x = x_ref[at * block : (at + 1) * block, :]
        x32 = x.astype(jnp.float32)
        sq = jnp.sum(x32 * x32, axis=1, keepdims=True)
        lin = to_column(lin_ref[at : at + 1, :], mask)
        base = (2.0 - sq / width - ALPHA * lin) / EPS
        base = jnp.broadcast_to(base, (block, block))
        la = F * jnp.log(to_column(mass_ref[at : at + 1, :], mask))
        la_ref[s * block : (s + 1) * block, :] = jnp.broadcast_to(la, (block, block))
        if waits:
            waits[s].wait()

        def tiles(p, _):
            y = feat[s, pl.ds(p * STEP, STEP)].reshape(STEP * block, width)
            y32 = y.astype(jnp.float32)
            y2 = y32 * y32
            ysq = jnp.sum(y2[:, : width // 2] + y2[:, width // 2 :], axis=1, keepdims=True)
            cross = lax.dot_general(x, y, NT, preferred_element_type=jnp.float32)
            for q in range(STEP):
                cols = slice(q * block, (q + 1) * block)
                row = to_row(ysq[cols, :], mask)
                e = (2.0 / (width * EPS)) * cross[:, cols] + (base - row * (1.0 / (width * EPS)))
                start = pl.multiple_of((s * slots + p * STEP + q) * block, block)
                k_ref[pl.ds(start, block), :] = jnp.exp(e)
            return 0

        lax.fori_loop(0, steps_of(live[at]), tiles, 0)


def first_build(live_hbm, x_hbm, feat, lin_hbm, mass_hbm, *refs):
    k_ref, la_ref, x_ref, lin_ref, mass_ref, *rest = refs
    later, (live, own, sems) = rest[:-3], rest[-3:]
    each = own.shape[0]
    copies = [(live_hbm, live), (x_hbm, x_ref), (lin_hbm, lin_ref), (mass_hbm, mass_ref)]
    copies += [(feat.at[s], own.at[s]) for s in range(each)]
    copies += [(feat.at[pl.ds((i + 1) * each, each)], to) for i, to in enumerate(later)]
    copies = [pltpu.make_async_copy(f, t, sems.at[i]) for i, (f, t) in enumerate(copies)]
    for c in copies:
        c.start()
    for c in copies[:4]:
        c.wait()
    build_tiles(
        live, 0, x_ref, lin_ref, mass_ref, own, copies[4 : 4 + each], k_ref, la_ref
    )
    for c in copies[4 + each :]:
        c.wait()


def later_build(first, live, x_ref, feat, lin_ref, mass_ref, k_ref, la_ref):
    build_tiles(live, first, x_ref, lin_ref, mass_ref, feat, (), k_ref, la_ref)


def sweep(live, tgt, idx_ref, w_ref, k_refs, la_refs, dense_ref, acc_ref, u_ref, col_ref):
    blocks, slots = tgt.shape
    block = w_ref.shape[1]
    every = w_ref.shape[0] - 8
    each = blocks // len(k_refs)
    w_ref[every:, :] = jnp.zeros((8, block), jnp.float32)
    for s in range(blocks):
        k_ref = k_refs[s // each]

        def add_row(p, acc):
            for q in range(STEP):
                k = p * STEP + q
                row = jnp.where(k < live[s], tgt[s, k], every)
                start = pl.multiple_of(((s % each) * slots + k) * block, block)
                acc = acc + k_ref[pl.ds(start, block), :] * w_ref[pl.ds(row, 1), :]
            return acc

        acc_ref[s * block : (s + 1) * block, :] = lax.fori_loop(
            0, steps_of(live[s]), add_row, jnp.zeros((block, block), jnp.float32)
        )
    for s in range(blocks):
        rows = pl.ds(s * block, block)
        total = jnp.sum(acc_ref[rows, :], axis=1, keepdims=True)
        la = la_refs[s // each][pl.ds((s % each) * block, block), :]
        u_ref[rows, :] = jnp.exp(la - F * jnp.log(total))
    col_ref[...] = jnp.zeros_like(col_ref)
    for s in range(blocks):
        k_ref = k_refs[s // each]
        u = u_ref[s * block : (s + 1) * block, :]

        def add_col(p, _):
            for q in range(STEP):
                k = p * STEP + q
                start = pl.multiple_of(((s % each) * slots + k) * block, block)
                col_ref[pl.ds(s * slots + k, 1), :] = jnp.sum(
                    k_ref[pl.ds(start, block), :] * u, axis=0, keepdims=True
                )
            return 0

        lax.fori_loop(0, steps_of(live[s]), add_col, 0)
    col = col_ref[...]
    rows = lax.broadcasted_iota(jnp.int32, (every, blocks * slots), 0)
    hit = jnp.where(rows == idx_ref[...], 1.0, 0.0).astype(jnp.bfloat16)
    dense = jnp.zeros((every, block), jnp.float32)
    for _ in range(3):
        piece = col.astype(jnp.bfloat16)
        dense += jnp.dot(hit, piece, preferred_element_type=jnp.float32)
        col = col - piece.astype(jnp.float32)
    dense_ref[...] = dense


def power_of_ratio(num, den):
    return jnp.exp(F * (jnp.log(num) - jnp.log(den)))


def first_sweep(npieces, live, tgt, me, idx_ref, *refs):
    k_refs, la_refs = refs[:npieces], refs[npieces : 2 * npieces]
    parts = refs[2 * npieces : 2 * npieces + 2]
    dense_ref, b_ref, et_ref, tot_ref, w_ref, acc_ref, u_ref, col_ref = refs[2 * npieces + 2 :]
    local = tgt.shape[0]
    n = b_ref.shape[0] // local
    bits = n.bit_length() - 1
    am = jnp.zeros((local, b_ref.shape[1]), jnp.float32)
    for at in range(n):
        m = sum(((at >> r) & 1) << (bits - 1 - r) for r in range(bits))
        part = parts[at // (n // 2)]
        at = (at % (n // 2)) * 3 * local
        rows = pl.ds(pl.multiple_of((me[0] ^ m) * local, local), local)
        b = part[at : at + local, :]
        et = jnp.exp((-ALPHA / EPS) * part[at + local : at + 2 * local, :])
        b_ref[rows, :] = b
        et_ref[rows, :] = et
        w_ref[rows, :] = jnp.where(b > 0.0, et, 0.0)
        am += part[at + 2 * local : at + 3 * local, :]
    tot = jnp.sqrt(total_of(am) * total_of(b_ref[...]))
    tot_ref[...] = jnp.broadcast_to(tot, tot_ref.shape)
    sweep(live, tgt, idx_ref, w_ref, k_refs, la_refs, dense_ref, acc_ref, u_ref, col_ref)


def new_scale(me, mine, other, b_ref, et_ref, tot_ref):
    b = b_ref[...]
    col = jnp.where((me[0] & 1) == 1, mine[...], other[...]) * et_ref[...]
    t = jnp.where(b > 0.0, power_of_ratio(b, col), 0.0)
    return t, jnp.sqrt(tot_ref[0:1, 0:1] / total_of(t * col))


def next_sweep(npieces, live, tgt, me, idx_ref, mine, other, b_ref, et_ref, tot_ref, *refs):
    k_refs, la_refs = refs[:npieces], refs[npieces : 2 * npieces]
    dense_ref, u_ref, w_ref, acc_ref, col_ref = refs[2 * npieces :]
    t, factor = new_scale(me, mine, other, b_ref, et_ref, tot_ref)
    w_ref[: b_ref.shape[0], :] = t * (factor * et_ref[...])
    sweep(live, tgt, idx_ref, w_ref, k_refs, la_refs, dense_ref, acc_ref, u_ref, col_ref)


def last_kernel(me, mine, other, b_ref, et_ref, tot_ref, u_ref, src_ref, tgt_ref, t_ref):
    local, block = src_ref.shape
    t, factor = new_scale(me, mine, other, b_ref, et_ref, tot_ref)
    t_ref[...] = t * factor
    tgt_ref[...] = t_ref[pl.ds(pl.multiple_of(me[0] * local, local), local), :]
    mask = diag_mask(block)
    for s in range(local):
        src_ref[s : s + 1, :] = to_row(u_ref[s * block : (s + 1) * block, :] * factor, mask)


def call(kernel, ins, outs, scratch=(), smem=0, hbm=(), vmem_mb=12, **cost):
    specs = [pl.BlockSpec(memory_space=SMEM)] * smem
    for at in range(smem, len(ins)):
        specs.append(pl.BlockSpec(memory_space=pl.ANY if at in hbm else VMEM))
    ins = [
        pltpu.with_memory_space_constraint(x, pltpu.HBM) if at in hbm else x
        for at, x in enumerate(ins)
    ]
    return pl.pallas_call(
        kernel,
        out_shape=outs,
        in_specs=specs,
        out_specs=[pl.BlockSpec(memory_space=VMEM)] * len(outs),
        scratch_shapes=scratch,
        compiler_params=pltpu.CompilerParams(vmem_limit_bytes=vmem_mb << 20),
        cost_estimate=pl.CostEstimate(**cost) if cost else None,
    )(*ins)


def exchange(x, n, d, cores=(0, 1)):
    return lax.ppermute(x, "src", [(i, i ^ d) for i in range(n) if i & 1 in cores])


def shards(
    src_feat, tile_feat, tile_tgt, tile_live, src_lin, tgt_lin, src_mass, tgt_mass, tgt_count
):
    f32 = jnp.float32
    local, slots, block, width = tile_feat.shape
    n = lax.axis_size("src")
    me = lax.axis_index("src").astype(jnp.int32).reshape(1)
    every = local * n
    pairs = local * slots
    lin = src_lin.reshape(local, block)
    amass = src_mass.reshape(local, block)
    part = jnp.concatenate([tgt_mass, tgt_lin, src_mass]).reshape(3 * local, block)
    count = jnp.concatenate([tgt_count, jnp.full((2 * local,), block, jnp.int32)])
    part = jnp.where(lax.broadcasted_iota(jnp.int32, part.shape, 1) < count[:, None], part, 0.0)

    def shape(rows, cols=block, dtype=f32):
        return pltpu.VMEM((rows, cols), dtype)

    each = local // PIECES
    feats = pltpu.VMEM((each, slots, block, width), tile_feat.dtype)
    cost = dict(
        flops=2 * each * slots * block * block * width,
        bytes_accessed=2 * each * slots * block * width,
        transcendentals=each * slots * block * block,
    )
    order = []
    d = n // 2
    while d:
        order.append(d)
        d //= 2
    kern, la = [], []
    for at, d in enumerate(order):
        got = exchange(part, n, d)
        if at == 0:
            k0, la0, xv, linv, massv, *later = call(
                first_build,
                (tile_live, src_feat, tile_feat, lin, amass),
                (
                    shape(each * slots * block),
                    shape(each * block),
                    shape(local * block, width, src_feat.dtype),
                    shape(local),
                    shape(local),
                    *[feats] * (PIECES - 1),
                ),
                scratch=[
                    SMEM((local,), jnp.int32),
                    feats,
                    pltpu.SemaphoreType.DMA((4 + each + PIECES - 1,)),
                ],
                hbm=(0, 1, 2, 3, 4),
                **cost,
            )
            kern.append(k0)
            la.append(la0)
        elif at < PIECES:
            k0, la0 = call(
                functools.partial(later_build, at * each),
                (tile_live, xv, later[at - 1], linv, massv),
                (shape(each * slots * block), shape(each * block)),
                smem=1,
                **cost,
            )
            kern.append(k0)
            la.append(la0)
        if d > 1:
            part = jnp.stack([part, got], axis=0).reshape(-1, block)
            if at < PIECES - 1:
                part, later[at], kern[-1] = lax.optimization_barrier(
                    (part, later[at], kern[-1])
                )
    slot = lax.broadcasted_iota(jnp.int32, (local, slots), 1)
    idx = jnp.where(slot < tile_live[:, None], tile_tgt, -1).reshape(1, pairs)
    acc = VMEM((local * block, block), f32)
    col = VMEM((pairs, block), f32)
    w = VMEM((every + 8, block), f32)
    mine, b_all, et_all, tot = call(
        functools.partial(first_sweep, PIECES),
        (tile_live, tile_tgt, me, idx, *kern, *la, part, got),
        (shape(every), shape(every), shape(every), shape(8)),
        scratch=[w, acc, acc, col],
        smem=3,
    )
    u = None
    for iteration in range(ITERS):
        mine = mine + exchange(mine, n, 1, (0,))
        d = 2
        while d < n:
            mine = mine + exchange(mine, n, d, (1,))
            d *= 2
        other = exchange(mine, n, 1, (1,))
        if iteration < ITERS - 1:
            mine, u = call(
                functools.partial(next_sweep, PIECES),
                (tile_live, tile_tgt, me, idx, mine, other, b_all, et_all, tot, *kern, *la),
                (shape(every), shape(local * block)),
                scratch=[w, acc, col],
                smem=3,
            )
    src, tgt = call(
        last_kernel,
        (me, mine, other, b_all, et_all, tot, u),
        [jax.ShapeDtypeStruct((local, block), f32)] * 2,
        scratch=[VMEM((every, block), f32)],
        smem=1,
    )
    return (src.reshape(-1), tgt.reshape(-1))


def solution(mesh):
    split = P(("pairs", "src"))
    rows = P(("pairs", "src"), None)
    in_specs = (rows, P(("pairs", "src"), None, None, None), rows) + (split,) * 6
    return jax.shard_map(
        shards, mesh=mesh, in_specs=in_specs, out_specs=(split, split), check_vma=False
    )
```

profile of v0, /device:TPU:0, one launch (start us, length us, event | category | flops | bytes accessed | tf_op | source)
XLA Modules:
  0.0 103.2 jit_solution(1135855800958293505)
XLA Ops:
  0.6 0.7 concatenate.28
  1.3 0.8 maximum_select_fusion.1
  2.1 4.0 %collective-permute-start = (f32[24,128]{1,0:T(8,128)S(1)}, f32[24,128]{1,0:T(8,128)S(1)}, u32[]{:S(2)}, u32[]{:S(2)}) collective-permute-start(f32[24,128]{1,0:T(8,128)S(1)} %maximum_select_fusion.1), channel_id=1, source_target_pairs={{0,8},{1,9},{2,10},{3,11},{4,12},{5,13},{6,14},{7,15},{8,0},{9,1},... | collective-permute-start | bytes 36872 | tf_op jit(solution)/shard_map/ppermute | solution.py:225
  6.1 0.8 maximum_select_fusion
  6.9 0.0 copy-start.7
  6.9 3.8 %shard_map.104 = (f32[4096,128]{1,0:T(8,128)S(1)}, f32[256,128]{1,0:T(8,128)S(1)}, bf16[1024,256]{1,0:T(8,128)(2,1)S(1)}, f32[8,128]{1,0:T(8,128)S(1)}, f32[8,12...) custom-call(s32[8]{0:T(128)} %live.11, ...), custom_call_target="tpu_custom_call" | custom-call | flops 268435456 | bytes 2097152 | tf_op jit(solution)/shard_map/pallas_call | solution.py:213
  10.7 0.0 copy-start.4
  10.7 1.4 %copy-done.4 = bf16[2,16,128,256]{3,2,1,0:T(8,128)(2,1)} copy-done((bf16[2,16,128,256]{3,2,1,0:T(8,128)(2,1)}, bf16[2,16,128,256]{3,2,1,0:T(8,128)(2,1)S(1)}, u32[]{:S(2)}) %copy-start.4) | copy-done | bytes 2097176
  12.1 0.0 collective-permute-done
  12.1 1.6 %collective-permute-start.1 = (f32[48,128]{1,0:T(8,128)S(1)}, f32[48,128]{1,0:T(8,128)S(1)}, u32[]{:S(2)}, u32[]{:S(2)}) collective-permute-start(f32[48,128]{1,0:T(8,128)S(1)} %bitcast.22), channel_id=1, source_target_pairs={{0,4},{1,5},{2,6},{3,7},{4,0},{5,1},{6,2},{7,3},{8,12},{9,13},{10,... | collective-permute-start | bytes 73736 | tf_op jit(solution)/shard_map/ppermute | solution.py:225
  13.6 0.0 copy-done.7
  13.6 2.0 %shard_map.105 = (f32[4096,128]{1,0:T(8,128)S(1)}, f32[256,128]{1,0:T(8,128)S(1)}) custom-call(s32[8]{0:T(128)S(1)} %copy-done.7, bf16[1024,256]{1,0:T(8,128)(2,1)S(1)} %get-tuple-element.39.x_ref, bf16[2,16,128,256]{3,2,1,0:T(8,128)(2,1)S(1)} %get-tuple-element.40.feat, f32[8,128]{1,0:T(8,128)S(1)} %get-tuple-element.41.lin_ref, ...), custom_call_target="tpu_custom_call" | custom-call | flops 268435456 | bytes 2097152 | tf_op jit(solution)/shard_map/pallas_call | solution.py:213
  15.6 0.0 copy-start
  15.6 1.3 %copy-done = f32[4096,128]{1,0:T(8,128)} copy-done((f32[4096,128]{1,0:T(8,128)}, f32[4096,128]{1,0:T(8,128)S(1)}, u32[]{:S(2)}) %copy-start) | copy-done | bytes 2097176
  17.0 0.0 copy-start.6
  17.0 0.0 collective-permute-done.1
  17.0 1.6 %collective-permute-start.2 = (f32[96,128]{1,0:T(8,128)S(1)}, f32[96,128]{1,0:T(8,128)S(1)}, u32[]{:S(2)}, u32[]{:S(2)}) collective-permute-start(f32[96,128]{1,0:T(8,128)S(1)} %bitcast.20), channel_id=1, source_target_pairs={{0,2},{1,3},{2,0},{3,1},{4,6},{5,7},{6,4},{7,5},{8,10},{9,11},{10,... | collective-permute-start | bytes 147464 | tf_op jit(solution)/shard_map/ppermute | solution.py:225
  18.6 2.2 %shard_map.106 = (f32[4096,128]{1,0:T(8,128)S(1)}, f32[256,128]{1,0:T(8,128)S(1)}) custom-call(s32[8]{0:T(128)S(1)} %copy-done.7, bf16[1024,256]{1,0:T(8,128)(2,1)S(1)} %get-tuple-element.39.x_ref, bf16[2,16,128,256]{3,2,1,0:T(8,128)(2,1)S(1)} %get-tuple-element.47.feat, f32[8,128]{1,0:T(8,128)S(1)} %get-tuple-element.41.lin_ref, ...), custom_call_target="tpu_custom_call" | custom-call | flops 268435456 | bytes 2097152 | tf_op jit(solution)/shard_map/pallas_call | solution.py:213
  20.8 0.0 copy-start.2
  20.8 1.3 %copy-done.2 = f32[4096,128]{1,0:T(8,128)} copy-done((f32[4096,128]{1,0:T(8,128)}, f32[4096,128]{1,0:T(8,128)S(1)}, u32[]{:S(2)}) %copy-start.2) | copy-done | bytes 2097176
  22.2 0.0 collective-permute-done.2
  22.2 0.1 collective-permute-start.3
  22.2 0.0 copy-done.6
  22.3 0.1 fusion
  22.3 0.1 reshape.105.idx_ref
  22.4 1.6 %copy-done.5 = bf16[2,16,128,256]{3,2,1,0:T(8,128)(2,1)S(1)} copy-done((bf16[2,16,128,256]{3,2,1,0:T(8,128)(2,1)S(1)}, bf16[2,16,128,256]{3,2,1,0:T(8,128)(2,1)}, u32[]{:S(2)}) %copy-start.5) | copy-done | bytes 2097176
  24.0 1.3 %shard_map.107 = (f32[4096,128]{1,0:T(8,128)S(1)}, f32[256,128]{1,0:T(8,128)S(1)}) custom-call(s32[8]{0:T(128)S(1)} %copy-done.7, bf16[1024,256]{1,0:T(8,128)(2,1)S(1)} %get-tuple-element.39.x_ref, bf16[2,16,128,256]{3,2,1,0:T(8,128)(2,1)S(1)} %copy-done.5, f32[8,128]{1,0:T(8,128)S(1)} %get-tuple-element.41.lin_ref, f32[8,128]{1,0:T(8,128)S(1)} %get-tuple-element.42.mass_ref), custom_call_target="tpu_custom_call" | custom-call | flops 268435456 | bytes 2097152 | tf_op jit(solution)/shard_map/pallas_call | solution.py:213
  25.3 0.0 collective-permute-done.3.refs_9_
  25.3 0.3 copy-done.1
  25.6 1.6 %copy-done.3 = f32[4096,128]{1,0:T(8,128)S(1)} copy-done((f32[4096,128]{1,0:T(8,128)S(1)}, f32[4096,128]{1,0:T(8,128)}, u32[]{:S(2)}) %copy-start.3) | copy-done | bytes 2097176
  27.2 2.4 %shard_map.108 = (f32[128,128]{1,0:T(8,128)S(1)}, f32[128,128]{1,0:T(8,128)S(1)}, f32[128,128]{1,0:T(8,128)S(1)}, f32[8,128]{1,0:T(8,128)S(1)}) custom-call(s32[8]{0:T(128)S(1)} %copy-done.7, s32[8,16]{1,0:T(8,128)S(1)} %copy-done.6, s32[1]{0:T(128)} %bitcast.me, s32[1,128]{1,0:T(1,128)S(1)} %reshape.105.idx_ref, f32[4096,128]{1,0:T(8,128)S(1)} %get-tuple-element.36.refs_0_, ...), custom_call_target="tpu_custom_call" | custom-call | tf_op jit(solution)/shard_map/pallas_call | solution.py:213
  29.6 3.6 %collective-permute-start.4 = (f32[128,128]{1,0:T(8,128)S(1)}, f32[128,128]{1,0:T(8,128)S(1)}, u32[]{:S(2)}, u32[]{:S(2)}) collective-permute-start(f32[128,128]{1,0:T(8,128)S(1)} %get-tuple-element.57), channel_id=1, source_target_pairs={{0,1},{2,3},{4,5},{6,7},{8,9},{10,11},{12,13},{14,15},{16,17},{18,... | collective-permute-start | bytes 196616 | tf_op jit(solution)/shard_map/ppermute | solution.py:225
  33.2 0.9 collective-permute-done.4
  34.1 0.7 collective-permute-start.5
  34.8 0.0 collective-permute-done.5
  34.8 0.7 collective-permute-start.6
  35.5 0.0 collective-permute-done.6
  35.5 0.7 collective-permute-start.7
  36.2 0.0 collective-permute-done.7
  36.2 1.3 %collective-permute-start.8 = (f32[128,128]{1,0:T(8,128)S(1)}, f32[128,128]{1,0:T(8,128)S(1)}, u32[]{:S(2)}, u32[]{:S(2)}) collective-permute-start(f32[128,128]{1,0:T(8,128)S(1)} %add.41.mine), channel_id=1, source_target_pairs={{1,0},{3,2},{5,4},{7,6},{9,8},{11,10},{13,12},{15,14},{17,16},{19,... | collective-permute-start | bytes 196616 | tf_op jit(solution)/shard_map/ppermute | solution.py:225
  37.5 15.4 %collective-permute-done.8.other = f32[128,128]{1,0:T(8,128)S(1)} collective-permute-done((f32[128,128]{1,0:T(8,128)S(1)}, f32[128,128]{1,0:T(8,128)S(1)}, u32[]{:S(2)}, u32[]{:S(2)}) %collective-permute-start.8) | collective-permute-done | bytes 65568 | tf_op jit(solution)/shard_map/ppermute | solution.py:225
  52.9 3.1 %shard_map.109 = (f32[128,128]{1,0:T(8,128)S(1)}, f32[1024,128]{1,0:T(8,128)}) custom-call(s32[8]{0:T(128)S(1)} %copy-done.7, s32[8,16]{1,0:T(8,128)S(1)} %copy-done.6, s32[1]{0:T(128)} %bitcast.me, s32[1,128]{1,0:T(1,128)S(1)} %reshape.105.idx_ref, f32[128,128]{1,0:T(8,128)S(1)} %add.41.mine, f32[128,128]{1,0:T(8,128)S(1)} %collective-permute-done.8.other, ...), custom_call_target="tpu_custom_call" | custom-call | tf_op jit(solution)/shard_map/pallas_call | solution.py:213
  55.9 2.3 %collective-permute-start.9 = (f32[128,128]{1,0:T(8,128)S(1)}, f32[128,128]{1,0:T(8,128)S(1)}, u32[]{:S(2)}, u32[]{:S(2)}) collective-permute-start(f32[128,128]{1,0:T(8,128)S(1)} %get-tuple-element.61), channel_id=1, source_target_pairs={{0,1},{2,3},{4,5},{6,7},{8,9},{10,11},{12,13},{14,15},{16,17},{18,... | collective-permute-start | bytes 196616 | tf_op jit(solution)/shard_map/ppermute | solution.py:225
  58.2 0.9 collective-permute-done.9
  59.1 0.7 collective-permute-start.10
  59.8 0.0 collective-permute-done.10
  59.8 0.7 collective-permute-start.11
  60.5 0.0 collective-permute-done.11
  60.5 0.7 collective-permute-start.12
  61.2 0.0 collective-permute-done.12
  61.2 1.3 %collective-permute-start.13 = (f32[128,128]{1,0:T(8,128)S(1)}, f32[128,128]{1,0:T(8,128)S(1)}, u32[]{:S(2)}, u32[]{:S(2)}) collective-permute-start(f32[128,128]{1,0:T(8,128)S(1)} %add.45.mine), channel_id=1, source_target_pairs={{1,0},{3,2},{5,4},{7,6},{9,8},{11,10},{13,12},{15,14},{17,16},{19,... | collective-permute-start | bytes 196616 | tf_op jit(solution)/shard_map/ppermute | solution.py:225
  62.5 15.4 %collective-permute-done.13.other = f32[128,128]{1,0:T(8,128)S(1)} collective-permute-done((f32[128,128]{1,0:T(8,128)S(1)}, f32[128,128]{1,0:T(8,128)S(1)}, u32[]{:S(2)}, u32[]{:S(2)}) %collective-permute-start.13) | collective-permute-done | bytes 65568 | tf_op jit(solution)/shard_map/ppermute | solution.py:225
  77.9 2.4 %shard_map.110 = (f32[128,128]{1,0:T(8,128)S(1)}, f32[1024,128]{1,0:T(8,128)S(1)}) custom-call(s32[8]{0:T(128)S(1)} %copy-done.7, s32[8,16]{1,0:T(8,128)S(1)} %copy-done.6, s32[1]{0:T(128)} %bitcast.me, s32[1,128]{1,0:T(1,128)S(1)} %reshape.105.idx_ref, f32[128,128]{1,0:T(8,128)S(1)} %add.45.mine, f32[128,128]{1,0:T(8,128)S(1)} %collective-permute-done.13.other, ...), custom_call_target="tpu_custom_call" | custom-call | tf_op jit(solution)/shard_map/pallas_call | solution.py:213
  80.3 2.3 %collective-permute-start.14 = (f32[128,128]{1,0:T(8,128)S(1)}, f32[128,128]{1,0:T(8,128)S(1)}, u32[]{:S(2)}, u32[]{:S(2)}) collective-permute-start(f32[128,128]{1,0:T(8,128)S(1)} %get-tuple-element.62), channel_id=1, source_target_pairs={{0,1},{2,3},{4,5},{6,7},{8,9},{10,11},{12,13},{14,15},{16,17},{18,... | collective-permute-start | bytes 196616 | tf_op jit(solution)/shard_map/ppermute | solution.py:225
  82.7 0.9 collective-permute-done.14
  83.5 0.7 collective-permute-start.15
  84.2 0.0 collective-permute-done.15
  84.2 0.7 collective-permute-start.16
  84.9 0.0 collective-permute-done.16
  84.9 0.7 collective-permute-start.17
  85.6 0.0 collective-permute-done.17
  85.7 1.3 %collective-permute-start.18 = (f32[128,128]{1,0:T(8,128)S(1)}, f32[128,128]{1,0:T(8,128)S(1)}, u32[]{:S(2)}, u32[]{:S(2)}) collective-permute-start(f32[128,128]{1,0:T(8,128)S(1)} %add.49.mine), channel_id=1, source_target_pairs={{1,0},{3,2},{5,4},{7,6},{9,8},{11,10},{13,12},{15,14},{17,16},{19,... | collective-permute-start | bytes 196616 | tf_op jit(solution)/shard_map/ppermute | solution.py:225
  87.0 15.4 %collective-permute-done.18.other = f32[128,128]{1,0:T(8,128)S(1)} collective-permute-done((f32[128,128]{1,0:T(8,128)S(1)}, f32[128,128]{1,0:T(8,128)S(1)}, u32[]{:S(2)}, u32[]{:S(2)}) %collective-permute-start.18) | collective-permute-done | bytes 65568 | tf_op jit(solution)/shard_map/ppermute | solution.py:225
  102.3 0.8 shard_map.111
  (18 shorter events, 0.1 us)
Async XLA Ops:
  2.1 10.0 %collective-permute-start = (f32[24,128]{1,0:T(8,128)S(1)}, f32[24,128]{1,0:T(8,128)S(1)}, u32[]{:S(2)}, u32[]{:S(2)}) collective-permute-start(f32[24,128]{1,0:T(8,128)S(1)} %maximum_select_fusion.1), channel_id=1, source_target_pairs={{0,8},{1,9},{2,10},{3,11},{4,12},{5,13},{6,14},{7,15},{8,0},{9,1},... | collective-permute-start | bytes 36872 | tf_op jit(solution)/shard_map/ppermute | solution.py:225
  6.9 6.7 %copy-start.7 = (s32[8]{0:T(128)S(1)}, s32[8]{0:T(128)}, u32[]{:S(2)}) copy-start(s32[8]{0:T(128)} %live.11) | copy-start | bytes 100
  10.7 1.4 %copy-start.4 = (bf16[2,16,128,256]{3,2,1,0:T(8,128)(2,1)}, bf16[2,16,128,256]{3,2,1,0:T(8,128)(2,1)S(1)}, u32[]{:S(2)}) copy-start(bf16[2,16,128,256]{3,2,1,0:T(8,128)(2,1)S(1)} %get-tuple-element.50.feat) | copy-start | bytes 6291460
  12.1 4.9 %collective-permute-start.1 = (f32[48,128]{1,0:T(8,128)S(1)}, f32[48,128]{1,0:T(8,128)S(1)}, u32[]{:S(2)}, u32[]{:S(2)}) collective-permute-start(f32[48,128]{1,0:T(8,128)S(1)} %bitcast.22), channel_id=1, source_target_pairs={{0,4},{1,5},{2,6},{3,7},{4,0},{5,1},{6,2},{7,3},{8,12},{9,13},{10,... | collective-permute-start | bytes 73736 | tf_op jit(solution)/shard_map/ppermute | solution.py:225
  15.6 1.4 %copy-start = (f32[4096,128]{1,0:T(8,128)}, f32[4096,128]{1,0:T(8,128)S(1)}, u32[]{:S(2)}) copy-start(f32[4096,128]{1,0:T(8,128)S(1)} %get-tuple-element.44.refs_1_) | copy-start | bytes 6291460
  17.0 5.3 %copy-start.6 = (s32[8,16]{1,0:T(8,128)S(1)}, s32[8,16]{1,0:T(8,128)}, u32[]{:S(2)}) copy-start(s32[8,16]{1,0:T(8,128)} %tgt.5) | copy-start | bytes 1540
  17.0 5.2 %collective-permute-start.2 = (f32[96,128]{1,0:T(8,128)S(1)}, f32[96,128]{1,0:T(8,128)S(1)}, u32[]{:S(2)}, u32[]{:S(2)}) collective-permute-start(f32[96,128]{1,0:T(8,128)S(1)} %bitcast.20), channel_id=1, source_target_pairs={{0,2},{1,3},{2,0},{3,1},{4,6},{5,7},{6,4},{7,5},{8,10},{9,11},{10,... | collective-permute-start | bytes 147464 | tf_op jit(solution)/shard_map/ppermute | solution.py:225
  20.8 1.3 %copy-start.2 = (f32[4096,128]{1,0:T(8,128)}, f32[4096,128]{1,0:T(8,128)S(1)}, u32[]{:S(2)}) copy-start(f32[4096,128]{1,0:T(8,128)S(1)} %get-tuple-element.49.refs_2_) | copy-start | bytes 6291460
  22.2 3.1 %collective-permute-start.3 = (f32[192,128]{1,0:T(8,128)S(1)}, f32[192,128]{1,0:T(8,128)S(1)}, u32[]{:S(2)}, u32[]{:S(2)}) collective-permute-start(f32[192,128]{1,0:T(8,128)S(1)} %bitcast.18), channel_id=1, source_target_pairs={{0,1},{1,0},{2,3},{3,2},{4,5},{5,4},{6,7},{7,6},{8,9},{9,8},{10,11... | collective-permute-start | bytes 294920 | tf_op jit(solution)/shard_map/ppermute | solution.py:225
  22.4 1.6 %copy-start.5 = (bf16[2,16,128,256]{3,2,1,0:T(8,128)(2,1)S(1)}, bf16[2,16,128,256]{3,2,1,0:T(8,128)(2,1)}, u32[]{:S(2)}) copy-start(bf16[2,16,128,256]{3,2,1,0:T(8,128)(2,1)} %copy-done.4) | copy-start | bytes 6291460
  24.0 1.6 %copy-start.1 = (f32[4096,128]{1,0:T(8,128)S(1)}, f32[4096,128]{1,0:T(8,128)}, u32[]{:S(2)}) copy-start(f32[4096,128]{1,0:T(8,128)} %copy-done) | copy-start | bytes 6291460
  25.6 1.6 %copy-start.3 = (f32[4096,128]{1,0:T(8,128)S(1)}, f32[4096,128]{1,0:T(8,128)}, u32[]{:S(2)}) copy-start(f32[4096,128]{1,0:T(8,128)} %copy-done.2) | copy-start | bytes 6291460
  29.6 4.4 %collective-permute-start.4 = (f32[128,128]{1,0:T(8,128)S(1)}, f32[128,128]{1,0:T(8,128)S(1)}, u32[]{:S(2)}, u32[]{:S(2)}) collective-permute-start(f32[128,128]{1,0:T(8,128)S(1)} %get-tuple-element.57), channel_id=1, source_target_pairs={{0,1},{2,3},{4,5},{6,7},{8,9},{10,11},{12,13},{14,15},{16,17},{18,... | collective-permute-start | bytes 196616 | tf_op jit(solution)/shard_map/ppermute | solution.py:225
  34.1 0.7 collective-permute-start.5
  34.8 0.7 collective-permute-start.6
  35.5 0.7 collective-permute-start.7
  36.2 16.7 %collective-permute-start.8 = (f32[128,128]{1,0:T(8,128)S(1)}, f32[128,128]{1,0:T(8,128)S(1)}, u32[]{:S(2)}, u32[]{:S(2)}) collective-permute-start(f32[128,128]{1,0:T(8,128)S(1)} %add.41.mine), channel_id=1, source_target_pairs={{1,0},{3,2},{5,4},{7,6},{9,8},{11,10},{13,12},{15,14},{17,16},{19,... | collective-permute-start | bytes 196616 | tf_op jit(solution)/shard_map/ppermute | solution.py:225
  55.9 3.2 %collective-permute-start.9 = (f32[128,128]{1,0:T(8,128)S(1)}, f32[128,128]{1,0:T(8,128)S(1)}, u32[]{:S(2)}, u32[]{:S(2)}) collective-permute-start(f32[128,128]{1,0:T(8,128)S(1)} %get-tuple-element.61), channel_id=1, source_target_pairs={{0,1},{2,3},{4,5},{6,7},{8,9},{10,11},{12,13},{14,15},{16,17},{18,... | collective-permute-start | bytes 196616 | tf_op jit(solution)/shard_map/ppermute | solution.py:225
  59.1 0.7 collective-permute-start.10
  59.8 0.7 collective-permute-start.11
  60.5 0.7 collective-permute-start.12
  61.2 16.7 %collective-permute-start.13 = (f32[128,128]{1,0:T(8,128)S(1)}, f32[128,128]{1,0:T(8,128)S(1)}, u32[]{:S(2)}, u32[]{:S(2)}) collective-permute-start(f32[128,128]{1,0:T(8,128)S(1)} %add.45.mine), channel_id=1, source_target_pairs={{1,0},{3,2},{5,4},{7,6},{9,8},{11,10},{13,12},{15,14},{17,16},{19,... | collective-permute-start | bytes 196616 | tf_op jit(solution)/shard_map/ppermute | solution.py:225
  80.3 3.2 %collective-permute-start.14 = (f32[128,128]{1,0:T(8,128)S(1)}, f32[128,128]{1,0:T(8,128)S(1)}, u32[]{:S(2)}, u32[]{:S(2)}) collective-permute-start(f32[128,128]{1,0:T(8,128)S(1)} %get-tuple-element.62), channel_id=1, source_target_pairs={{0,1},{2,3},{4,5},{6,7},{8,9},{10,11},{12,13},{14,15},{16,17},{18,... | collective-permute-start | bytes 196616 | tf_op jit(solution)/shard_map/ppermute | solution.py:225
  83.5 0.7 collective-permute-start.15
  84.2 0.7 collective-permute-start.16
  84.9 0.7 collective-permute-start.17
  85.7 16.7 %collective-permute-start.18 = (f32[128,128]{1,0:T(8,128)S(1)}, f32[128,128]{1,0:T(8,128)S(1)}, u32[]{:S(2)}, u32[]{:S(2)}) collective-permute-start(f32[128,128]{1,0:T(8,128)S(1)} %add.49.mine), channel_id=1, source_target_pairs={{1,0},{3,2},{5,4},{7,6},{9,8},{11,10},{13,12},{15,14},{17,16},{19,... | collective-permute-start | bytes 196616 | tf_op jit(solution)/shard_map/ppermute | solution.py:225
where the time goes:
time: 103 us
  waiting for transfers between devices  48.8 us (47%)
  starting transfers between devices  25.3 us (25%)
  Pallas kernels  18 us (17%)
  local copies, waits for them, and re-layouts  8.27 us (8%)
  other arithmetic  1.79 us (2%)
    ppermute x19, waiting for transfers between devices, exchange(): lax.ppermute(x, 'src', [(i, i ^ d) for i in range(n) if i & 1 in cores])  48.8 us
    ppermute x19, starting transfers between devices, exchange(): lax.ppermute(x, 'src', [(i, i ^ d) for i in range(n) if i & 1 in cores])  25.3 us
    pallas_call x8, Pallas kernels, call(): pl.pallas_call(kernel, out_shape=outs, in_specs=specs, out_specs=[pl.Bloc...  18 us
    unnamed x16, local copies, waits for them, and re-layouts  7.53 us
  transfers between devices with their start and end apart: 19, of which 6 were waited for; matrix products, arithmetic and copies ran while one was open for 1% of the time, Pallas kernels for 9%

commit v1 on v0

--- a/solution.py
+++ b/solution.py
@@ -34,12 +34,32 @@
     return jnp.sum(jnp.where(mask, column, 0.0), axis=0, keepdims=True)
 
 
+def position():
+    return lax.axis_index("src").astype(jnp.int32)
+
+
 def total_of(x):
     return jnp.sum(jnp.sum(x, axis=0, keepdims=True), axis=1, keepdims=True)
 
 
 def steps_of(live_s):
     return (live_s + (STEP - 1)) // STEP
+
+
+def pack_kernel(count_hbm, mass_hbm, lin_hbm, amass_hbm, out_ref, count, sems):
+    local, block = mass_hbm.shape
+    copies = [(count_hbm, count)]
+    for i, x in enumerate((mass_hbm, lin_hbm, amass_hbm)):
+        copies.append((x, out_ref.at[pl.ds(i * local, local)]))
+    copies = [pltpu.make_async_copy(f, t, sems.at[i]) for i, (f, t) in enumerate(copies)]
+    for c in copies:
+        c.start()
+    for c in copies:
+        c.wait()
+    lane = lax.broadcasted_iota(jnp.int32, (1, block), 1)
+    for i in range(local):
+        row = slice(i, i + 1)
+        out_ref[row, :] = jnp.where(lane < count[i], out_ref[row, :], 0.0)
 
 
 def build_tiles(live, first, x_ref, lin_ref, mass_ref, feat, waits, k_ref, la_ref):
@@ -75,22 +95,30 @@
         lax.fori_loop(0, steps_of(live[at]), tiles, 0)
 
 
-def first_build(live_hbm, x_hbm, feat, lin_hbm, mass_hbm, *refs):
-    k_ref, la_ref, x_ref, lin_ref, mass_ref, *rest = refs
-    later, (live, own, sems) = rest[:-3], rest[-3:]
+def first_build(live_hbm, tgt_hbm, x_hbm, feat, lin_hbm, mass_hbm, *refs):
+    k_ref, la_ref, hit_ref, x_ref, lin_ref, mass_ref, *rest = refs
+    later, (live, tgt, flags, own, sems) = rest[:-5], rest[-5:]
     each = own.shape[0]
+    slots = tgt.shape[1]
     copies = [(live_hbm, live), (x_hbm, x_ref), (lin_hbm, lin_ref), (mass_hbm, mass_ref)]
+    copies += [(tgt_hbm, tgt)]
     copies += [(feat.at[s], own.at[s]) for s in range(each)]
     copies += [(feat.at[pl.ds((i + 1) * each, each)], to) for i, to in enumerate(later)]
     copies = [pltpu.make_async_copy(f, t, sems.at[i]) for i, (f, t) in enumerate(copies)]
     for c in copies:
         c.start()
-    for c in copies[:4]:
+    for c in copies[:5]:
         c.wait()
+    lane = lax.broadcasted_iota(jnp.int32, (1, flags.shape[1]), 1)
+    for at in range(flags.shape[0]):
+        s, k = divmod(at, slots)
+        row = jnp.where(k < live[s], tgt[s, k], -1)
+        flags[at : at + 1, :] = jnp.where(lane == row, 1.0, 0.0)
+    hit_ref[...] = jnp.transpose(flags[...]).astype(jnp.bfloat16)
     build_tiles(
-        live, 0, x_ref, lin_ref, mass_ref, own, copies[4 : 4 + each], k_ref, la_ref
-    )
-    for c in copies[4 + each :]:
+        live, 0, x_ref, lin_ref, mass_ref, own, copies[5 : 5 + each], k_ref, la_ref
+    )
+    for c in copies[5 + each :]:
         c.wait()
 
 
@@ -98,7 +126,7 @@
     build_tiles(live, first, x_ref, lin_ref, mass_ref, feat, (), k_ref, la_ref)
 
 
-def sweep(live, tgt, idx_ref, w_ref, k_refs, la_refs, dense_ref, acc_ref, u_ref, col_ref):
+def sweep(live, tgt, hit_ref, w_ref, k_refs, la_refs, dense_ref, acc_ref, u_ref, col_ref):
     blocks, slots = tgt.shape
     block = w_ref.shape[1]
     every = w_ref.shape[0] - 8
@@ -139,8 +167,7 @@
 
         lax.fori_loop(0, steps_of(live[s]), add_col, 0)
     col = col_ref[...]
-    rows = lax.broadcasted_iota(jnp.int32, (every, blocks * slots), 0)
-    hit = jnp.where(rows == idx_ref[...], 1.0, 0.0).astype(jnp.bfloat16)
+    hit = hit_ref[...]
     dense = jnp.zeros((every, block), jnp.float32)
     for _ in range(3):
         piece = col.astype(jnp.bfloat16)
@@ -153,7 +180,7 @@
     return jnp.exp(F * (jnp.log(num) - jnp.log(den)))
 
 
-def first_sweep(npieces, live, tgt, me, idx_ref, *refs):
+def first_sweep(npieces, live, tgt, hit_ref, *refs):
     k_refs, la_refs = refs[:npieces], refs[npieces : 2 * npieces]
     parts = refs[2 * npieces : 2 * npieces + 2]
     dense_ref, b_ref, et_ref, tot_ref, w_ref, acc_ref, u_ref, col_ref = refs[2 * npieces + 2 :]
@@ -165,7 +192,7 @@
         m = sum(((at >> r) & 1) << (bits - 1 - r) for r in range(bits))
         part = parts[at // (n // 2)]
         at = (at % (n // 2)) * 3 * local
-        rows = pl.ds(pl.multiple_of((me[0] ^ m) * local, local), local)
+        rows = pl.ds(pl.multiple_of((position() ^ m) * local, local), local)
         b = part[at : at + local, :]
         et = jnp.exp((-ALPHA / EPS) * part[at + local : at + 2 * local, :])
         b_ref[rows, :] = b
@@ -174,29 +201,29 @@
         am += part[at + 2 * local : at + 3 * local, :]
     tot = jnp.sqrt(total_of(am) * total_of(b_ref[...]))
     tot_ref[...] = jnp.broadcast_to(tot, tot_ref.shape)
-    sweep(live, tgt, idx_ref, w_ref, k_refs, la_refs, dense_ref, acc_ref, u_ref, col_ref)
-
-
-def new_scale(me, mine, other, b_ref, et_ref, tot_ref):
+    sweep(live, tgt, hit_ref, w_ref, k_refs, la_refs, dense_ref, acc_ref, u_ref, col_ref)
+
+
+def new_scale(mine, other, b_ref, et_ref, tot_ref):
     b = b_ref[...]
-    col = jnp.where((me[0] & 1) == 1, mine[...], other[...]) * et_ref[...]
+    col = jnp.where(position() & 1 == 1, mine[...], other[...]) * et_ref[...]
     t = jnp.where(b > 0.0, power_of_ratio(b, col), 0.0)
     return t, jnp.sqrt(tot_ref[0:1, 0:1] / total_of(t * col))
 
 
-def next_sweep(npieces, live, tgt, me, idx_ref, mine, other, b_ref, et_ref, tot_ref, *refs):
+def next_sweep(npieces, live, tgt, hit_ref, mine, other, b_ref, et_ref, tot_ref, *refs):
     k_refs, la_refs = refs[:npieces], refs[npieces : 2 * npieces]
     dense_ref, u_ref, w_ref, acc_ref, col_ref = refs[2 * npieces :]
-    t, factor = new_scale(me, mine, other, b_ref, et_ref, tot_ref)
+    t, factor = new_scale(mine, other, b_ref, et_ref, tot_ref)
     w_ref[: b_ref.shape[0], :] = t * (factor * et_ref[...])
-    sweep(live, tgt, idx_ref, w_ref, k_refs, la_refs, dense_ref, acc_ref, u_ref, col_ref)
-
-
-def last_kernel(me, mine, other, b_ref, et_ref, tot_ref, u_ref, src_ref, tgt_ref, t_ref):
+    sweep(live, tgt, hit_ref, w_ref, k_refs, la_refs, dense_ref, acc_ref, u_ref, col_ref)
+
+
+def last_kernel(mine, other, b_ref, et_ref, tot_ref, u_ref, src_ref, tgt_ref, t_ref):
     local, block = src_ref.shape
-    t, factor = new_scale(me, mine, other, b_ref, et_ref, tot_ref)
+    t, factor = new_scale(mine, other, b_ref, et_ref, tot_ref)
     t_ref[...] = t * factor
-    tgt_ref[...] = t_ref[pl.ds(pl.multiple_of(me[0] * local, local), local), :]
+    tgt_ref[...] = t_ref[pl.ds(pl.multiple_of(position() * local, local), local), :]
     mask = diag_mask(block)
     for s in range(local):
         src_ref[s : s + 1, :] = to_row(u_ref[s * block : (s + 1) * block, :] * factor, mask)
@@ -222,7 +249,7 @@
 
 
 def exchange(x, n, d, cores=(0, 1)):
-    return lax.ppermute(x, "src", [(i, i ^ d) for i in range(n) if i & 1 in cores])
+    return lax.ppermute(x, "src", [(i, i ^ d if i & 1 in cores else i) for i in range(n)])
 
 
 def shards(
@@ -231,18 +258,20 @@
     f32 = jnp.float32
     local, slots, block, width = tile_feat.shape
     n = lax.axis_size("src")
-    me = lax.axis_index("src").astype(jnp.int32).reshape(1)
     every = local * n
     pairs = local * slots
     lin = src_lin.reshape(local, block)
     amass = src_mass.reshape(local, block)
-    part = jnp.concatenate([tgt_mass, tgt_lin, src_mass]).reshape(3 * local, block)
-    count = jnp.concatenate([tgt_count, jnp.full((2 * local,), block, jnp.int32)])
-    part = jnp.where(lax.broadcasted_iota(jnp.int32, part.shape, 1) < count[:, None], part, 0.0)
-
     def shape(rows, cols=block, dtype=f32):
         return pltpu.VMEM((rows, cols), dtype)
 
+    (part,) = call(
+        pack_kernel,
+        (tgt_count, tgt_mass.reshape(local, block), tgt_lin.reshape(local, block), amass),
+        (shape(3 * local),),
+        scratch=[SMEM((local,), jnp.int32), pltpu.SemaphoreType.DMA((4,))],
+        hbm=(0, 1, 2, 3),
+    )
     each = local // PIECES
     feats = pltpu.VMEM((each, slots, block, width), tile_feat.dtype)
     cost = dict(
@@ -259,12 +288,13 @@
     for at, d in enumerate(order):
         got = exchange(part, n, d)
         if at == 0:
-            k0, la0, xv, linv, massv, *later = call(
+            k0, la0, hit, xv, linv, massv, *later = call(
                 first_build,
-                (tile_live, src_feat, tile_feat, lin, amass),
+                (tile_live, tile_tgt, src_feat, tile_feat, lin, amass),
                 (
                     shape(each * slots * block),
                     shape(each * block),
+                    shape(every, pairs, jnp.bfloat16),
                     shape(local * block, width, src_feat.dtype),
                     shape(local),
                     shape(local),
@@ -272,10 +302,12 @@
                 ),
                 scratch=[
                     SMEM((local,), jnp.int32),
+                    SMEM((local, slots), jnp.int32),
+                    VMEM((pairs, every), f32),
                     feats,
-                    pltpu.SemaphoreType.DMA((4 + each + PIECES - 1,)),
+                    pltpu.SemaphoreType.DMA((5 + each + PIECES - 1,)),
                 ],
-                hbm=(0, 1, 2, 3, 4),
+                hbm=(0, 1, 2, 3, 4, 5),
                 **cost,
             )
             kern.append(k0)
@@ -296,40 +328,37 @@
                 part, later[at], kern[-1] = lax.optimization_barrier(
                     (part, later[at], kern[-1])
                 )
-    slot = lax.broadcasted_iota(jnp.int32, (local, slots), 1)
-    idx = jnp.where(slot < tile_live[:, None], tile_tgt, -1).reshape(1, pairs)
     acc = VMEM((local * block, block), f32)
     col = VMEM((pairs, block), f32)
     w = VMEM((every + 8, block), f32)
     mine, b_all, et_all, tot = call(
         functools.partial(first_sweep, PIECES),
-        (tile_live, tile_tgt, me, idx, *kern, *la, part, got),
+        (tile_live, tile_tgt, hit, *kern, *la, part, got),
         (shape(every), shape(every), shape(every), shape(8)),
         scratch=[w, acc, acc, col],
-        smem=3,
+        smem=2,
     )
     u = None
     for iteration in range(ITERS):
-        mine = mine + exchange(mine, n, 1, (0,))
+        mine = mine + exchange(mine, n, 1)
         d = 2
         while d < n:
             mine = mine + exchange(mine, n, d, (1,))
             d *= 2
-        other = exchange(mine, n, 1, (1,))
+        other = exchange(mine, n, 1)
         if iteration < ITERS - 1:
             mine, u = call(
                 functools.partial(next_sweep, PIECES),
-                (tile_live, tile_tgt, me, idx, mine, other, b_all, et_all, tot, *kern, *la),
+                (tile_live, tile_tgt, hit, mine, other, b_all, et_all, tot, *kern, *la),
                 (shape(every), shape(local * block)),
                 scratch=[w, acc, col],
-                smem=3,
+                smem=2,
             )
     src, tgt = call(
         last_kernel,
-        (me, mine, other, b_all, et_all, tot, u),
+        (mine, other, b_all, et_all, tot, u),
         [jax.ShapeDtypeStruct((local, block), f32)] * 2,
         scratch=[VMEM((every, block), f32)],
-        smem=1,
     )
     return (src.reshape(-1), tgt.reshape(-1))
 

time: 103 us -> 87.3 us (0.85)
  waiting for transfers between devices: 48.8 us -> 6.59 us
  starting transfers between devices: 25.3 us -> 58.3 us
  local copies, waits for them, and re-layouts: 8.27 us -> 0.01 us
  Pallas kernels: 18 us -> 21.4 us
  other arithmetic: 1.79 us -> 0.15 us
    ppermute x19, waiting for transfers between devices: 48.8 us -> 6.59 us  [exchange(): lax.ppermute(x, 'src', [(i, i ^ d if i & 1 in cores else i) for i in rang...]
    ppermute x19, starting transfers between devices: 25.3 us -> 58.3 us  [exchange(): lax.ppermute(x, 'src', [(i, i ^ d if i & 1 in cores else i) for i in rang...]
    unnamed x16 -> x4, local copies, waits for them, and re-layouts: 7.53 us -> 0.01 us
    pallas_call x8 -> x9, Pallas kernels: 18 us -> 21.4 us  [call(): pl.pallas_call(kernel, out_shape=outs, in_specs=specs, out_specs=[pl.Bloc...]
    select_n x3 -> x0, other arithmetic: 1.65 us -> none  [the longest x2 1.58 us: shards(): jnp.where(lax.broadcasted_iota(jnp.int32, part.shape, 1) < count[:, None]...]
  transfers between devices with their start and end apart: 19 -> 19, of which waited for: 6 -> 7; matrix products, arithmetic and copies ran while one was open for 1% -> 0% of each run, Pallas kernels for 9% -> 12%
where the time goes in v1:
time: 87.3 us; the launch traced here: 87.4 us
  starting transfers between devices  58.3 us (67%)
  Pallas kernels  21.4 us (25%)
  waiting for transfers between devices  6.59 us (8%)
  between operations  0.98 us (1%)
    ppermute x19, starting transfers between devices, exchange(): lax.ppermute(x, 'src', [(i, i ^ d if i & 1 in cores else i) for i in rang...  58.3 us
    pallas_call x9, Pallas kernels, call(): pl.pallas_call(kernel, out_shape=outs, in_specs=specs, out_specs=[pl.Bloc...  21.4 us
    ppermute x19, waiting for transfers between devices, exchange(): lax.ppermute(x, 'src', [(i, i ^ d if i & 1 in cores else i) for i in rang...  6.59 us
  transfers between devices with their start and end apart: 19, of which 7 were waited for; matrix products, arithmetic and copies ran while one was open for 0% of the time, Pallas kernels for 12%

profile of v1, /device:TPU:0, one launch (start us, length us, event | category | flops | bytes accessed | tf_op | source)
XLA Modules:
  0.0 87.4 jit_solution(9831807643998321489)
XLA Ops:
  0.6 0.8 shard_map.105
  1.4 4.1 %collective-permute-start = (f32[24,128]{1,0:T(8,128)S(1)}, f32[24,128]{1,0:T(8,128)S(1)}, u32[]{:S(2)}, u32[]{:S(2)}) collective-permute-start(f32[24,128]{1,0:T(8,128)S(1)} %shard_map.105), channel_id=1, source_target_pairs={{0,8},{1,9},{2,10},{3,11},{4,12},{5,13},{6,14},{7,15},{8,0},{9,1},... | collective-permute-start | bytes 36872 | tf_op jit(solution)/shard_map/ppermute | solution.py:252
  5.5 0.0 copy-start.1
  5.5 3.8 %shard_map.104 = (f32[4096,128]{1,0:T(8,128)S(1)}, f32[256,128]{1,0:T(8,128)S(1)}, bf16[128,128]{1,0:T(8,128)(2,1)S(1)}, bf16[1024,256]{1,0:T(8,128)(2,1)S(1)}, ...) custom-call(s32[8]{0:T(128)} %live.11, ...), custom_call_target="tpu_custom_call" | custom-call | flops 268435456 | bytes 2097152 | tf_op jit(solution)/shard_map/pallas_call | solution.py:240
  9.3 0.0 collective-permute-done
  9.3 1.6 %collective-permute-start.1 = (f32[48,128]{1,0:T(8,128)S(1)}, f32[48,128]{1,0:T(8,128)S(1)}, u32[]{:S(2)}, u32[]{:S(2)}) collective-permute-start(f32[48,128]{1,0:T(8,128)S(1)} %bitcast.20), channel_id=1, source_target_pairs={{0,4},{1,5},{2,6},{3,7},{4,0},{5,1},{6,2},{7,3},{8,12},{9,13},{10,... | collective-permute-start | bytes 73736 | tf_op jit(solution)/shard_map/ppermute | solution.py:252
  10.9 0.0 copy-done.1
  10.9 2.5 %shard_map.106 = (f32[4096,128]{1,0:T(8,128)S(1)}, f32[256,128]{1,0:T(8,128)S(1)}) custom-call(s32[8]{0:T(128)S(1)} %copy-done.1, bf16[1024,256]{1,0:T(8,128)(2,1)S(1)} %get-tuple-element.41.x_ref, bf16[2,16,128,256]{3,2,1,0:T(8,128)(2,1)S(1)} %get-tuple-element.42.feat, f32[8,128]{1,0:T(8,128)S(1)} %get-tuple-element.43.lin_ref, ...), custom_call_target="tpu_custom_call" | custom-call | flops 268435456 | bytes 2097152 | tf_op jit(solution)/shard_map/pallas_call | solution.py:240
  13.4 0.0 collective-permute-done.1
  13.4 0.0 copy-start
  13.5 1.8 %collective-permute-start.2 = (f32[96,128]{1,0:T(8,128)S(1)}, f32[96,128]{1,0:T(8,128)S(1)}, u32[]{:S(2)}, u32[]{:S(2)}) collective-permute-start(f32[96,128]{1,0:T(8,128)S(1)} %bitcast.18), channel_id=1, source_target_pairs={{0,2},{1,3},{2,0},{3,1},{4,6},{5,7},{6,4},{7,5},{8,10},{9,11},{10,... | collective-permute-start | bytes 147464 | tf_op jit(solution)/shard_map/ppermute | solution.py:252
  15.3 2.0 %shard_map.107 = (f32[4096,128]{1,0:T(8,128)S(1)}, f32[256,128]{1,0:T(8,128)S(1)}) custom-call(s32[8]{0:T(128)S(1)} %copy-done.1, bf16[1024,256]{1,0:T(8,128)(2,1)S(1)} %get-tuple-element.41.x_ref, bf16[2,16,128,256]{3,2,1,0:T(8,128)(2,1)S(1)} %get-tuple-element.49.feat, f32[8,128]{1,0:T(8,128)S(1)} %get-tuple-element.43.lin_ref, ...), custom_call_target="tpu_custom_call" | custom-call | flops 268435456 | bytes 2097152 | tf_op jit(solution)/shard_map/pallas_call | solution.py:240
  17.3 0.3 collective-permute-done.2
  17.6 0.1 collective-permute-start.3
  17.7 2.5 %shard_map.108 = (f32[4096,128]{1,0:T(8,128)S(1)}, f32[256,128]{1,0:T(8,128)S(1)}) custom-call(s32[8]{0:T(128)S(1)} %copy-done.1, bf16[1024,256]{1,0:T(8,128)(2,1)S(1)} %get-tuple-element.41.x_ref, bf16[2,16,128,256]{3,2,1,0:T(8,128)(2,1)S(1)} %get-tuple-element.52.feat, f32[8,128]{1,0:T(8,128)S(1)} %get-tuple-element.43.lin_ref, ...), custom_call_target="tpu_custom_call" | custom-call | flops 268435456 | bytes 2097152 | tf_op jit(solution)/shard_map/pallas_call | solution.py:240
  20.2 0.0 collective-permute-done.3.refs_9_
  20.2 0.0 copy-done
  20.2 2.8 %shard_map.109 = (f32[128,128]{1,0:T(8,128)S(1)}, f32[128,128]{1,0:T(8,128)S(1)}, f32[128,128]{1,0:T(8,128)S(1)}, f32[8,128]{1,0:T(8,128)S(1)}) custom-call(s32[8]{0:T(128)S(1)} %copy-done.1, s32[8,16]{1,0:T(8,128)S(1)} %copy-done, bf16[128,128]{1,0:T(8,128)(2,1)S(1)} %get-tuple-element.35.hit_ref, f32[4096,128]{1,0:T(8,128)S(1)} %get-tuple-element.38.refs_0_, ...), custom_call_target="tpu_custom_call" | custom-call | tf_op jit(solution)/shard_map/pallas_call | solution.py:240
  23.1 0.1 collective-permute-start.4
  23.1 1.2 %collective-permute-done.4 = f32[128,128]{1,0:T(8,128)S(1)} collective-permute-done((f32[128,128]{1,0:T(8,128)S(1)}, f32[128,128]{1,0:T(8,128)S(1)}, u32[]{:S(2)}, u32[]{:S(2)}) %collective-permute-start.4) | collective-permute-done | bytes 65568 | tf_op jit(solution)/shard_map/ppermute | solution.py:252
  24.4 0.7 collective-permute-start.5
  25.1 0.0 collective-permute-done.5
  25.1 0.7 collective-permute-start.6
  25.8 0.0 collective-permute-done.6
  25.8 0.7 collective-permute-start.7
  26.5 0.0 collective-permute-done.7
  26.5 14.9 %collective-permute-start.8 = (f32[128,128]{1,0:T(8,128)S(1)}, f32[128,128]{1,0:T(8,128)S(1)}, u32[]{:S(2)}, u32[]{:S(2)}) collective-permute-start(f32[128,128]{1,0:T(8,128)S(1)} %add.39.mine), channel_id=1, source_target_pairs={{0,1},{1,0},{2,3},{3,2},{4,5},{5,4},{6,7},{7,6},{8,9},{9,8},{10,11... | collective-permute-start | bytes 196616 | tf_op jit(solution)/shard_map/ppermute | solution.py:252
  41.4 0.9 %collective-permute-done.8.other = f32[128,128]{1,0:T(8,128)S(1)} collective-permute-done((f32[128,128]{1,0:T(8,128)S(1)}, f32[128,128]{1,0:T(8,128)S(1)}, u32[]{:S(2)}, u32[]{:S(2)}) %collective-permute-start.8) | collective-permute-done | bytes 65568 | tf_op jit(solution)/shard_map/ppermute | solution.py:252
  42.3 3.4 %shard_map.110 = (f32[128,128]{1,0:T(8,128)S(1)}, f32[1024,128]{1,0:T(8,128)}) custom-call(s32[8]{0:T(128)S(1)} %copy-done.1, s32[8,16]{1,0:T(8,128)S(1)} %copy-done, bf16[128,128]{1,0:T(8,128)(2,1)S(1)} %get-tuple-element.35.hit_ref, f32[128,128]{1,0:T(8,128)S(1)} %add.39.mine, f32[128,128]{1,0:T(8,128)S(1)} %collective-permute-done.8.other, ...), custom_call_target="tpu_custom_call" | custom-call | tf_op jit(solution)/shard_map/pallas_call | solution.py:240
  45.7 0.1 collective-permute-start.9
  45.8 1.1 %collective-permute-done.9 = f32[128,128]{1,0:T(8,128)S(1)} collective-permute-done((f32[128,128]{1,0:T(8,128)S(1)}, f32[128,128]{1,0:T(8,128)S(1)}, u32[]{:S(2)}, u32[]{:S(2)}) %collective-permute-start.9) | collective-permute-done | bytes 65568 | tf_op jit(solution)/shard_map/ppermute | solution.py:252
  47.0 0.7 collective-permute-start.10
  47.7 0.0 collective-permute-done.10
  47.7 0.7 collective-permute-start.11
  48.4 0.0 collective-permute-done.11
  48.4 0.7 collective-permute-start.12
  49.1 0.0 collective-permute-done.12
  49.1 14.9 %collective-permute-start.13 = (f32[128,128]{1,0:T(8,128)S(1)}, f32[128,128]{1,0:T(8,128)S(1)}, u32[]{:S(2)}, u32[]{:S(2)}) collective-permute-start(f32[128,128]{1,0:T(8,128)S(1)} %add.43.mine), channel_id=1, source_target_pairs={{0,1},{1,0},{2,3},{3,2},{4,5},{5,4},{6,7},{7,6},{8,9},{9,8},{10,11... | collective-permute-start | bytes 196616 | tf_op jit(solution)/shard_map/ppermute | solution.py:252
  64.0 0.9 %collective-permute-done.13.other = f32[128,128]{1,0:T(8,128)S(1)} collective-permute-done((f32[128,128]{1,0:T(8,128)S(1)}, f32[128,128]{1,0:T(8,128)S(1)}, u32[]{:S(2)}, u32[]{:S(2)}) %collective-permute-start.13) | collective-permute-done | bytes 65568 | tf_op jit(solution)/shard_map/ppermute | solution.py:252
  64.9 2.8 %shard_map.111 = (f32[128,128]{1,0:T(8,128)S(1)}, f32[1024,128]{1,0:T(8,128)S(1)}) custom-call(s32[8]{0:T(128)S(1)} %copy-done.1, s32[8,16]{1,0:T(8,128)S(1)} %copy-done, bf16[128,128]{1,0:T(8,128)(2,1)S(1)} %get-tuple-element.35.hit_ref, f32[128,128]{1,0:T(8,128)S(1)} %add.43.mine, f32[128,128]{1,0:T(8,128)S(1)} %collective-permute-done.13.other, ...), custom_call_target="tpu_custom_call" | custom-call | tf_op jit(solution)/shard_map/pallas_call | solution.py:240
  67.7 0.2 collective-permute-start.14
  67.8 1.1 %collective-permute-done.14 = f32[128,128]{1,0:T(8,128)S(1)} collective-permute-done((f32[128,128]{1,0:T(8,128)S(1)}, f32[128,128]{1,0:T(8,128)S(1)}, u32[]{:S(2)}, u32[]{:S(2)}) %collective-permute-start.14) | collective-permute-done | bytes 65568 | tf_op jit(solution)/shard_map/ppermute | solution.py:252
  69.0 0.7 collective-permute-start.15
  69.7 0.0 collective-permute-done.15
  69.7 0.7 collective-permute-start.16
  70.4 0.0 collective-permute-done.16
  70.4 0.7 collective-permute-start.17
  71.1 0.0 collective-permute-done.17
  71.1 14.6 %collective-permute-start.18 = (f32[128,128]{1,0:T(8,128)S(1)}, f32[128,128]{1,0:T(8,128)S(1)}, u32[]{:S(2)}, u32[]{:S(2)}) collective-permute-start(f32[128,128]{1,0:T(8,128)S(1)} %add.47.mine), channel_id=1, source_target_pairs={{0,1},{1,0},{2,3},{3,2},{4,5},{5,4},{6,7},{7,6},{8,9},{9,8},{10,11... | collective-permute-start | bytes 196616 | tf_op jit(solution)/shard_map/ppermute | solution.py:252
  85.7 0.9 %collective-permute-done.18.other = f32[128,128]{1,0:T(8,128)S(1)} collective-permute-done((f32[128,128]{1,0:T(8,128)S(1)}, f32[128,128]{1,0:T(8,128)S(1)}, u32[]{:S(2)}, u32[]{:S(2)}) %collective-permute-start.18) | collective-permute-done | bytes 65568 | tf_op jit(solution)/shard_map/ppermute | solution.py:252
  86.6 0.8 shard_map.112
  (15 shorter events, 0.1 us)
Async XLA Ops:
  1.4 7.9 %collective-permute-start = (f32[24,128]{1,0:T(8,128)S(1)}, f32[24,128]{1,0:T(8,128)S(1)}, u32[]{:S(2)}, u32[]{:S(2)}) collective-permute-start(f32[24,128]{1,0:T(8,128)S(1)} %shard_map.105), channel_id=1, source_target_pairs={{0,8},{1,9},{2,10},{3,11},{4,12},{5,13},{6,14},{7,15},{8,0},{9,1},... | collective-permute-start | bytes 36872 | tf_op jit(solution)/shard_map/ppermute | solution.py:252
  5.5 5.4 %copy-start.1 = (s32[8]{0:T(128)S(1)}, s32[8]{0:T(128)}, u32[]{:S(2)}) copy-start(s32[8]{0:T(128)} %live.11) | copy-start | bytes 100
  9.3 4.1 %collective-permute-start.1 = (f32[48,128]{1,0:T(8,128)S(1)}, f32[48,128]{1,0:T(8,128)S(1)}, u32[]{:S(2)}, u32[]{:S(2)}) collective-permute-start(f32[48,128]{1,0:T(8,128)S(1)} %bitcast.20), channel_id=1, source_target_pairs={{0,4},{1,5},{2,6},{3,7},{4,0},{5,1},{6,2},{7,3},{8,12},{9,13},{10,... | collective-permute-start | bytes 73736 | tf_op jit(solution)/shard_map/ppermute | solution.py:252
  13.4 6.8 %copy-start = (s32[8,16]{1,0:T(8,128)S(1)}, s32[8,16]{1,0:T(8,128)}, u32[]{:S(2)}) copy-start(s32[8,16]{1,0:T(8,128)} %tgt.5) | copy-start | bytes 1540
  13.5 4.2 %collective-permute-start.2 = (f32[96,128]{1,0:T(8,128)S(1)}, f32[96,128]{1,0:T(8,128)S(1)}, u32[]{:S(2)}, u32[]{:S(2)}) collective-permute-start(f32[96,128]{1,0:T(8,128)S(1)} %bitcast.18), channel_id=1, source_target_pairs={{0,2},{1,3},{2,0},{3,1},{4,6},{5,7},{6,4},{7,5},{8,10},{9,11},{10,... | collective-permute-start | bytes 147464 | tf_op jit(solution)/shard_map/ppermute | solution.py:252
  17.6 2.6 %collective-permute-start.3 = (f32[192,128]{1,0:T(8,128)S(1)}, f32[192,128]{1,0:T(8,128)S(1)}, u32[]{:S(2)}, u32[]{:S(2)}) collective-permute-start(f32[192,128]{1,0:T(8,128)S(1)} %bitcast.15), channel_id=1, source_target_pairs={{0,1},{1,0},{2,3},{3,2},{4,5},{5,4},{6,7},{7,6},{8,9},{9,8},{10,11... | collective-permute-start | bytes 294920 | tf_op jit(solution)/shard_map/ppermute | solution.py:252
  23.1 1.3 %collective-permute-start.4 = (f32[128,128]{1,0:T(8,128)S(1)}, f32[128,128]{1,0:T(8,128)S(1)}, u32[]{:S(2)}, u32[]{:S(2)}) collective-permute-start(f32[128,128]{1,0:T(8,128)S(1)} %get-tuple-element.59), channel_id=1, source_target_pairs={{0,1},{1,0},{2,3},{3,2},{4,5},{5,4},{6,7},{7,6},{8,9},{9,8},{10,11... | collective-permute-start | bytes 196616 | tf_op jit(solution)/shard_map/ppermute | solution.py:252
  24.4 0.7 collective-permute-start.5
  25.1 0.7 collective-permute-start.6
  25.8 0.7 collective-permute-start.7
  26.5 15.8 %collective-permute-start.8 = (f32[128,128]{1,0:T(8,128)S(1)}, f32[128,128]{1,0:T(8,128)S(1)}, u32[]{:S(2)}, u32[]{:S(2)}) collective-permute-start(f32[128,128]{1,0:T(8,128)S(1)} %add.39.mine), channel_id=1, source_target_pairs={{0,1},{1,0},{2,3},{3,2},{4,5},{5,4},{6,7},{7,6},{8,9},{9,8},{10,11... | collective-permute-start | bytes 196616 | tf_op jit(solution)/shard_map/ppermute | solution.py:252
  45.7 1.3 %collective-permute-start.9 = (f32[128,128]{1,0:T(8,128)S(1)}, f32[128,128]{1,0:T(8,128)S(1)}, u32[]{:S(2)}, u32[]{:S(2)}) collective-permute-start(f32[128,128]{1,0:T(8,128)S(1)} %get-tuple-element.63), channel_id=1, source_target_pairs={{0,1},{1,0},{2,3},{3,2},{4,5},{5,4},{6,7},{7,6},{8,9},{9,8},{10,11... | collective-permute-start | bytes 196616 | tf_op jit(solution)/shard_map/ppermute | solution.py:252
  47.0 0.7 collective-permute-start.10
  47.7 0.7 collective-permute-start.11
  48.4 0.7 collective-permute-start.12
  49.1 15.8 %collective-permute-start.13 = (f32[128,128]{1,0:T(8,128)S(1)}, f32[128,128]{1,0:T(8,128)S(1)}, u32[]{:S(2)}, u32[]{:S(2)}) collective-permute-start(f32[128,128]{1,0:T(8,128)S(1)} %add.43.mine), channel_id=1, source_target_pairs={{0,1},{1,0},{2,3},{3,2},{4,5},{5,4},{6,7},{7,6},{8,9},{9,8},{10,11... | collective-permute-start | bytes 196616 | tf_op jit(solution)/shard_map/ppermute | solution.py:252
  67.7 1.3 %collective-permute-start.14 = (f32[128,128]{1,0:T(8,128)S(1)}, f32[128,128]{1,0:T(8,128)S(1)}, u32[]{:S(2)}, u32[]{:S(2)}) collective-permute-start(f32[128,128]{1,0:T(8,128)S(1)} %get-tuple-element.64), channel_id=1, source_target_pairs={{0,1},{1,0},{2,3},{3,2},{4,5},{5,4},{6,7},{7,6},{8,9},{9,8},{10,11... | collective-permute-start | bytes 196616 | tf_op jit(solution)/shard_map/ppermute | solution.py:252
  69.0 0.7 collective-permute-start.15
  69.7 0.7 collective-permute-start.16
  70.4 0.7 collective-permute-start.17
  71.1 15.5 %collective-permute-start.18 = (f32[128,128]{1,0:T(8,128)S(1)}, f32[128,128]{1,0:T(8,128)S(1)}, u32[]{:S(2)}, u32[]{:S(2)}) collective-permute-start(f32[128,128]{1,0:T(8,128)S(1)} %add.47.mine), channel_id=1, source_target_pairs={{0,1},{1,0},{2,3},{3,2},{4,5},{5,4},{6,7},{7,6},{8,9},{9,8},{10,11... | collective-permute-start | bytes 196616 | tf_op jit(solution)/shard_map/ppermute | solution.py:252

commit v2 on v1

--- a/solution.py
+++ b/solution.py
@@ -204,24 +204,24 @@
     sweep(live, tgt, hit_ref, w_ref, k_refs, la_refs, dense_ref, acc_ref, u_ref, col_ref)
 
 
-def new_scale(mine, other, b_ref, et_ref, tot_ref):
+def new_scale(mine, b_ref, et_ref, tot_ref):
     b = b_ref[...]
-    col = jnp.where(position() & 1 == 1, mine[...], other[...]) * et_ref[...]
+    col = mine[...] * et_ref[...]
     t = jnp.where(b > 0.0, power_of_ratio(b, col), 0.0)
     return t, jnp.sqrt(tot_ref[0:1, 0:1] / total_of(t * col))
 
 
-def next_sweep(npieces, live, tgt, hit_ref, mine, other, b_ref, et_ref, tot_ref, *refs):
+def next_sweep(npieces, live, tgt, hit_ref, mine, b_ref, et_ref, tot_ref, *refs):
     k_refs, la_refs = refs[:npieces], refs[npieces : 2 * npieces]
     dense_ref, u_ref, w_ref, acc_ref, col_ref = refs[2 * npieces :]
-    t, factor = new_scale(mine, other, b_ref, et_ref, tot_ref)
+    t, factor = new_scale(mine, b_ref, et_ref, tot_ref)
     w_ref[: b_ref.shape[0], :] = t * (factor * et_ref[...])
     sweep(live, tgt, hit_ref, w_ref, k_refs, la_refs, dense_ref, acc_ref, u_ref, col_ref)
 
 
-def last_kernel(mine, other, b_ref, et_ref, tot_ref, u_ref, src_ref, tgt_ref, t_ref):
+def last_kernel(mine, b_ref, et_ref, tot_ref, u_ref, src_ref, tgt_ref, t_ref):
     local, block = src_ref.shape
-    t, factor = new_scale(mine, other, b_ref, et_ref, tot_ref)
+    t, factor = new_scale(mine, b_ref, et_ref, tot_ref)
     t_ref[...] = t * factor
     tgt_ref[...] = t_ref[pl.ds(pl.multiple_of(position() * local, local), local), :]
     mask = diag_mask(block)
@@ -248,8 +248,8 @@
     )(*ins)
 
 
-def exchange(x, n, d, cores=(0, 1)):
-    return lax.ppermute(x, "src", [(i, i ^ d if i & 1 in cores else i) for i in range(n)])
+def exchange(x, n, d):
+    return lax.ppermute(x, "src", [(i, i ^ d) for i in range(n)])
 
 
 def shards(
@@ -340,23 +340,20 @@
     )
     u = None
     for iteration in range(ITERS):
-        mine = mine + exchange(mine, n, 1)
-        d = 2
-        while d < n:
-            mine = mine + exchange(mine, n, d, (1,))
-            d *= 2
-        other = exchange(mine, n, 1)
+        parts = lax.all_to_all(mine.reshape(n, local, block), "src", 0, 0)
+        own = jnp.broadcast_to(jnp.sum(parts, axis=0), (n, local, block))
+        mine = lax.all_to_all(own, "src", 0, 0).reshape(every, block)
         if iteration < ITERS - 1:
             mine, u = call(
                 functools.partial(next_sweep, PIECES),
-                (tile_live, tile_tgt, hit, mine, other, b_all, et_all, tot, *kern, *la),
+                (tile_live, tile_tgt, hit, mine, b_all, et_all, tot, *kern, *la),
                 (shape(every), shape(local * block)),
                 scratch=[w, acc, col],
                 smem=2,
             )
     src, tgt = call(
         last_kernel,
-        (mine, other, b_all, et_all, tot, u),
+        (mine, b_all, et_all, tot, u),
         [jax.ShapeDtypeStruct((local, block), f32)] * 2,
         scratch=[VMEM((every, block), f32)],
     )

time: 87.3 us -> 98.4 us (1.13)
  blocking collectives: 0 us -> 58.9 us
  starting transfers between devices: 58.3 us -> 7.07 us
  local copies, waits for them, and re-layouts: 0.01 us -> 9.59 us
  waiting for transfers between devices: 6.59 us -> 0.9 us
    all_to_all x0 -> x6, blocking collectives: none -> 58.9 us  [the longest x3 30.5 us: shards(): parts = lax.all_to_all(mine.reshape(n, local, block), 'src', 0, 0)]
    ppermute x19 -> x4, starting transfers between devices: 58.3 us -> 7.07 us  [exchange(): return lax.ppermute(x, 'src', [(i, i ^ d) for i in range(n)])]
    unnamed x4 -> x22, local copies, waits for them, and re-layouts: 0.01 us -> 9.57 us
    ppermute x19 -> x4, waiting for transfers between devices: 6.59 us -> 0.9 us  [exchange(): return lax.ppermute(x, 'src', [(i, i ^ d) for i in range(n)])]
  transfers between devices with their start and end apart: 19 -> 4, of which waited for: 7 -> 1; matrix products, arithmetic and copies ran while one was open for 0% -> 0% of each run, Pallas kernels for 12% -> 10%
where the time goes in v2:
time: 98.4 us; the launch traced here: 97.9 us
  blocking collectives  58.9 us (60%)
  Pallas kernels  20.5 us (21%)
  local copies, waits for them, and re-layouts  9.59 us (10%)
  starting transfers between devices  7.07 us (7%)
    all_to_all x3, blocking collectives, shards(): parts = lax.all_to_all(mine.reshape(n, local, block), 'src', 0, 0)  30.5 us
    all_to_all x3, blocking collectives, shards(): mine = lax.all_to_all(own, 'src', 0, 0).reshape(every, block)  28.4 us
    pallas_call x9, Pallas kernels, call(): pl.pallas_call(kernel, out_shape=outs, in_specs=specs, out_specs=[pl.Bloc...  20.5 us
    unnamed x22, local copies, waits for them, and re-layouts  9.57 us
    ppermute x4, starting transfers between devices, exchange(): return lax.ppermute(x, 'src', [(i, i ^ d) for i in range(n)])  7.07 us
  transfers between devices with their start and end apart: 4, of which 1 were waited for; matrix products, arithmetic and copies ran while one was open for 0% of the time, Pallas kernels for 10%

profile of v2, /device:TPU:0, one launch (start us, length us, event | category | flops | bytes accessed | tf_op | source)
XLA Modules:
  0.0 97.9 jit_solution(5520669436130627306)
XLA Ops:
  0.6 0.8 shard_map.105
  1.4 4.1 %collective-permute-start = (f32[24,128]{1,0:T(8,128)S(1)}, f32[24,128]{1,0:T(8,128)S(1)}, u32[]{:S(2)}, u32[]{:S(2)}) collective-permute-start(f32[24,128]{1,0:T(8,128)S(1)} %shard_map.105), channel_id=1, source_target_pairs={{0,8},{1,9},{2,10},{3,11},{4,12},{5,13},{6,14},{7,15},{8,0},{9,1},... | collective-permute-start | bytes 36872 | tf_op jit(solution)/shard_map/ppermute | solution.py:252
  5.5 0.0 copy-start.10
  5.5 3.8 %shard_map.104 = (f32[4096,128]{1,0:T(8,128)S(1)}, f32[256,128]{1,0:T(8,128)S(1)}, bf16[128,128]{1,0:T(8,128)(2,1)S(1)}, bf16[1024,256]{1,0:T(8,128)(2,1)S(1)}, ...) custom-call(s32[8]{0:T(128)} %live.11, ...), custom_call_target="tpu_custom_call" | custom-call | flops 268435456 | bytes 2097152 | tf_op jit(solution)/shard_map/pallas_call | solution.py:240
  9.3 0.0 collective-permute-done
  9.3 1.6 %collective-permute-start.1 = (f32[48,128]{1,0:T(8,128)S(1)}, f32[48,128]{1,0:T(8,128)S(1)}, u32[]{:S(2)}, u32[]{:S(2)}) collective-permute-start(f32[48,128]{1,0:T(8,128)S(1)} %bitcast.32), channel_id=1, source_target_pairs={{0,4},{1,5},{2,6},{3,7},{4,0},{5,1},{6,2},{7,3},{8,12},{9,13},{10,... | collective-permute-start | bytes 73736 | tf_op jit(solution)/shard_map/ppermute | solution.py:252
  10.9 0.0 copy-done.10
  10.9 2.5 %shard_map.106 = (f32[4096,128]{1,0:T(8,128)S(1)}, f32[256,128]{1,0:T(8,128)S(1)}) custom-call(s32[8]{0:T(128)S(1)} %copy-done.10, bf16[1024,256]{1,0:T(8,128)(2,1)S(1)} %get-tuple-element.41.x_ref, bf16[2,16,128,256]{3,2,1,0:T(8,128)(2,1)S(1)} %get-tuple-element.42.feat, f32[8,128]{1,0:T(8,128)S(1)} %get-tuple-element.43.lin_ref, ...), custom_call_target="tpu_custom_call" | custom-call | flops 268435456 | bytes 2097152 | tf_op jit(solution)/shard_map/pallas_call | solution.py:240
  13.4 0.0 copy-start
  13.4 0.0 collective-permute-done.1
  13.5 0.0 copy-start.9
  13.5 1.3 %collective-permute-start.2 = (f32[96,128]{1,0:T(8,128)S(1)}, f32[96,128]{1,0:T(8,128)S(1)}, u32[]{:S(2)}, u32[]{:S(2)}) collective-permute-start(f32[96,128]{1,0:T(8,128)S(1)} %bitcast.30), channel_id=1, source_target_pairs={{0,2},{1,3},{2,0},{3,1},{4,6},{5,7},{6,4},{7,5},{8,10},{9,11},{10,... | collective-permute-start | bytes 147464 | tf_op jit(solution)/shard_map/ppermute | solution.py:252
  14.7 2.0 %shard_map.107 = (f32[4096,128]{1,0:T(8,128)S(1)}, f32[256,128]{1,0:T(8,128)S(1)}) custom-call(s32[8]{0:T(128)S(1)} %copy-done.10, bf16[1024,256]{1,0:T(8,128)(2,1)S(1)} %get-tuple-element.41.x_ref, bf16[2,16,128,256]{3,2,1,0:T(8,128)(2,1)S(1)} %get-tuple-element.49.feat, f32[8,128]{1,0:T(8,128)S(1)} %get-tuple-element.43.lin_ref, ...), custom_call_target="tpu_custom_call" | custom-call | flops 268435456 | bytes 2097152 | tf_op jit(solution)/shard_map/pallas_call | solution.py:240
  16.7 0.0 copy-start.3
  16.7 0.9 collective-permute-done.2
  17.6 0.1 collective-permute-start.3
  17.7 2.0 %shard_map.108 = (f32[4096,128]{1,0:T(8,128)S(1)}, f32[256,128]{1,0:T(8,128)S(1)}) custom-call(s32[8]{0:T(128)S(1)} %copy-done.10, bf16[1024,256]{1,0:T(8,128)(2,1)S(1)} %get-tuple-element.41.x_ref, bf16[2,16,128,256]{3,2,1,0:T(8,128)(2,1)S(1)} %get-tuple-element.52.feat, f32[8,128]{1,0:T(8,128)S(1)} %get-tuple-element.43.lin_ref, ...), custom_call_target="tpu_custom_call" | custom-call | flops 268435456 | bytes 2097152 | tf_op jit(solution)/shard_map/pallas_call | solution.py:240
  19.7 0.0 copy-start.6
  19.7 0.0 collective-permute-done.3.refs_9_
  19.7 0.0 copy-done
  19.7 0.0 copy-done.9
  19.8 2.7 %shard_map.109 = (f32[128,128]{1,0:T(8,128)S(1)}, f32[128,128]{1,0:T(8,128)S(1)}, f32[128,128]{1,0:T(8,128)S(1)}, f32[8,128]{1,0:T(8,128)S(1)}) custom-call(s32[8]{0:T(128)S(1)} %copy-done.10, s32[8,16]{1,0:T(8,128)S(1)} %copy-done.9, bf16[128,128]{1,0:T(8,128)(2,1)S(1)} %get-tuple-element.35.hit_ref, f32[4096,128]{1,0:T(8,128)S(1)} %get-tuple-element.38.refs_0_, ...), custom_call_target="tpu_custom_call" | custom-call | tf_op jit(solution)/shard_map/pallas_call | solution.py:240
  22.5 0.0 copy-done.3
  22.5 0.0 copy-done.6
  22.5 11.5 %all_to_all.30 = f32[16,8,128]{2,1,0:T(8,128)S(1)} all-to-all(f32[16,8,128]{2,1,0:T(8,128)S(1)} %bitcast.27), channel_id=1, replica_groups=mesh['pairs'=2,'src'=16] {'src'}, dimensions={0} | all-to-all | bytes 131072 | tf_op jit(solution)/shard_map/all_to_all | solution.py:343
  34.1 9.5 %all_to_all.31 = f32[16,8,128]{2,1,0:T(8,128)S(1)} all-to-all(f32[16,8,128]{2,1,0:T(8,128)S(1)} %broadcast_in_dim.9), channel_id=1, replica_groups=mesh['pairs'=2,'src'=16] {'src'}, dimensions={0} | all-to-all | bytes 131072 | tf_op jit(solution)/shard_map/all_to_all | solution.py:345
  43.5 0.0 copy-start.1
  43.5 1.6 %copy-done.1 = f32[4096,128]{1,0:T(8,128)S(1)} copy-done((f32[4096,128]{1,0:T(8,128)S(1)}, f32[4096,128]{1,0:T(8,128)}, u32[]{:S(2)}) %copy-start.1) | copy-done | bytes 2097176
  45.1 0.0 copy-start.4
  45.1 1.6 %copy-done.4 = f32[4096,128]{1,0:T(8,128)S(1)} copy-done((f32[4096,128]{1,0:T(8,128)S(1)}, f32[4096,128]{1,0:T(8,128)}, u32[]{:S(2)}) %copy-start.4) | copy-done | bytes 2097176
  46.7 0.0 copy-start.7
  46.7 1.6 %copy-done.7 = f32[4096,128]{1,0:T(8,128)S(1)} copy-done((f32[4096,128]{1,0:T(8,128)S(1)}, f32[4096,128]{1,0:T(8,128)}, u32[]{:S(2)}) %copy-start.7) | copy-done | bytes 2097176
  48.3 3.3 %shard_map.110 = (f32[128,128]{1,0:T(8,128)S(1)}, f32[1024,128]{1,0:T(8,128)}) custom-call(s32[8]{0:T(128)S(1)} %copy-done.10, s32[8,16]{1,0:T(8,128)S(1)} %copy-done.9, bf16[128,128]{1,0:T(8,128)(2,1)S(1)} %get-tuple-element.35.hit_ref, f32[128,128]{1,0:T(8,128)S(1)} %bitcast.24, f32[128,128]{1,0:T(8,128)S(1)} %get-tuple-element.60.b_ref, ...), custom_call_target="tpu_custom_call" | custom-call | tf_op jit(solution)/shard_map/pallas_call | solution.py:240
  51.6 9.5 %all_to_all.32 = f32[16,8,128]{2,1,0:T(8,128)S(1)} all-to-all(f32[16,8,128]{2,1,0:T(8,128)S(1)} %bitcast.28), channel_id=1, replica_groups=mesh['pairs'=2,'src'=16] {'src'}, dimensions={0} | all-to-all | bytes 131072 | tf_op jit(solution)/shard_map/all_to_all | solution.py:343
  61.1 9.5 %all_to_all.33 = f32[16,8,128]{2,1,0:T(8,128)S(1)} all-to-all(f32[16,8,128]{2,1,0:T(8,128)S(1)} %broadcast_in_dim.10), channel_id=1, replica_groups=mesh['pairs'=2,'src'=16] {'src'}, dimensions={0} | all-to-all | bytes 131072 | tf_op jit(solution)/shard_map/all_to_all | solution.py:345
  70.6 0.0 copy-start.2
  70.6 1.6 %copy-done.2 = f32[4096,128]{1,0:T(8,128)S(1)} copy-done((f32[4096,128]{1,0:T(8,128)S(1)}, f32[4096,128]{1,0:T(8,128)}, u32[]{:S(2)}) %copy-start.2) | copy-done | bytes 2097176
  72.2 0.0 copy-start.5
  72.2 1.6 %copy-done.5 = f32[4096,128]{1,0:T(8,128)S(1)} copy-done((f32[4096,128]{1,0:T(8,128)S(1)}, f32[4096,128]{1,0:T(8,128)}, u32[]{:S(2)}) %copy-start.5) | copy-done | bytes 2097176
  73.8 0.0 copy-start.8
  73.8 1.6 %copy-done.8 = f32[4096,128]{1,0:T(8,128)S(1)} copy-done((f32[4096,128]{1,0:T(8,128)S(1)}, f32[4096,128]{1,0:T(8,128)}, u32[]{:S(2)}) %copy-start.8) | copy-done | bytes 2097176
  75.4 2.7 %shard_map.111 = (f32[128,128]{1,0:T(8,128)S(1)}, f32[1024,128]{1,0:T(8,128)S(1)}) custom-call(s32[8]{0:T(128)S(1)} %copy-done.10, s32[8,16]{1,0:T(8,128)S(1)} %copy-done.9, bf16[128,128]{1,0:T(8,128)(2,1)S(1)} %get-tuple-element.35.hit_ref, f32[128,128]{1,0:T(8,128)S(1)} %bitcast.23, f32[128,128]{1,0:T(8,128)S(1)} %get-tuple-element.60.b_ref, ...), custom_call_target="tpu_custom_call" | custom-call | tf_op jit(solution)/shard_map/pallas_call | solution.py:240
  78.1 9.5 %all_to_all.34 = f32[16,8,128]{2,1,0:T(8,128)S(1)} all-to-all(f32[16,8,128]{2,1,0:T(8,128)S(1)} %bitcast.26), channel_id=1, replica_groups=mesh['pairs'=2,'src'=16] {'src'}, dimensions={0} | all-to-all | bytes 131072 | tf_op jit(solution)/shard_map/all_to_all | solution.py:343
  87.6 9.5 %all_to_all.35 = f32[16,8,128]{2,1,0:T(8,128)S(1)} all-to-all(f32[16,8,128]{2,1,0:T(8,128)S(1)} %broadcast_in_dim.11), channel_id=1, replica_groups=mesh['pairs'=2,'src'=16] {'src'}, dimensions={0} | all-to-all | bytes 131072 | tf_op jit(solution)/shard_map/all_to_all | solution.py:345
  97.1 0.8 shard_map.112
  (9 shorter events, 0.1 us)
Async XLA Ops:
  1.4 7.9 %collective-permute-start = (f32[24,128]{1,0:T(8,128)S(1)}, f32[24,128]{1,0:T(8,128)S(1)}, u32[]{:S(2)}, u32[]{:S(2)}) collective-permute-start(f32[24,128]{1,0:T(8,128)S(1)} %shard_map.105), channel_id=1, source_target_pairs={{0,8},{1,9},{2,10},{3,11},{4,12},{5,13},{6,14},{7,15},{8,0},{9,1},... | collective-permute-start | bytes 36872 | tf_op jit(solution)/shard_map/ppermute | solution.py:252
  5.5 5.4 %copy-start.10 = (s32[8]{0:T(128)S(1)}, s32[8]{0:T(128)}, u32[]{:S(2)}) copy-start(s32[8]{0:T(128)} %live.11) | copy-start | bytes 100
  9.3 4.1 %collective-permute-start.1 = (f32[48,128]{1,0:T(8,128)S(1)}, f32[48,128]{1,0:T(8,128)S(1)}, u32[]{:S(2)}, u32[]{:S(2)}) collective-permute-start(f32[48,128]{1,0:T(8,128)S(1)} %bitcast.32), channel_id=1, source_target_pairs={{0,4},{1,5},{2,6},{3,7},{4,0},{5,1},{6,2},{7,3},{8,12},{9,13},{10,... | collective-permute-start | bytes 73736 | tf_op jit(solution)/shard_map/ppermute | solution.py:252
  13.4 6.3 %copy-start = (f32[4096,128]{1,0:T(8,128)}, f32[4096,128]{1,0:T(8,128)S(1)}, u32[]{:S(2)}) copy-start(f32[4096,128]{1,0:T(8,128)S(1)} %get-tuple-element.46.refs_1_) | copy-start | bytes 6291460
  13.5 6.3 %copy-start.9 = (s32[8,16]{1,0:T(8,128)S(1)}, s32[8,16]{1,0:T(8,128)}, u32[]{:S(2)}) copy-start(s32[8,16]{1,0:T(8,128)} %tgt.5) | copy-start | bytes 1540
  13.5 4.2 %collective-permute-start.2 = (f32[96,128]{1,0:T(8,128)S(1)}, f32[96,128]{1,0:T(8,128)S(1)}, u32[]{:S(2)}, u32[]{:S(2)}) collective-permute-start(f32[96,128]{1,0:T(8,128)S(1)} %bitcast.30), channel_id=1, source_target_pairs={{0,2},{1,3},{2,0},{3,1},{4,6},{5,7},{6,4},{7,5},{8,10},{9,11},{10,... | collective-permute-start | bytes 147464 | tf_op jit(solution)/shard_map/ppermute | solution.py:252
  16.7 5.8 %copy-start.3 = (f32[4096,128]{1,0:T(8,128)}, f32[4096,128]{1,0:T(8,128)S(1)}, u32[]{:S(2)}) copy-start(f32[4096,128]{1,0:T(8,128)S(1)} %get-tuple-element.51.refs_2_) | copy-start | bytes 6291460
  17.6 2.1 %collective-permute-start.3 = (f32[192,128]{1,0:T(8,128)S(1)}, f32[192,128]{1,0:T(8,128)S(1)}, u32[]{:S(2)}, u32[]{:S(2)}) collective-permute-start(f32[192,128]{1,0:T(8,128)S(1)} %bitcast.21), channel_id=1, source_target_pairs={{0,1},{1,0},{2,3},{3,2},{4,5},{5,4},{6,7},{7,6},{8,9},{9,8},{10,11... | collective-permute-start | bytes 294920 | tf_op jit(solution)/shard_map/ppermute | solution.py:252
  19.7 2.8 %copy-start.6 = (f32[4096,128]{1,0:T(8,128)}, f32[4096,128]{1,0:T(8,128)S(1)}, u32[]{:S(2)}) copy-start(f32[4096,128]{1,0:T(8,128)S(1)} %get-tuple-element.53.refs_3_) | copy-start | bytes 6291460
  43.5 1.6 %copy-start.1 = (f32[4096,128]{1,0:T(8,128)S(1)}, f32[4096,128]{1,0:T(8,128)}, u32[]{:S(2)}) copy-start(f32[4096,128]{1,0:T(8,128)} %copy-done) | copy-start | bytes 6291460
  45.1 1.6 %copy-start.4 = (f32[4096,128]{1,0:T(8,128)S(1)}, f32[4096,128]{1,0:T(8,128)}, u32[]{:S(2)}) copy-start(f32[4096,128]{1,0:T(8,128)} %copy-done.3) | copy-start | bytes 6291460
  46.7 1.6 %copy-start.7 = (f32[4096,128]{1,0:T(8,128)S(1)}, f32[4096,128]{1,0:T(8,128)}, u32[]{:S(2)}) copy-start(f32[4096,128]{1,0:T(8,128)} %copy-done.6) | copy-start | bytes 6291460
  70.6 1.6 %copy-start.2 = (f32[4096,128]{1,0:T(8,128)S(1)}, f32[4096,128]{1,0:T(8,128)}, u32[]{:S(2)}) copy-start(f32[4096,128]{1,0:T(8,128)} %copy-done) | copy-start | bytes 6291460
  72.2 1.6 %copy-start.5 = (f32[4096,128]{1,0:T(8,128)S(1)}, f32[4096,128]{1,0:T(8,128)}, u32[]{:S(2)}) copy-start(f32[4096,128]{1,0:T(8,128)} %copy-done.3) | copy-start | bytes 6291460
  73.8 1.6 %copy-start.8 = (f32[4096,128]{1,0:T(8,128)S(1)}, f32[4096,128]{1,0:T(8,128)}, u32[]{:S(2)}) copy-start(f32[4096,128]{1,0:T(8,128)} %copy-done.6) | copy-start | bytes 6291460

commit v3 on v1

--- a/solution.py
+++ b/solution.py
@@ -186,10 +186,10 @@
     dense_ref, b_ref, et_ref, tot_ref, w_ref, acc_ref, u_ref, col_ref = refs[2 * npieces + 2 :]
     local = tgt.shape[0]
     n = b_ref.shape[0] // local
-    bits = n.bit_length() - 1
     am = jnp.zeros((local, b_ref.shape[1]), jnp.float32)
+    order = distances(n)
     for at in range(n):
-        m = sum(((at >> r) & 1) << (bits - 1 - r) for r in range(bits))
+        m = functools.reduce(lambda p, q: p ^ q, [d for r, d in enumerate(order) if at >> r & 1], 0)
         part = parts[at // (n // 2)]
         at = (at % (n // 2)) * 3 * local
         rows = pl.ds(pl.multiple_of((position() ^ m) * local, local), local)
@@ -206,7 +206,7 @@
 
 def new_scale(mine, other, b_ref, et_ref, tot_ref):
     b = b_ref[...]
-    col = jnp.where(position() & 1 == 1, mine[...], other[...]) * et_ref[...]
+    col = (mine[...] + other[...]) * et_ref[...]
     t = jnp.where(b > 0.0, power_of_ratio(b, col), 0.0)
     return t, jnp.sqrt(tot_ref[0:1, 0:1] / total_of(t * col))
 
@@ -248,8 +248,12 @@
     )(*ins)
 
 
-def exchange(x, n, d, cores=(0, 1)):
-    return lax.ppermute(x, "src", [(i, i ^ d if i & 1 in cores else i) for i in range(n)])
+def distances(n):
+    return [d | 1 for d in (n >> r for r in range(1, n.bit_length()))]
+
+
+def exchange(x, n, d):
+    return lax.ppermute(x, "src", [(i, i ^ d) for i in range(n)])
 
 
 def shards(
@@ -279,11 +283,7 @@
         bytes_accessed=2 * each * slots * block * width,
         transcendentals=each * slots * block * block,
     )
-    order = []
-    d = n // 2
-    while d:
-        order.append(d)
-        d //= 2
+    order = distances(n)
     kern, la = [], []
     for at, d in enumerate(order):
         got = exchange(part, n, d)
@@ -322,7 +322,7 @@
             )
             kern.append(k0)
             la.append(la0)
-        if d > 1:
+        if at < len(order) - 1:
             part = jnp.stack([part, got], axis=0).reshape(-1, block)
             if at < PIECES - 1:
                 part, later[at], kern[-1] = lax.optimization_barrier(
@@ -340,23 +340,22 @@
     )
     u = None
     for iteration in range(ITERS):
-        mine = mine + exchange(mine, n, 1)
-        d = 2
-        while d < n:
-            mine = mine + exchange(mine, n, d, (1,))
-            d *= 2
-        other = exchange(mine, n, 1)
+        for d in order[::-1][:-1]:
+            mine = mine + exchange(mine, n, d)
+        other = exchange(mine, n, order[0])
         if iteration < ITERS - 1:
-            mine, u = call(
+            last = iteration == ITERS - 2
+            outs = (shape(every), shape(local * block)) if last else (shape(every),)
+            mine, *u = call(
                 functools.partial(next_sweep, PIECES),
                 (tile_live, tile_tgt, hit, mine, other, b_all, et_all, tot, *kern, *la),
-                (shape(every), shape(local * block)),
-                scratch=[w, acc, col],
+                outs,
+                scratch=[w, acc, col] if last else [acc, w, acc, col],
                 smem=2,
             )
     src, tgt = call(
         last_kernel,
-        (mine, other, b_all, et_all, tot, u),
+        (mine, other, b_all, et_all, tot, *u),
         [jax.ShapeDtypeStruct((local, block), f32)] * 2,
         scratch=[VMEM((every, block), f32)],
     )

time: 87.3 us -> 76.3 us (0.87)
  starting transfers between devices: 58.3 us -> 14.8 us
  waiting for transfers between devices: 6.59 us -> 41.3 us
  Pallas kernels: 21.4 us -> 18.6 us
    ppermute x19 -> x16, starting transfers between devices: 58.3 us -> 14.8 us  [exchange(): return lax.ppermute(x, 'src', [(i, i ^ d) for i in range(n)])]
    ppermute x19 -> x16, waiting for transfers between devices: 6.59 us -> 41.3 us  [exchange(): return lax.ppermute(x, 'src', [(i, i ^ d) for i in range(n)])]
    pallas_call x9, Pallas kernels: 21.4 us -> 18.6 us  [call(): pl.pallas_call(kernel, out_shape=outs, in_specs=specs, out_specs=[pl.Bloc...]
  transfers between devices with their start and end apart: 19 -> 16, of which waited for: 7 -> 13; matrix products, arithmetic and copies ran while one was open for 0% -> 0% of each run, Pallas kernels for 12% -> 13%
where the time goes in v3:
time: 76.3 us; the launch traced here: 75.7 us
  waiting for transfers between devices  41.3 us (54%)
  Pallas kernels  18.6 us (24%)
  starting transfers between devices  14.8 us (19%)
  between operations  0.84 us (1%)
    ppermute x16, waiting for transfers between devices, exchange(): return lax.ppermute(x, 'src', [(i, i ^ d) for i in range(n)])  41.3 us
    pallas_call x9, Pallas kernels, call(): pl.pallas_call(kernel, out_shape=outs, in_specs=specs, out_specs=[pl.Bloc...  18.6 us
    ppermute x16, starting transfers between devices, exchange(): return lax.ppermute(x, 'src', [(i, i ^ d) for i in range(n)])  14.8 us
  transfers between devices with their start and end apart: 16, of which 13 were waited for; matrix products, arithmetic and copies ran while one was open for 0% of the time, Pallas kernels for 13%

profile of v3, /device:TPU:0, one launch (start us, length us, event | category | flops | bytes accessed | tf_op | source)
XLA Modules:
  0.0 75.7 jit_solution(1566964029466494919)
XLA Ops:
  0.6 0.8 %shard_map.105 = f32[24,128]{1,0:T(8,128)S(1)} custom-call(s32[8]{0:T(128)} %count_hbm.1, f32[8,128]{1,0:T(8,128)} %bitcast.28, f32[8,128]{1,0:T(8,128)} %bitcast.29, f32[8,128]{1,0:T(8,128)} %bitcast.24), custom_call_target="tpu_custom_call" | custom-call | tf_op jit(solution)/shard_map/pallas_call | solution.py:240
  1.4 3.5 %collective-permute-start = (f32[24,128]{1,0:T(8,128)S(1)}, f32[24,128]{1,0:T(8,128)S(1)}, u32[]{:S(2)}, u32[]{:S(2)}) collective-permute-start(f32[24,128]{1,0:T(8,128)S(1)} %shard_map.105), channel_id=1, source_target_pairs={{0,9},{1,8},{2,11},{3,10},{4,13},{5,12},{6,15},{7,14},{8,1},{9,0},... | collective-permute-start | bytes 36872 | tf_op jit(solution)/shard_map/ppermute | solution.py:256
  4.9 0.0 copy-start.1
  4.9 3.8 %shard_map.104 = (f32[4096,128]{1,0:T(8,128)S(1)}, f32[256,128]{1,0:T(8,128)S(1)}, bf16[128,128]{1,0:T(8,128)(2,1)S(1)}, bf16[1024,256]{1,0:T(8,128)(2,1)S(1)}, ...) custom-call(s32[8]{0:T(128)} %live.11, ...), custom_call_target="tpu_custom_call" | custom-call | flops 268435456 | bytes 2097152 | tf_op jit(solution)/shard_map/pallas_call | solution.py:240
  8.7 0.0 collective-permute-done
  8.7 1.9 %collective-permute-start.1 = (f32[48,128]{1,0:T(8,128)S(1)}, f32[48,128]{1,0:T(8,128)S(1)}, u32[]{:S(2)}, u32[]{:S(2)}) collective-permute-start(f32[48,128]{1,0:T(8,128)S(1)} %bitcast.20), channel_id=1, source_target_pairs={{0,5},{1,4},{2,7},{3,6},{4,1},{5,0},{6,3},{7,2},{8,13},{9,12},{10,... | collective-permute-start | bytes 73736 | tf_op jit(solution)/shard_map/ppermute | solution.py:256
  10.7 0.0 copy-done.1
  10.7 2.2 %shard_map.106 = (f32[4096,128]{1,0:T(8,128)S(1)}, f32[256,128]{1,0:T(8,128)S(1)}) custom-call(s32[8]{0:T(128)S(1)} %copy-done.1, bf16[1024,256]{1,0:T(8,128)(2,1)S(1)} %get-tuple-element.40.x_ref, bf16[2,16,128,256]{3,2,1,0:T(8,128)(2,1)S(1)} %get-tuple-element.41.feat, f32[8,128]{1,0:T(8,128)S(1)} %get-tuple-element.42.lin_ref, ...), custom_call_target="tpu_custom_call" | custom-call | flops 268435456 | bytes 2097152 | tf_op jit(solution)/shard_map/pallas_call | solution.py:240
  12.9 0.0 collective-permute-done.1
  12.9 0.0 copy-start
  12.9 0.9 %collective-permute-start.2 = (f32[96,128]{1,0:T(8,128)S(1)}, f32[96,128]{1,0:T(8,128)S(1)}, u32[]{:S(2)}, u32[]{:S(2)}) collective-permute-start(f32[96,128]{1,0:T(8,128)S(1)} %bitcast.18), channel_id=1, source_target_pairs={{0,3},{1,2},{2,1},{3,0},{4,7},{5,6},{6,5},{7,4},{8,11},{9,10},{10,... | collective-permute-start | bytes 147464 | tf_op jit(solution)/shard_map/ppermute | solution.py:256
  13.9 2.0 %shard_map.107 = (f32[4096,128]{1,0:T(8,128)S(1)}, f32[256,128]{1,0:T(8,128)S(1)}) custom-call(s32[8]{0:T(128)S(1)} %copy-done.1, bf16[1024,256]{1,0:T(8,128)(2,1)S(1)} %get-tuple-element.40.x_ref, bf16[2,16,128,256]{3,2,1,0:T(8,128)(2,1)S(1)} %get-tuple-element.48.feat, f32[8,128]{1,0:T(8,128)S(1)} %get-tuple-element.42.lin_ref, ...), custom_call_target="tpu_custom_call" | custom-call | flops 268435456 | bytes 2097152 | tf_op jit(solution)/shard_map/pallas_call | solution.py:240
  15.9 0.9 %collective-permute-done.2 = f32[96,128]{1,0:T(8,128)S(1)} collective-permute-done((f32[96,128]{1,0:T(8,128)S(1)}, f32[96,128]{1,0:T(8,128)S(1)}, u32[]{:S(2)}, u32[]{:S(2)}) %collective-permute-start.2) | collective-permute-done | bytes 49184 | tf_op jit(solution)/shard_map/ppermute | solution.py:256
  16.7 0.2 collective-permute-start.3
  16.9 1.5 %shard_map.108 = (f32[4096,128]{1,0:T(8,128)S(1)}, f32[256,128]{1,0:T(8,128)S(1)}) custom-call(s32[8]{0:T(128)S(1)} %copy-done.1, bf16[1024,256]{1,0:T(8,128)(2,1)S(1)} %get-tuple-element.40.x_ref, bf16[2,16,128,256]{3,2,1,0:T(8,128)(2,1)S(1)} %get-tuple-element.51.feat, f32[8,128]{1,0:T(8,128)S(1)} %get-tuple-element.42.lin_ref, ...), custom_call_target="tpu_custom_call" | custom-call | flops 268435456 | bytes 2097152 | tf_op jit(solution)/shard_map/pallas_call | solution.py:240
  18.5 0.0 collective-permute-done.3.refs_9_
  18.5 0.0 copy-done
  18.5 2.5 %shard_map.109 = (f32[128,128]{1,0:T(8,128)S(1)}, f32[128,128]{1,0:T(8,128)S(1)}, f32[128,128]{1,0:T(8,128)S(1)}, f32[8,128]{1,0:T(8,128)S(1)}) custom-call(s32[8]{0:T(128)S(1)} %copy-done.1, s32[8,16]{1,0:T(8,128)S(1)} %copy-done, bf16[128,128]{1,0:T(8,128)(2,1)S(1)} %get-tuple-element.34.hit_ref, f32[4096,128]{1,0:T(8,128)S(1)} %get-tuple-element.37.refs_0_, ...), custom_call_target="tpu_custom_call" | custom-call | tf_op jit(solution)/shard_map/pallas_call | solution.py:240
  21.0 1.4 %collective-permute-start.4 = (f32[128,128]{1,0:T(8,128)S(1)}, f32[128,128]{1,0:T(8,128)S(1)}, u32[]{:S(2)}, u32[]{:S(2)}) collective-permute-start(f32[128,128]{1,0:T(8,128)S(1)} %get-tuple-element.58), channel_id=1, source_target_pairs={{0,1},{1,0},{2,3},{3,2},{4,5},{5,4},{6,7},{7,6},{8,9},{9,8},{10,11... | collective-permute-start | bytes 196616 | tf_op jit(solution)/shard_map/ppermute | solution.py:256
  22.4 0.9 %collective-permute-done.4 = f32[128,128]{1,0:T(8,128)S(1)} collective-permute-done((f32[128,128]{1,0:T(8,128)S(1)}, f32[128,128]{1,0:T(8,128)S(1)}, u32[]{:S(2)}, u32[]{:S(2)}) %collective-permute-start.4) | collective-permute-done | bytes 65568 | tf_op jit(solution)/shard_map/ppermute | solution.py:256
  23.3 2.3 %collective-permute-start.5 = (f32[128,128]{1,0:T(8,128)S(1)}, f32[128,128]{1,0:T(8,128)S(1)}, u32[]{:S(2)}, u32[]{:S(2)}) collective-permute-start(f32[128,128]{1,0:T(8,128)S(1)} %add.27), channel_id=1, source_target_pairs={{0,3},{1,2},{2,1},{3,0},{4,7},{5,6},{6,5},{7,4},{8,11},{9,10},{10,... | collective-permute-start | bytes 196616 | tf_op jit(solution)/shard_map/ppermute | solution.py:256
  25.6 2.3 %collective-permute-done.5 = f32[128,128]{1,0:T(8,128)S(1)} collective-permute-done((f32[128,128]{1,0:T(8,128)S(1)}, f32[128,128]{1,0:T(8,128)S(1)}, u32[]{:S(2)}, u32[]{:S(2)}) %collective-permute-start.5) | collective-permute-done | bytes 65568 | tf_op jit(solution)/shard_map/ppermute | solution.py:256
  27.9 0.1 collective-permute-start.6
  28.0 4.0 %collective-permute-done.6 = f32[128,128]{1,0:T(8,128)S(1)} collective-permute-done((f32[128,128]{1,0:T(8,128)S(1)}, f32[128,128]{1,0:T(8,128)S(1)}, u32[]{:S(2)}, u32[]{:S(2)}) %collective-permute-start.6) | collective-permute-done | bytes 65568 | tf_op jit(solution)/shard_map/ppermute | solution.py:256
  32.1 0.1 collective-permute-start.7
  32.1 6.0 %collective-permute-done.7.other = f32[128,128]{1,0:T(8,128)S(1)} collective-permute-done((f32[128,128]{1,0:T(8,128)S(1)}, f32[128,128]{1,0:T(8,128)S(1)}, u32[]{:S(2)}, u32[]{:S(2)}) %collective-permute-start.7) | collective-permute-done | bytes 65568 | tf_op jit(solution)/shard_map/ppermute | solution.py:256
  38.1 2.5 %shard_map.110 = f32[128,128]{1,0:T(8,128)S(1)} custom-call(s32[8]{0:T(128)S(1)} %copy-done.1, s32[8,16]{1,0:T(8,128)S(1)} %copy-done, bf16[128,128]{1,0:T(8,128)(2,1)S(1)} %get-tuple-element.34.hit_ref, f32[128,128]{1,0:T(8,128)S(1)} %add.29.mine, f32[128,128]{1,0:T(8,128)S(1)} %collective-permute-done.7.other, f32[128,128]{1,0:T(8,128)S(1)} %get-tuple-element.59.b_ref, ...), custom_call_target="tpu_custom_call" | custom-call | tf_op jit(solution)/shard_map/pallas_call | solution.py:240
  40.7 0.2 collective-permute-start.8
  40.8 1.1 %collective-permute-done.8 = f32[128,128]{1,0:T(8,128)S(1)} collective-permute-done((f32[128,128]{1,0:T(8,128)S(1)}, f32[128,128]{1,0:T(8,128)S(1)}, u32[]{:S(2)}, u32[]{:S(2)}) %collective-permute-start.8) | collective-permute-done | bytes 65568 | tf_op jit(solution)/shard_map/ppermute | solution.py:256
  42.0 1.9 %collective-permute-start.9 = (f32[128,128]{1,0:T(8,128)S(1)}, f32[128,128]{1,0:T(8,128)S(1)}, u32[]{:S(2)}, u32[]{:S(2)}) collective-permute-start(f32[128,128]{1,0:T(8,128)S(1)} %add.30), channel_id=1, source_target_pairs={{0,3},{1,2},{2,1},{3,0},{4,7},{5,6},{6,5},{7,4},{8,11},{9,10},{10,... | collective-permute-start | bytes 196616 | tf_op jit(solution)/shard_map/ppermute | solution.py:256
  43.9 2.3 %collective-permute-done.9 = f32[128,128]{1,0:T(8,128)S(1)} collective-permute-done((f32[128,128]{1,0:T(8,128)S(1)}, f32[128,128]{1,0:T(8,128)S(1)}, u32[]{:S(2)}, u32[]{:S(2)}) %collective-permute-start.9) | collective-permute-done | bytes 65568 | tf_op jit(solution)/shard_map/ppermute | solution.py:256
  46.2 0.1 collective-permute-start.10
  46.3 4.1 %collective-permute-done.10 = f32[128,128]{1,0:T(8,128)S(1)} collective-permute-done((f32[128,128]{1,0:T(8,128)S(1)}, f32[128,128]{1,0:T(8,128)S(1)}, u32[]{:S(2)}, u32[]{:S(2)}) %collective-permute-start.10) | collective-permute-done | bytes 65568 | tf_op jit(solution)/shard_map/ppermute | solution.py:256
  50.4 0.1 collective-permute-start.11
  50.5 6.1 %collective-permute-done.11.other = f32[128,128]{1,0:T(8,128)S(1)} collective-permute-done((f32[128,128]{1,0:T(8,128)S(1)}, f32[128,128]{1,0:T(8,128)S(1)}, u32[]{:S(2)}, u32[]{:S(2)}) %collective-permute-start.11) | collective-permute-done | bytes 65568 | tf_op jit(solution)/shard_map/ppermute | solution.py:256
  56.5 2.5 %shard_map.111 = (f32[128,128]{1,0:T(8,128)S(1)}, f32[1024,128]{1,0:T(8,128)S(1)}) custom-call(s32[8]{0:T(128)S(1)} %copy-done.1, s32[8,16]{1,0:T(8,128)S(1)} %copy-done, bf16[128,128]{1,0:T(8,128)(2,1)S(1)} %get-tuple-element.34.hit_ref, f32[128,128]{1,0:T(8,128)S(1)} %add.32.mine, f32[128,128]{1,0:T(8,128)S(1)} %collective-permute-done.11.other, ...), custom_call_target="tpu_custom_call" | custom-call | tf_op jit(solution)/shard_map/pallas_call | solution.py:240
  59.0 0.2 collective-permute-start.12
  59.2 1.1 %collective-permute-done.12 = f32[128,128]{1,0:T(8,128)S(1)} collective-permute-done((f32[128,128]{1,0:T(8,128)S(1)}, f32[128,128]{1,0:T(8,128)S(1)}, u32[]{:S(2)}, u32[]{:S(2)}) %collective-permute-start.12) | collective-permute-done | bytes 65568 | tf_op jit(solution)/shard_map/ppermute | solution.py:256
  60.4 1.9 %collective-permute-start.13 = (f32[128,128]{1,0:T(8,128)S(1)}, f32[128,128]{1,0:T(8,128)S(1)}, u32[]{:S(2)}, u32[]{:S(2)}) collective-permute-start(f32[128,128]{1,0:T(8,128)S(1)} %add.33), channel_id=1, source_target_pairs={{0,3},{1,2},{2,1},{3,0},{4,7},{5,6},{6,5},{7,4},{8,11},{9,10},{10,... | collective-permute-start | bytes 196616 | tf_op jit(solution)/shard_map/ppermute | solution.py:256
  62.2 2.3 %collective-permute-done.13 = f32[128,128]{1,0:T(8,128)S(1)} collective-permute-done((f32[128,128]{1,0:T(8,128)S(1)}, f32[128,128]{1,0:T(8,128)S(1)}, u32[]{:S(2)}, u32[]{:S(2)}) %collective-permute-start.13) | collective-permute-done | bytes 65568 | tf_op jit(solution)/shard_map/ppermute | solution.py:256
  64.5 0.1 collective-permute-start.14
  64.6 4.1 %collective-permute-done.14 = f32[128,128]{1,0:T(8,128)S(1)} collective-permute-done((f32[128,128]{1,0:T(8,128)S(1)}, f32[128,128]{1,0:T(8,128)S(1)}, u32[]{:S(2)}, u32[]{:S(2)}) %collective-permute-start.14) | collective-permute-done | bytes 65568 | tf_op jit(solution)/shard_map/ppermute | solution.py:256
  68.7 0.1 collective-permute-start.15
  68.8 6.1 %collective-permute-done.15.other = f32[128,128]{1,0:T(8,128)S(1)} collective-permute-done((f32[128,128]{1,0:T(8,128)S(1)}, f32[128,128]{1,0:T(8,128)S(1)}, u32[]{:S(2)}, u32[]{:S(2)}) %collective-permute-start.15) | collective-permute-done | bytes 65568 | tf_op jit(solution)/shard_map/ppermute | solution.py:256
  74.8 0.8 %shard_map.112 = (f32[8,128]{1,0:T(8,128)}, f32[8,128]{1,0:T(8,128)}) custom-call(f32[128,128]{1,0:T(8,128)S(1)} %add.35.mine, f32[128,128]{1,0:T(8,128)S(1)} %collective-permute-done.15.other, f32[128,128]{1,0:T(8,128)S(1)} %get-tuple-element.59.b_ref, f32[128,128]{1,0:T(8,128)S(1)} %get-tuple-element.60.et_ref, f32[8,128]{1,0:T(8,128)S(1)} %get-tuple-element.61.tot_ref, ...), custom_call_target="tpu_custom_call" | custom-call | tf_op jit(solution)/shard_map/pallas_call | solution.py:240
  (12 shorter events, 0.1 us)
Async XLA Ops:
  1.4 7.3 %collective-permute-start = (f32[24,128]{1,0:T(8,128)S(1)}, f32[24,128]{1,0:T(8,128)S(1)}, u32[]{:S(2)}, u32[]{:S(2)}) collective-permute-start(f32[24,128]{1,0:T(8,128)S(1)} %shard_map.105), channel_id=1, source_target_pairs={{0,9},{1,8},{2,11},{3,10},{4,13},{5,12},{6,15},{7,14},{8,1},{9,0},... | collective-permute-start | bytes 36872 | tf_op jit(solution)/shard_map/ppermute | solution.py:256
  4.9 5.7 %copy-start.1 = (s32[8]{0:T(128)S(1)}, s32[8]{0:T(128)}, u32[]{:S(2)}) copy-start(s32[8]{0:T(128)} %live.11) | copy-start | bytes 100
  8.7 4.2 %collective-permute-start.1 = (f32[48,128]{1,0:T(8,128)S(1)}, f32[48,128]{1,0:T(8,128)S(1)}, u32[]{:S(2)}, u32[]{:S(2)}) collective-permute-start(f32[48,128]{1,0:T(8,128)S(1)} %bitcast.20), channel_id=1, source_target_pairs={{0,5},{1,4},{2,7},{3,6},{4,1},{5,0},{6,3},{7,2},{8,13},{9,12},{10,... | collective-permute-start | bytes 73736 | tf_op jit(solution)/shard_map/ppermute | solution.py:256
  12.9 5.6 %copy-start = (s32[8,16]{1,0:T(8,128)S(1)}, s32[8,16]{1,0:T(8,128)}, u32[]{:S(2)}) copy-start(s32[8,16]{1,0:T(8,128)} %tgt.5) | copy-start | bytes 1540
  12.9 3.8 %collective-permute-start.2 = (f32[96,128]{1,0:T(8,128)S(1)}, f32[96,128]{1,0:T(8,128)S(1)}, u32[]{:S(2)}, u32[]{:S(2)}) collective-permute-start(f32[96,128]{1,0:T(8,128)S(1)} %bitcast.18), channel_id=1, source_target_pairs={{0,3},{1,2},{2,1},{3,0},{4,7},{5,6},{6,5},{7,4},{8,11},{9,10},{10,... | collective-permute-start | bytes 147464 | tf_op jit(solution)/shard_map/ppermute | solution.py:256
  16.7 1.7 %collective-permute-start.3 = (f32[192,128]{1,0:T(8,128)S(1)}, f32[192,128]{1,0:T(8,128)S(1)}, u32[]{:S(2)}, u32[]{:S(2)}) collective-permute-start(f32[192,128]{1,0:T(8,128)S(1)} %bitcast.15), channel_id=1, source_target_pairs={{0,1},{1,0},{2,3},{3,2},{4,5},{5,4},{6,7},{7,6},{8,9},{9,8},{10,11... | collective-permute-start | bytes 294920 | tf_op jit(solution)/shard_map/ppermute | solution.py:256
  21.0 2.3 %collective-permute-start.4 = (f32[128,128]{1,0:T(8,128)S(1)}, f32[128,128]{1,0:T(8,128)S(1)}, u32[]{:S(2)}, u32[]{:S(2)}) collective-permute-start(f32[128,128]{1,0:T(8,128)S(1)} %get-tuple-element.58), channel_id=1, source_target_pairs={{0,1},{1,0},{2,3},{3,2},{4,5},{5,4},{6,7},{7,6},{8,9},{9,8},{10,11... | collective-permute-start | bytes 196616 | tf_op jit(solution)/shard_map/ppermute | solution.py:256
  23.3 4.6 %collective-permute-start.5 = (f32[128,128]{1,0:T(8,128)S(1)}, f32[128,128]{1,0:T(8,128)S(1)}, u32[]{:S(2)}, u32[]{:S(2)}) collective-permute-start(f32[128,128]{1,0:T(8,128)S(1)} %add.27), channel_id=1, source_target_pairs={{0,3},{1,2},{2,1},{3,0},{4,7},{5,6},{6,5},{7,4},{8,11},{9,10},{10,... | collective-permute-start | bytes 196616 | tf_op jit(solution)/shard_map/ppermute | solution.py:256
  27.9 4.1 %collective-permute-start.6 = (f32[128,128]{1,0:T(8,128)S(1)}, f32[128,128]{1,0:T(8,128)S(1)}, u32[]{:S(2)}, u32[]{:S(2)}) collective-permute-start(f32[128,128]{1,0:T(8,128)S(1)} %add.28), channel_id=1, source_target_pairs={{0,5},{1,4},{2,7},{3,6},{4,1},{5,0},{6,3},{7,2},{8,13},{9,12},{10,... | collective-permute-start | bytes 196616 | tf_op jit(solution)/shard_map/ppermute | solution.py:256
  32.1 6.1 %collective-permute-start.7 = (f32[128,128]{1,0:T(8,128)S(1)}, f32[128,128]{1,0:T(8,128)S(1)}, u32[]{:S(2)}, u32[]{:S(2)}) collective-permute-start(f32[128,128]{1,0:T(8,128)S(1)} %add.29.mine), channel_id=1, source_target_pairs={{0,9},{1,8},{2,11},{3,10},{4,13},{5,12},{6,15},{7,14},{8,1},{9,0},... | collective-permute-start | bytes 196616 | tf_op jit(solution)/shard_map/ppermute | solution.py:256
  40.7 1.3 %collective-permute-start.8 = (f32[128,128]{1,0:T(8,128)S(1)}, f32[128,128]{1,0:T(8,128)S(1)}, u32[]{:S(2)}, u32[]{:S(2)}) collective-permute-start(f32[128,128]{1,0:T(8,128)S(1)} %shard_map.110), channel_id=1, source_target_pairs={{0,1},{1,0},{2,3},{3,2},{4,5},{5,4},{6,7},{7,6},{8,9},{9,8},{10,11... | collective-permute-start | bytes 196616 | tf_op jit(solution)/shard_map/ppermute | solution.py:256
  42.0 4.2 %collective-permute-start.9 = (f32[128,128]{1,0:T(8,128)S(1)}, f32[128,128]{1,0:T(8,128)S(1)}, u32[]{:S(2)}, u32[]{:S(2)}) collective-permute-start(f32[128,128]{1,0:T(8,128)S(1)} %add.30), channel_id=1, source_target_pairs={{0,3},{1,2},{2,1},{3,0},{4,7},{5,6},{6,5},{7,4},{8,11},{9,10},{10,... | collective-permute-start | bytes 196616 | tf_op jit(solution)/shard_map/ppermute | solution.py:256
  46.2 4.2 %collective-permute-start.10 = (f32[128,128]{1,0:T(8,128)S(1)}, f32[128,128]{1,0:T(8,128)S(1)}, u32[]{:S(2)}, u32[]{:S(2)}) collective-permute-start(f32[128,128]{1,0:T(8,128)S(1)} %add.31), channel_id=1, source_target_pairs={{0,5},{1,4},{2,7},{3,6},{4,1},{5,0},{6,3},{7,2},{8,13},{9,12},{10,... | collective-permute-start | bytes 196616 | tf_op jit(solution)/shard_map/ppermute | solution.py:256
  50.4 6.2 %collective-permute-start.11 = (f32[128,128]{1,0:T(8,128)S(1)}, f32[128,128]{1,0:T(8,128)S(1)}, u32[]{:S(2)}, u32[]{:S(2)}) collective-permute-start(f32[128,128]{1,0:T(8,128)S(1)} %add.32.mine), channel_id=1, source_target_pairs={{0,9},{1,8},{2,11},{3,10},{4,13},{5,12},{6,15},{7,14},{8,1},{9,0},... | collective-permute-start | bytes 196616 | tf_op jit(solution)/shard_map/ppermute | solution.py:256
  59.0 1.3 %collective-permute-start.12 = (f32[128,128]{1,0:T(8,128)S(1)}, f32[128,128]{1,0:T(8,128)S(1)}, u32[]{:S(2)}, u32[]{:S(2)}) collective-permute-start(f32[128,128]{1,0:T(8,128)S(1)} %get-tuple-element.62), channel_id=1, source_target_pairs={{0,1},{1,0},{2,3},{3,2},{4,5},{5,4},{6,7},{7,6},{8,9},{9,8},{10,11... | collective-permute-start | bytes 196616 | tf_op jit(solution)/shard_map/ppermute | solution.py:256
  60.4 4.1 %collective-permute-start.13 = (f32[128,128]{1,0:T(8,128)S(1)}, f32[128,128]{1,0:T(8,128)S(1)}, u32[]{:S(2)}, u32[]{:S(2)}) collective-permute-start(f32[128,128]{1,0:T(8,128)S(1)} %add.33), channel_id=1, source_target_pairs={{0,3},{1,2},{2,1},{3,0},{4,7},{5,6},{6,5},{7,4},{8,11},{9,10},{10,... | collective-permute-start | bytes 196616 | tf_op jit(solution)/shard_map/ppermute | solution.py:256
  64.5 4.2 %collective-permute-start.14 = (f32[128,128]{1,0:T(8,128)S(1)}, f32[128,128]{1,0:T(8,128)S(1)}, u32[]{:S(2)}, u32[]{:S(2)}) collective-permute-start(f32[128,128]{1,0:T(8,128)S(1)} %add.34), channel_id=1, source_target_pairs={{0,5},{1,4},{2,7},{3,6},{4,1},{5,0},{6,3},{7,2},{8,13},{9,12},{10,... | collective-permute-start | bytes 196616 | tf_op jit(solution)/shard_map/ppermute | solution.py:256
  68.7 6.2 %collective-permute-start.15 = (f32[128,128]{1,0:T(8,128)S(1)}, f32[128,128]{1,0:T(8,128)S(1)}, u32[]{:S(2)}, u32[]{:S(2)}) collective-permute-start(f32[128,128]{1,0:T(8,128)S(1)} %add.35.mine), channel_id=1, source_target_pairs={{0,9},{1,8},{2,11},{3,10},{4,13},{5,12},{6,15},{7,14},{8,1},{9,0},... | collective-permute-start | bytes 196616 | tf_op jit(solution)/shard_map/ppermute | solution.py:256

commit v4 on v3

--- a/solution.py
+++ b/solution.py
@@ -13,6 +13,7 @@
 ALPHA = 0.5
 F = RHO / (RHO + EPS)
 STEP = 4
+ABSENT = -1e30
 PIECES = 4
 
 VMEM = pltpu.VMEM
@@ -36,6 +37,13 @@
 
 def position():
     return lax.axis_index("src").astype(jnp.int32)
+
+
+def half_flip(every):
+    at = position()
+    for r in (16, 8, 4, 2, 1):
+        at = at ^ (at >> r)
+    return (at & 1) * (every // 2)
 
 
 def total_of(x):
@@ -62,7 +70,7 @@
         out_ref[row, :] = jnp.where(lane < count[i], out_ref[row, :], 0.0)
 
 
-def build_tiles(live, first, x_ref, lin_ref, mass_ref, feat, waits, k_ref, la_ref):
+def build_tiles(steps, first, x_ref, lin_ref, mass_ref, feat, waits, k_ref, la_ref):
     blocks, slots, block, width = feat.shape
     mask = diag_mask(block)
     for s in range(blocks):
@@ -92,11 +100,11 @@
                 k_ref[pl.ds(start, block), :] = jnp.exp(e)
             return 0
 
-        lax.fori_loop(0, steps_of(live[at]), tiles, 0)
+        lax.fori_loop(0, steps(at), tiles, 0)
 
 
 def first_build(live_hbm, tgt_hbm, x_hbm, feat, lin_hbm, mass_hbm, *refs):
-    k_ref, la_ref, hit_ref, x_ref, lin_ref, mass_ref, *rest = refs
+    k_ref, la_ref, plan_ref, hit_ref, x_ref, lin_ref, mass_ref, *rest = refs
     later, (live, tgt, flags, own, sems) = rest[:-5], rest[-5:]
     each = own.shape[0]
     slots = tgt.shape[1]
@@ -109,25 +117,30 @@
         c.start()
     for c in copies[:5]:
         c.wait()
-    lane = lax.broadcasted_iota(jnp.int32, (1, flags.shape[1]), 1)
+    every = flags.shape[1]
+    flip = half_flip(every)
+    lane = lax.broadcasted_iota(jnp.int32, (1, every), 1)
     for at in range(flags.shape[0]):
         s, k = divmod(at, slots)
-        row = jnp.where(k < live[s], tgt[s, k], -1)
+        row = jnp.where(k < live[s], tgt[s, k] ^ flip, every)
+        plan_ref[s, k] = row
         flags[at : at + 1, :] = jnp.where(lane == row, 1.0, 0.0)
+    for s in range(tgt.shape[0]):
+        plan_ref[tgt.shape[0], s] = steps_of(live[s])
     hit_ref[...] = jnp.transpose(flags[...]).astype(jnp.bfloat16)
     build_tiles(
-        live, 0, x_ref, lin_ref, mass_ref, own, copies[5 : 5 + each], k_ref, la_ref
+        lambda s: steps_of(live[s]), 0, x_ref, lin_ref, mass_ref, own, copies[5 : 5 + each], k_ref, la_ref
     )
     for c in copies[5 + each :]:
         c.wait()
 
 
-def later_build(first, live, x_ref, feat, lin_ref, mass_ref, k_ref, la_ref):
-    build_tiles(live, first, x_ref, lin_ref, mass_ref, feat, (), k_ref, la_ref)
-
-
-def sweep(live, tgt, hit_ref, w_ref, k_refs, la_refs, dense_ref, acc_ref, u_ref, col_ref):
-    blocks, slots = tgt.shape
+def later_build(first, plan, x_ref, feat, lin_ref, mass_ref, k_ref, la_ref):
+    build_tiles(lambda s: plan[plan.shape[0] - 1, s], first, x_ref, lin_ref, mass_ref, feat, (), k_ref, la_ref)
+
+
+def sweep(plan, hit_ref, w_ref, k_refs, la_refs, keep_ref, send_ref, acc_ref, u_ref, col_ref):
+    blocks, slots = plan.shape[0] - 1, plan.shape[1]
     block = w_ref.shape[1]
     every = w_ref.shape[0] - 8
     each = blocks // len(k_refs)
@@ -138,13 +151,13 @@
         def add_row(p, acc):
             for q in range(STEP):
                 k = p * STEP + q
-                row = jnp.where(k < live[s], tgt[s, k], every)
+                row = plan[s, k]
                 start = pl.multiple_of(((s % each) * slots + k) * block, block)
                 acc = acc + k_ref[pl.ds(start, block), :] * w_ref[pl.ds(row, 1), :]
             return acc
 
         acc_ref[s * block : (s + 1) * block, :] = lax.fori_loop(
-            0, steps_of(live[s]), add_row, jnp.zeros((block, block), jnp.float32)
+            0, plan[blocks, s], add_row, jnp.zeros((block, block), jnp.float32)
         )
     for s in range(blocks):
         rows = pl.ds(s * block, block)
@@ -165,7 +178,7 @@
                 )
             return 0
 
-        lax.fori_loop(0, steps_of(live[s]), add_col, 0)
+        lax.fori_loop(0, plan[blocks, s], add_col, 0)
     col = col_ref[...]
     hit = hit_ref[...]
     dense = jnp.zeros((every, block), jnp.float32)
@@ -173,57 +186,66 @@
         piece = col.astype(jnp.bfloat16)
         dense += jnp.dot(hit, piece, preferred_element_type=jnp.float32)
         col = col - piece.astype(jnp.float32)
-    dense_ref[...] = dense
-
-
-def power_of_ratio(num, den):
-    return jnp.exp(F * (jnp.log(num) - jnp.log(den)))
-
-
-def first_sweep(npieces, live, tgt, hit_ref, *refs):
+    keep_ref[...] = dense[: every // 2, :]
+    send_ref[...] = dense[every // 2 :, :]
+
+
+def first_sweep(npieces, plan, hit_ref, *refs):
     k_refs, la_refs = refs[:npieces], refs[npieces : 2 * npieces]
     parts = refs[2 * npieces : 2 * npieces + 2]
-    dense_ref, b_ref, et_ref, tot_ref, w_ref, acc_ref, u_ref, col_ref = refs[2 * npieces + 2 :]
-    local = tgt.shape[0]
-    n = b_ref.shape[0] // local
-    am = jnp.zeros((local, b_ref.shape[1]), jnp.float32)
+    keep_ref, send_ref, fb_ref, et_ref, tot_ref, w_ref, acc_ref, u_ref, col_ref = refs[
+        2 * npieces + 2 :
+    ]
+    local = plan.shape[0] - 1
+    flip = half_flip(fb_ref.shape[0])
+    n = fb_ref.shape[0] // local
+    am = jnp.zeros((local, fb_ref.shape[1]), jnp.float32)
+    bm = am
     order = distances(n)
     for at in range(n):
         m = functools.reduce(lambda p, q: p ^ q, [d for r, d in enumerate(order) if at >> r & 1], 0)
         part = parts[at // (n // 2)]
         at = (at % (n // 2)) * 3 * local
-        rows = pl.ds(pl.multiple_of((position() ^ m) * local, local), local)
+        rows = pl.ds(pl.multiple_of(((position() ^ m) * local) ^ flip, local), local)
         b = part[at : at + local, :]
         et = jnp.exp((-ALPHA / EPS) * part[at + local : at + 2 * local, :])
-        b_ref[rows, :] = b
+        fb_ref[rows, :] = jnp.where(b > 0.0, F * jnp.log(b), ABSENT)
         et_ref[rows, :] = et
         w_ref[rows, :] = jnp.where(b > 0.0, et, 0.0)
+        bm += b
         am += part[at + 2 * local : at + 3 * local, :]
-    tot = jnp.sqrt(total_of(am) * total_of(b_ref[...]))
+    tot = jnp.sqrt(total_of(am) * total_of(bm))
     tot_ref[...] = jnp.broadcast_to(tot, tot_ref.shape)
-    sweep(live, tgt, hit_ref, w_ref, k_refs, la_refs, dense_ref, acc_ref, u_ref, col_ref)
-
-
-def new_scale(mine, other, b_ref, et_ref, tot_ref):
-    b = b_ref[...]
-    col = (mine[...] + other[...]) * et_ref[...]
-    t = jnp.where(b > 0.0, power_of_ratio(b, col), 0.0)
-    return t, jnp.sqrt(tot_ref[0:1, 0:1] / total_of(t * col))
-
-
-def next_sweep(npieces, live, tgt, hit_ref, mine, other, b_ref, et_ref, tot_ref, *refs):
+    sweep(plan, hit_ref, w_ref, k_refs, la_refs, keep_ref, send_ref, acc_ref, u_ref, col_ref)
+
+
+def new_scale(keep, other, fb_ref, et_ref, tot_ref, t_ref):
+    half = keep.shape[0]
+    mass = jnp.zeros((1, keep.shape[1]), jnp.float32)
+    for at, sums in ((0, keep), (half, other)):
+        rows = slice(at, at + half)
+        fb = fb_ref[rows, :]
+        col = sums[...] * et_ref[rows, :]
+        t = jnp.where(fb > ABSENT, jnp.exp(fb - F * jnp.log(col)), 0.0)
+        t_ref[rows, :] = t
+        mass += jnp.sum(t * col, axis=0, keepdims=True)
+    return jnp.sqrt(tot_ref[0:1, 0:1] / jnp.sum(mass, axis=1, keepdims=True))
+
+
+def next_sweep(npieces, plan, hit_ref, keep, other, fb_ref, et_ref, tot_ref, *refs):
     k_refs, la_refs = refs[:npieces], refs[npieces : 2 * npieces]
-    dense_ref, u_ref, w_ref, acc_ref, col_ref = refs[2 * npieces :]
-    t, factor = new_scale(mine, other, b_ref, et_ref, tot_ref)
-    w_ref[: b_ref.shape[0], :] = t * (factor * et_ref[...])
-    sweep(live, tgt, hit_ref, w_ref, k_refs, la_refs, dense_ref, acc_ref, u_ref, col_ref)
-
-
-def last_kernel(mine, other, b_ref, et_ref, tot_ref, u_ref, src_ref, tgt_ref, t_ref):
+    keep_ref, send_ref, u_ref, w_ref, acc_ref, col_ref = refs[2 * npieces :]
+    factor = new_scale(keep, other, fb_ref, et_ref, tot_ref, w_ref)
+    rows = slice(0, fb_ref.shape[0])
+    w_ref[rows, :] = w_ref[rows, :] * (factor * et_ref[...])
+    sweep(plan, hit_ref, w_ref, k_refs, la_refs, keep_ref, send_ref, acc_ref, u_ref, col_ref)
+
+
+def last_kernel(keep, other, fb_ref, et_ref, tot_ref, u_ref, src_ref, tgt_ref, t_ref):
     local, block = src_ref.shape
-    t, factor = new_scale(mine, other, b_ref, et_ref, tot_ref)
-    t_ref[...] = t * factor
-    tgt_ref[...] = t_ref[pl.ds(pl.multiple_of(position() * local, local), local), :]
+    factor = new_scale(keep, other, fb_ref, et_ref, tot_ref, t_ref)
+    own = (position() * local) ^ half_flip(fb_ref.shape[0])
+    tgt_ref[...] = t_ref[pl.ds(pl.multiple_of(own, local), local), :] * factor
     mask = diag_mask(block)
     for s in range(local):
         src_ref[s : s + 1, :] = to_row(u_ref[s * block : (s + 1) * block, :] * factor, mask)
@@ -241,7 +263,9 @@
         kernel,
         out_shape=outs,
         in_specs=specs,
-        out_specs=[pl.BlockSpec(memory_space=VMEM)] * len(outs),
+        out_specs=[
+            pl.BlockSpec(memory_space=SMEM if out.dtype == jnp.int32 else VMEM) for out in outs
+        ],
         scratch_shapes=scratch,
         compiler_params=pltpu.CompilerParams(vmem_limit_bytes=vmem_mb << 20),
         cost_estimate=pl.CostEstimate(**cost) if cost else None,
@@ -288,12 +312,13 @@
     for at, d in enumerate(order):
         got = exchange(part, n, d)
         if at == 0:
-            k0, la0, hit, xv, linv, massv, *later = call(
+            k0, la0, plan, hit, xv, linv, massv, *later = call(
                 first_build,
                 (tile_live, tile_tgt, src_feat, tile_feat, lin, amass),
                 (
                     shape(each * slots * block),
                     shape(each * block),
+                    SMEM((local + 1, slots), jnp.int32),
                     shape(every, pairs, jnp.bfloat16),
                     shape(local * block, width, src_feat.dtype),
                     shape(local),
@@ -315,7 +340,7 @@
         elif at < PIECES:
             k0, la0 = call(
                 functools.partial(later_build, at * each),
-                (tile_live, xv, later[at - 1], linv, massv),
+                (plan, xv, later[at - 1], linv, massv),
                 (shape(each * slots * block), shape(each * block)),
                 smem=1,
                 **cost,
@@ -331,31 +356,33 @@
     acc = VMEM((local * block, block), f32)
     col = VMEM((pairs, block), f32)
     w = VMEM((every + 8, block), f32)
-    mine, b_all, et_all, tot = call(
+    half = every // 2
+    keep, send, fb, et, tot = call(
         functools.partial(first_sweep, PIECES),
-        (tile_live, tile_tgt, hit, *kern, *la, part, got),
-        (shape(every), shape(every), shape(every), shape(8)),
+        (plan, hit, *kern, *la, part, got),
+        (shape(half), shape(half), shape(every), shape(every), shape(8)),
         scratch=[w, acc, acc, col],
-        smem=2,
+        smem=1,
     )
     u = None
     for iteration in range(ITERS):
-        for d in order[::-1][:-1]:
-            mine = mine + exchange(mine, n, d)
-        other = exchange(mine, n, order[0])
+        keep = keep + exchange(send, n, order[-1])
+        for d in order[-2::-1]:
+            keep = keep + exchange(keep, n, d)
+        other = exchange(keep, n, order[-1])
         if iteration < ITERS - 1:
             last = iteration == ITERS - 2
-            outs = (shape(every), shape(local * block)) if last else (shape(every),)
-            mine, *u = call(
+            outs = (shape(half), shape(half)) + ((shape(local * block),) if last else ())
+            keep, send, *u = call(
                 functools.partial(next_sweep, PIECES),
-                (tile_live, tile_tgt, hit, mine, other, b_all, et_all, tot, *kern, *la),
+                (plan, hit, keep, other, fb, et, tot, *kern, *la),
                 outs,
                 scratch=[w, acc, col] if last else [acc, w, acc, col],
-                smem=2,
+                smem=1,
             )
     src, tgt = call(
         last_kernel,
-        (mine, other, b_all, et_all, tot, *u),
+        (keep, other, fb, et, tot, *u),
         [jax.ShapeDtypeStruct((local, block), f32)] * 2,
         scratch=[VMEM((every, block), f32)],
     )

time: 76.3 us -> 66.1 us (0.87)
  waiting for transfers between devices: 41.3 us -> 29.8 us
  starting transfers between devices: 14.8 us -> 18.7 us
  Pallas kernels: 18.6 us -> 16.2 us
    ppermute x16 -> x19, waiting for transfers between devices: 41.3 us -> 29.8 us  [exchange(): return lax.ppermute(x, 'src', [(i, i ^ d) for i in range(n)])]
    ppermute x16 -> x19, starting transfers between devices: 14.8 us -> 18.7 us  [exchange(): return lax.ppermute(x, 'src', [(i, i ^ d) for i in range(n)])]
    pallas_call x9, Pallas kernels: 18.6 us -> 16.2 us  [call(): pl.pallas_call(kernel, out_shape=outs, in_specs=specs, out_specs=[pl.Bloc...]
  transfers between devices with their start and end apart: 16 -> 19, of which waited for: 13 -> 16; matrix products, arithmetic and copies ran while one was open for 0% -> 0% of each run, Pallas kernels for 13% -> 13%
where the time goes in v4:
time: 66.1 us; the launch traced here: 65.5 us
  waiting for transfers between devices  29.8 us (45%)
  starting transfers between devices  18.7 us (28%)
  Pallas kernels  16.2 us (25%)
  between operations  0.78 us (1%)
    ppermute x19, waiting for transfers between devices, exchange(): return lax.ppermute(x, 'src', [(i, i ^ d) for i in range(n)])  29.8 us
    ppermute x19, starting transfers between devices, exchange(): return lax.ppermute(x, 'src', [(i, i ^ d) for i in range(n)])  18.7 us
    pallas_call x9, Pallas kernels, call(): pl.pallas_call(kernel, out_shape=outs, in_specs=specs, out_specs=[pl.Bloc...  16.2 us
  transfers between devices with their start and end apart: 19, of which 16 were waited for; matrix products, arithmetic and copies ran while one was open for 0% of the time, Pallas kernels for 13%

profile of v4, /device:TPU:0, one launch (start us, length us, event | category | flops | bytes accessed | tf_op | source)
XLA Modules:
  0.0 65.5 jit_solution(12405259353076422962)
XLA Ops:
  0.6 0.8 %shard_map.105 = f32[24,128]{1,0:T(8,128)S(1)} custom-call(s32[8]{0:T(128)} %count_hbm.1, f32[8,128]{1,0:T(8,128)} %bitcast.28, f32[8,128]{1,0:T(8,128)} %bitcast.29, f32[8,128]{1,0:T(8,128)} %bitcast.24), custom_call_target="tpu_custom_call" | custom-call | tf_op jit(solution)/shard_map/pallas_call | solution.py:262
  1.4 3.5 %collective-permute-start = (f32[24,128]{1,0:T(8,128)S(1)}, f32[24,128]{1,0:T(8,128)S(1)}, u32[]{:S(2)}, u32[]{:S(2)}) collective-permute-start(f32[24,128]{1,0:T(8,128)S(1)} %shard_map.105), channel_id=1, source_target_pairs={{0,9},{1,8},{2,11},{3,10},{4,13},{5,12},{6,15},{7,14},{8,1},{9,0},... | collective-permute-start | bytes 36872 | tf_op jit(solution)/shard_map/ppermute | solution.py:280
  4.9 3.8 %shard_map.104 = (f32[4096,128]{1,0:T(8,128)S(1)}, f32[256,128]{1,0:T(8,128)S(1)}, s32[9,16]{1,0:T(8,128)S(4)}, bf16[128,128]{1,0:T(8,128)(2,1)S(1)}, bf16[1024,...) custom-call(s32[8]{0:T(128)} %live_hbm.1, ...), custom_call_target="tpu_custom_call" | custom-call | flops 268435456 | bytes 2097152 | tf_op jit(solution)/shard_map/pallas_call | solution.py:262
  8.7 0.0 collective-permute-done
  8.7 1.9 %collective-permute-start.1 = (f32[48,128]{1,0:T(8,128)S(1)}, f32[48,128]{1,0:T(8,128)S(1)}, u32[]{:S(2)}, u32[]{:S(2)}) collective-permute-start(f32[48,128]{1,0:T(8,128)S(1)} %bitcast.20), channel_id=1, source_target_pairs={{0,5},{1,4},{2,7},{3,6},{4,1},{5,0},{6,3},{7,2},{8,13},{9,12},{10,... | collective-permute-start | bytes 73736 | tf_op jit(solution)/shard_map/ppermute | solution.py:280
  10.7 1.7 %shard_map.106 = (f32[4096,128]{1,0:T(8,128)S(1)}, f32[256,128]{1,0:T(8,128)S(1)}) custom-call(s32[9,16]{1,0:T(8,128)S(4)} %get-tuple-element.39.plan, bf16[1024,256]{1,0:T(8,128)(2,1)S(1)} %get-tuple-element.46.x_ref, bf16[2,16,128,256]{3,2,1,0:T(8,128)(2,1)S(1)} %get-tuple-element.47.feat, f32[8,128]{1,0:T(8,128)S(1)} %get-tuple-element.48.lin_ref, ...), custom_call_target="tpu_custom_call" | custom-call | flops 268435456 | bytes 2097152 | tf_op jit(solution)/shard_map/pallas_call | solution.py:262
  12.3 0.0 collective-permute-done.1
  12.4 1.5 %collective-permute-start.2 = (f32[96,128]{1,0:T(8,128)S(1)}, f32[96,128]{1,0:T(8,128)S(1)}, u32[]{:S(2)}, u32[]{:S(2)}) collective-permute-start(f32[96,128]{1,0:T(8,128)S(1)} %bitcast.18), channel_id=1, source_target_pairs={{0,3},{1,2},{2,1},{3,0},{4,7},{5,6},{6,5},{7,4},{8,11},{9,10},{10,... | collective-permute-start | bytes 147464 | tf_op jit(solution)/shard_map/ppermute | solution.py:280
  13.9 1.2 %shard_map.107 = (f32[4096,128]{1,0:T(8,128)S(1)}, f32[256,128]{1,0:T(8,128)S(1)}) custom-call(s32[9,16]{1,0:T(8,128)S(4)} %get-tuple-element.39.plan, bf16[1024,256]{1,0:T(8,128)(2,1)S(1)} %get-tuple-element.46.x_ref, bf16[2,16,128,256]{3,2,1,0:T(8,128)(2,1)S(1)} %get-tuple-element.54.feat, f32[8,128]{1,0:T(8,128)S(1)} %get-tuple-element.48.lin_ref, ...), custom_call_target="tpu_custom_call" | custom-call | flops 268435456 | bytes 2097152 | tf_op jit(solution)/shard_map/pallas_call | solution.py:262
  15.1 1.0 %collective-permute-done.2 = f32[96,128]{1,0:T(8,128)S(1)} collective-permute-done((f32[96,128]{1,0:T(8,128)S(1)}, f32[96,128]{1,0:T(8,128)S(1)}, u32[]{:S(2)}, u32[]{:S(2)}) %collective-permute-start.2) | collective-permute-done | bytes 49184 | tf_op jit(solution)/shard_map/ppermute | solution.py:280
  16.1 0.3 collective-permute-start.3
  16.4 1.7 %shard_map.108 = (f32[4096,128]{1,0:T(8,128)S(1)}, f32[256,128]{1,0:T(8,128)S(1)}) custom-call(s32[9,16]{1,0:T(8,128)S(4)} %get-tuple-element.39.plan, bf16[1024,256]{1,0:T(8,128)(2,1)S(1)} %get-tuple-element.46.x_ref, bf16[2,16,128,256]{3,2,1,0:T(8,128)(2,1)S(1)} %get-tuple-element.57.feat, f32[8,128]{1,0:T(8,128)S(1)} %get-tuple-element.48.lin_ref, ...), custom_call_target="tpu_custom_call" | custom-call | flops 268435456 | bytes 2097152 | tf_op jit(solution)/shard_map/pallas_call | solution.py:262
  18.1 0.0 collective-permute-done.3.refs_9_
  18.1 2.0 %shard_map.109 = (f32[64,128]{1,0:T(8,128)S(1)}, f32[64,128]{1,0:T(8,128)S(1)}, f32[128,128]{1,0:T(8,128)S(1)}, f32[128,128]{1,0:T(8,128)S(1)}, f32[8,128]{1,0:T(8,128)S(1)}) custom-call(s32[9,16]{1,0:T(8,128)S(4)} %get-tuple-element.39.plan, bf16[128,128]{1,0:T(8,128)(2,1)S(1)} %get-tuple-element.40.hit_ref, f32[4096,128]{1,0:T(8,128)S(1)} %get-tuple-element.43.refs_0_, ...), custom_call_target="tpu_custom_call" | custom-call | tf_op jit(solution)/shard_map/pallas_call | solution.py:262
  20.1 0.1 collective-permute-start.4
  20.2 1.2 %collective-permute-done.4 = f32[64,128]{1,0:T(8,128)S(1)} collective-permute-done((f32[64,128]{1,0:T(8,128)S(1)}, f32[64,128]{1,0:T(8,128)S(1)}, u32[]{:S(2)}, u32[]{:S(2)}) %collective-permute-start.4) | collective-permute-done | bytes 32800 | tf_op jit(solution)/shard_map/ppermute | solution.py:280
  21.4 1.5 %collective-permute-start.5 = (f32[64,128]{1,0:T(8,128)S(1)}, f32[64,128]{1,0:T(8,128)S(1)}, u32[]{:S(2)}, u32[]{:S(2)}) collective-permute-start(f32[64,128]{1,0:T(8,128)S(1)} %add.36), channel_id=1, source_target_pairs={{0,3},{1,2},{2,1},{3,0},{4,7},{5,6},{6,5},{7,4},{8,11},{9,10},{10,... | collective-permute-start | bytes 98312 | tf_op jit(solution)/shard_map/ppermute | solution.py:280
  22.9 1.8 %collective-permute-done.5 = f32[64,128]{1,0:T(8,128)S(1)} collective-permute-done((f32[64,128]{1,0:T(8,128)S(1)}, f32[64,128]{1,0:T(8,128)S(1)}, u32[]{:S(2)}, u32[]{:S(2)}) %collective-permute-start.5) | collective-permute-done | bytes 32800 | tf_op jit(solution)/shard_map/ppermute | solution.py:280
  24.8 1.2 %collective-permute-start.6 = (f32[64,128]{1,0:T(8,128)S(1)}, f32[64,128]{1,0:T(8,128)S(1)}, u32[]{:S(2)}, u32[]{:S(2)}) collective-permute-start(f32[64,128]{1,0:T(8,128)S(1)} %add.37), channel_id=1, source_target_pairs={{0,5},{1,4},{2,7},{3,6},{4,1},{5,0},{6,3},{7,2},{8,13},{9,12},{10,... | collective-permute-start | bytes 98312 | tf_op jit(solution)/shard_map/ppermute | solution.py:280
  26.0 2.1 %collective-permute-done.6 = f32[64,128]{1,0:T(8,128)S(1)} collective-permute-done((f32[64,128]{1,0:T(8,128)S(1)}, f32[64,128]{1,0:T(8,128)S(1)}, u32[]{:S(2)}, u32[]{:S(2)}) %collective-permute-start.6) | collective-permute-done | bytes 32800 | tf_op jit(solution)/shard_map/ppermute | solution.py:280
  28.1 0.8 %collective-permute-start.7 = (f32[64,128]{1,0:T(8,128)S(1)}, f32[64,128]{1,0:T(8,128)S(1)}, u32[]{:S(2)}, u32[]{:S(2)}) collective-permute-start(f32[64,128]{1,0:T(8,128)S(1)} %add.38), channel_id=1, source_target_pairs={{0,9},{1,8},{2,11},{3,10},{4,13},{5,12},{6,15},{7,14},{8,1},{9,0},... | collective-permute-start | bytes 98312 | tf_op jit(solution)/shard_map/ppermute | solution.py:280
  28.9 3.4 %collective-permute-done.7 = f32[64,128]{1,0:T(8,128)S(1)} collective-permute-done((f32[64,128]{1,0:T(8,128)S(1)}, f32[64,128]{1,0:T(8,128)S(1)}, u32[]{:S(2)}, u32[]{:S(2)}) %collective-permute-start.7) | collective-permute-done | bytes 32800 | tf_op jit(solution)/shard_map/ppermute | solution.py:280
  32.3 0.2 collective-permute-start.8
  32.5 1.0 %collective-permute-done.8.other = f32[64,128]{1,0:T(8,128)S(1)} collective-permute-done((f32[64,128]{1,0:T(8,128)S(1)}, f32[64,128]{1,0:T(8,128)S(1)}, u32[]{:S(2)}, u32[]{:S(2)}) %collective-permute-start.8) | collective-permute-done | bytes 32800 | tf_op jit(solution)/shard_map/ppermute | solution.py:280
  33.6 2.1 %shard_map.110 = (f32[64,128]{1,0:T(8,128)S(1)}, f32[64,128]{1,0:T(8,128)S(1)}) custom-call(s32[9,16]{1,0:T(8,128)S(4)} %get-tuple-element.39.plan, bf16[128,128]{1,0:T(8,128)(2,1)S(1)} %get-tuple-element.40.hit_ref, f32[64,128]{1,0:T(8,128)S(1)} %add.39.keep, f32[64,128]{1,0:T(8,128)S(1)} %collective-permute-done.8.other, ...), custom_call_target="tpu_custom_call" | custom-call | tf_op jit(solution)/shard_map/pallas_call | solution.py:262
  35.6 0.1 collective-permute-start.9
  35.7 1.2 %collective-permute-done.9 = f32[64,128]{1,0:T(8,128)S(1)} collective-permute-done((f32[64,128]{1,0:T(8,128)S(1)}, f32[64,128]{1,0:T(8,128)S(1)}, u32[]{:S(2)}, u32[]{:S(2)}) %collective-permute-start.9) | collective-permute-done | bytes 32800 | tf_op jit(solution)/shard_map/ppermute | solution.py:280
  36.9 1.4 %collective-permute-start.10 = (f32[64,128]{1,0:T(8,128)S(1)}, f32[64,128]{1,0:T(8,128)S(1)}, u32[]{:S(2)}, u32[]{:S(2)}) collective-permute-start(f32[64,128]{1,0:T(8,128)S(1)} %add.40), channel_id=1, source_target_pairs={{0,3},{1,2},{2,1},{3,0},{4,7},{5,6},{6,5},{7,4},{8,11},{9,10},{10,... | collective-permute-start | bytes 98312 | tf_op jit(solution)/shard_map/ppermute | solution.py:280
  38.3 1.9 %collective-permute-done.10 = f32[64,128]{1,0:T(8,128)S(1)} collective-permute-done((f32[64,128]{1,0:T(8,128)S(1)}, f32[64,128]{1,0:T(8,128)S(1)}, u32[]{:S(2)}, u32[]{:S(2)}) %collective-permute-start.10) | collective-permute-done | bytes 32800 | tf_op jit(solution)/shard_map/ppermute | solution.py:280
  40.3 1.2 %collective-permute-start.11 = (f32[64,128]{1,0:T(8,128)S(1)}, f32[64,128]{1,0:T(8,128)S(1)}, u32[]{:S(2)}, u32[]{:S(2)}) collective-permute-start(f32[64,128]{1,0:T(8,128)S(1)} %add.41), channel_id=1, source_target_pairs={{0,5},{1,4},{2,7},{3,6},{4,1},{5,0},{6,3},{7,2},{8,13},{9,12},{10,... | collective-permute-start | bytes 98312 | tf_op jit(solution)/shard_map/ppermute | solution.py:280
  41.4 2.2 %collective-permute-done.11 = f32[64,128]{1,0:T(8,128)S(1)} collective-permute-done((f32[64,128]{1,0:T(8,128)S(1)}, f32[64,128]{1,0:T(8,128)S(1)}, u32[]{:S(2)}, u32[]{:S(2)}) %collective-permute-start.11) | collective-permute-done | bytes 32800 | tf_op jit(solution)/shard_map/ppermute | solution.py:280
  43.6 1.0 %collective-permute-start.12 = (f32[64,128]{1,0:T(8,128)S(1)}, f32[64,128]{1,0:T(8,128)S(1)}, u32[]{:S(2)}, u32[]{:S(2)}) collective-permute-start(f32[64,128]{1,0:T(8,128)S(1)} %add.42), channel_id=1, source_target_pairs={{0,9},{1,8},{2,11},{3,10},{4,13},{5,12},{6,15},{7,14},{8,1},{9,0},... | collective-permute-start | bytes 98312 | tf_op jit(solution)/shard_map/ppermute | solution.py:280
  44.6 3.3 %collective-permute-done.12 = f32[64,128]{1,0:T(8,128)S(1)} collective-permute-done((f32[64,128]{1,0:T(8,128)S(1)}, f32[64,128]{1,0:T(8,128)S(1)}, u32[]{:S(2)}, u32[]{:S(2)}) %collective-permute-start.12) | collective-permute-done | bytes 32800 | tf_op jit(solution)/shard_map/ppermute | solution.py:280
  47.9 0.2 collective-permute-start.13
  48.0 1.0 %collective-permute-done.13.other = f32[64,128]{1,0:T(8,128)S(1)} collective-permute-done((f32[64,128]{1,0:T(8,128)S(1)}, f32[64,128]{1,0:T(8,128)S(1)}, u32[]{:S(2)}, u32[]{:S(2)}) %collective-permute-start.13) | collective-permute-done | bytes 32800 | tf_op jit(solution)/shard_map/ppermute | solution.py:280
  49.1 2.1 %shard_map.111 = (f32[64,128]{1,0:T(8,128)S(1)}, f32[64,128]{1,0:T(8,128)S(1)}, f32[1024,128]{1,0:T(8,128)S(1)}) custom-call(s32[9,16]{1,0:T(8,128)S(4)} %get-tuple-element.39.plan, bf16[128,128]{1,0:T(8,128)(2,1)S(1)} %get-tuple-element.40.hit_ref, f32[64,128]{1,0:T(8,128)S(1)} %add.43.keep, f32[64,128]{1,0:T(8,128)S(1)} %collective-permute-done.13.other, ...), custom_call_target="tpu_custom_call" | custom-call | tf_op jit(solution)/shard_map/pallas_call | solution.py:262
  51.2 0.1 collective-permute-start.14
  51.3 1.2 %collective-permute-done.14 = f32[64,128]{1,0:T(8,128)S(1)} collective-permute-done((f32[64,128]{1,0:T(8,128)S(1)}, f32[64,128]{1,0:T(8,128)S(1)}, u32[]{:S(2)}, u32[]{:S(2)}) %collective-permute-start.14) | collective-permute-done | bytes 32800 | tf_op jit(solution)/shard_map/ppermute | solution.py:280
  52.5 1.3 %collective-permute-start.15 = (f32[64,128]{1,0:T(8,128)S(1)}, f32[64,128]{1,0:T(8,128)S(1)}, u32[]{:S(2)}, u32[]{:S(2)}) collective-permute-start(f32[64,128]{1,0:T(8,128)S(1)} %add.44), channel_id=1, source_target_pairs={{0,3},{1,2},{2,1},{3,0},{4,7},{5,6},{6,5},{7,4},{8,11},{9,10},{10,... | collective-permute-start | bytes 98312 | tf_op jit(solution)/shard_map/ppermute | solution.py:280
  53.8 2.1 %collective-permute-done.15 = f32[64,128]{1,0:T(8,128)S(1)} collective-permute-done((f32[64,128]{1,0:T(8,128)S(1)}, f32[64,128]{1,0:T(8,128)S(1)}, u32[]{:S(2)}, u32[]{:S(2)}) %collective-permute-start.15) | collective-permute-done | bytes 32800 | tf_op jit(solution)/shard_map/ppermute | solution.py:280
  55.8 1.1 %collective-permute-start.16 = (f32[64,128]{1,0:T(8,128)S(1)}, f32[64,128]{1,0:T(8,128)S(1)}, u32[]{:S(2)}, u32[]{:S(2)}) collective-permute-start(f32[64,128]{1,0:T(8,128)S(1)} %add.45), channel_id=1, source_target_pairs={{0,5},{1,4},{2,7},{3,6},{4,1},{5,0},{6,3},{7,2},{8,13},{9,12},{10,... | collective-permute-start | bytes 98312 | tf_op jit(solution)/shard_map/ppermute | solution.py:280
  56.9 2.2 %collective-permute-done.16 = f32[64,128]{1,0:T(8,128)S(1)} collective-permute-done((f32[64,128]{1,0:T(8,128)S(1)}, f32[64,128]{1,0:T(8,128)S(1)}, u32[]{:S(2)}, u32[]{:S(2)}) %collective-permute-start.16) | collective-permute-done | bytes 32800 | tf_op jit(solution)/shard_map/ppermute | solution.py:280
  59.2 1.2 %collective-permute-start.17 = (f32[64,128]{1,0:T(8,128)S(1)}, f32[64,128]{1,0:T(8,128)S(1)}, u32[]{:S(2)}, u32[]{:S(2)}) collective-permute-start(f32[64,128]{1,0:T(8,128)S(1)} %add.46), channel_id=1, source_target_pairs={{0,9},{1,8},{2,11},{3,10},{4,13},{5,12},{6,15},{7,14},{8,1},{9,0},... | collective-permute-start | bytes 98312 | tf_op jit(solution)/shard_map/ppermute | solution.py:280
  60.3 3.1 %collective-permute-done.17 = f32[64,128]{1,0:T(8,128)S(1)} collective-permute-done((f32[64,128]{1,0:T(8,128)S(1)}, f32[64,128]{1,0:T(8,128)S(1)}, u32[]{:S(2)}, u32[]{:S(2)}) %collective-permute-start.17) | collective-permute-done | bytes 32800 | tf_op jit(solution)/shard_map/ppermute | solution.py:280
  63.4 0.2 collective-permute-start.18
  63.6 1.0 %collective-permute-done.18.other = f32[64,128]{1,0:T(8,128)S(1)} collective-permute-done((f32[64,128]{1,0:T(8,128)S(1)}, f32[64,128]{1,0:T(8,128)S(1)}, u32[]{:S(2)}, u32[]{:S(2)}) %collective-permute-start.18) | collective-permute-done | bytes 32800 | tf_op jit(solution)/shard_map/ppermute | solution.py:280
  64.6 0.8 %shard_map.112 = (f32[8,128]{1,0:T(8,128)}, f32[8,128]{1,0:T(8,128)}) custom-call(f32[64,128]{1,0:T(8,128)S(1)} %add.47.keep, f32[64,128]{1,0:T(8,128)S(1)} %collective-permute-done.18.other, f32[128,128]{1,0:T(8,128)S(1)} %get-tuple-element.66.fb_ref, f32[128,128]{1,0:T(8,128)S(1)} %get-tuple-element.67.et_ref, f32[8,128]{1,0:T(8,128)S(1)} %get-tuple-element.68.tot_ref, ...), custom_call_target="tpu_custom_call" | custom-call | tf_op jit(solution)/shard_map/pallas_call | solution.py:262
  (15 shorter events, 0.1 us)
Async XLA Ops:
  1.4 7.3 %collective-permute-start = (f32[24,128]{1,0:T(8,128)S(1)}, f32[24,128]{1,0:T(8,128)S(1)}, u32[]{:S(2)}, u32[]{:S(2)}) collective-permute-start(f32[24,128]{1,0:T(8,128)S(1)} %shard_map.105), channel_id=1, source_target_pairs={{0,9},{1,8},{2,11},{3,10},{4,13},{5,12},{6,15},{7,14},{8,1},{9,0},... | collective-permute-start | bytes 36872 | tf_op jit(solution)/shard_map/ppermute | solution.py:280
  8.7 3.6 %collective-permute-start.1 = (f32[48,128]{1,0:T(8,128)S(1)}, f32[48,128]{1,0:T(8,128)S(1)}, u32[]{:S(2)}, u32[]{:S(2)}) collective-permute-start(f32[48,128]{1,0:T(8,128)S(1)} %bitcast.20), channel_id=1, source_target_pairs={{0,5},{1,4},{2,7},{3,6},{4,1},{5,0},{6,3},{7,2},{8,13},{9,12},{10,... | collective-permute-start | bytes 73736 | tf_op jit(solution)/shard_map/ppermute | solution.py:280
  12.4 3.7 %collective-permute-start.2 = (f32[96,128]{1,0:T(8,128)S(1)}, f32[96,128]{1,0:T(8,128)S(1)}, u32[]{:S(2)}, u32[]{:S(2)}) collective-permute-start(f32[96,128]{1,0:T(8,128)S(1)} %bitcast.18), channel_id=1, source_target_pairs={{0,3},{1,2},{2,1},{3,0},{4,7},{5,6},{6,5},{7,4},{8,11},{9,10},{10,... | collective-permute-start | bytes 147464 | tf_op jit(solution)/shard_map/ppermute | solution.py:280
  16.1 2.0 %collective-permute-start.3 = (f32[192,128]{1,0:T(8,128)S(1)}, f32[192,128]{1,0:T(8,128)S(1)}, u32[]{:S(2)}, u32[]{:S(2)}) collective-permute-start(f32[192,128]{1,0:T(8,128)S(1)} %bitcast.15), channel_id=1, source_target_pairs={{0,1},{1,0},{2,3},{3,2},{4,5},{5,4},{6,7},{7,6},{8,9},{9,8},{10,11... | collective-permute-start | bytes 294920 | tf_op jit(solution)/shard_map/ppermute | solution.py:280
  20.1 1.3 %collective-permute-start.4 = (f32[64,128]{1,0:T(8,128)S(1)}, f32[64,128]{1,0:T(8,128)S(1)}, u32[]{:S(2)}, u32[]{:S(2)}) collective-permute-start(f32[64,128]{1,0:T(8,128)S(1)} %get-tuple-element.65), channel_id=1, source_target_pairs={{0,1},{1,0},{2,3},{3,2},{4,5},{5,4},{6,7},{7,6},{8,9},{9,8},{10,11... | collective-permute-start | bytes 98312 | tf_op jit(solution)/shard_map/ppermute | solution.py:280
  21.4 3.3 %collective-permute-start.5 = (f32[64,128]{1,0:T(8,128)S(1)}, f32[64,128]{1,0:T(8,128)S(1)}, u32[]{:S(2)}, u32[]{:S(2)}) collective-permute-start(f32[64,128]{1,0:T(8,128)S(1)} %add.36), channel_id=1, source_target_pairs={{0,3},{1,2},{2,1},{3,0},{4,7},{5,6},{6,5},{7,4},{8,11},{9,10},{10,... | collective-permute-start | bytes 98312 | tf_op jit(solution)/shard_map/ppermute | solution.py:280
  24.8 3.3 %collective-permute-start.6 = (f32[64,128]{1,0:T(8,128)S(1)}, f32[64,128]{1,0:T(8,128)S(1)}, u32[]{:S(2)}, u32[]{:S(2)}) collective-permute-start(f32[64,128]{1,0:T(8,128)S(1)} %add.37), channel_id=1, source_target_pairs={{0,5},{1,4},{2,7},{3,6},{4,1},{5,0},{6,3},{7,2},{8,13},{9,12},{10,... | collective-permute-start | bytes 98312 | tf_op jit(solution)/shard_map/ppermute | solution.py:280
  28.1 4.2 %collective-permute-start.7 = (f32[64,128]{1,0:T(8,128)S(1)}, f32[64,128]{1,0:T(8,128)S(1)}, u32[]{:S(2)}, u32[]{:S(2)}) collective-permute-start(f32[64,128]{1,0:T(8,128)S(1)} %add.38), channel_id=1, source_target_pairs={{0,9},{1,8},{2,11},{3,10},{4,13},{5,12},{6,15},{7,14},{8,1},{9,0},... | collective-permute-start | bytes 98312 | tf_op jit(solution)/shard_map/ppermute | solution.py:280
  32.3 1.2 %collective-permute-start.8 = (f32[64,128]{1,0:T(8,128)S(1)}, f32[64,128]{1,0:T(8,128)S(1)}, u32[]{:S(2)}, u32[]{:S(2)}) collective-permute-start(f32[64,128]{1,0:T(8,128)S(1)} %add.39.keep), channel_id=1, source_target_pairs={{0,1},{1,0},{2,3},{3,2},{4,5},{5,4},{6,7},{7,6},{8,9},{9,8},{10,11... | collective-permute-start | bytes 98312 | tf_op jit(solution)/shard_map/ppermute | solution.py:280
  35.6 1.3 %collective-permute-start.9 = (f32[64,128]{1,0:T(8,128)S(1)}, f32[64,128]{1,0:T(8,128)S(1)}, u32[]{:S(2)}, u32[]{:S(2)}) collective-permute-start(f32[64,128]{1,0:T(8,128)S(1)} %get-tuple-element.70), channel_id=1, source_target_pairs={{0,1},{1,0},{2,3},{3,2},{4,5},{5,4},{6,7},{7,6},{8,9},{9,8},{10,11... | collective-permute-start | bytes 98312 | tf_op jit(solution)/shard_map/ppermute | solution.py:280
  36.9 3.3 %collective-permute-start.10 = (f32[64,128]{1,0:T(8,128)S(1)}, f32[64,128]{1,0:T(8,128)S(1)}, u32[]{:S(2)}, u32[]{:S(2)}) collective-permute-start(f32[64,128]{1,0:T(8,128)S(1)} %add.40), channel_id=1, source_target_pairs={{0,3},{1,2},{2,1},{3,0},{4,7},{5,6},{6,5},{7,4},{8,11},{9,10},{10,... | collective-permute-start | bytes 98312 | tf_op jit(solution)/shard_map/ppermute | solution.py:280
  40.3 3.3 %collective-permute-start.11 = (f32[64,128]{1,0:T(8,128)S(1)}, f32[64,128]{1,0:T(8,128)S(1)}, u32[]{:S(2)}, u32[]{:S(2)}) collective-permute-start(f32[64,128]{1,0:T(8,128)S(1)} %add.41), channel_id=1, source_target_pairs={{0,5},{1,4},{2,7},{3,6},{4,1},{5,0},{6,3},{7,2},{8,13},{9,12},{10,... | collective-permute-start | bytes 98312 | tf_op jit(solution)/shard_map/ppermute | solution.py:280
  43.6 4.2 %collective-permute-start.12 = (f32[64,128]{1,0:T(8,128)S(1)}, f32[64,128]{1,0:T(8,128)S(1)}, u32[]{:S(2)}, u32[]{:S(2)}) collective-permute-start(f32[64,128]{1,0:T(8,128)S(1)} %add.42), channel_id=1, source_target_pairs={{0,9},{1,8},{2,11},{3,10},{4,13},{5,12},{6,15},{7,14},{8,1},{9,0},... | collective-permute-start | bytes 98312 | tf_op jit(solution)/shard_map/ppermute | solution.py:280
  47.9 1.2 %collective-permute-start.13 = (f32[64,128]{1,0:T(8,128)S(1)}, f32[64,128]{1,0:T(8,128)S(1)}, u32[]{:S(2)}, u32[]{:S(2)}) collective-permute-start(f32[64,128]{1,0:T(8,128)S(1)} %add.43.keep), channel_id=1, source_target_pairs={{0,1},{1,0},{2,3},{3,2},{4,5},{5,4},{6,7},{7,6},{8,9},{9,8},{10,11... | collective-permute-start | bytes 98312 | tf_op jit(solution)/shard_map/ppermute | solution.py:280
  51.2 1.3 %collective-permute-start.14 = (f32[64,128]{1,0:T(8,128)S(1)}, f32[64,128]{1,0:T(8,128)S(1)}, u32[]{:S(2)}, u32[]{:S(2)}) collective-permute-start(f32[64,128]{1,0:T(8,128)S(1)} %get-tuple-element.72), channel_id=1, source_target_pairs={{0,1},{1,0},{2,3},{3,2},{4,5},{5,4},{6,7},{7,6},{8,9},{9,8},{10,11... | collective-permute-start | bytes 98312 | tf_op jit(solution)/shard_map/ppermute | solution.py:280
  52.5 3.3 %collective-permute-start.15 = (f32[64,128]{1,0:T(8,128)S(1)}, f32[64,128]{1,0:T(8,128)S(1)}, u32[]{:S(2)}, u32[]{:S(2)}) collective-permute-start(f32[64,128]{1,0:T(8,128)S(1)} %add.44), channel_id=1, source_target_pairs={{0,3},{1,2},{2,1},{3,0},{4,7},{5,6},{6,5},{7,4},{8,11},{9,10},{10,... | collective-permute-start | bytes 98312 | tf_op jit(solution)/shard_map/ppermute | solution.py:280
  55.8 3.3 %collective-permute-start.16 = (f32[64,128]{1,0:T(8,128)S(1)}, f32[64,128]{1,0:T(8,128)S(1)}, u32[]{:S(2)}, u32[]{:S(2)}) collective-permute-start(f32[64,128]{1,0:T(8,128)S(1)} %add.45), channel_id=1, source_target_pairs={{0,5},{1,4},{2,7},{3,6},{4,1},{5,0},{6,3},{7,2},{8,13},{9,12},{10,... | collective-permute-start | bytes 98312 | tf_op jit(solution)/shard_map/ppermute | solution.py:280
  59.2 4.2 %collective-permute-start.17 = (f32[64,128]{1,0:T(8,128)S(1)}, f32[64,128]{1,0:T(8,128)S(1)}, u32[]{:S(2)}, u32[]{:S(2)}) collective-permute-start(f32[64,128]{1,0:T(8,128)S(1)} %add.46), channel_id=1, source_target_pairs={{0,9},{1,8},{2,11},{3,10},{4,13},{5,12},{6,15},{7,14},{8,1},{9,0},... | collective-permute-start | bytes 98312 | tf_op jit(solution)/shard_map/ppermute | solution.py:280
  63.4 1.2 %collective-permute-start.18 = (f32[64,128]{1,0:T(8,128)S(1)}, f32[64,128]{1,0:T(8,128)S(1)}, u32[]{:S(2)}, u32[]{:S(2)}) collective-permute-start(f32[64,128]{1,0:T(8,128)S(1)} %add.47.keep), channel_id=1, source_target_pairs={{0,1},{1,0},{2,3},{3,2},{4,5},{5,4},{6,7},{7,6},{8,9},{9,8},{10,11... | collective-permute-start | bytes 98312 | tf_op jit(solution)/shard_map/ppermute | solution.py:280

commit v5 on v4

--- a/solution.py
+++ b/solution.py
@@ -12,9 +12,10 @@
 RHO = 1.0
 ALPHA = 0.5
 F = RHO / (RHO + EPS)
+LOG2E = 1.4426950408889634
 STEP = 4
 ABSENT = -1e30
-PIECES = 4
+PIECES = (2, 2, 3, 1)
 
 VMEM = pltpu.VMEM
 SMEM = pltpu.SMEM
@@ -72,6 +73,7 @@
 
 def build_tiles(steps, first, x_ref, lin_ref, mass_ref, feat, waits, k_ref, la_ref):
     blocks, slots, block, width = feat.shape
+    scale = LOG2E / (width * EPS)
     mask = diag_mask(block)
     for s in range(blocks):
         at = first + s
@@ -79,7 +81,7 @@
         x32 = x.astype(jnp.float32)
         sq = jnp.sum(x32 * x32, axis=1, keepdims=True)
         lin = to_column(lin_ref[at : at + 1, :], mask)
-        base = (2.0 - sq / width - ALPHA * lin) / EPS
+        base = (2.0 - sq / width - ALPHA * lin) * (LOG2E / EPS)
         base = jnp.broadcast_to(base, (block, block))
         la = F * jnp.log(to_column(mass_ref[at : at + 1, :], mask))
         la_ref[s * block : (s + 1) * block, :] = jnp.broadcast_to(la, (block, block))
@@ -95,23 +97,21 @@
             for q in range(STEP):
                 cols = slice(q * block, (q + 1) * block)
                 row = to_row(ysq[cols, :], mask)
-                e = (2.0 / (width * EPS)) * cross[:, cols] + (base - row * (1.0 / (width * EPS)))
+                e = (2.0 * scale) * cross[:, cols] + (base - row * scale)
                 start = pl.multiple_of((s * slots + p * STEP + q) * block, block)
-                k_ref[pl.ds(start, block), :] = jnp.exp(e)
+                k_ref[pl.ds(start, block), :] = jnp.exp2(e)
             return 0
 
         lax.fori_loop(0, steps(at), tiles, 0)
 
 
-def first_build(live_hbm, tgt_hbm, x_hbm, feat, lin_hbm, mass_hbm, *refs):
-    k_ref, la_ref, plan_ref, hit_ref, x_ref, lin_ref, mass_ref, *rest = refs
-    later, (live, tgt, flags, own, sems) = rest[:-5], rest[-5:]
-    each = own.shape[0]
-    slots = tgt.shape[1]
-    copies = [(live_hbm, live), (x_hbm, x_ref), (lin_hbm, lin_ref), (mass_hbm, mass_ref)]
-    copies += [(tgt_hbm, tgt)]
-    copies += [(feat.at[s], own.at[s]) for s in range(each)]
-    copies += [(feat.at[pl.ds((i + 1) * each, each)], to) for i, to in enumerate(later)]
+def first_build(live_hbm, tgt_hbm, x_hbm, lin_hbm, mass_hbm, feat, *refs):
+    k_ref, la_ref, next_ref, plan_ref, hit_ref, x_ref, lin_ref, mass_ref = refs[:8]
+    live, tgt, flags, own, sems = refs[8:]
+    size, slots = own.shape[:2]
+    copies = [(live_hbm, live), (tgt_hbm, tgt), (x_hbm, x_ref), (lin_hbm, lin_ref), (mass_hbm, mass_ref)]
+    copies += [(feat.at[s], own.at[s]) for s in range(size)]
+    copies += [(feat.at[pl.ds(size, next_ref.shape[0])], next_ref)]
     copies = [pltpu.make_async_copy(f, t, sems.at[i]) for i, (f, t) in enumerate(copies)]
     for c in copies:
         c.start()
@@ -129,30 +129,48 @@
         plan_ref[tgt.shape[0], s] = steps_of(live[s])
     hit_ref[...] = jnp.transpose(flags[...]).astype(jnp.bfloat16)
     build_tiles(
-        lambda s: steps_of(live[s]), 0, x_ref, lin_ref, mass_ref, own, copies[5 : 5 + each], k_ref, la_ref
-    )
-    for c in copies[5 + each :]:
-        c.wait()
-
-
-def later_build(first, plan, x_ref, feat, lin_ref, mass_ref, k_ref, la_ref):
-    build_tiles(lambda s: plan[plan.shape[0] - 1, s], first, x_ref, lin_ref, mass_ref, feat, (), k_ref, la_ref)
+        lambda s: steps_of(live[s]), 0, x_ref, lin_ref, mass_ref, own, copies[5:-1], k_ref, la_ref
+    )
+    copies[-1].wait()
+
+
+def later_build(first, plan, x_ref, lin_ref, mass_ref, own, feat, k_ref, la_ref, *rest):
+    copy = None
+    if rest:
+        next_ref, sem = rest
+        copy = pltpu.make_async_copy(
+            feat.at[pl.ds(first + own.shape[0], next_ref.shape[0])], next_ref, sem
+        )
+        copy.start()
+    build_tiles(
+        lambda s: plan[plan.shape[0] - 1, s], first, x_ref, lin_ref, mass_ref, own, (), k_ref, la_ref
+    )
+    if copy:
+        copy.wait()
+
+
+def place(s):
+    piece = 0
+    while s >= PIECES[piece]:
+        s -= PIECES[piece]
+        piece += 1
+    return piece, s
 
 
 def sweep(plan, hit_ref, w_ref, k_refs, la_refs, keep_ref, send_ref, acc_ref, u_ref, col_ref):
     blocks, slots = plan.shape[0] - 1, plan.shape[1]
     block = w_ref.shape[1]
     every = w_ref.shape[0] - 8
-    each = blocks // len(k_refs)
     w_ref[every:, :] = jnp.zeros((8, block), jnp.float32)
     for s in range(blocks):
-        k_ref = k_refs[s // each]
+        piece, at = place(s)
+        k_ref, base = k_refs[piece], at * slots
 
         def add_row(p, acc):
             for q in range(STEP):
                 k = p * STEP + q
                 row = plan[s, k]
-                start = pl.multiple_of(((s % each) * slots + k) * block, block)
+                start = pl.multiple_of((base + k) * block, block)
                 acc = acc + k_ref[pl.ds(start, block), :] * w_ref[pl.ds(row, 1), :]
             return acc
 
@@ -162,17 +180,19 @@
     for s in range(blocks):
         rows = pl.ds(s * block, block)
         total = jnp.sum(acc_ref[rows, :], axis=1, keepdims=True)
-        la = la_refs[s // each][pl.ds((s % each) * block, block), :]
+        piece, at = place(s)
+        la = la_refs[piece][pl.ds(at * block, block), :]
         u_ref[rows, :] = jnp.exp(la - F * jnp.log(total))
     col_ref[...] = jnp.zeros_like(col_ref)
     for s in range(blocks):
-        k_ref = k_refs[s // each]
+        piece, at = place(s)
+        k_ref, base = k_refs[piece], at * slots
         u = u_ref[s * block : (s + 1) * block, :]
 
         def add_col(p, _):
             for q in range(STEP):
                 k = p * STEP + q
-                start = pl.multiple_of(((s % each) * slots + k) * block, block)
+                start = pl.multiple_of((base + k) * block, block)
                 col_ref[pl.ds(s * slots + k, 1), :] = jnp.sum(
                     k_ref[pl.ds(start, block), :] * u, axis=0, keepdims=True
                 )
@@ -182,7 +202,7 @@
     col = col_ref[...]
     hit = hit_ref[...]
     dense = jnp.zeros((every, block), jnp.float32)
-    for _ in range(3):
+    for _ in range(2):
         piece = col.astype(jnp.bfloat16)
         dense += jnp.dot(hit, piece, preferred_element_type=jnp.float32)
         col = col - piece.astype(jnp.float32)
@@ -300,65 +320,69 @@
         scratch=[SMEM((local,), jnp.int32), pltpu.SemaphoreType.DMA((4,))],
         hbm=(0, 1, 2, 3),
     )
-    each = local // PIECES
-    feats = pltpu.VMEM((each, slots, block, width), tile_feat.dtype)
-    cost = dict(
-        flops=2 * each * slots * block * block * width,
-        bytes_accessed=2 * each * slots * block * width,
-        transcendentals=each * slots * block * block,
-    )
+    def feats(size):
+        return pltpu.VMEM((size, slots, block, width), tile_feat.dtype)
+
     order = distances(n)
     kern, la = [], []
+    following = None
     for at, d in enumerate(order):
         got = exchange(part, n, d)
+        if at < len(PIECES):
+            size = PIECES[at]
+            ahead = [feats(PIECES[at + 1])] if at + 1 < len(PIECES) else []
+            outs = (shape(size * slots * block), shape(size * block), *ahead)
+            cost = dict(
+                flops=2 * size * slots * block * block * width,
+                bytes_accessed=2 * size * slots * block * width,
+                transcendentals=size * slots * block * block,
+            )
         if at == 0:
-            k0, la0, plan, hit, xv, linv, massv, *later = call(
+            k0, la0, following, plan, hit, xv, linv, massv = call(
                 first_build,
-                (tile_live, tile_tgt, src_feat, tile_feat, lin, amass),
+                (tile_live, tile_tgt, src_feat, lin, amass, tile_feat),
                 (
-                    shape(each * slots * block),
-                    shape(each * block),
+                    *outs,
                     SMEM((local + 1, slots), jnp.int32),
                     shape(every, pairs, jnp.bfloat16),
                     shape(local * block, width, src_feat.dtype),
                     shape(local),
                     shape(local),
-                    *[feats] * (PIECES - 1),
                 ),
                 scratch=[
                     SMEM((local,), jnp.int32),
                     SMEM((local, slots), jnp.int32),
                     VMEM((pairs, every), f32),
-                    feats,
-                    pltpu.SemaphoreType.DMA((5 + each + PIECES - 1,)),
+                    feats(size),
+                    pltpu.SemaphoreType.DMA((6 + size,)),
                 ],
                 hbm=(0, 1, 2, 3, 4, 5),
                 **cost,
             )
-            kern.append(k0)
-            la.append(la0)
-        elif at < PIECES:
-            k0, la0 = call(
-                functools.partial(later_build, at * each),
-                (plan, xv, later[at - 1], linv, massv),
-                (shape(each * slots * block), shape(each * block)),
+        elif at < len(PIECES):
+            k0, la0, *following = call(
+                functools.partial(later_build, sum(PIECES[:at])),
+                (plan, xv, linv, massv, following, tile_feat),
+                outs,
+                scratch=[pltpu.SemaphoreType.DMA] if ahead else [],
                 smem=1,
+                hbm=(5,),
                 **cost,
             )
+            following = following[0] if following else None
+        if at < len(PIECES):
             kern.append(k0)
             la.append(la0)
         if at < len(order) - 1:
             part = jnp.stack([part, got], axis=0).reshape(-1, block)
-            if at < PIECES - 1:
-                part, later[at], kern[-1] = lax.optimization_barrier(
-                    (part, later[at], kern[-1])
-                )
+            if at < len(PIECES) - 1:
+                part, following, kern[-1] = lax.optimization_barrier((part, following, kern[-1]))
     acc = VMEM((local * block, block), f32)
     col = VMEM((pairs, block), f32)
     w = VMEM((every + 8, block), f32)
     half = every // 2
     keep, send, fb, et, tot = call(
-        functools.partial(first_sweep, PIECES),
+        functools.partial(first_sweep, len(PIECES)),
         (plan, hit, *kern, *la, part, got),
         (shape(half), shape(half), shape(every), shape(every), shape(8)),
         scratch=[w, acc, acc, col],
@@ -374,7 +398,7 @@
             last = iteration == ITERS - 2
             outs = (shape(half), shape(half)) + ((shape(local * block),) if last else ())
             keep, send, *u = call(
-                functools.partial(next_sweep, PIECES),
+                functools.partial(next_sweep, len(PIECES)),
                 (plan, hit, keep, other, fb, et, tot, *kern, *la),
                 outs,
                 scratch=[w, acc, col] if last else [acc, w, acc, col],

time: 66.1 us -> 66.6 us (level)
  waiting for transfers between devices: 29.8 us -> 31.3 us
  Pallas kernels: 16.2 us -> 15.1 us
    ppermute x19, waiting for transfers between devices: 29.8 us -> 31.3 us  [exchange(): return lax.ppermute(x, 'src', [(i, i ^ d) for i in range(n)])]
    pallas_call x9, Pallas kernels: 16.2 us -> 15.1 us  [call(): pl.pallas_call(kernel, out_shape=outs, in_specs=specs, out_specs=[pl.Bloc...]
  transfers between devices with their start and end apart: 19 -> 19, of which waited for: 16 -> 17; matrix products, arithmetic and copies ran while one was open for 0% -> 0% of each run, Pallas kernels for 13% -> 12%
where the time goes in v5:
time: 66.6 us; the launch traced here: 66.4 us
  waiting for transfers between devices  31.3 us (47%)
  starting transfers between devices  19.2 us (29%)
  Pallas kernels  15.1 us (23%)
  between operations  0.76 us (1%)
    ppermute x19, waiting for transfers between devices, exchange(): return lax.ppermute(x, 'src', [(i, i ^ d) for i in range(n)])  31.3 us
    ppermute x19, starting transfers between devices, exchange(): return lax.ppermute(x, 'src', [(i, i ^ d) for i in range(n)])  19.2 us
    pallas_call x9, Pallas kernels, call(): pl.pallas_call(kernel, out_shape=outs, in_specs=specs, out_specs=[pl.Bloc...  15.1 us
  transfers between devices with their start and end apart: 19, of which 17 were waited for; matrix products, arithmetic and copies ran while one was open for 0% of the time, Pallas kernels for 12%

profile of v5, /device:TPU:0, one launch (start us, length us, event | category | flops | bytes accessed | tf_op | source)
XLA Modules:
  0.0 66.4 jit_solution(7550176633775303085)
XLA Ops:
  0.6 0.8 %shard_map.105 = f32[24,128]{1,0:T(8,128)S(1)} custom-call(s32[8]{0:T(128)} %count_hbm.1, f32[8,128]{1,0:T(8,128)} %bitcast.28, f32[8,128]{1,0:T(8,128)} %bitcast.29, f32[8,128]{1,0:T(8,128)} %bitcast.24), custom_call_target="tpu_custom_call" | custom-call | tf_op jit(solution)/shard_map/pallas_call | solution.py:282
  1.4 3.5 %collective-permute-start = (f32[24,128]{1,0:T(8,128)S(1)}, f32[24,128]{1,0:T(8,128)S(1)}, u32[]{:S(2)}, u32[]{:S(2)}) collective-permute-start(f32[24,128]{1,0:T(8,128)S(1)} %shard_map.105), channel_id=1, source_target_pairs={{0,9},{1,8},{2,11},{3,10},{4,13},{5,12},{6,15},{7,14},{8,1},{9,0},... | collective-permute-start | bytes 36872 | tf_op jit(solution)/shard_map/ppermute | solution.py:300
  4.9 3.6 %shard_map.104 = (f32[4096,128]{1,0:T(8,128)S(1)}, f32[256,128]{1,0:T(8,128)S(1)}, bf16[2,16,128,256]{3,2,1,0:T(8,128)(2,1)S(1)}, s32[9,16]{1,0:T(8,128)S(4)}, b...) custom-call(s32[8]{0:T(128)} %live_hbm.1, ...), custom_call_target="tpu_custom_call" | custom-call | flops 268435456 | bytes 2097152 | tf_op jit(solution)/shard_map/pallas_call | solution.py:282
  8.6 0.0 collective-permute-done
  8.6 1.9 %collective-permute-start.1 = (f32[48,128]{1,0:T(8,128)S(1)}, f32[48,128]{1,0:T(8,128)S(1)}, u32[]{:S(2)}, u32[]{:S(2)}) collective-permute-start(f32[48,128]{1,0:T(8,128)S(1)} %bitcast.20), channel_id=1, source_target_pairs={{0,5},{1,4},{2,7},{3,6},{4,1},{5,0},{6,3},{7,2},{8,13},{9,12},{10,... | collective-permute-start | bytes 73736 | tf_op jit(solution)/shard_map/ppermute | solution.py:300
  10.5 1.9 %shard_map.106 = (f32[4096,128]{1,0:T(8,128)S(1)}, f32[256,128]{1,0:T(8,128)S(1)}, bf16[3,16,128,256]{3,2,1,0:T(8,128)(2,1)S(1)}) custom-call(s32[9,16]{1,0:T(8,128)S(4)} %get-tuple-element.39.plan, bf16[1024,256]{1,0:T(8,128)(2,1)S(1)} %get-tuple-element.45.x_ref, f32[8,128]{1,0:T(8,128)S(1)} %get-tuple-element.46.lin_ref, ...), custom_call_target="tpu_custom_call" | custom-call | flops 268435456 | bytes 2097152 | tf_op jit(solution)/shard_map/pallas_call | solution.py:282
  12.4 0.0 collective-permute-done.1
  12.4 0.8 %collective-permute-start.2 = (f32[96,128]{1,0:T(8,128)S(1)}, f32[96,128]{1,0:T(8,128)S(1)}, u32[]{:S(2)}, u32[]{:S(2)}) collective-permute-start(f32[96,128]{1,0:T(8,128)S(1)} %bitcast.18), channel_id=1, source_target_pairs={{0,3},{1,2},{2,1},{3,0},{4,7},{5,6},{6,5},{7,4},{8,11},{9,10},{10,... | collective-permute-start | bytes 147464 | tf_op jit(solution)/shard_map/ppermute | solution.py:300
  13.2 2.1 %shard_map.107 = (f32[6144,128]{1,0:T(8,128)S(1)}, f32[384,128]{1,0:T(8,128)S(1)}, bf16[1,16,128,256]{3,2,1,0:T(8,128)(2,1)S(1)}) custom-call(s32[9,16]{1,0:T(8,128)S(4)} %get-tuple-element.39.plan, bf16[1024,256]{1,0:T(8,128)(2,1)S(1)} %get-tuple-element.45.x_ref, f32[8,128]{1,0:T(8,128)S(1)} %get-tuple-element.46.lin_ref, ...), custom_call_target="tpu_custom_call" | custom-call | flops 402653184 | bytes 3145728 | tf_op jit(solution)/shard_map/pallas_call | solution.py:282
  15.3 1.2 %collective-permute-done.2 = f32[96,128]{1,0:T(8,128)S(1)} collective-permute-done((f32[96,128]{1,0:T(8,128)S(1)}, f32[96,128]{1,0:T(8,128)S(1)}, u32[]{:S(2)}, u32[]{:S(2)}) %collective-permute-start.2) | collective-permute-done | bytes 49184 | tf_op jit(solution)/shard_map/ppermute | solution.py:300
  16.5 0.2 collective-permute-start.3
  16.7 0.6 shard_map.108
  17.3 0.6 collective-permute-done.3.refs_9_
  17.9 1.7 %shard_map.109 = (f32[64,128]{1,0:T(8,128)S(1)}, f32[64,128]{1,0:T(8,128)S(1)}, f32[128,128]{1,0:T(8,128)S(1)}, f32[128,128]{1,0:T(8,128)S(1)}, f32[8,128]{1,0:T(8,128)S(1)}) custom-call(s32[9,16]{1,0:T(8,128)S(4)} %get-tuple-element.39.plan, bf16[128,128]{1,0:T(8,128)(2,1)S(1)} %get-tuple-element.40.hit_ref, f32[4096,128]{1,0:T(8,128)S(1)} %get-tuple-element.43.refs_0_, ...), custom_call_target="tpu_custom_call" | custom-call | tf_op jit(solution)/shard_map/pallas_call | solution.py:282
  19.6 0.1 collective-permute-start.4
  19.7 1.2 %collective-permute-done.4 = f32[64,128]{1,0:T(8,128)S(1)} collective-permute-done((f32[64,128]{1,0:T(8,128)S(1)}, f32[64,128]{1,0:T(8,128)S(1)}, u32[]{:S(2)}, u32[]{:S(2)}) %collective-permute-start.4) | collective-permute-done | bytes 32800 | tf_op jit(solution)/shard_map/ppermute | solution.py:300
  20.9 1.0 %collective-permute-start.5 = (f32[64,128]{1,0:T(8,128)S(1)}, f32[64,128]{1,0:T(8,128)S(1)}, u32[]{:S(2)}, u32[]{:S(2)}) collective-permute-start(f32[64,128]{1,0:T(8,128)S(1)} %add.36), channel_id=1, source_target_pairs={{0,3},{1,2},{2,1},{3,0},{4,7},{5,6},{6,5},{7,4},{8,11},{9,10},{10,... | collective-permute-start | bytes 98312 | tf_op jit(solution)/shard_map/ppermute | solution.py:300
  21.9 2.3 %collective-permute-done.5 = f32[64,128]{1,0:T(8,128)S(1)} collective-permute-done((f32[64,128]{1,0:T(8,128)S(1)}, f32[64,128]{1,0:T(8,128)S(1)}, u32[]{:S(2)}, u32[]{:S(2)}) %collective-permute-start.5) | collective-permute-done | bytes 32800 | tf_op jit(solution)/shard_map/ppermute | solution.py:300
  24.2 1.0 %collective-permute-start.6 = (f32[64,128]{1,0:T(8,128)S(1)}, f32[64,128]{1,0:T(8,128)S(1)}, u32[]{:S(2)}, u32[]{:S(2)}) collective-permute-start(f32[64,128]{1,0:T(8,128)S(1)} %add.37), channel_id=1, source_target_pairs={{0,5},{1,4},{2,7},{3,6},{4,1},{5,0},{6,3},{7,2},{8,13},{9,12},{10,... | collective-permute-start | bytes 98312 | tf_op jit(solution)/shard_map/ppermute | solution.py:300
  25.2 2.3 %collective-permute-done.6 = f32[64,128]{1,0:T(8,128)S(1)} collective-permute-done((f32[64,128]{1,0:T(8,128)S(1)}, f32[64,128]{1,0:T(8,128)S(1)}, u32[]{:S(2)}, u32[]{:S(2)}) %collective-permute-start.6) | collective-permute-done | bytes 32800 | tf_op jit(solution)/shard_map/ppermute | solution.py:300
  27.6 1.8 %collective-permute-start.7 = (f32[64,128]{1,0:T(8,128)S(1)}, f32[64,128]{1,0:T(8,128)S(1)}, u32[]{:S(2)}, u32[]{:S(2)}) collective-permute-start(f32[64,128]{1,0:T(8,128)S(1)} %add.38), channel_id=1, source_target_pairs={{0,9},{1,8},{2,11},{3,10},{4,13},{5,12},{6,15},{7,14},{8,1},{9,0},... | collective-permute-start | bytes 98312 | tf_op jit(solution)/shard_map/ppermute | solution.py:300
  29.4 2.4 %collective-permute-done.7 = f32[64,128]{1,0:T(8,128)S(1)} collective-permute-done((f32[64,128]{1,0:T(8,128)S(1)}, f32[64,128]{1,0:T(8,128)S(1)}, u32[]{:S(2)}, u32[]{:S(2)}) %collective-permute-start.7) | collective-permute-done | bytes 32800 | tf_op jit(solution)/shard_map/ppermute | solution.py:300
  31.8 0.9 %collective-permute-start.8 = (f32[64,128]{1,0:T(8,128)S(1)}, f32[64,128]{1,0:T(8,128)S(1)}, u32[]{:S(2)}, u32[]{:S(2)}) collective-permute-start(f32[64,128]{1,0:T(8,128)S(1)} %add.39.keep), channel_id=1, source_target_pairs={{0,1},{1,0},{2,3},{3,2},{4,5},{5,4},{6,7},{7,6},{8,9},{9,8},{10,11... | collective-permute-start | bytes 98312 | tf_op jit(solution)/shard_map/ppermute | solution.py:300
  32.7 0.9 %collective-permute-done.8.other = f32[64,128]{1,0:T(8,128)S(1)} collective-permute-done((f32[64,128]{1,0:T(8,128)S(1)}, f32[64,128]{1,0:T(8,128)S(1)}, u32[]{:S(2)}, u32[]{:S(2)}) %collective-permute-start.8) | collective-permute-done | bytes 32800 | tf_op jit(solution)/shard_map/ppermute | solution.py:300
  33.6 1.8 %shard_map.110 = (f32[64,128]{1,0:T(8,128)S(1)}, f32[64,128]{1,0:T(8,128)S(1)}) custom-call(s32[9,16]{1,0:T(8,128)S(4)} %get-tuple-element.39.plan, bf16[128,128]{1,0:T(8,128)(2,1)S(1)} %get-tuple-element.40.hit_ref, f32[64,128]{1,0:T(8,128)S(1)} %add.39.keep, f32[64,128]{1,0:T(8,128)S(1)} %collective-permute-done.8.other, ...), custom_call_target="tpu_custom_call" | custom-call | tf_op jit(solution)/shard_map/pallas_call | solution.py:282
  35.3 0.1 collective-permute-start.9
  35.4 1.2 %collective-permute-done.9 = f32[64,128]{1,0:T(8,128)S(1)} collective-permute-done((f32[64,128]{1,0:T(8,128)S(1)}, f32[64,128]{1,0:T(8,128)S(1)}, u32[]{:S(2)}, u32[]{:S(2)}) %collective-permute-start.9) | collective-permute-done | bytes 32800 | tf_op jit(solution)/shard_map/ppermute | solution.py:300
  36.6 1.7 %collective-permute-start.10 = (f32[64,128]{1,0:T(8,128)S(1)}, f32[64,128]{1,0:T(8,128)S(1)}, u32[]{:S(2)}, u32[]{:S(2)}) collective-permute-start(f32[64,128]{1,0:T(8,128)S(1)} %add.40), channel_id=1, source_target_pairs={{0,3},{1,2},{2,1},{3,0},{4,7},{5,6},{6,5},{7,4},{8,11},{9,10},{10,... | collective-permute-start | bytes 98312 | tf_op jit(solution)/shard_map/ppermute | solution.py:300
  38.4 1.6 %collective-permute-done.10 = f32[64,128]{1,0:T(8,128)S(1)} collective-permute-done((f32[64,128]{1,0:T(8,128)S(1)}, f32[64,128]{1,0:T(8,128)S(1)}, u32[]{:S(2)}, u32[]{:S(2)}) %collective-permute-start.10) | collective-permute-done | bytes 32800 | tf_op jit(solution)/shard_map/ppermute | solution.py:300
  40.0 0.7 %collective-permute-start.11 = (f32[64,128]{1,0:T(8,128)S(1)}, f32[64,128]{1,0:T(8,128)S(1)}, u32[]{:S(2)}, u32[]{:S(2)}) collective-permute-start(f32[64,128]{1,0:T(8,128)S(1)} %add.41), channel_id=1, source_target_pairs={{0,5},{1,4},{2,7},{3,6},{4,1},{5,0},{6,3},{7,2},{8,13},{9,12},{10,... | collective-permute-start | bytes 98312 | tf_op jit(solution)/shard_map/ppermute | solution.py:300
  40.7 2.6 %collective-permute-done.11 = f32[64,128]{1,0:T(8,128)S(1)} collective-permute-done((f32[64,128]{1,0:T(8,128)S(1)}, f32[64,128]{1,0:T(8,128)S(1)}, u32[]{:S(2)}, u32[]{:S(2)}) %collective-permute-start.11) | collective-permute-done | bytes 32800 | tf_op jit(solution)/shard_map/ppermute | solution.py:300
  43.3 1.8 %collective-permute-start.12 = (f32[64,128]{1,0:T(8,128)S(1)}, f32[64,128]{1,0:T(8,128)S(1)}, u32[]{:S(2)}, u32[]{:S(2)}) collective-permute-start(f32[64,128]{1,0:T(8,128)S(1)} %add.42), channel_id=1, source_target_pairs={{0,9},{1,8},{2,11},{3,10},{4,13},{5,12},{6,15},{7,14},{8,1},{9,0},... | collective-permute-start | bytes 98312 | tf_op jit(solution)/shard_map/ppermute | solution.py:300
  45.1 3.2 %collective-permute-done.12 = f32[64,128]{1,0:T(8,128)S(1)} collective-permute-done((f32[64,128]{1,0:T(8,128)S(1)}, f32[64,128]{1,0:T(8,128)S(1)}, u32[]{:S(2)}, u32[]{:S(2)}) %collective-permute-start.12) | collective-permute-done | bytes 32800 | tf_op jit(solution)/shard_map/ppermute | solution.py:300
  48.3 0.1 collective-permute-start.13
  48.4 1.1 %collective-permute-done.13.other = f32[64,128]{1,0:T(8,128)S(1)} collective-permute-done((f32[64,128]{1,0:T(8,128)S(1)}, f32[64,128]{1,0:T(8,128)S(1)}, u32[]{:S(2)}, u32[]{:S(2)}) %collective-permute-start.13) | collective-permute-done | bytes 32800 | tf_op jit(solution)/shard_map/ppermute | solution.py:300
  49.5 1.8 %shard_map.111 = (f32[64,128]{1,0:T(8,128)S(1)}, f32[64,128]{1,0:T(8,128)S(1)}, f32[1024,128]{1,0:T(8,128)S(1)}) custom-call(s32[9,16]{1,0:T(8,128)S(4)} %get-tuple-element.39.plan, bf16[128,128]{1,0:T(8,128)(2,1)S(1)} %get-tuple-element.40.hit_ref, f32[64,128]{1,0:T(8,128)S(1)} %add.43.keep, f32[64,128]{1,0:T(8,128)S(1)} %collective-permute-done.13.other, ...), custom_call_target="tpu_custom_call" | custom-call | tf_op jit(solution)/shard_map/pallas_call | solution.py:282
  51.3 0.1 collective-permute-start.14
  51.4 1.2 %collective-permute-done.14 = f32[64,128]{1,0:T(8,128)S(1)} collective-permute-done((f32[64,128]{1,0:T(8,128)S(1)}, f32[64,128]{1,0:T(8,128)S(1)}, u32[]{:S(2)}, u32[]{:S(2)}) %collective-permute-start.14) | collective-permute-done | bytes 32800 | tf_op jit(solution)/shard_map/ppermute | solution.py:300
  52.6 2.0 %collective-permute-start.15 = (f32[64,128]{1,0:T(8,128)S(1)}, f32[64,128]{1,0:T(8,128)S(1)}, u32[]{:S(2)}, u32[]{:S(2)}) collective-permute-start(f32[64,128]{1,0:T(8,128)S(1)} %add.44), channel_id=1, source_target_pairs={{0,3},{1,2},{2,1},{3,0},{4,7},{5,6},{6,5},{7,4},{8,11},{9,10},{10,... | collective-permute-start | bytes 98312 | tf_op jit(solution)/shard_map/ppermute | solution.py:300
  54.6 1.6 %collective-permute-done.15 = f32[64,128]{1,0:T(8,128)S(1)} collective-permute-done((f32[64,128]{1,0:T(8,128)S(1)}, f32[64,128]{1,0:T(8,128)S(1)}, u32[]{:S(2)}, u32[]{:S(2)}) %collective-permute-start.15) | collective-permute-done | bytes 32800 | tf_op jit(solution)/shard_map/ppermute | solution.py:300
  56.2 0.0 collective-permute-start.16
  56.2 3.3 %collective-permute-done.16 = f32[64,128]{1,0:T(8,128)S(1)} collective-permute-done((f32[64,128]{1,0:T(8,128)S(1)}, f32[64,128]{1,0:T(8,128)S(1)}, u32[]{:S(2)}, u32[]{:S(2)}) %collective-permute-start.16) | collective-permute-done | bytes 32800 | tf_op jit(solution)/shard_map/ppermute | solution.py:300
  59.5 1.3 %collective-permute-start.17 = (f32[64,128]{1,0:T(8,128)S(1)}, f32[64,128]{1,0:T(8,128)S(1)}, u32[]{:S(2)}, u32[]{:S(2)}) collective-permute-start(f32[64,128]{1,0:T(8,128)S(1)} %add.46), channel_id=1, source_target_pairs={{0,9},{1,8},{2,11},{3,10},{4,13},{5,12},{6,15},{7,14},{8,1},{9,0},... | collective-permute-start | bytes 98312 | tf_op jit(solution)/shard_map/ppermute | solution.py:300
  60.9 3.5 %collective-permute-done.17 = f32[64,128]{1,0:T(8,128)S(1)} collective-permute-done((f32[64,128]{1,0:T(8,128)S(1)}, f32[64,128]{1,0:T(8,128)S(1)}, u32[]{:S(2)}, u32[]{:S(2)}) %collective-permute-start.17) | collective-permute-done | bytes 32800 | tf_op jit(solution)/shard_map/ppermute | solution.py:300
  64.4 0.1 collective-permute-start.18
  64.5 1.1 %collective-permute-done.18.other = f32[64,128]{1,0:T(8,128)S(1)} collective-permute-done((f32[64,128]{1,0:T(8,128)S(1)}, f32[64,128]{1,0:T(8,128)S(1)}, u32[]{:S(2)}, u32[]{:S(2)}) %collective-permute-start.18) | collective-permute-done | bytes 32800 | tf_op jit(solution)/shard_map/ppermute | solution.py:300
  65.6 0.8 %shard_map.112 = (f32[8,128]{1,0:T(8,128)}, f32[8,128]{1,0:T(8,128)}) custom-call(f32[64,128]{1,0:T(8,128)S(1)} %add.47.keep, f32[64,128]{1,0:T(8,128)S(1)} %collective-permute-done.18.other, f32[128,128]{1,0:T(8,128)S(1)} %get-tuple-element.66.fb_ref, f32[128,128]{1,0:T(8,128)S(1)} %get-tuple-element.67.et_ref, f32[8,128]{1,0:T(8,128)S(1)} %get-tuple-element.68.tot_ref, ...), custom_call_target="tpu_custom_call" | custom-call | tf_op jit(solution)/shard_map/pallas_call | solution.py:282
  (15 shorter events, 0.1 us)
Async XLA Ops:
  1.4 7.2 %collective-permute-start = (f32[24,128]{1,0:T(8,128)S(1)}, f32[24,128]{1,0:T(8,128)S(1)}, u32[]{:S(2)}, u32[]{:S(2)}) collective-permute-start(f32[24,128]{1,0:T(8,128)S(1)} %shard_map.105), channel_id=1, source_target_pairs={{0,9},{1,8},{2,11},{3,10},{4,13},{5,12},{6,15},{7,14},{8,1},{9,0},... | collective-permute-start | bytes 36872 | tf_op jit(solution)/shard_map/ppermute | solution.py:300
  8.6 3.8 %collective-permute-start.1 = (f32[48,128]{1,0:T(8,128)S(1)}, f32[48,128]{1,0:T(8,128)S(1)}, u32[]{:S(2)}, u32[]{:S(2)}) collective-permute-start(f32[48,128]{1,0:T(8,128)S(1)} %bitcast.20), channel_id=1, source_target_pairs={{0,5},{1,4},{2,7},{3,6},{4,1},{5,0},{6,3},{7,2},{8,13},{9,12},{10,... | collective-permute-start | bytes 73736 | tf_op jit(solution)/shard_map/ppermute | solution.py:300
  12.4 4.1 %collective-permute-start.2 = (f32[96,128]{1,0:T(8,128)S(1)}, f32[96,128]{1,0:T(8,128)S(1)}, u32[]{:S(2)}, u32[]{:S(2)}) collective-permute-start(f32[96,128]{1,0:T(8,128)S(1)} %bitcast.18), channel_id=1, source_target_pairs={{0,3},{1,2},{2,1},{3,0},{4,7},{5,6},{6,5},{7,4},{8,11},{9,10},{10,... | collective-permute-start | bytes 147464 | tf_op jit(solution)/shard_map/ppermute | solution.py:300
  16.5 1.4 %collective-permute-start.3 = (f32[192,128]{1,0:T(8,128)S(1)}, f32[192,128]{1,0:T(8,128)S(1)}, u32[]{:S(2)}, u32[]{:S(2)}) collective-permute-start(f32[192,128]{1,0:T(8,128)S(1)} %bitcast.15), channel_id=1, source_target_pairs={{0,1},{1,0},{2,3},{3,2},{4,5},{5,4},{6,7},{7,6},{8,9},{9,8},{10,11... | collective-permute-start | bytes 294920 | tf_op jit(solution)/shard_map/ppermute | solution.py:300
  19.6 1.3 %collective-permute-start.4 = (f32[64,128]{1,0:T(8,128)S(1)}, f32[64,128]{1,0:T(8,128)S(1)}, u32[]{:S(2)}, u32[]{:S(2)}) collective-permute-start(f32[64,128]{1,0:T(8,128)S(1)} %get-tuple-element.65), channel_id=1, source_target_pairs={{0,1},{1,0},{2,3},{3,2},{4,5},{5,4},{6,7},{7,6},{8,9},{9,8},{10,11... | collective-permute-start | bytes 98312 | tf_op jit(solution)/shard_map/ppermute | solution.py:300
  20.9 3.3 %collective-permute-start.5 = (f32[64,128]{1,0:T(8,128)S(1)}, f32[64,128]{1,0:T(8,128)S(1)}, u32[]{:S(2)}, u32[]{:S(2)}) collective-permute-start(f32[64,128]{1,0:T(8,128)S(1)} %add.36), channel_id=1, source_target_pairs={{0,3},{1,2},{2,1},{3,0},{4,7},{5,6},{6,5},{7,4},{8,11},{9,10},{10,... | collective-permute-start | bytes 98312 | tf_op jit(solution)/shard_map/ppermute | solution.py:300
  24.2 3.3 %collective-permute-start.6 = (f32[64,128]{1,0:T(8,128)S(1)}, f32[64,128]{1,0:T(8,128)S(1)}, u32[]{:S(2)}, u32[]{:S(2)}) collective-permute-start(f32[64,128]{1,0:T(8,128)S(1)} %add.37), channel_id=1, source_target_pairs={{0,5},{1,4},{2,7},{3,6},{4,1},{5,0},{6,3},{7,2},{8,13},{9,12},{10,... | collective-permute-start | bytes 98312 | tf_op jit(solution)/shard_map/ppermute | solution.py:300
  27.6 4.2 %collective-permute-start.7 = (f32[64,128]{1,0:T(8,128)S(1)}, f32[64,128]{1,0:T(8,128)S(1)}, u32[]{:S(2)}, u32[]{:S(2)}) collective-permute-start(f32[64,128]{1,0:T(8,128)S(1)} %add.38), channel_id=1, source_target_pairs={{0,9},{1,8},{2,11},{3,10},{4,13},{5,12},{6,15},{7,14},{8,1},{9,0},... | collective-permute-start | bytes 98312 | tf_op jit(solution)/shard_map/ppermute | solution.py:300
  31.8 1.7 %collective-permute-start.8 = (f32[64,128]{1,0:T(8,128)S(1)}, f32[64,128]{1,0:T(8,128)S(1)}, u32[]{:S(2)}, u32[]{:S(2)}) collective-permute-start(f32[64,128]{1,0:T(8,128)S(1)} %add.39.keep), channel_id=1, source_target_pairs={{0,1},{1,0},{2,3},{3,2},{4,5},{5,4},{6,7},{7,6},{8,9},{9,8},{10,11... | collective-permute-start | bytes 98312 | tf_op jit(solution)/shard_map/ppermute | solution.py:300
  35.3 1.3 %collective-permute-start.9 = (f32[64,128]{1,0:T(8,128)S(1)}, f32[64,128]{1,0:T(8,128)S(1)}, u32[]{:S(2)}, u32[]{:S(2)}) collective-permute-start(f32[64,128]{1,0:T(8,128)S(1)} %get-tuple-element.70), channel_id=1, source_target_pairs={{0,1},{1,0},{2,3},{3,2},{4,5},{5,4},{6,7},{7,6},{8,9},{9,8},{10,11... | collective-permute-start | bytes 98312 | tf_op jit(solution)/shard_map/ppermute | solution.py:300
  36.6 3.3 %collective-permute-start.10 = (f32[64,128]{1,0:T(8,128)S(1)}, f32[64,128]{1,0:T(8,128)S(1)}, u32[]{:S(2)}, u32[]{:S(2)}) collective-permute-start(f32[64,128]{1,0:T(8,128)S(1)} %add.40), channel_id=1, source_target_pairs={{0,3},{1,2},{2,1},{3,0},{4,7},{5,6},{6,5},{7,4},{8,11},{9,10},{10,... | collective-permute-start | bytes 98312 | tf_op jit(solution)/shard_map/ppermute | solution.py:300
  40.0 3.3 %collective-permute-start.11 = (f32[64,128]{1,0:T(8,128)S(1)}, f32[64,128]{1,0:T(8,128)S(1)}, u32[]{:S(2)}, u32[]{:S(2)}) collective-permute-start(f32[64,128]{1,0:T(8,128)S(1)} %add.41), channel_id=1, source_target_pairs={{0,5},{1,4},{2,7},{3,6},{4,1},{5,0},{6,3},{7,2},{8,13},{9,12},{10,... | collective-permute-start | bytes 98312 | tf_op jit(solution)/shard_map/ppermute | solution.py:300
  43.3 5.0 %collective-permute-start.12 = (f32[64,128]{1,0:T(8,128)S(1)}, f32[64,128]{1,0:T(8,128)S(1)}, u32[]{:S(2)}, u32[]{:S(2)}) collective-permute-start(f32[64,128]{1,0:T(8,128)S(1)} %add.42), channel_id=1, source_target_pairs={{0,9},{1,8},{2,11},{3,10},{4,13},{5,12},{6,15},{7,14},{8,1},{9,0},... | collective-permute-start | bytes 98312 | tf_op jit(solution)/shard_map/ppermute | solution.py:300
  48.3 1.2 %collective-permute-start.13 = (f32[64,128]{1,0:T(8,128)S(1)}, f32[64,128]{1,0:T(8,128)S(1)}, u32[]{:S(2)}, u32[]{:S(2)}) collective-permute-start(f32[64,128]{1,0:T(8,128)S(1)} %add.43.keep), channel_id=1, source_target_pairs={{0,1},{1,0},{2,3},{3,2},{4,5},{5,4},{6,7},{7,6},{8,9},{9,8},{10,11... | collective-permute-start | bytes 98312 | tf_op jit(solution)/shard_map/ppermute | solution.py:300
  51.3 1.3 %collective-permute-start.14 = (f32[64,128]{1,0:T(8,128)S(1)}, f32[64,128]{1,0:T(8,128)S(1)}, u32[]{:S(2)}, u32[]{:S(2)}) collective-permute-start(f32[64,128]{1,0:T(8,128)S(1)} %get-tuple-element.72), channel_id=1, source_target_pairs={{0,1},{1,0},{2,3},{3,2},{4,5},{5,4},{6,7},{7,6},{8,9},{9,8},{10,11... | collective-permute-start | bytes 98312 | tf_op jit(solution)/shard_map/ppermute | solution.py:300
  52.6 3.6 %collective-permute-start.15 = (f32[64,128]{1,0:T(8,128)S(1)}, f32[64,128]{1,0:T(8,128)S(1)}, u32[]{:S(2)}, u32[]{:S(2)}) collective-permute-start(f32[64,128]{1,0:T(8,128)S(1)} %add.44), channel_id=1, source_target_pairs={{0,3},{1,2},{2,1},{3,0},{4,7},{5,6},{6,5},{7,4},{8,11},{9,10},{10,... | collective-permute-start | bytes 98312 | tf_op jit(solution)/shard_map/ppermute | solution.py:300
  56.2 3.3 %collective-permute-start.16 = (f32[64,128]{1,0:T(8,128)S(1)}, f32[64,128]{1,0:T(8,128)S(1)}, u32[]{:S(2)}, u32[]{:S(2)}) collective-permute-start(f32[64,128]{1,0:T(8,128)S(1)} %add.45), channel_id=1, source_target_pairs={{0,5},{1,4},{2,7},{3,6},{4,1},{5,0},{6,3},{7,2},{8,13},{9,12},{10,... | collective-permute-start | bytes 98312 | tf_op jit(solution)/shard_map/ppermute | solution.py:300
  59.5 4.8 %collective-permute-start.17 = (f32[64,128]{1,0:T(8,128)S(1)}, f32[64,128]{1,0:T(8,128)S(1)}, u32[]{:S(2)}, u32[]{:S(2)}) collective-permute-start(f32[64,128]{1,0:T(8,128)S(1)} %add.46), channel_id=1, source_target_pairs={{0,9},{1,8},{2,11},{3,10},{4,13},{5,12},{6,15},{7,14},{8,1},{9,0},... | collective-permute-start | bytes 98312 | tf_op jit(solution)/shard_map/ppermute | solution.py:300
  64.4 1.2 %collective-permute-start.18 = (f32[64,128]{1,0:T(8,128)S(1)}, f32[64,128]{1,0:T(8,128)S(1)}, u32[]{:S(2)}, u32[]{:S(2)}) collective-permute-start(f32[64,128]{1,0:T(8,128)S(1)} %add.47.keep), channel_id=1, source_target_pairs={{0,1},{1,0},{2,3},{3,2},{4,5},{5,4},{6,7},{7,6},{8,9},{9,8},{10,11... | collective-permute-start | bytes 98312 | tf_op jit(solution)/shard_map/ppermute | solution.py:300

commit v6 on v5

--- a/solution.py
+++ b/solution.py
@@ -14,6 +14,7 @@
 F = RHO / (RHO + EPS)
 LOG2E = 1.4426950408889634
 STEP = 4
+FAR = 4
 ABSENT = -1e30
 PIECES = (2, 2, 3, 1)
 
@@ -41,7 +42,7 @@
 
 
 def half_flip(every):
-    at = position()
+    at = position() & (lax.axis_size("src") // FAR - 1)
     for r in (16, 8, 4, 2, 1):
         at = at ^ (at >> r)
     return (at & 1) * (every // 2)
@@ -391,8 +392,12 @@
     u = None
     for iteration in range(ITERS):
         keep = keep + exchange(send, n, order[-1])
-        for d in order[-2::-1]:
+        for d in order[-2:1:-1]:
             keep = keep + exchange(keep, n, d)
+        near = n // FAR
+        groups = [[i + near * z for z in range(FAR)] for i in range(near)]
+        sums = lax.all_gather(keep, "src", axis_index_groups=groups, axis=0)
+        keep = functools.reduce(lambda p, q: p + q, [sums[z] for z in range(FAR)])
         other = exchange(keep, n, order[-1])
         if iteration < ITERS - 1:
             last = iteration == ITERS - 2

time: 66.6 us -> 81.8 us (1.23)
  blocking collectives: 0 us -> 40.1 us
  waiting for transfers between devices: 31.3 us -> 12.2 us
  starting transfers between devices: 19.2 us -> 14.2 us
  Pallas kernels: 15.1 us -> 14.1 us
    all_gather x0 -> x3, blocking collectives: none -> 40.1 us  [shards(): sums = lax.all_gather(keep, 'src', axis_index_groups=groups, axis=0)]
    ppermute x19 -> x13, waiting for transfers between devices: 31.3 us -> 12.2 us  [exchange(): return lax.ppermute(x, 'src', [(i, i ^ d) for i in range(n)])]
    ppermute x19 -> x13, starting transfers between devices: 19.2 us -> 14.2 us  [exchange(): return lax.ppermute(x, 'src', [(i, i ^ d) for i in range(n)])]
    pallas_call x9, Pallas kernels: 15.1 us -> 14.1 us  [call(): pl.pallas_call(kernel, out_shape=outs, in_specs=specs, out_specs=[pl.Bloc...]
  transfers between devices with their start and end apart: 19 -> 13, of which waited for: 17 -> 11; matrix products, arithmetic and copies ran while one was open for 0% -> 0% of each run, Pallas kernels for 12% -> 9%
where the time goes in v6:
time: 81.8 us; the launch traced here: 81.5 us
  blocking collectives  40.1 us (49%)
  starting transfers between devices  14.2 us (17%)
  Pallas kernels  14.1 us (17%)
  waiting for transfers between devices  12.2 us (15%)
    all_gather x3, blocking collectives, shards(): sums = lax.all_gather(keep, 'src', axis_index_groups=groups, axis=0)  40.1 us
    ppermute x13, starting transfers between devices, exchange(): return lax.ppermute(x, 'src', [(i, i ^ d) for i in range(n)])  14.2 us
    pallas_call x9, Pallas kernels, call(): pl.pallas_call(kernel, out_shape=outs, in_specs=specs, out_specs=[pl.Bloc...  14.1 us
    ppermute x13, waiting for transfers between devices, exchange(): return lax.ppermute(x, 'src', [(i, i ^ d) for i in range(n)])  12.2 us
  transfers between devices with their start and end apart: 13, of which 11 were waited for; matrix products, arithmetic and copies ran while one was open for 0% of the time, Pallas kernels for 9%

profile of v6, /device:TPU:0, one launch (start us, length us, event | category | flops | bytes accessed | tf_op | source)
XLA Modules:
  0.0 81.5 jit_solution(11460013059223604300)
XLA Ops:
  0.6 0.8 shard_map.105
  1.4 3.5 %collective-permute-start = (f32[24,128]{1,0:T(8,128)S(1)}, f32[24,128]{1,0:T(8,128)S(1)}, u32[]{:S(2)}, u32[]{:S(2)}) collective-permute-start(f32[24,128]{1,0:T(8,128)S(1)} %shard_map.105), channel_id=1, source_target_pairs={{0,9},{1,8},{2,11},{3,10},{4,13},{5,12},{6,15},{7,14},{8,1},{9,0},... | collective-permute-start | bytes 36872 | tf_op jit(solution)/shard_map/ppermute | solution.py:301
  4.9 3.1 %shard_map.104 = (f32[4096,128]{1,0:T(8,128)S(1)}, f32[256,128]{1,0:T(8,128)S(1)}, bf16[2,16,128,256]{3,2,1,0:T(8,128)(2,1)S(1)}, s32[9,16]{1,0:T(8,128)S(4)}, b...) custom-call(s32[8]{0:T(128)} %live_hbm.1, ...), custom_call_target="tpu_custom_call" | custom-call | flops 268435456 | bytes 2097152 | tf_op jit(solution)/shard_map/pallas_call | solution.py:283
  8.1 0.0 collective-permute-done
  8.1 2.2 %collective-permute-start.1 = (f32[48,128]{1,0:T(8,128)S(1)}, f32[48,128]{1,0:T(8,128)S(1)}, u32[]{:S(2)}, u32[]{:S(2)}) collective-permute-start(f32[48,128]{1,0:T(8,128)S(1)} %bitcast.20), channel_id=1, source_target_pairs={{0,5},{1,4},{2,7},{3,6},{4,1},{5,0},{6,3},{7,2},{8,13},{9,12},{10,... | collective-permute-start | bytes 73736 | tf_op jit(solution)/shard_map/ppermute | solution.py:301
  10.2 1.9 %shard_map.106 = (f32[4096,128]{1,0:T(8,128)S(1)}, f32[256,128]{1,0:T(8,128)S(1)}, bf16[3,16,128,256]{3,2,1,0:T(8,128)(2,1)S(1)}) custom-call(s32[9,16]{1,0:T(8,128)S(4)} %get-tuple-element.39.plan, bf16[1024,256]{1,0:T(8,128)(2,1)S(1)} %get-tuple-element.45.x_ref, f32[8,128]{1,0:T(8,128)S(1)} %get-tuple-element.46.lin_ref, ...), custom_call_target="tpu_custom_call" | custom-call | flops 268435456 | bytes 2097152 | tf_op jit(solution)/shard_map/pallas_call | solution.py:283
  12.2 0.0 collective-permute-done.1
  12.2 1.3 %collective-permute-start.2 = (f32[96,128]{1,0:T(8,128)S(1)}, f32[96,128]{1,0:T(8,128)S(1)}, u32[]{:S(2)}, u32[]{:S(2)}) collective-permute-start(f32[96,128]{1,0:T(8,128)S(1)} %bitcast.18), channel_id=1, source_target_pairs={{0,3},{1,2},{2,1},{3,0},{4,7},{5,6},{6,5},{7,4},{8,11},{9,10},{10,... | collective-permute-start | bytes 147464 | tf_op jit(solution)/shard_map/ppermute | solution.py:301
  13.5 1.6 %shard_map.107 = (f32[6144,128]{1,0:T(8,128)S(1)}, f32[384,128]{1,0:T(8,128)S(1)}, bf16[1,16,128,256]{3,2,1,0:T(8,128)(2,1)S(1)}) custom-call(s32[9,16]{1,0:T(8,128)S(4)} %get-tuple-element.39.plan, bf16[1024,256]{1,0:T(8,128)(2,1)S(1)} %get-tuple-element.45.x_ref, f32[8,128]{1,0:T(8,128)S(1)} %get-tuple-element.46.lin_ref, ...), custom_call_target="tpu_custom_call" | custom-call | flops 402653184 | bytes 3145728 | tf_op jit(solution)/shard_map/pallas_call | solution.py:283
  15.1 0.8 collective-permute-done.2
  15.9 0.3 collective-permute-start.3
  16.2 0.6 shard_map.108
  16.8 0.4 collective-permute-done.3.refs_9_
  17.2 1.7 %shard_map.109 = (f32[64,128]{1,0:T(8,128)S(1)}, f32[64,128]{1,0:T(8,128)S(1)}, f32[128,128]{1,0:T(8,128)S(1)}, f32[128,128]{1,0:T(8,128)S(1)}, f32[8,128]{1,0:T(8,128)S(1)}) custom-call(s32[9,16]{1,0:T(8,128)S(4)} %get-tuple-element.39.plan, bf16[128,128]{1,0:T(8,128)(2,1)S(1)} %get-tuple-element.40.hit_ref, f32[4096,128]{1,0:T(8,128)S(1)} %get-tuple-element.43.refs_0_, ...), custom_call_target="tpu_custom_call" | custom-call | tf_op jit(solution)/shard_map/pallas_call | solution.py:283
  18.9 0.5 collective-permute-start.4
  19.4 0.9 %collective-permute-done.4 = f32[64,128]{1,0:T(8,128)S(1)} collective-permute-done((f32[64,128]{1,0:T(8,128)S(1)}, f32[64,128]{1,0:T(8,128)S(1)}, u32[]{:S(2)}, u32[]{:S(2)}) %collective-permute-start.4) | collective-permute-done | bytes 32800 | tf_op jit(solution)/shard_map/ppermute | solution.py:301
  20.3 1.7 %collective-permute-start.5 = (f32[64,128]{1,0:T(8,128)S(1)}, f32[64,128]{1,0:T(8,128)S(1)}, u32[]{:S(2)}, u32[]{:S(2)}) collective-permute-start(f32[64,128]{1,0:T(8,128)S(1)} %add.57), channel_id=1, source_target_pairs={{0,3},{1,2},{2,1},{3,0},{4,7},{5,6},{6,5},{7,4},{8,11},{9,10},{10,... | collective-permute-start | bytes 98312 | tf_op jit(solution)/shard_map/ppermute | solution.py:301
  22.0 1.7 %collective-permute-done.5 = f32[64,128]{1,0:T(8,128)S(1)} collective-permute-done((f32[64,128]{1,0:T(8,128)S(1)}, f32[64,128]{1,0:T(8,128)S(1)}, u32[]{:S(2)}, u32[]{:S(2)}) %collective-permute-start.5) | collective-permute-done | bytes 32800 | tf_op jit(solution)/shard_map/ppermute | solution.py:301
  23.7 13.3 %all-gather = f32[256,128]{1,0:T(8,128)S(1)} all-gather(f32[64,128]{1,0:T(8,128)S(1)} %add.58), channel_id=2, replica_groups={{0,4,8,12},{1,5,9,13},{2,6,10,14},{3,7,11,15},{16,20,24,28},{17,21,25,2..., dimensions={0}, use_global_device_ids=true | all-gather | bytes 163840 | tf_op jit(solution)/shard_map/all_gather | solution.py:399
  37.0 0.1 collective-permute-start.6
  37.1 1.2 %collective-permute-done.6.other = f32[64,128]{1,0:T(8,128)S(1)} collective-permute-done((f32[64,128]{1,0:T(8,128)S(1)}, f32[64,128]{1,0:T(8,128)S(1)}, u32[]{:S(2)}, u32[]{:S(2)}) %collective-permute-start.6) | collective-permute-done | bytes 32800 | tf_op jit(solution)/shard_map/ppermute | solution.py:301
  38.3 1.8 %shard_map.110 = (f32[64,128]{1,0:T(8,128)S(1)}, f32[64,128]{1,0:T(8,128)S(1)}) custom-call(s32[9,16]{1,0:T(8,128)S(4)} %get-tuple-element.39.plan, bf16[128,128]{1,0:T(8,128)(2,1)S(1)} %get-tuple-element.40.hit_ref, f32[64,128]{1,0:T(8,128)S(1)} %slice_add_fusion.6.keep, f32[64,128]{1,0:T(8,128)S(1)} %collective-permute-done.6.other, ...), custom_call_target="tpu_custom_call" | custom-call | tf_op jit(solution)/shard_map/pallas_call | solution.py:283
  40.0 0.4 collective-permute-start.7
  40.5 0.9 %collective-permute-done.7 = f32[64,128]{1,0:T(8,128)S(1)} collective-permute-done((f32[64,128]{1,0:T(8,128)S(1)}, f32[64,128]{1,0:T(8,128)S(1)}, u32[]{:S(2)}, u32[]{:S(2)}) %collective-permute-start.7) | collective-permute-done | bytes 32800 | tf_op jit(solution)/shard_map/ppermute | solution.py:301
  41.3 1.9 %collective-permute-start.8 = (f32[64,128]{1,0:T(8,128)S(1)}, f32[64,128]{1,0:T(8,128)S(1)}, u32[]{:S(2)}, u32[]{:S(2)}) collective-permute-start(f32[64,128]{1,0:T(8,128)S(1)} %add.63), channel_id=1, source_target_pairs={{0,3},{1,2},{2,1},{3,0},{4,7},{5,6},{6,5},{7,4},{8,11},{9,10},{10,... | collective-permute-start | bytes 98312 | tf_op jit(solution)/shard_map/ppermute | solution.py:301
  43.2 1.6 %collective-permute-done.8 = f32[64,128]{1,0:T(8,128)S(1)} collective-permute-done((f32[64,128]{1,0:T(8,128)S(1)}, f32[64,128]{1,0:T(8,128)S(1)}, u32[]{:S(2)}, u32[]{:S(2)}) %collective-permute-start.8) | collective-permute-done | bytes 32800 | tf_op jit(solution)/shard_map/ppermute | solution.py:301
  44.8 13.4 %all-gather.1 = f32[256,128]{1,0:T(8,128)S(1)} all-gather(f32[64,128]{1,0:T(8,128)S(1)} %add.64), channel_id=3, replica_groups={{0,4,8,12},{1,5,9,13},{2,6,10,14},{3,7,11,15},{16,20,24,28},{17,21,25,2..., dimensions={0}, use_global_device_ids=true | all-gather | bytes 163840 | tf_op jit(solution)/shard_map/all_gather | solution.py:399
  58.2 0.1 collective-permute-start.9
  58.3 1.2 %collective-permute-done.9.other = f32[64,128]{1,0:T(8,128)S(1)} collective-permute-done((f32[64,128]{1,0:T(8,128)S(1)}, f32[64,128]{1,0:T(8,128)S(1)}, u32[]{:S(2)}, u32[]{:S(2)}) %collective-permute-start.9) | collective-permute-done | bytes 32800 | tf_op jit(solution)/shard_map/ppermute | solution.py:301
  59.5 1.8 %shard_map.111 = (f32[64,128]{1,0:T(8,128)S(1)}, f32[64,128]{1,0:T(8,128)S(1)}, f32[1024,128]{1,0:T(8,128)S(1)}) custom-call(s32[9,16]{1,0:T(8,128)S(4)} %get-tuple-element.39.plan, bf16[128,128]{1,0:T(8,128)(2,1)S(1)} %get-tuple-element.40.hit_ref, f32[64,128]{1,0:T(8,128)S(1)} %slice_add_fusion.3.keep, f32[64,128]{1,0:T(8,128)S(1)} %collective-permute-done.9.other, ...), custom_call_target="tpu_custom_call" | custom-call | tf_op jit(solution)/shard_map/pallas_call | solution.py:283
  61.3 0.4 collective-permute-start.10
  61.7 0.9 %collective-permute-done.10 = f32[64,128]{1,0:T(8,128)S(1)} collective-permute-done((f32[64,128]{1,0:T(8,128)S(1)}, f32[64,128]{1,0:T(8,128)S(1)}, u32[]{:S(2)}, u32[]{:S(2)}) %collective-permute-start.10) | collective-permute-done | bytes 32800 | tf_op jit(solution)/shard_map/ppermute | solution.py:301
  62.6 1.9 %collective-permute-start.11 = (f32[64,128]{1,0:T(8,128)S(1)}, f32[64,128]{1,0:T(8,128)S(1)}, u32[]{:S(2)}, u32[]{:S(2)}) collective-permute-start(f32[64,128]{1,0:T(8,128)S(1)} %add.69), channel_id=1, source_target_pairs={{0,3},{1,2},{2,1},{3,0},{4,7},{5,6},{6,5},{7,4},{8,11},{9,10},{10,... | collective-permute-start | bytes 98312 | tf_op jit(solution)/shard_map/ppermute | solution.py:301
  64.4 1.6 %collective-permute-done.11 = f32[64,128]{1,0:T(8,128)S(1)} collective-permute-done((f32[64,128]{1,0:T(8,128)S(1)}, f32[64,128]{1,0:T(8,128)S(1)}, u32[]{:S(2)}, u32[]{:S(2)}) %collective-permute-start.11) | collective-permute-done | bytes 32800 | tf_op jit(solution)/shard_map/ppermute | solution.py:301
  66.0 13.4 %all-gather.2 = f32[256,128]{1,0:T(8,128)S(1)} all-gather(f32[64,128]{1,0:T(8,128)S(1)} %add.70), channel_id=4, replica_groups={{0,4,8,12},{1,5,9,13},{2,6,10,14},{3,7,11,15},{16,20,24,28},{17,21,25,2..., dimensions={0}, use_global_device_ids=true | all-gather | bytes 163840 | tf_op jit(solution)/shard_map/all_gather | solution.py:399
  79.4 0.1 collective-permute-start.12
  79.5 1.2 %collective-permute-done.12.other = f32[64,128]{1,0:T(8,128)S(1)} collective-permute-done((f32[64,128]{1,0:T(8,128)S(1)}, f32[64,128]{1,0:T(8,128)S(1)}, u32[]{:S(2)}, u32[]{:S(2)}) %collective-permute-start.12) | collective-permute-done | bytes 32800 | tf_op jit(solution)/shard_map/ppermute | solution.py:301
  80.7 0.8 %shard_map.112 = (f32[8,128]{1,0:T(8,128)}, f32[8,128]{1,0:T(8,128)}) custom-call(f32[64,128]{1,0:T(8,128)S(1)} %slice_add_fusion.keep, f32[64,128]{1,0:T(8,128)S(1)} %collective-permute-done.12.other, f32[128,128]{1,0:T(8,128)S(1)} %get-tuple-element.66.fb_ref, f32[128,128]{1,0:T(8,128)S(1)} %get-tuple-element.67.et_ref, ...), custom_call_target="tpu_custom_call" | custom-call | tf_op jit(solution)/shard_map/pallas_call | solution.py:283
  (12 shorter events, 0.1 us)
Async XLA Ops:
  1.4 6.7 %collective-permute-start = (f32[24,128]{1,0:T(8,128)S(1)}, f32[24,128]{1,0:T(8,128)S(1)}, u32[]{:S(2)}, u32[]{:S(2)}) collective-permute-start(f32[24,128]{1,0:T(8,128)S(1)} %shard_map.105), channel_id=1, source_target_pairs={{0,9},{1,8},{2,11},{3,10},{4,13},{5,12},{6,15},{7,14},{8,1},{9,0},... | collective-permute-start | bytes 36872 | tf_op jit(solution)/shard_map/ppermute | solution.py:301
  8.1 4.1 %collective-permute-start.1 = (f32[48,128]{1,0:T(8,128)S(1)}, f32[48,128]{1,0:T(8,128)S(1)}, u32[]{:S(2)}, u32[]{:S(2)}) collective-permute-start(f32[48,128]{1,0:T(8,128)S(1)} %bitcast.20), channel_id=1, source_target_pairs={{0,5},{1,4},{2,7},{3,6},{4,1},{5,0},{6,3},{7,2},{8,13},{9,12},{10,... | collective-permute-start | bytes 73736 | tf_op jit(solution)/shard_map/ppermute | solution.py:301
  12.2 3.7 %collective-permute-start.2 = (f32[96,128]{1,0:T(8,128)S(1)}, f32[96,128]{1,0:T(8,128)S(1)}, u32[]{:S(2)}, u32[]{:S(2)}) collective-permute-start(f32[96,128]{1,0:T(8,128)S(1)} %bitcast.18), channel_id=1, source_target_pairs={{0,3},{1,2},{2,1},{3,0},{4,7},{5,6},{6,5},{7,4},{8,11},{9,10},{10,... | collective-permute-start | bytes 147464 | tf_op jit(solution)/shard_map/ppermute | solution.py:301
  15.9 1.4 %collective-permute-start.3 = (f32[192,128]{1,0:T(8,128)S(1)}, f32[192,128]{1,0:T(8,128)S(1)}, u32[]{:S(2)}, u32[]{:S(2)}) collective-permute-start(f32[192,128]{1,0:T(8,128)S(1)} %bitcast.15), channel_id=1, source_target_pairs={{0,1},{1,0},{2,3},{3,2},{4,5},{5,4},{6,7},{7,6},{8,9},{9,8},{10,11... | collective-permute-start | bytes 294920 | tf_op jit(solution)/shard_map/ppermute | solution.py:301
  18.9 1.4 %collective-permute-start.4 = (f32[64,128]{1,0:T(8,128)S(1)}, f32[64,128]{1,0:T(8,128)S(1)}, u32[]{:S(2)}, u32[]{:S(2)}) collective-permute-start(f32[64,128]{1,0:T(8,128)S(1)} %get-tuple-element.65), channel_id=1, source_target_pairs={{0,1},{1,0},{2,3},{3,2},{4,5},{5,4},{6,7},{7,6},{8,9},{9,8},{10,11... | collective-permute-start | bytes 98312 | tf_op jit(solution)/shard_map/ppermute | solution.py:301
  20.3 3.3 %collective-permute-start.5 = (f32[64,128]{1,0:T(8,128)S(1)}, f32[64,128]{1,0:T(8,128)S(1)}, u32[]{:S(2)}, u32[]{:S(2)}) collective-permute-start(f32[64,128]{1,0:T(8,128)S(1)} %add.57), channel_id=1, source_target_pairs={{0,3},{1,2},{2,1},{3,0},{4,7},{5,6},{6,5},{7,4},{8,11},{9,10},{10,... | collective-permute-start | bytes 98312 | tf_op jit(solution)/shard_map/ppermute | solution.py:301
  37.0 1.3 %collective-permute-start.6 = (f32[64,128]{1,0:T(8,128)S(1)}, f32[64,128]{1,0:T(8,128)S(1)}, u32[]{:S(2)}, u32[]{:S(2)}) collective-permute-start(f32[64,128]{1,0:T(8,128)S(1)} %slice_add_fusion.6.keep), channel_id=1, source_target_pairs={{0,1},{1,0},{2,3},{3,2},{4,5},{5,4},{6,7},{7,6},{8,9},{9,8},{10,11... | collective-permute-start | bytes 98312 | tf_op jit(solution)/shard_map/ppermute | solution.py:301
  40.0 1.3 %collective-permute-start.7 = (f32[64,128]{1,0:T(8,128)S(1)}, f32[64,128]{1,0:T(8,128)S(1)}, u32[]{:S(2)}, u32[]{:S(2)}) collective-permute-start(f32[64,128]{1,0:T(8,128)S(1)} %get-tuple-element.70), channel_id=1, source_target_pairs={{0,1},{1,0},{2,3},{3,2},{4,5},{5,4},{6,7},{7,6},{8,9},{9,8},{10,11... | collective-permute-start | bytes 98312 | tf_op jit(solution)/shard_map/ppermute | solution.py:301
  41.3 3.5 %collective-permute-start.8 = (f32[64,128]{1,0:T(8,128)S(1)}, f32[64,128]{1,0:T(8,128)S(1)}, u32[]{:S(2)}, u32[]{:S(2)}) collective-permute-start(f32[64,128]{1,0:T(8,128)S(1)} %add.63), channel_id=1, source_target_pairs={{0,3},{1,2},{2,1},{3,0},{4,7},{5,6},{6,5},{7,4},{8,11},{9,10},{10,... | collective-permute-start | bytes 98312 | tf_op jit(solution)/shard_map/ppermute | solution.py:301
  58.2 1.3 %collective-permute-start.9 = (f32[64,128]{1,0:T(8,128)S(1)}, f32[64,128]{1,0:T(8,128)S(1)}, u32[]{:S(2)}, u32[]{:S(2)}) collective-permute-start(f32[64,128]{1,0:T(8,128)S(1)} %slice_add_fusion.3.keep), channel_id=1, source_target_pairs={{0,1},{1,0},{2,3},{3,2},{4,5},{5,4},{6,7},{7,6},{8,9},{9,8},{10,11... | collective-permute-start | bytes 98312 | tf_op jit(solution)/shard_map/ppermute | solution.py:301
  61.3 1.3 %collective-permute-start.10 = (f32[64,128]{1,0:T(8,128)S(1)}, f32[64,128]{1,0:T(8,128)S(1)}, u32[]{:S(2)}, u32[]{:S(2)}) collective-permute-start(f32[64,128]{1,0:T(8,128)S(1)} %get-tuple-element.72), channel_id=1, source_target_pairs={{0,1},{1,0},{2,3},{3,2},{4,5},{5,4},{6,7},{7,6},{8,9},{9,8},{10,11... | collective-permute-start | bytes 98312 | tf_op jit(solution)/shard_map/ppermute | solution.py:301
  62.6 3.4 %collective-permute-start.11 = (f32[64,128]{1,0:T(8,128)S(1)}, f32[64,128]{1,0:T(8,128)S(1)}, u32[]{:S(2)}, u32[]{:S(2)}) collective-permute-start(f32[64,128]{1,0:T(8,128)S(1)} %add.69), channel_id=1, source_target_pairs={{0,3},{1,2},{2,1},{3,0},{4,7},{5,6},{6,5},{7,4},{8,11},{9,10},{10,... | collective-permute-start | bytes 98312 | tf_op jit(solution)/shard_map/ppermute | solution.py:301
  79.4 1.3 %collective-permute-start.12 = (f32[64,128]{1,0:T(8,128)S(1)}, f32[64,128]{1,0:T(8,128)S(1)}, u32[]{:S(2)}, u32[]{:S(2)}) collective-permute-start(f32[64,128]{1,0:T(8,128)S(1)} %slice_add_fusion.keep), channel_id=1, source_target_pairs={{0,1},{1,0},{2,3},{3,2},{4,5},{5,4},{6,7},{7,6},{8,9},{9,8},{10,11... | collective-permute-start | bytes 98312 | tf_op jit(solution)/shard_map/ppermute | solution.py:301

commit v7 on v5

--- a/solution.py
+++ b/solution.py
@@ -15,7 +15,7 @@
 LOG2E = 1.4426950408889634
 STEP = 4
 ABSENT = -1e30
-PIECES = (2, 2, 3, 1)
+PIECES = (2, 3, 3)
 
 VMEM = pltpu.VMEM
 SMEM = pltpu.SMEM
@@ -40,19 +40,19 @@
     return lax.axis_index("src").astype(jnp.int32)
 
 
-def half_flip(every):
-    at = position()
-    for r in (16, 8, 4, 2, 1):
-        at = at ^ (at >> r)
-    return (at & 1) * (every // 2)
+def parity(x):
+    for r in (4, 2, 1):
+        x = x ^ (x >> r)
+    return x & 1
+
+
+def place_of(block, local, half, me):
+    owner = block >> (local.bit_length() - 1)
+    return parity(owner ^ me) * half + (owner >> 1) * local + (block & (local - 1))
 
 
 def total_of(x):
     return jnp.sum(jnp.sum(x, axis=0, keepdims=True), axis=1, keepdims=True)
-
-
-def steps_of(live_s):
-    return (live_s + (STEP - 1)) // STEP
 
 
 def pack_kernel(count_hbm, mass_hbm, lin_hbm, amass_hbm, out_ref, count, sems):
@@ -71,7 +71,7 @@
         out_ref[row, :] = jnp.where(lane < count[i], out_ref[row, :], 0.0)
 
 
-def build_tiles(steps, first, x_ref, lin_ref, mass_ref, feat, waits, k_ref, la_ref):
+def build_tiles(plan, first, x_ref, lin_ref, mass_ref, feat, waits, k_ref, la_ref):
     blocks, slots, block, width = feat.shape
     scale = LOG2E / (width * EPS)
     mask = diag_mask(block)
@@ -89,7 +89,8 @@
             waits[s].wait()
 
         def tiles(p, _):
-            y = feat[s, pl.ds(p * STEP, STEP)].reshape(STEP * block, width)
+            y = [feat[s, plan[at, p * STEP + q]] for q in range(STEP)]
+            y = jnp.concatenate(y, axis=0)
             y32 = y.astype(jnp.float32)
             y2 = y32 * y32
             ysq = jnp.sum(y2[:, : width // 2] + y2[:, width // 2 :], axis=1, keepdims=True)
@@ -102,7 +103,7 @@
                 k_ref[pl.ds(start, block), :] = jnp.exp2(e)
             return 0
 
-        lax.fori_loop(0, steps(at), tiles, 0)
+        lax.fori_loop(0, plan[2 * lin_ref.shape[0], at], tiles, 0)
 
 
 def first_build(live_hbm, tgt_hbm, x_hbm, lin_hbm, mass_hbm, feat, *refs):
@@ -118,19 +119,34 @@
     for c in copies[:5]:
         c.wait()
     every = flags.shape[1]
-    flip = half_flip(every)
+    local = tgt.shape[0]
+    me = position()
     lane = lax.broadcasted_iota(jnp.int32, (1, every), 1)
+    for s in range(local):
+        rows = [place_of(tgt[s, k], local, every // 2, me) for k in range(slots)]
+        mine = [jnp.where(r < every // 2, 1, 0) for r in rows]
+        used = [jnp.where(k < live[s], 1, 0) for k in range(slots)]
+        own_count = functools.reduce(lambda p, q: p + q, [m * v for m, v in zip(mine, used)])
+        at_own, at_other = jnp.int32(0), own_count
+        for q in range(STEP):
+            plan_ref[s, live[s] + q] = 0
+            plan_ref[local + s, live[s] + q] = every
+        for k in range(slots):
+            at = jnp.where(mine[k] == 1, at_own, at_other)
+            at = jnp.where(used[k] == 1, at, slots + STEP)
+            plan_ref[s, at] = k
+            plan_ref[local + s, at] = rows[k]
+            at_own += mine[k] * used[k]
+            at_other += (1 - mine[k]) * used[k]
+        plan_ref[2 * local, s] = (live[s] + (STEP - 1)) // STEP
+        plan_ref[2 * local + 1, s] = (own_count + (STEP - 1)) // STEP
+        plan_ref[2 * local + 2, s] = own_count // STEP
     for at in range(flags.shape[0]):
         s, k = divmod(at, slots)
-        row = jnp.where(k < live[s], tgt[s, k] ^ flip, every)
-        plan_ref[s, k] = row
+        row = jnp.where(k < live[s], plan_ref[local + s, k], every)
         flags[at : at + 1, :] = jnp.where(lane == row, 1.0, 0.0)
-    for s in range(tgt.shape[0]):
-        plan_ref[tgt.shape[0], s] = steps_of(live[s])
     hit_ref[...] = jnp.transpose(flags[...]).astype(jnp.bfloat16)
-    build_tiles(
-        lambda s: steps_of(live[s]), 0, x_ref, lin_ref, mass_ref, own, copies[5:-1], k_ref, la_ref
-    )
+    build_tiles(plan_ref, 0, x_ref, lin_ref, mass_ref, own, copies[5:-1], k_ref, la_ref)
     copies[-1].wait()
 
 
@@ -142,9 +158,7 @@
             feat.at[pl.ds(first + own.shape[0], next_ref.shape[0])], next_ref, sem
         )
         copy.start()
-    build_tiles(
-        lambda s: plan[plan.shape[0] - 1, s], first, x_ref, lin_ref, mass_ref, own, (), k_ref, la_ref
-    )
+    build_tiles(plan, first, x_ref, lin_ref, mass_ref, own, (), k_ref, la_ref)
     if copy:
         copy.wait()
 
@@ -157,11 +171,9 @@
     return piece, s
 
 
-def sweep(plan, hit_ref, w_ref, k_refs, la_refs, keep_ref, send_ref, acc_ref, u_ref, col_ref):
-    blocks, slots = plan.shape[0] - 1, plan.shape[1]
-    block = w_ref.shape[1]
-    every = w_ref.shape[0] - 8
-    w_ref[every:, :] = jnp.zeros((8, block), jnp.float32)
+def add_rows(plan, span, w_ref, k_refs, done):
+    blocks, block = (plan.shape[0] - 3) // 2, w_ref.shape[1]
+    slots = plan.shape[1] - 2 * STEP
     for s in range(blocks):
         piece, at = place(s)
         k_ref, base = k_refs[piece], at * slots
@@ -169,20 +181,18 @@
         def add_row(p, acc):
             for q in range(STEP):
                 k = p * STEP + q
-                row = plan[s, k]
                 start = pl.multiple_of((base + k) * block, block)
-                acc = acc + k_ref[pl.ds(start, block), :] * w_ref[pl.ds(row, 1), :]
+                w = w_ref[pl.ds(plan[blocks + s, k], 1), :]
+                acc = acc + k_ref[pl.ds(start, block), :] * w
             return acc
 
-        acc_ref[s * block : (s + 1) * block, :] = lax.fori_loop(
-            0, plan[blocks, s], add_row, jnp.zeros((block, block), jnp.float32)
-        )
-    for s in range(blocks):
-        rows = pl.ds(s * block, block)
-        total = jnp.sum(acc_ref[rows, :], axis=1, keepdims=True)
-        piece, at = place(s)
-        la = la_refs[piece][pl.ds(at * block, block), :]
-        u_ref[rows, :] = jnp.exp(la - F * jnp.log(total))
+        first, last = span(s)
+        done(s, lax.fori_loop(first, last, add_row, jnp.zeros((block, block), jnp.float32)))
+
+
+def add_columns(plan, span, u_ref, k_refs, hit, col_ref):
+    blocks, block = (plan.shape[0] - 3) // 2, col_ref.shape[1]
+    slots = plan.shape[1] - 2 * STEP
     col_ref[...] = jnp.zeros_like(col_ref)
     for s in range(blocks):
         piece, at = place(s)
@@ -198,74 +208,139 @@
                 )
             return 0
 
-        lax.fori_loop(0, plan[blocks, s], add_col, 0)
+        first, last = span(s)
+        lax.fori_loop(first, last, add_col, 0)
     col = col_ref[...]
-    hit = hit_ref[...]
-    dense = jnp.zeros((every, block), jnp.float32)
+    dense = jnp.zeros((hit.shape[0], block), jnp.float32)
     for _ in range(2):
-        piece = col.astype(jnp.bfloat16)
-        dense += jnp.dot(hit, piece, preferred_element_type=jnp.float32)
-        col = col - piece.astype(jnp.float32)
-    keep_ref[...] = dense[: every // 2, :]
-    send_ref[...] = dense[every // 2 :, :]
-
-
-def first_sweep(npieces, plan, hit_ref, *refs):
-    k_refs, la_refs = refs[:npieces], refs[npieces : 2 * npieces]
-    parts = refs[2 * npieces : 2 * npieces + 2]
-    keep_ref, send_ref, fb_ref, et_ref, tot_ref, w_ref, acc_ref, u_ref, col_ref = refs[
-        2 * npieces + 2 :
-    ]
-    local = plan.shape[0] - 1
-    flip = half_flip(fb_ref.shape[0])
-    n = fb_ref.shape[0] // local
-    am = jnp.zeros((local, fb_ref.shape[1]), jnp.float32)
+        term = col.astype(jnp.bfloat16)
+        dense += jnp.dot(hit, term, preferred_element_type=jnp.float32)
+        col = col - term.astype(jnp.float32)
+    return dense
+
+
+def own_span(plan):
+    local = (plan.shape[0] - 3) // 2
+    return lambda s: (0, plan[2 * local + 1, s])
+
+
+def other_span(plan):
+    local = (plan.shape[0] - 3) // 2
+    return lambda s: (plan[2 * local + 2, s], plan[2 * local, s])
+
+
+def spread(w_ref, w, other):
+    half = w.shape[0]
+    zeros = jnp.zeros((half, w.shape[1]), jnp.float32)
+    w_ref[:half, :] = zeros if other else w
+    w_ref[half : 2 * half, :] = w if other else zeros
+    w_ref[2 * half :, :] = zeros[:8, :]
+
+
+def unpack(part, fb_ref, et_ref):
+    half, block = fb_ref.shape
+    n = lax.axis_size("src")
+    local = 2 * half // n
+    order = distances(n)
+    am = jnp.zeros((local, block), jnp.float32)
     bm = am
-    order = distances(n)
-    for at in range(n):
+    for at in range(n // 2):
         m = functools.reduce(lambda p, q: p ^ q, [d for r, d in enumerate(order) if at >> r & 1], 0)
-        part = parts[at // (n // 2)]
-        at = (at % (n // 2)) * 3 * local
-        rows = pl.ds(pl.multiple_of(((position() ^ m) * local) ^ flip, local), local)
+        rows = pl.ds(pl.multiple_of(((position() ^ m) >> 1) * local, local), local)
+        at = at * 3 * local
         b = part[at : at + local, :]
-        et = jnp.exp((-ALPHA / EPS) * part[at + local : at + 2 * local, :])
         fb_ref[rows, :] = jnp.where(b > 0.0, F * jnp.log(b), ABSENT)
-        et_ref[rows, :] = et
-        w_ref[rows, :] = jnp.where(b > 0.0, et, 0.0)
+        et_ref[rows, :] = jnp.exp((-ALPHA / EPS) * part[at + local : at + 2 * local, :])
         bm += b
         am += part[at + 2 * local : at + 3 * local, :]
-    tot = jnp.sqrt(total_of(am) * total_of(bm))
+    return am, bm
+
+
+def half_scale(sums, fb_ref, et_ref):
+    fb = fb_ref[...]
+    col = sums[...] * et_ref[...]
+    t = jnp.where(fb > ABSENT, jnp.exp(fb - F * jnp.log(col)), 0.0)
+    return t, jnp.sum(t * col, axis=0, keepdims=True)
+
+
+def finish(plan, hit_ref, factor, acc_ref, w_ref, k_refs, la_refs, send_ref, u_ref, col_ref):
+    block = w_ref.shape[1]
+
+    def scale(s, acc):
+        rows = pl.ds(s * block, block)
+        total = jnp.sum(acc + acc_ref[rows, :], axis=1, keepdims=True)
+        if factor is not None:
+            total = total * factor
+        piece, at = place(s)
+        la = la_refs[piece][pl.ds(at * block, block), :]
+        u_ref[rows, :] = jnp.exp(la - F * jnp.log(total))
+
+    add_rows(plan, other_span(plan), w_ref, k_refs, scale)
+    hit = hit_ref[send_ref.shape[0] :, :]
+    send_ref[...] = add_columns(plan, other_span(plan), u_ref, k_refs, hit, col_ref)
+
+
+def keep_rows(acc_ref):
+    block = acc_ref.shape[1]
+
+    def keep(s, acc):
+        acc_ref[s * block : (s + 1) * block, :] = acc
+
+    return keep
+
+
+def first_own(plan, part, *refs):
+    k_refs, (acc_ref, fb_ref, et_ref, sums_ref, w_ref) = refs[:-5], refs[-5:]
+    am, bm = unpack(part, fb_ref, et_ref)
+    sums_ref[:8, :], sums_ref[8:, :] = am, bm
+    spread(w_ref, jnp.where(fb_ref[...] > ABSENT, et_ref[...], 0.0), False)
+    add_rows(plan, own_span(plan), w_ref, k_refs, keep_rows(acc_ref))
+
+
+def first_other(plan, hit_ref, part, sums_ref, acc_ref, *refs):
+    pieces = len(PIECES)
+    k_refs, la_refs = refs[:pieces], refs[pieces : 2 * pieces]
+    send_ref, u_ref, fb_ref, et_ref, tot_ref, w_ref, col_ref = refs[2 * pieces :]
+    am, bm = unpack(part, fb_ref, et_ref)
+    tot = jnp.sqrt(total_of(am + sums_ref[:8, :]) * total_of(bm + sums_ref[8:, :]))
     tot_ref[...] = jnp.broadcast_to(tot, tot_ref.shape)
-    sweep(plan, hit_ref, w_ref, k_refs, la_refs, keep_ref, send_ref, acc_ref, u_ref, col_ref)
-
-
-def new_scale(keep, other, fb_ref, et_ref, tot_ref, t_ref):
-    half = keep.shape[0]
-    mass = jnp.zeros((1, keep.shape[1]), jnp.float32)
-    for at, sums in ((0, keep), (half, other)):
-        rows = slice(at, at + half)
-        fb = fb_ref[rows, :]
-        col = sums[...] * et_ref[rows, :]
-        t = jnp.where(fb > ABSENT, jnp.exp(fb - F * jnp.log(col)), 0.0)
-        t_ref[rows, :] = t
-        mass += jnp.sum(t * col, axis=0, keepdims=True)
-    return jnp.sqrt(tot_ref[0:1, 0:1] / jnp.sum(mass, axis=1, keepdims=True))
-
-
-def next_sweep(npieces, plan, hit_ref, keep, other, fb_ref, et_ref, tot_ref, *refs):
-    k_refs, la_refs = refs[:npieces], refs[npieces : 2 * npieces]
-    keep_ref, send_ref, u_ref, w_ref, acc_ref, col_ref = refs[2 * npieces :]
-    factor = new_scale(keep, other, fb_ref, et_ref, tot_ref, w_ref)
-    rows = slice(0, fb_ref.shape[0])
-    w_ref[rows, :] = w_ref[rows, :] * (factor * et_ref[...])
-    sweep(plan, hit_ref, w_ref, k_refs, la_refs, keep_ref, send_ref, acc_ref, u_ref, col_ref)
-
-
-def last_kernel(keep, other, fb_ref, et_ref, tot_ref, u_ref, src_ref, tgt_ref, t_ref):
+    spread(w_ref, jnp.where(fb_ref[...] > ABSENT, et_ref[...], 0.0), True)
+    finish(plan, hit_ref, None, acc_ref, w_ref, k_refs, la_refs, send_ref, u_ref, col_ref)
+
+
+def next_own(plan, sums, fb_ref, et_ref, *refs):
+    k_refs, (acc_ref, mass_ref, w_ref) = refs[:-3], refs[-3:]
+    t, mass = half_scale(sums, fb_ref, et_ref)
+    mass_ref[...] = jnp.broadcast_to(mass, mass_ref.shape)
+    spread(w_ref, t * et_ref[...], False)
+    add_rows(plan, own_span(plan), w_ref, k_refs, keep_rows(acc_ref))
+
+
+def next_other(plan, hit_ref, sums, fb_ref, et_ref, tot_ref, mass_ref, acc_ref, *refs):
+    pieces = len(PIECES)
+    k_refs, la_refs = refs[:pieces], refs[pieces : 2 * pieces]
+    send_ref, u_ref, w_ref, col_ref = refs[2 * pieces :]
+    t, mass = half_scale(sums, fb_ref, et_ref)
+    mass = jnp.sum(mass + mass_ref[0:1, :], axis=1, keepdims=True)
+    factor = jnp.sqrt(tot_ref[0:1, 0:1] / mass)
+    spread(w_ref, t * et_ref[...], True)
+    finish(plan, hit_ref, factor, acc_ref, w_ref, k_refs, la_refs, send_ref, u_ref, col_ref)
+
+
+def own_columns(plan, hit_ref, u_ref, *refs):
+    k_refs, (keep_ref, col_ref) = refs[:-2], refs[-2:]
+    hit = hit_ref[: keep_ref.shape[0], :]
+    keep_ref[...] = add_columns(plan, own_span(plan), u_ref, k_refs, hit, col_ref)
+
+
+def last_kernel(keep, other, fb0, et0, fb1, et1, tot_ref, u_ref, src_ref, tgt_ref, t_ref):
     local, block = src_ref.shape
-    factor = new_scale(keep, other, fb_ref, et_ref, tot_ref, t_ref)
-    own = (position() * local) ^ half_flip(fb_ref.shape[0])
-    tgt_ref[...] = t_ref[pl.ds(pl.multiple_of(own, local), local), :] * factor
+    t, mass = half_scale(keep, fb0, et0)
+    t_ref[...] = t
+    mass += half_scale(other, fb1, et1)[1]
+    factor = jnp.sqrt(tot_ref[0:1, 0:1] / jnp.sum(mass, axis=1, keepdims=True))
+    own = pl.multiple_of((position() >> 1) * local, local)
+    tgt_ref[...] = t_ref[pl.ds(own, local), :] * factor
     mask = diag_mask(block)
     for s in range(local):
         src_ref[s : s + 1, :] = to_row(u_ref[s * block : (s + 1) * block, :] * factor, mask)
@@ -343,7 +418,7 @@
                 (tile_live, tile_tgt, src_feat, lin, amass, tile_feat),
                 (
                     *outs,
-                    SMEM((local + 1, slots), jnp.int32),
+                    SMEM((2 * local + 3, slots + 2 * STEP), jnp.int32),
                     shape(every, pairs, jnp.bfloat16),
                     shape(local * block, width, src_feat.dtype),
                     shape(local),
@@ -377,38 +452,49 @@
             part = jnp.stack([part, got], axis=0).reshape(-1, block)
             if at < len(PIECES) - 1:
                 part, following, kern[-1] = lax.optimization_barrier((part, following, kern[-1]))
-    acc = VMEM((local * block, block), f32)
+    half = every // 2
+    tall = shape(local * block)
+    w = VMEM((every + 8, block), f32)
     col = VMEM((pairs, block), f32)
-    w = VMEM((every + 8, block), f32)
-    half = every // 2
-    keep, send, fb, et, tot = call(
-        functools.partial(first_sweep, len(PIECES)),
-        (plan, hit, *kern, *la, part, got),
-        (shape(half), shape(half), shape(every), shape(every), shape(8)),
-        scratch=[w, acc, acc, col],
+    acc, fb0, et0, sums = call(
+        first_own,
+        (plan, part, *kern),
+        (tall, shape(half), shape(half), shape(16)),
+        scratch=[w],
         smem=1,
     )
-    u = None
+    send, u, fb1, et1, tot = call(
+        first_other,
+        (plan, hit, got, sums, acc, *kern, *la),
+        (shape(half), tall, shape(half), shape(half), shape(8)),
+        scratch=[w, col],
+        smem=1,
+    )
     for iteration in range(ITERS):
-        keep = keep + exchange(send, n, order[-1])
+        got = exchange(send, n, order[-1])
+        (keep,) = call(
+            own_columns, (plan, hit, u, *kern), (shape(half),), scratch=[col], smem=1
+        )
+        keep = keep + got
         for d in order[-2::-1]:
             keep = keep + exchange(keep, n, d)
         other = exchange(keep, n, order[-1])
         if iteration < ITERS - 1:
-            last = iteration == ITERS - 2
-            outs = (shape(half), shape(half)) + ((shape(local * block),) if last else ())
-            keep, send, *u = call(
-                functools.partial(next_sweep, len(PIECES)),
-                (plan, hit, keep, other, fb, et, tot, *kern, *la),
-                outs,
-                scratch=[w, acc, col] if last else [acc, w, acc, col],
+            acc, mass = call(
+                next_own, (plan, keep, fb0, et0, *kern), (tall, shape(8)), scratch=[w], smem=1
+            )
+            send, u = call(
+                next_other,
+                (plan, hit, other, fb1, et1, tot, mass, acc, *kern, *la),
+                (shape(half), tall),
+                scratch=[w, col],
                 smem=1,
             )
     src, tgt = call(
         last_kernel,
-        (keep, other, fb, et, tot, *u),
+        (keep, other, fb0, et0, fb1, et1, tot, u),
         [jax.ShapeDtypeStruct((local, block), f32)] * 2,
-        scratch=[VMEM((every, block), f32)],
+        scratch=[VMEM((half, block), f32)],
     )
     return (src.reshape(-1), tgt.reshape(-1))
 

time: 66.6 us -> 71.9 us (1.080)
  starting transfers between devices: 19.2 us -> 8.81 us
  waiting for transfers between devices: 31.3 us -> 39.7 us
  Pallas kernels: 15.1 us -> 23 us
    ppermute x19, starting transfers between devices: 19.2 us -> 8.81 us  [exchange(): return lax.ppermute(x, 'src', [(i, i ^ d) for i in range(n)])]
    ppermute x19, waiting for transfers between devices: 31.3 us -> 39.7 us  [exchange(): return lax.ppermute(x, 'src', [(i, i ^ d) for i in range(n)])]
    pallas_call x9 -> x14, Pallas kernels: 15.1 us -> 23 us  [call(): pl.pallas_call(kernel, out_shape=outs, in_specs=specs, out_specs=[pl.Bloc...]
  transfers between devices with their start and end apart: 19 -> 19, of which waited for: 17 -> 16; matrix products, arithmetic and copies ran while one was open for 0% -> 0% of each run, Pallas kernels for 12% -> 19%
where the time goes in v7:
time: 71.9 us; the launch traced here: 72.4 us
  waiting for transfers between devices  39.7 us (55%)
  Pallas kernels  23 us (32%)
  starting transfers between devices  8.81 us (12%)
  between operations  0.81 us (1%)
    ppermute x19, waiting for transfers between devices, exchange(): return lax.ppermute(x, 'src', [(i, i ^ d) for i in range(n)])  39.7 us
    pallas_call x14, Pallas kernels, call(): pl.pallas_call(kernel, out_shape=outs, in_specs=specs, out_specs=[pl.Bloc...  23 us
    ppermute x19, starting transfers between devices, exchange(): return lax.ppermute(x, 'src', [(i, i ^ d) for i in range(n)])  8.81 us
  transfers between devices with their start and end apart: 19, of which 16 were waited for; matrix products, arithmetic and copies ran while one was open for 0% of the time, Pallas kernels for 19%

profile of v7, /device:TPU:0, one launch (start us, length us, event | category | flops | bytes accessed | tf_op | source)
XLA Modules:
  0.0 72.4 jit_solution(777403489598535063)
XLA Ops:
  0.6 0.8 %shard_map.105 = f32[24,128]{1,0:T(8,128)S(1)} custom-call(s32[8]{0:T(128)} %count_hbm.1, f32[8,128]{1,0:T(8,128)} %bitcast.28, f32[8,128]{1,0:T(8,128)} %bitcast.29, f32[8,128]{1,0:T(8,128)} %bitcast.24), custom_call_target="tpu_custom_call" | custom-call | tf_op jit(solution)/shard_map/pallas_call | solution.py:357
  1.4 3.5 %collective-permute-start = (f32[24,128]{1,0:T(8,128)S(1)}, f32[24,128]{1,0:T(8,128)S(1)}, u32[]{:S(2)}, u32[]{:S(2)}) collective-permute-start(f32[24,128]{1,0:T(8,128)S(1)} %shard_map.105), channel_id=1, source_target_pairs={{0,9},{1,8},{2,11},{3,10},{4,13},{5,12},{6,15},{7,14},{8,1},{9,0},... | collective-permute-start | bytes 36872 | tf_op jit(solution)/shard_map/ppermute | solution.py:375
  4.9 5.4 %shard_map.104 = (f32[4096,128]{1,0:T(8,128)S(1)}, f32[256,128]{1,0:T(8,128)S(1)}, bf16[3,16,128,256]{3,2,1,0:T(8,128)(2,1)S(1)}, s32[19,24]{1,0:T(8,128)S(4)}, ...) custom-call(s32[8]{0:T(128)} %live_hbm.1, ...), custom_call_target="tpu_custom_call" | custom-call | flops 268435456 | bytes 2097152 | tf_op jit(solution)/shard_map/pallas_call | solution.py:357
  10.3 0.0 collective-permute-done
  10.4 1.4 %collective-permute-start.1 = (f32[48,128]{1,0:T(8,128)S(1)}, f32[48,128]{1,0:T(8,128)S(1)}, u32[]{:S(2)}, u32[]{:S(2)}) collective-permute-start(f32[48,128]{1,0:T(8,128)S(1)} %bitcast.20), channel_id=1, source_target_pairs={{0,5},{1,4},{2,7},{3,6},{4,1},{5,0},{6,3},{7,2},{8,13},{9,12},{10,... | collective-permute-start | bytes 73736 | tf_op jit(solution)/shard_map/ppermute | solution.py:375
  11.8 2.8 %shard_map.106 = (f32[6144,128]{1,0:T(8,128)S(1)}, f32[384,128]{1,0:T(8,128)S(1)}, bf16[3,16,128,256]{3,2,1,0:T(8,128)(2,1)S(1)}) custom-call(s32[19,24]{1,0:T(8,128)S(4)} %get-tuple-element.40.plan, bf16[1024,256]{1,0:T(8,128)(2,1)S(1)} %get-tuple-element.45.x_ref, f32[8,128]{1,0:T(8,128)S(1)} %get-tuple-element.46.lin_ref, ...), custom_call_target="tpu_custom_call" | custom-call | flops 402653184 | bytes 3145728 | tf_op jit(solution)/shard_map/pallas_call | solution.py:357
  14.6 0.0 collective-permute-done.1
  14.7 0.8 %collective-permute-start.2 = (f32[96,128]{1,0:T(8,128)S(1)}, f32[96,128]{1,0:T(8,128)S(1)}, u32[]{:S(2)}, u32[]{:S(2)}) collective-permute-start(f32[96,128]{1,0:T(8,128)S(1)} %bitcast.18), channel_id=1, source_target_pairs={{0,3},{1,2},{2,1},{3,0},{4,7},{5,6},{6,5},{7,4},{8,11},{9,10},{10,... | collective-permute-start | bytes 147464 | tf_op jit(solution)/shard_map/ppermute | solution.py:375
  15.5 3.1 %collective-permute-done.2 = f32[96,128]{1,0:T(8,128)S(1)} collective-permute-done((f32[96,128]{1,0:T(8,128)S(1)}, f32[96,128]{1,0:T(8,128)S(1)}, u32[]{:S(2)}, u32[]{:S(2)}) %collective-permute-start.2) | collective-permute-done | bytes 49184 | tf_op jit(solution)/shard_map/ppermute | solution.py:375
  18.6 0.1 collective-permute-start.3
  18.7 2.1 %shard_map.107 = (f32[6144,128]{1,0:T(8,128)S(1)}, f32[384,128]{1,0:T(8,128)S(1)}) custom-call(s32[19,24]{1,0:T(8,128)S(4)} %get-tuple-element.40.plan, bf16[1024,256]{1,0:T(8,128)(2,1)S(1)} %get-tuple-element.45.x_ref, f32[8,128]{1,0:T(8,128)S(1)} %get-tuple-element.46.lin_ref, f32[8,128]{1,0:T(8,128)S(1)} %get-tuple-element.47.mass_ref, ...), custom_call_target="tpu_custom_call" | custom-call | flops 402653184 | bytes 3145728 | tf_op jit(solution)/shard_map/pallas_call | solution.py:357
  20.8 0.5 shard_map.108
  21.2 0.0 collective-permute-done.3.part
  21.2 2.0 %shard_map.109 = (f32[64,128]{1,0:T(8,128)S(1)}, f32[1024,128]{1,0:T(8,128)S(1)}, f32[64,128]{1,0:T(8,128)S(1)}, f32[64,128]{1,0:T(8,128)S(1)}, f32[8,128]{1,0:T(8,128)S(1)}) custom-call(s32[19,24]{1,0:T(8,128)S(4)} %get-tuple-element.40.plan, bf16[128,128]{1,0:T(8,128)(2,1)S(1)} %get-tuple-element.41.hit_ref, f32[192,128]{1,0:T(8,128)S(1)} %collective-permute-done.3.part, ...), custom_call_target="tpu_custom_call" | custom-call | tf_op jit(solution)/shard_map/pallas_call | solution.py:357
  23.3 0.7 %collective-permute-start.4 = (f32[64,128]{1,0:T(8,128)S(1)}, f32[64,128]{1,0:T(8,128)S(1)}, u32[]{:S(2)}, u32[]{:S(2)}) collective-permute-start(f32[64,128]{1,0:T(8,128)S(1)} %get-tuple-element.62), channel_id=1, source_target_pairs={{0,1},{1,0},{2,3},{3,2},{4,5},{5,4},{6,7},{7,6},{8,9},{9,8},{10,11... | collective-permute-start | bytes 98312 | tf_op jit(solution)/shard_map/ppermute | solution.py:375
  24.0 0.7 shard_map.110
  24.7 0.2 collective-permute-done.4
  24.9 0.7 collective-permute-start.5
  25.6 2.7 %collective-permute-done.5 = f32[64,128]{1,0:T(8,128)S(1)} collective-permute-done((f32[64,128]{1,0:T(8,128)S(1)}, f32[64,128]{1,0:T(8,128)S(1)}, u32[]{:S(2)}, u32[]{:S(2)}) %collective-permute-start.5) | collective-permute-done | bytes 32800 | tf_op jit(solution)/shard_map/ppermute | solution.py:375
  28.3 0.7 collective-permute-start.6
  28.9 2.7 %collective-permute-done.6 = f32[64,128]{1,0:T(8,128)S(1)} collective-permute-done((f32[64,128]{1,0:T(8,128)S(1)}, f32[64,128]{1,0:T(8,128)S(1)}, u32[]{:S(2)}, u32[]{:S(2)}) %collective-permute-start.6) | collective-permute-done | bytes 32800 | tf_op jit(solution)/shard_map/ppermute | solution.py:375
  31.6 0.1 collective-permute-start.7
  31.7 5.0 %collective-permute-done.7 = f32[64,128]{1,0:T(8,128)S(1)} collective-permute-done((f32[64,128]{1,0:T(8,128)S(1)}, f32[64,128]{1,0:T(8,128)S(1)}, u32[]{:S(2)}, u32[]{:S(2)}) %collective-permute-start.7) | collective-permute-done | bytes 32800 | tf_op jit(solution)/shard_map/ppermute | solution.py:375
  36.7 0.1 collective-permute-start.8
  36.8 0.5 shard_map.111
  37.2 0.6 collective-permute-done.8.sums
  37.9 2.8 %shard_map.112 = (f32[64,128]{1,0:T(8,128)S(1)}, f32[1024,128]{1,0:T(8,128)S(1)}) custom-call(s32[19,24]{1,0:T(8,128)S(4)} %get-tuple-element.40.plan, bf16[128,128]{1,0:T(8,128)(2,1)S(1)} %get-tuple-element.41.hit_ref, f32[64,128]{1,0:T(8,128)S(1)} %collective-permute-done.8.sums, f32[64,128]{1,0:T(8,128)S(1)} %get-tuple-element.63.fb_ref.fb1, ...), custom_call_target="tpu_custom_call" | custom-call | tf_op jit(solution)/shard_map/pallas_call | solution.py:357
  40.7 0.2 collective-permute-start.9
  40.9 0.7 shard_map.113
  41.6 0.4 collective-permute-done.9
  42.0 0.0 collective-permute-start.10
  42.0 3.3 %collective-permute-done.10 = f32[64,128]{1,0:T(8,128)S(1)} collective-permute-done((f32[64,128]{1,0:T(8,128)S(1)}, f32[64,128]{1,0:T(8,128)S(1)}, u32[]{:S(2)}, u32[]{:S(2)}) %collective-permute-start.10) | collective-permute-done | bytes 32800 | tf_op jit(solution)/shard_map/ppermute | solution.py:375
  45.3 0.0 collective-permute-start.11
  45.3 3.3 %collective-permute-done.11 = f32[64,128]{1,0:T(8,128)S(1)} collective-permute-done((f32[64,128]{1,0:T(8,128)S(1)}, f32[64,128]{1,0:T(8,128)S(1)}, u32[]{:S(2)}, u32[]{:S(2)}) %collective-permute-start.11) | collective-permute-done | bytes 32800 | tf_op jit(solution)/shard_map/ppermute | solution.py:375
  48.7 0.0 collective-permute-start.12
  48.7 4.8 %collective-permute-done.12 = f32[64,128]{1,0:T(8,128)S(1)} collective-permute-done((f32[64,128]{1,0:T(8,128)S(1)}, f32[64,128]{1,0:T(8,128)S(1)}, u32[]{:S(2)}, u32[]{:S(2)}) %collective-permute-start.12) | collective-permute-done | bytes 32800 | tf_op jit(solution)/shard_map/ppermute | solution.py:375
  53.5 0.1 collective-permute-start.13
  53.6 0.5 shard_map.114
  54.1 0.6 collective-permute-done.13.sums
  54.7 2.8 %shard_map.115 = (f32[64,128]{1,0:T(8,128)S(1)}, f32[1024,128]{1,0:T(8,128)S(1)}) custom-call(s32[19,24]{1,0:T(8,128)S(4)} %get-tuple-element.40.plan, bf16[128,128]{1,0:T(8,128)(2,1)S(1)} %get-tuple-element.41.hit_ref, f32[64,128]{1,0:T(8,128)S(1)} %collective-permute-done.13.sums, f32[64,128]{1,0:T(8,128)S(1)} %get-tuple-element.63.fb_ref.fb1, ...), custom_call_target="tpu_custom_call" | custom-call | tf_op jit(solution)/shard_map/pallas_call | solution.py:357
  57.5 0.2 collective-permute-start.14
  57.8 0.7 shard_map.116
  58.4 0.4 collective-permute-done.14
  58.8 0.0 collective-permute-start.15
  58.8 3.3 %collective-permute-done.15 = f32[64,128]{1,0:T(8,128)S(1)} collective-permute-done((f32[64,128]{1,0:T(8,128)S(1)}, f32[64,128]{1,0:T(8,128)S(1)}, u32[]{:S(2)}, u32[]{:S(2)}) %collective-permute-start.15) | collective-permute-done | bytes 32800 | tf_op jit(solution)/shard_map/ppermute | solution.py:375
  62.2 0.0 collective-permute-start.16
  62.2 3.3 %collective-permute-done.16 = f32[64,128]{1,0:T(8,128)S(1)} collective-permute-done((f32[64,128]{1,0:T(8,128)S(1)}, f32[64,128]{1,0:T(8,128)S(1)}, u32[]{:S(2)}, u32[]{:S(2)}) %collective-permute-start.16) | collective-permute-done | bytes 32800 | tf_op jit(solution)/shard_map/ppermute | solution.py:375
  65.5 0.0 collective-permute-start.17
  65.5 4.8 %collective-permute-done.17 = f32[64,128]{1,0:T(8,128)S(1)} collective-permute-done((f32[64,128]{1,0:T(8,128)S(1)}, f32[64,128]{1,0:T(8,128)S(1)}, u32[]{:S(2)}, u32[]{:S(2)}) %collective-permute-start.17) | collective-permute-done | bytes 32800 | tf_op jit(solution)/shard_map/ppermute | solution.py:375
  70.3 0.1 collective-permute-start.18
  70.5 1.1 %collective-permute-done.18.other = f32[64,128]{1,0:T(8,128)S(1)} collective-permute-done((f32[64,128]{1,0:T(8,128)S(1)}, f32[64,128]{1,0:T(8,128)S(1)}, u32[]{:S(2)}, u32[]{:S(2)}) %collective-permute-start.18) | collective-permute-done | bytes 32800 | tf_op jit(solution)/shard_map/ppermute | solution.py:375
  71.5 0.8 %shard_map.117 = (f32[8,128]{1,0:T(8,128)}, f32[8,128]{1,0:T(8,128)}) custom-call(f32[64,128]{1,0:T(8,128)S(1)} %add.47.keep, f32[64,128]{1,0:T(8,128)S(1)} %collective-permute-done.18.other, f32[64,128]{1,0:T(8,128)S(1)} %get-tuple-element.66.fb_ref.fb0, f32[64,128]{1,0:T(8,128)S(1)} %get-tuple-element.67.et_ref.et0, ...), custom_call_target="tpu_custom_call" | custom-call | tf_op jit(solution)/shard_map/pallas_call | solution.py:357
  (15 shorter events, 0.1 us)
Async XLA Ops:
  1.4 8.9 %collective-permute-start = (f32[24,128]{1,0:T(8,128)S(1)}, f32[24,128]{1,0:T(8,128)S(1)}, u32[]{:S(2)}, u32[]{:S(2)}) collective-permute-start(f32[24,128]{1,0:T(8,128)S(1)} %shard_map.105), channel_id=1, source_target_pairs={{0,9},{1,8},{2,11},{3,10},{4,13},{5,12},{6,15},{7,14},{8,1},{9,0},... | collective-permute-start | bytes 36872 | tf_op jit(solution)/shard_map/ppermute | solution.py:375
  10.4 4.3 %collective-permute-start.1 = (f32[48,128]{1,0:T(8,128)S(1)}, f32[48,128]{1,0:T(8,128)S(1)}, u32[]{:S(2)}, u32[]{:S(2)}) collective-permute-start(f32[48,128]{1,0:T(8,128)S(1)} %bitcast.20), channel_id=1, source_target_pairs={{0,5},{1,4},{2,7},{3,6},{4,1},{5,0},{6,3},{7,2},{8,13},{9,12},{10,... | collective-permute-start | bytes 73736 | tf_op jit(solution)/shard_map/ppermute | solution.py:375
  14.7 3.9 %collective-permute-start.2 = (f32[96,128]{1,0:T(8,128)S(1)}, f32[96,128]{1,0:T(8,128)S(1)}, u32[]{:S(2)}, u32[]{:S(2)}) collective-permute-start(f32[96,128]{1,0:T(8,128)S(1)} %bitcast.18), channel_id=1, source_target_pairs={{0,3},{1,2},{2,1},{3,0},{4,7},{5,6},{6,5},{7,4},{8,11},{9,10},{10,... | collective-permute-start | bytes 147464 | tf_op jit(solution)/shard_map/ppermute | solution.py:375
  18.6 2.7 %collective-permute-start.3 = (f32[192,128]{1,0:T(8,128)S(1)}, f32[192,128]{1,0:T(8,128)S(1)}, u32[]{:S(2)}, u32[]{:S(2)}) collective-permute-start(f32[192,128]{1,0:T(8,128)S(1)} %bitcast.15), channel_id=1, source_target_pairs={{0,1},{1,0},{2,3},{3,2},{4,5},{5,4},{6,7},{7,6},{8,9},{9,8},{10,11... | collective-permute-start | bytes 294920 | tf_op jit(solution)/shard_map/ppermute | solution.py:375
  23.3 1.6 %collective-permute-start.4 = (f32[64,128]{1,0:T(8,128)S(1)}, f32[64,128]{1,0:T(8,128)S(1)}, u32[]{:S(2)}, u32[]{:S(2)}) collective-permute-start(f32[64,128]{1,0:T(8,128)S(1)} %get-tuple-element.62), channel_id=1, source_target_pairs={{0,1},{1,0},{2,3},{3,2},{4,5},{5,4},{6,7},{7,6},{8,9},{9,8},{10,11... | collective-permute-start | bytes 98312 | tf_op jit(solution)/shard_map/ppermute | solution.py:375
  24.9 3.3 %collective-permute-start.5 = (f32[64,128]{1,0:T(8,128)S(1)}, f32[64,128]{1,0:T(8,128)S(1)}, u32[]{:S(2)}, u32[]{:S(2)}) collective-permute-start(f32[64,128]{1,0:T(8,128)S(1)} %add.36), channel_id=1, source_target_pairs={{0,3},{1,2},{2,1},{3,0},{4,7},{5,6},{6,5},{7,4},{8,11},{9,10},{10,... | collective-permute-start | bytes 98312 | tf_op jit(solution)/shard_map/ppermute | solution.py:375
  28.3 3.3 %collective-permute-start.6 = (f32[64,128]{1,0:T(8,128)S(1)}, f32[64,128]{1,0:T(8,128)S(1)}, u32[]{:S(2)}, u32[]{:S(2)}) collective-permute-start(f32[64,128]{1,0:T(8,128)S(1)} %add.37), channel_id=1, source_target_pairs={{0,5},{1,4},{2,7},{3,6},{4,1},{5,0},{6,3},{7,2},{8,13},{9,12},{10,... | collective-permute-start | bytes 98312 | tf_op jit(solution)/shard_map/ppermute | solution.py:375
  31.6 5.0 %collective-permute-start.7 = (f32[64,128]{1,0:T(8,128)S(1)}, f32[64,128]{1,0:T(8,128)S(1)}, u32[]{:S(2)}, u32[]{:S(2)}) collective-permute-start(f32[64,128]{1,0:T(8,128)S(1)} %add.38), channel_id=1, source_target_pairs={{0,9},{1,8},{2,11},{3,10},{4,13},{5,12},{6,15},{7,14},{8,1},{9,0},... | collective-permute-start | bytes 98312 | tf_op jit(solution)/shard_map/ppermute | solution.py:375
  36.7 1.2 %collective-permute-start.8 = (f32[64,128]{1,0:T(8,128)S(1)}, f32[64,128]{1,0:T(8,128)S(1)}, u32[]{:S(2)}, u32[]{:S(2)}) collective-permute-start(f32[64,128]{1,0:T(8,128)S(1)} %add.39.sums), channel_id=1, source_target_pairs={{0,1},{1,0},{2,3},{3,2},{4,5},{5,4},{6,7},{7,6},{8,9},{9,8},{10,11... | collective-permute-start | bytes 98312 | tf_op jit(solution)/shard_map/ppermute | solution.py:375
  40.7 1.3 %collective-permute-start.9 = (f32[64,128]{1,0:T(8,128)S(1)}, f32[64,128]{1,0:T(8,128)S(1)}, u32[]{:S(2)}, u32[]{:S(2)}) collective-permute-start(f32[64,128]{1,0:T(8,128)S(1)} %get-tuple-element.71), channel_id=1, source_target_pairs={{0,1},{1,0},{2,3},{3,2},{4,5},{5,4},{6,7},{7,6},{8,9},{9,8},{10,11... | collective-permute-start | bytes 98312 | tf_op jit(solution)/shard_map/ppermute | solution.py:375
  42.0 3.3 %collective-permute-start.10 = (f32[64,128]{1,0:T(8,128)S(1)}, f32[64,128]{1,0:T(8,128)S(1)}, u32[]{:S(2)}, u32[]{:S(2)}) collective-permute-start(f32[64,128]{1,0:T(8,128)S(1)} %add.40), channel_id=1, source_target_pairs={{0,3},{1,2},{2,1},{3,0},{4,7},{5,6},{6,5},{7,4},{8,11},{9,10},{10,... | collective-permute-start | bytes 98312 | tf_op jit(solution)/shard_map/ppermute | solution.py:375
  45.3 3.3 %collective-permute-start.11 = (f32[64,128]{1,0:T(8,128)S(1)}, f32[64,128]{1,0:T(8,128)S(1)}, u32[]{:S(2)}, u32[]{:S(2)}) collective-permute-start(f32[64,128]{1,0:T(8,128)S(1)} %add.41), channel_id=1, source_target_pairs={{0,5},{1,4},{2,7},{3,6},{4,1},{5,0},{6,3},{7,2},{8,13},{9,12},{10,... | collective-permute-start | bytes 98312 | tf_op jit(solution)/shard_map/ppermute | solution.py:375
  48.7 4.8 %collective-permute-start.12 = (f32[64,128]{1,0:T(8,128)S(1)}, f32[64,128]{1,0:T(8,128)S(1)}, u32[]{:S(2)}, u32[]{:S(2)}) collective-permute-start(f32[64,128]{1,0:T(8,128)S(1)} %add.42), channel_id=1, source_target_pairs={{0,9},{1,8},{2,11},{3,10},{4,13},{5,12},{6,15},{7,14},{8,1},{9,0},... | collective-permute-start | bytes 98312 | tf_op jit(solution)/shard_map/ppermute | solution.py:375
  53.5 1.2 %collective-permute-start.13 = (f32[64,128]{1,0:T(8,128)S(1)}, f32[64,128]{1,0:T(8,128)S(1)}, u32[]{:S(2)}, u32[]{:S(2)}) collective-permute-start(f32[64,128]{1,0:T(8,128)S(1)} %add.43.sums), channel_id=1, source_target_pairs={{0,1},{1,0},{2,3},{3,2},{4,5},{5,4},{6,7},{7,6},{8,9},{9,8},{10,11... | collective-permute-start | bytes 98312 | tf_op jit(solution)/shard_map/ppermute | solution.py:375
  57.5 1.3 %collective-permute-start.14 = (f32[64,128]{1,0:T(8,128)S(1)}, f32[64,128]{1,0:T(8,128)S(1)}, u32[]{:S(2)}, u32[]{:S(2)}) collective-permute-start(f32[64,128]{1,0:T(8,128)S(1)} %get-tuple-element.75), channel_id=1, source_target_pairs={{0,1},{1,0},{2,3},{3,2},{4,5},{5,4},{6,7},{7,6},{8,9},{9,8},{10,11... | collective-permute-start | bytes 98312 | tf_op jit(solution)/shard_map/ppermute | solution.py:375
  58.8 3.3 %collective-permute-start.15 = (f32[64,128]{1,0:T(8,128)S(1)}, f32[64,128]{1,0:T(8,128)S(1)}, u32[]{:S(2)}, u32[]{:S(2)}) collective-permute-start(f32[64,128]{1,0:T(8,128)S(1)} %add.44), channel_id=1, source_target_pairs={{0,3},{1,2},{2,1},{3,0},{4,7},{5,6},{6,5},{7,4},{8,11},{9,10},{10,... | collective-permute-start | bytes 98312 | tf_op jit(solution)/shard_map/ppermute | solution.py:375
  62.2 3.3 %collective-permute-start.16 = (f32[64,128]{1,0:T(8,128)S(1)}, f32[64,128]{1,0:T(8,128)S(1)}, u32[]{:S(2)}, u32[]{:S(2)}) collective-permute-start(f32[64,128]{1,0:T(8,128)S(1)} %add.45), channel_id=1, source_target_pairs={{0,5},{1,4},{2,7},{3,6},{4,1},{5,0},{6,3},{7,2},{8,13},{9,12},{10,... | collective-permute-start | bytes 98312 | tf_op jit(solution)/shard_map/ppermute | solution.py:375
  65.5 4.8 %collective-permute-start.17 = (f32[64,128]{1,0:T(8,128)S(1)}, f32[64,128]{1,0:T(8,128)S(1)}, u32[]{:S(2)}, u32[]{:S(2)}) collective-permute-start(f32[64,128]{1,0:T(8,128)S(1)} %add.46), channel_id=1, source_target_pairs={{0,9},{1,8},{2,11},{3,10},{4,13},{5,12},{6,15},{7,14},{8,1},{9,0},... | collective-permute-start | bytes 98312 | tf_op jit(solution)/shard_map/ppermute | solution.py:375
  70.3 1.2 %collective-permute-start.18 = (f32[64,128]{1,0:T(8,128)S(1)}, f32[64,128]{1,0:T(8,128)S(1)}, u32[]{:S(2)}, u32[]{:S(2)}) collective-permute-start(f32[64,128]{1,0:T(8,128)S(1)} %add.47.keep), channel_id=1, source_target_pairs={{0,1},{1,0},{2,3},{3,2},{4,5},{5,4},{6,7},{7,6},{8,9},{9,8},{10,11... | collective-permute-start | bytes 98312 | tf_op jit(solution)/shard_map/ppermute | solution.py:375

commit v8 on v7

--- a/solution.py
+++ b/solution.py
@@ -103,13 +103,13 @@
                 k_ref[pl.ds(start, block), :] = jnp.exp2(e)
             return 0
 
-        lax.fori_loop(0, plan[2 * lin_ref.shape[0], at], tiles, 0)
+        lax.fori_loop(0, plan[at, slots + STEP], tiles, 0)
 
 
 def first_build(live_hbm, tgt_hbm, x_hbm, lin_hbm, mass_hbm, feat, *refs):
     k_ref, la_ref, next_ref, plan_ref, hit_ref, x_ref, lin_ref, mass_ref = refs[:8]
-    live, tgt, flags, own, sems = refs[8:]
-    size, slots = own.shape[:2]
+    live, tgt, order_ref, own, sems = refs[8:]
+    size = own.shape[0]
     copies = [(live_hbm, live), (tgt_hbm, tgt), (x_hbm, x_ref), (lin_hbm, lin_ref), (mass_hbm, mass_ref)]
     copies += [(feat.at[s], own.at[s]) for s in range(size)]
     copies += [(feat.at[pl.ds(size, next_ref.shape[0])], next_ref)]
@@ -118,34 +118,46 @@
         c.start()
     for c in copies[:5]:
         c.wait()
-    every = flags.shape[1]
-    local = tgt.shape[0]
-    me = position()
-    lane = lax.broadcasted_iota(jnp.int32, (1, every), 1)
+    every = hit_ref.shape[0]
+    local, slots = tgt.shape
+    rows = place_of(tgt[...], local, every // 2, position())
+    sub = lax.broadcasted_iota(jnp.int32, (local, slots), 0)
+    lives = jnp.zeros((local, slots), jnp.int32)
     for s in range(local):
-        rows = [place_of(tgt[s, k], local, every // 2, me) for k in range(slots)]
-        mine = [jnp.where(r < every // 2, 1, 0) for r in rows]
-        used = [jnp.where(k < live[s], 1, 0) for k in range(slots)]
-        own_count = functools.reduce(lambda p, q: p + q, [m * v for m, v in zip(mine, used)])
-        at_own, at_other = jnp.int32(0), own_count
-        for q in range(STEP):
-            plan_ref[s, live[s] + q] = 0
-            plan_ref[local + s, live[s] + q] = every
-        for k in range(slots):
-            at = jnp.where(mine[k] == 1, at_own, at_other)
-            at = jnp.where(used[k] == 1, at, slots + STEP)
-            plan_ref[s, at] = k
-            plan_ref[local + s, at] = rows[k]
-            at_own += mine[k] * used[k]
-            at_other += (1 - mine[k]) * used[k]
-        plan_ref[2 * local, s] = (live[s] + (STEP - 1)) // STEP
-        plan_ref[2 * local + 1, s] = (own_count + (STEP - 1)) // STEP
-        plan_ref[2 * local + 2, s] = own_count // STEP
-    for at in range(flags.shape[0]):
-        s, k = divmod(at, slots)
-        row = jnp.where(k < live[s], plan_ref[local + s, k], every)
-        flags[at : at + 1, :] = jnp.where(lane == row, 1.0, 0.0)
-    hit_ref[...] = jnp.transpose(flags[...]).astype(jnp.bfloat16)
+        lives = jnp.where(sub == s, live[s], lives)
+    slot = lax.broadcasted_iota(jnp.int32, (local, slots), 1)
+    key = jnp.where(slot < lives, jnp.where(rows < every // 2, 0, slots), 2 * slots) + slot
+    rank = jnp.zeros((local, slots), jnp.int32)
+    for k in range(slots):
+        rank += jnp.where(key[:, k : k + 1] < key, 1, 0)
+    lanes = plan_ref.shape[1]
+    at = lax.broadcasted_iota(jnp.int32, (local, lanes), 1)
+    wide_sub = lax.broadcasted_iota(jnp.int32, (local, lanes), 0)
+    lives = jnp.zeros((local, lanes), jnp.int32)
+    for s in range(local):
+        lives = jnp.where(wide_sub == s, live[s], lives)
+    slot_at = jnp.zeros((local, lanes), jnp.int32)
+    row_at = jnp.zeros((local, lanes), jnp.int32)
+    own_count = jnp.zeros((local, lanes), jnp.int32)
+    for k in range(slots):
+        here = rank[:, k : k + 1] == at
+        slot_at = jnp.where(here, k, slot_at)
+        row_at = jnp.where(here, rows[:, k : k + 1], row_at)
+        own_count += jnp.where(key[:, k : k + 1] < slots, 1, 0)
+    slot_at = jnp.where(at < lives, slot_at, 0)
+    row_at = jnp.where(at < lives, row_at, every)
+    shift = STEP.bit_length() - 1
+    counts = ((lives + (STEP - 1)) >> shift, (own_count + (STEP - 1)) >> shift, own_count >> shift)
+    for i, c in enumerate(counts):
+        slot_at = jnp.where(at == slots + STEP + i, c, slot_at)
+    order_ref[:local, :] = slot_at
+    order_ref[local:, :] = row_at
+    to_smem = pltpu.make_async_copy(order_ref, plan_ref, sems.at[len(copies)])
+    to_smem.start()
+    index = jnp.concatenate([row_at[s : s + 1, :slots] for s in range(local)], axis=1)
+    rows = lax.broadcasted_iota(jnp.int32, hit_ref.shape, 0)
+    hit_ref[...] = jnp.where(rows == index, 1.0, 0.0).astype(jnp.bfloat16)
+    to_smem.wait()
     build_tiles(plan_ref, 0, x_ref, lin_ref, mass_ref, own, copies[5:-1], k_ref, la_ref)
     copies[-1].wait()
 
@@ -172,7 +184,7 @@
 
 
 def add_rows(plan, span, w_ref, k_refs, done):
-    blocks, block = (plan.shape[0] - 3) // 2, w_ref.shape[1]
+    blocks, block = plan.shape[0] // 2, w_ref.shape[1]
     slots = plan.shape[1] - 2 * STEP
     for s in range(blocks):
         piece, at = place(s)
@@ -191,7 +203,7 @@
 
 
 def add_columns(plan, span, u_ref, k_refs, hit, col_ref):
-    blocks, block = (plan.shape[0] - 3) // 2, col_ref.shape[1]
+    blocks, block = plan.shape[0] // 2, col_ref.shape[1]
     slots = plan.shape[1] - 2 * STEP
     col_ref[...] = jnp.zeros_like(col_ref)
     for s in range(blocks):
@@ -220,13 +232,13 @@
 
 
 def own_span(plan):
-    local = (plan.shape[0] - 3) // 2
-    return lambda s: (0, plan[2 * local + 1, s])
+    at = plan.shape[1] - STEP
+    return lambda s: (0, plan[s, at + 1])
 
 
 def other_span(plan):
-    local = (plan.shape[0] - 3) // 2
-    return lambda s: (plan[2 * local + 2, s], plan[2 * local, s])
+    at = plan.shape[1] - STEP
+    return lambda s: (plan[s, at + 2], plan[s, at])
 
 
 def spread(w_ref, w, other):
@@ -263,19 +275,15 @@
     return t, jnp.sum(t * col, axis=0, keepdims=True)
 
 
-def finish(plan, hit_ref, factor, acc_ref, w_ref, k_refs, la_refs, send_ref, u_ref, col_ref):
+def finish(plan, hit_ref, shift, acc_ref, w_ref, k_refs, la_refs, send_ref, u_ref, col_ref, sum_ref):
     block = w_ref.shape[1]
-
-    def scale(s, acc):
+    add_rows(plan, other_span(plan), w_ref, k_refs, keep_rows(sum_ref))
+    for s in range(plan.shape[0] // 2):
         rows = pl.ds(s * block, block)
-        total = jnp.sum(acc + acc_ref[rows, :], axis=1, keepdims=True)
-        if factor is not None:
-            total = total * factor
+        total = jnp.sum(sum_ref[rows, :] + acc_ref[rows, :], axis=1, keepdims=True)
         piece, at = place(s)
         la = la_refs[piece][pl.ds(at * block, block), :]
-        u_ref[rows, :] = jnp.exp(la - F * jnp.log(total))
-
-    add_rows(plan, other_span(plan), w_ref, k_refs, scale)
+        u_ref[rows, :] = jnp.exp((la - shift) - F * jnp.log(total))
     hit = hit_ref[send_ref.shape[0] :, :]
     send_ref[...] = add_columns(plan, other_span(plan), u_ref, k_refs, hit, col_ref)
 
@@ -300,12 +308,14 @@
 def first_other(plan, hit_ref, part, sums_ref, acc_ref, *refs):
     pieces = len(PIECES)
     k_refs, la_refs = refs[:pieces], refs[pieces : 2 * pieces]
-    send_ref, u_ref, fb_ref, et_ref, tot_ref, w_ref, col_ref = refs[2 * pieces :]
+    send_ref, u_ref, fb_ref, et_ref, tot_ref, w_ref, col_ref, sum_ref = refs[2 * pieces :]
     am, bm = unpack(part, fb_ref, et_ref)
     tot = jnp.sqrt(total_of(am + sums_ref[:8, :]) * total_of(bm + sums_ref[8:, :]))
     tot_ref[...] = jnp.broadcast_to(tot, tot_ref.shape)
     spread(w_ref, jnp.where(fb_ref[...] > ABSENT, et_ref[...], 0.0), True)
-    finish(plan, hit_ref, None, acc_ref, w_ref, k_refs, la_refs, send_ref, u_ref, col_ref)
+    finish(
+        plan, hit_ref, 0.0, acc_ref, w_ref, k_refs, la_refs, send_ref, u_ref, col_ref, sum_ref
+    )
 
 
 def next_own(plan, sums, fb_ref, et_ref, *refs):
@@ -319,12 +329,15 @@
 def next_other(plan, hit_ref, sums, fb_ref, et_ref, tot_ref, mass_ref, acc_ref, *refs):
     pieces = len(PIECES)
     k_refs, la_refs = refs[:pieces], refs[pieces : 2 * pieces]
-    send_ref, u_ref, w_ref, col_ref = refs[2 * pieces :]
+    send_ref, u_ref, w_ref, col_ref, sum_ref = refs[2 * pieces :]
     t, mass = half_scale(sums, fb_ref, et_ref)
+    spread(w_ref, t * et_ref[...], True)
     mass = jnp.sum(mass + mass_ref[0:1, :], axis=1, keepdims=True)
-    factor = jnp.sqrt(tot_ref[0:1, 0:1] / mass)
-    spread(w_ref, t * et_ref[...], True)
-    finish(plan, hit_ref, factor, acc_ref, w_ref, k_refs, la_refs, send_ref, u_ref, col_ref)
+    mass = jnp.broadcast_to(mass, (1, w_ref.shape[1]))
+    shift = (F / 2) * (jnp.log(tot_ref[0:1, :]) - jnp.log(mass))
+    finish(
+        plan, hit_ref, shift, acc_ref, w_ref, k_refs, la_refs, send_ref, u_ref, col_ref, sum_ref
+    )
 
 
 def own_columns(plan, hit_ref, u_ref, *refs):
@@ -418,7 +431,7 @@
                 (tile_live, tile_tgt, src_feat, lin, amass, tile_feat),
                 (
                     *outs,
-                    SMEM((2 * local + 3, slots + 2 * STEP), jnp.int32),
+                    SMEM((2 * local, slots + 2 * STEP), jnp.int32),
                     shape(every, pairs, jnp.bfloat16),
                     shape(local * block, width, src_feat.dtype),
                     shape(local),
@@ -426,10 +439,10 @@
                 ),
                 scratch=[
                     SMEM((local,), jnp.int32),
-                    SMEM((local, slots), jnp.int32),
-                    VMEM((pairs, every), f32),
+                    VMEM((local, slots), jnp.int32),
+                    VMEM((2 * local, slots + 2 * STEP), jnp.int32),
                     feats(size),
-                    pltpu.SemaphoreType.DMA((6 + size,)),
+                    pltpu.SemaphoreType.DMA((7 + size,)),
                 ],
                 hbm=(0, 1, 2, 3, 4, 5),
                 **cost,
@@ -452,6 +465,8 @@
             part = jnp.stack([part, got], axis=0).reshape(-1, block)
             if at < len(PIECES) - 1:
                 part, following, kern[-1] = lax.optimization_barrier((part, following, kern[-1]))
+            elif at < len(PIECES):
+                part, kern[-1] = lax.optimization_barrier((part, kern[-1]))
     half = every // 2
     tall = shape(local * block)
     w = VMEM((every + 8, block), f32)
@@ -467,7 +482,7 @@
         first_other,
         (plan, hit, got, sums, acc, *kern, *la),
         (shape(half), tall, shape(half), shape(half), shape(8)),
-        scratch=[w, col],
+        scratch=[w, col, VMEM((local * block, block), f32)],
         smem=1,
     )
     for iteration in range(ITERS):
@@ -487,7 +502,7 @@
                 next_other,
                 (plan, hit, other, fb1, et1, tot, mass, acc, *kern, *la),
                 (shape(half), tall),
-                scratch=[w, col],
+                scratch=[w, col, VMEM((local * block, block), f32)],
                 smem=1,
             )
     src, tgt = call(

time: 71.9 us -> 66.1 us (0.919); the launches traced: 72.4 us -> 65.4 us
  waiting for transfers between devices: 39.7 us -> 27.8 us
  starting transfers between devices: 8.81 us -> 19.6 us
  Pallas kernels: 23 us -> 17.2 us
    ppermute x19, waiting for transfers between devices: 39.7 us -> 27.8 us  [exchange(): return lax.ppermute(x, 'src', [(i, i ^ d) for i in range(n)])]
    ppermute x19, starting transfers between devices: 8.81 us -> 19.6 us  [exchange(): return lax.ppermute(x, 'src', [(i, i ^ d) for i in range(n)])]
    pallas_call x14, Pallas kernels: 23 us -> 17.2 us  [call(): pl.pallas_call(kernel, out_shape=outs, in_specs=specs, out_specs=[pl.Bloc...]
  transfers between devices with their start and end apart: 19 -> 19, of which waited for: 16 -> 17; matrix products, arithmetic and copies ran while one was open for 0% -> 0% of each run, Pallas kernels for 19% -> 17%
where the time goes in v8:
time: 66.1 us; the launch traced here: 65.4 us
  waiting for transfers between devices  27.8 us (42%)
  starting transfers between devices  19.6 us (30%)
  Pallas kernels  17.2 us (26%)
  between operations  0.76 us (1%)
    ppermute x19, waiting for transfers between devices, exchange(): return lax.ppermute(x, 'src', [(i, i ^ d) for i in range(n)])  27.8 us
    ppermute x19, starting transfers between devices, exchange(): return lax.ppermute(x, 'src', [(i, i ^ d) for i in range(n)])  19.6 us
    pallas_call x14, Pallas kernels, call(): pl.pallas_call(kernel, out_shape=outs, in_specs=specs, out_specs=[pl.Bloc...  17.2 us
  transfers between devices with their start and end apart: 19, of which 17 were waited for; matrix products, arithmetic and copies ran while one was open for 0% of the time, Pallas kernels for 17%

profile of v8, /device:TPU:0, one launch (start us, length us, event | category | flops | bytes accessed | tf_op | source)
XLA Modules:
  0.0 65.4 jit_solution(5443145751620748203)
XLA Ops:
  0.6 0.8 %shard_map.105 = f32[24,128]{1,0:T(8,128)S(1)} custom-call(s32[8]{0:T(128)} %count_hbm.1, f32[8,128]{1,0:T(8,128)} %bitcast.28, f32[8,128]{1,0:T(8,128)} %bitcast.29, f32[8,128]{1,0:T(8,128)} %bitcast.24), custom_call_target="tpu_custom_call" | custom-call | tf_op jit(solution)/shard_map/pallas_call | solution.py:370
  1.4 3.5 %collective-permute-start = (f32[24,128]{1,0:T(8,128)S(1)}, f32[24,128]{1,0:T(8,128)S(1)}, u32[]{:S(2)}, u32[]{:S(2)}) collective-permute-start(f32[24,128]{1,0:T(8,128)S(1)} %shard_map.105), channel_id=1, source_target_pairs={{0,9},{1,8},{2,11},{3,10},{4,13},{5,12},{6,15},{7,14},{8,1},{9,0},... | collective-permute-start | bytes 36872 | tf_op jit(solution)/shard_map/ppermute | solution.py:388
  4.9 4.1 %shard_map.104 = (f32[4096,128]{1,0:T(8,128)S(1)}, f32[256,128]{1,0:T(8,128)S(1)}, bf16[3,16,128,256]{3,2,1,0:T(8,128)(2,1)S(1)}, s32[16,24]{1,0:T(8,128)S(4)}, ...) custom-call(s32[8]{0:T(128)} %live_hbm.1, ...), custom_call_target="tpu_custom_call" | custom-call | flops 268435456 | bytes 2097152 | tf_op jit(solution)/shard_map/pallas_call | solution.py:370
  9.0 0.0 collective-permute-done
  9.0 1.4 %collective-permute-start.1 = (f32[48,128]{1,0:T(8,128)S(1)}, f32[48,128]{1,0:T(8,128)S(1)}, u32[]{:S(2)}, u32[]{:S(2)}) collective-permute-start(f32[48,128]{1,0:T(8,128)S(1)} %bitcast.20), channel_id=1, source_target_pairs={{0,5},{1,4},{2,7},{3,6},{4,1},{5,0},{6,3},{7,2},{8,13},{9,12},{10,... | collective-permute-start | bytes 73736 | tf_op jit(solution)/shard_map/ppermute | solution.py:388
  10.5 2.4 %shard_map.106 = (f32[6144,128]{1,0:T(8,128)S(1)}, f32[384,128]{1,0:T(8,128)S(1)}, bf16[3,16,128,256]{3,2,1,0:T(8,128)(2,1)S(1)}) custom-call(s32[16,24]{1,0:T(8,128)S(4)} %get-tuple-element.42.plan, bf16[1024,256]{1,0:T(8,128)(2,1)S(1)} %get-tuple-element.47.x_ref, f32[8,128]{1,0:T(8,128)S(1)} %get-tuple-element.48.lin_ref, ...), custom_call_target="tpu_custom_call" | custom-call | flops 402653184 | bytes 3145728 | tf_op jit(solution)/shard_map/pallas_call | solution.py:370
  12.8 0.0 collective-permute-done.1
  12.9 1.3 %collective-permute-start.2 = (f32[96,128]{1,0:T(8,128)S(1)}, f32[96,128]{1,0:T(8,128)S(1)}, u32[]{:S(2)}, u32[]{:S(2)}) collective-permute-start(f32[96,128]{1,0:T(8,128)S(1)} %bitcast.18), channel_id=1, source_target_pairs={{0,3},{1,2},{2,1},{3,0},{4,7},{5,6},{6,5},{7,4},{8,11},{9,10},{10,... | collective-permute-start | bytes 147464 | tf_op jit(solution)/shard_map/ppermute | solution.py:388
  14.2 1.8 %shard_map.107 = (f32[6144,128]{1,0:T(8,128)S(1)}, f32[384,128]{1,0:T(8,128)S(1)}) custom-call(s32[16,24]{1,0:T(8,128)S(4)} %get-tuple-element.42.plan, bf16[1024,256]{1,0:T(8,128)(2,1)S(1)} %get-tuple-element.47.x_ref, f32[8,128]{1,0:T(8,128)S(1)} %get-tuple-element.48.lin_ref, f32[8,128]{1,0:T(8,128)S(1)} %get-tuple-element.49.mass_ref, ...), custom_call_target="tpu_custom_call" | custom-call | flops 402653184 | bytes 3145728 | tf_op jit(solution)/shard_map/pallas_call | solution.py:370
  16.0 0.7 %collective-permute-done.2 = f32[96,128]{1,0:T(8,128)S(1)} collective-permute-done((f32[96,128]{1,0:T(8,128)S(1)}, f32[96,128]{1,0:T(8,128)S(1)}, u32[]{:S(2)}, u32[]{:S(2)}) %collective-permute-start.2) | collective-permute-done | bytes 49184 | tf_op jit(solution)/shard_map/ppermute | solution.py:388
  16.7 0.2 collective-permute-start.3
  16.9 0.4 shard_map.108
  17.3 0.8 %collective-permute-done.3.part = f32[192,128]{1,0:T(8,128)S(1)} collective-permute-done((f32[192,128]{1,0:T(8,128)S(1)}, f32[192,128]{1,0:T(8,128)S(1)}, u32[]{:S(2)}, u32[]{:S(2)}) %collective-permute-start.3) | collective-permute-done | bytes 98336 | tf_op jit(solution)/shard_map/ppermute | solution.py:388
  18.1 1.4 %shard_map.109 = (f32[64,128]{1,0:T(8,128)S(1)}, f32[1024,128]{1,0:T(8,128)S(1)}, f32[64,128]{1,0:T(8,128)S(1)}, f32[64,128]{1,0:T(8,128)S(1)}, f32[8,128]{1,0:T(8,128)S(1)}) custom-call(s32[16,24]{1,0:T(8,128)S(4)} %get-tuple-element.42.plan, bf16[128,128]{1,0:T(8,128)(2,1)S(1)} %get-tuple-element.43.hit_ref, f32[192,128]{1,0:T(8,128)S(1)} %collective-permute-done.3.part, ...), custom_call_target="tpu_custom_call" | custom-call | tf_op jit(solution)/shard_map/pallas_call | solution.py:370
  19.5 0.3 collective-permute-start.4
  19.8 0.6 shard_map.110
  20.4 0.4 collective-permute-done.4
  20.8 1.3 %collective-permute-start.5 = (f32[64,128]{1,0:T(8,128)S(1)}, f32[64,128]{1,0:T(8,128)S(1)}, u32[]{:S(2)}, u32[]{:S(2)}) collective-permute-start(f32[64,128]{1,0:T(8,128)S(1)} %add.36), channel_id=1, source_target_pairs={{0,3},{1,2},{2,1},{3,0},{4,7},{5,6},{6,5},{7,4},{8,11},{9,10},{10,... | collective-permute-start | bytes 98312 | tf_op jit(solution)/shard_map/ppermute | solution.py:388
  22.1 2.0 %collective-permute-done.5 = f32[64,128]{1,0:T(8,128)S(1)} collective-permute-done((f32[64,128]{1,0:T(8,128)S(1)}, f32[64,128]{1,0:T(8,128)S(1)}, u32[]{:S(2)}, u32[]{:S(2)}) %collective-permute-start.5) | collective-permute-done | bytes 32800 | tf_op jit(solution)/shard_map/ppermute | solution.py:388
  24.1 1.1 %collective-permute-start.6 = (f32[64,128]{1,0:T(8,128)S(1)}, f32[64,128]{1,0:T(8,128)S(1)}, u32[]{:S(2)}, u32[]{:S(2)}) collective-permute-start(f32[64,128]{1,0:T(8,128)S(1)} %add.37), channel_id=1, source_target_pairs={{0,5},{1,4},{2,7},{3,6},{4,1},{5,0},{6,3},{7,2},{8,13},{9,12},{10,... | collective-permute-start | bytes 98312 | tf_op jit(solution)/shard_map/ppermute | solution.py:388
  25.2 2.3 %collective-permute-done.6 = f32[64,128]{1,0:T(8,128)S(1)} collective-permute-done((f32[64,128]{1,0:T(8,128)S(1)}, f32[64,128]{1,0:T(8,128)S(1)}, u32[]{:S(2)}, u32[]{:S(2)}) %collective-permute-start.6) | collective-permute-done | bytes 32800 | tf_op jit(solution)/shard_map/ppermute | solution.py:388
  27.5 0.7 %collective-permute-start.7 = (f32[64,128]{1,0:T(8,128)S(1)}, f32[64,128]{1,0:T(8,128)S(1)}, u32[]{:S(2)}, u32[]{:S(2)}) collective-permute-start(f32[64,128]{1,0:T(8,128)S(1)} %add.38), channel_id=1, source_target_pairs={{0,9},{1,8},{2,11},{3,10},{4,13},{5,12},{6,15},{7,14},{8,1},{9,0},... | collective-permute-start | bytes 98312 | tf_op jit(solution)/shard_map/ppermute | solution.py:388
  28.1 3.5 %collective-permute-done.7 = f32[64,128]{1,0:T(8,128)S(1)} collective-permute-done((f32[64,128]{1,0:T(8,128)S(1)}, f32[64,128]{1,0:T(8,128)S(1)}, u32[]{:S(2)}, u32[]{:S(2)}) %collective-permute-start.7) | collective-permute-done | bytes 32800 | tf_op jit(solution)/shard_map/ppermute | solution.py:388
  31.7 0.2 collective-permute-start.8
  31.9 0.4 shard_map.111
  32.3 0.6 collective-permute-done.8.sums
  32.9 1.4 %shard_map.112 = (f32[64,128]{1,0:T(8,128)S(1)}, f32[1024,128]{1,0:T(8,128)S(1)}) custom-call(s32[16,24]{1,0:T(8,128)S(4)} %get-tuple-element.42.plan, bf16[128,128]{1,0:T(8,128)(2,1)S(1)} %get-tuple-element.43.hit_ref, f32[64,128]{1,0:T(8,128)S(1)} %collective-permute-done.8.sums, f32[64,128]{1,0:T(8,128)S(1)} %get-tuple-element.67.fb_ref.fb1, ...), custom_call_target="tpu_custom_call" | custom-call | tf_op jit(solution)/shard_map/pallas_call | solution.py:370
  34.4 0.3 collective-permute-start.9
  34.7 0.6 shard_map.113
  35.3 0.3 collective-permute-done.9
  35.6 1.9 %collective-permute-start.10 = (f32[64,128]{1,0:T(8,128)S(1)}, f32[64,128]{1,0:T(8,128)S(1)}, u32[]{:S(2)}, u32[]{:S(2)}) collective-permute-start(f32[64,128]{1,0:T(8,128)S(1)} %add.40), channel_id=1, source_target_pairs={{0,3},{1,2},{2,1},{3,0},{4,7},{5,6},{6,5},{7,4},{8,11},{9,10},{10,... | collective-permute-start | bytes 98312 | tf_op jit(solution)/shard_map/ppermute | solution.py:388
  37.5 1.6 %collective-permute-done.10 = f32[64,128]{1,0:T(8,128)S(1)} collective-permute-done((f32[64,128]{1,0:T(8,128)S(1)}, f32[64,128]{1,0:T(8,128)S(1)}, u32[]{:S(2)}, u32[]{:S(2)}) %collective-permute-start.10) | collective-permute-done | bytes 32800 | tf_op jit(solution)/shard_map/ppermute | solution.py:388
  39.1 1.0 %collective-permute-start.11 = (f32[64,128]{1,0:T(8,128)S(1)}, f32[64,128]{1,0:T(8,128)S(1)}, u32[]{:S(2)}, u32[]{:S(2)}) collective-permute-start(f32[64,128]{1,0:T(8,128)S(1)} %add.41), channel_id=1, source_target_pairs={{0,5},{1,4},{2,7},{3,6},{4,1},{5,0},{6,3},{7,2},{8,13},{9,12},{10,... | collective-permute-start | bytes 98312 | tf_op jit(solution)/shard_map/ppermute | solution.py:388
  40.1 2.4 %collective-permute-done.11 = f32[64,128]{1,0:T(8,128)S(1)} collective-permute-done((f32[64,128]{1,0:T(8,128)S(1)}, f32[64,128]{1,0:T(8,128)S(1)}, u32[]{:S(2)}, u32[]{:S(2)}) %collective-permute-start.11) | collective-permute-done | bytes 32800 | tf_op jit(solution)/shard_map/ppermute | solution.py:388
  42.5 1.4 %collective-permute-start.12 = (f32[64,128]{1,0:T(8,128)S(1)}, f32[64,128]{1,0:T(8,128)S(1)}, u32[]{:S(2)}, u32[]{:S(2)}) collective-permute-start(f32[64,128]{1,0:T(8,128)S(1)} %add.42), channel_id=1, source_target_pairs={{0,9},{1,8},{2,11},{3,10},{4,13},{5,12},{6,15},{7,14},{8,1},{9,0},... | collective-permute-start | bytes 98312 | tf_op jit(solution)/shard_map/ppermute | solution.py:388
  43.9 2.9 %collective-permute-done.12 = f32[64,128]{1,0:T(8,128)S(1)} collective-permute-done((f32[64,128]{1,0:T(8,128)S(1)}, f32[64,128]{1,0:T(8,128)S(1)}, u32[]{:S(2)}, u32[]{:S(2)}) %collective-permute-start.12) | collective-permute-done | bytes 32800 | tf_op jit(solution)/shard_map/ppermute | solution.py:388
  46.7 1.0 %collective-permute-start.13 = (f32[64,128]{1,0:T(8,128)S(1)}, f32[64,128]{1,0:T(8,128)S(1)}, u32[]{:S(2)}, u32[]{:S(2)}) collective-permute-start(f32[64,128]{1,0:T(8,128)S(1)} %add.43.sums), channel_id=1, source_target_pairs={{0,1},{1,0},{2,3},{3,2},{4,5},{5,4},{6,7},{7,6},{8,9},{9,8},{10,11... | collective-permute-start | bytes 98312 | tf_op jit(solution)/shard_map/ppermute | solution.py:388
  47.8 0.4 shard_map.114
  48.2 0.4 collective-permute-done.13.sums
  48.6 1.4 %shard_map.115 = (f32[64,128]{1,0:T(8,128)S(1)}, f32[1024,128]{1,0:T(8,128)S(1)}) custom-call(s32[16,24]{1,0:T(8,128)S(4)} %get-tuple-element.42.plan, bf16[128,128]{1,0:T(8,128)(2,1)S(1)} %get-tuple-element.43.hit_ref, f32[64,128]{1,0:T(8,128)S(1)} %collective-permute-done.13.sums, f32[64,128]{1,0:T(8,128)S(1)} %get-tuple-element.67.fb_ref.fb1, ...), custom_call_target="tpu_custom_call" | custom-call | tf_op jit(solution)/shard_map/pallas_call | solution.py:370
  50.1 0.5 collective-permute-start.14
  50.6 0.6 shard_map.116
  51.2 0.3 collective-permute-done.14
  51.4 1.9 %collective-permute-start.15 = (f32[64,128]{1,0:T(8,128)S(1)}, f32[64,128]{1,0:T(8,128)S(1)}, u32[]{:S(2)}, u32[]{:S(2)}) collective-permute-start(f32[64,128]{1,0:T(8,128)S(1)} %add.44), channel_id=1, source_target_pairs={{0,3},{1,2},{2,1},{3,0},{4,7},{5,6},{6,5},{7,4},{8,11},{9,10},{10,... | collective-permute-start | bytes 98312 | tf_op jit(solution)/shard_map/ppermute | solution.py:388
  53.4 1.6 %collective-permute-done.15 = f32[64,128]{1,0:T(8,128)S(1)} collective-permute-done((f32[64,128]{1,0:T(8,128)S(1)}, f32[64,128]{1,0:T(8,128)S(1)}, u32[]{:S(2)}, u32[]{:S(2)}) %collective-permute-start.15) | collective-permute-done | bytes 32800 | tf_op jit(solution)/shard_map/ppermute | solution.py:388
  55.0 0.2 collective-permute-start.16
  55.2 3.2 %collective-permute-done.16 = f32[64,128]{1,0:T(8,128)S(1)} collective-permute-done((f32[64,128]{1,0:T(8,128)S(1)}, f32[64,128]{1,0:T(8,128)S(1)}, u32[]{:S(2)}, u32[]{:S(2)}) %collective-permute-start.16) | collective-permute-done | bytes 32800 | tf_op jit(solution)/shard_map/ppermute | solution.py:388
  58.3 1.2 %collective-permute-start.17 = (f32[64,128]{1,0:T(8,128)S(1)}, f32[64,128]{1,0:T(8,128)S(1)}, u32[]{:S(2)}, u32[]{:S(2)}) collective-permute-start(f32[64,128]{1,0:T(8,128)S(1)} %add.46), channel_id=1, source_target_pairs={{0,9},{1,8},{2,11},{3,10},{4,13},{5,12},{6,15},{7,14},{8,1},{9,0},... | collective-permute-start | bytes 98312 | tf_op jit(solution)/shard_map/ppermute | solution.py:388
  59.6 3.8 %collective-permute-done.17 = f32[64,128]{1,0:T(8,128)S(1)} collective-permute-done((f32[64,128]{1,0:T(8,128)S(1)}, f32[64,128]{1,0:T(8,128)S(1)}, u32[]{:S(2)}, u32[]{:S(2)}) %collective-permute-start.17) | collective-permute-done | bytes 32800 | tf_op jit(solution)/shard_map/ppermute | solution.py:388
  63.3 0.1 collective-permute-start.18
  63.4 1.1 %collective-permute-done.18.other = f32[64,128]{1,0:T(8,128)S(1)} collective-permute-done((f32[64,128]{1,0:T(8,128)S(1)}, f32[64,128]{1,0:T(8,128)S(1)}, u32[]{:S(2)}, u32[]{:S(2)}) %collective-permute-start.18) | collective-permute-done | bytes 32800 | tf_op jit(solution)/shard_map/ppermute | solution.py:388
  64.5 0.8 %shard_map.117 = (f32[8,128]{1,0:T(8,128)}, f32[8,128]{1,0:T(8,128)}) custom-call(f32[64,128]{1,0:T(8,128)S(1)} %add.47.keep, f32[64,128]{1,0:T(8,128)S(1)} %collective-permute-done.18.other, f32[64,128]{1,0:T(8,128)S(1)} %get-tuple-element.70.fb_ref.fb0, f32[64,128]{1,0:T(8,128)S(1)} %get-tuple-element.71.et_ref.et0, ...), custom_call_target="tpu_custom_call" | custom-call | tf_op jit(solution)/shard_map/pallas_call | solution.py:370
  (15 shorter events, 0.1 us)
Async XLA Ops:
  1.4 7.6 %collective-permute-start = (f32[24,128]{1,0:T(8,128)S(1)}, f32[24,128]{1,0:T(8,128)S(1)}, u32[]{:S(2)}, u32[]{:S(2)}) collective-permute-start(f32[24,128]{1,0:T(8,128)S(1)} %shard_map.105), channel_id=1, source_target_pairs={{0,9},{1,8},{2,11},{3,10},{4,13},{5,12},{6,15},{7,14},{8,1},{9,0},... | collective-permute-start | bytes 36872 | tf_op jit(solution)/shard_map/ppermute | solution.py:388
  9.0 3.8 %collective-permute-start.1 = (f32[48,128]{1,0:T(8,128)S(1)}, f32[48,128]{1,0:T(8,128)S(1)}, u32[]{:S(2)}, u32[]{:S(2)}) collective-permute-start(f32[48,128]{1,0:T(8,128)S(1)} %bitcast.20), channel_id=1, source_target_pairs={{0,5},{1,4},{2,7},{3,6},{4,1},{5,0},{6,3},{7,2},{8,13},{9,12},{10,... | collective-permute-start | bytes 73736 | tf_op jit(solution)/shard_map/ppermute | solution.py:388
  12.9 3.8 %collective-permute-start.2 = (f32[96,128]{1,0:T(8,128)S(1)}, f32[96,128]{1,0:T(8,128)S(1)}, u32[]{:S(2)}, u32[]{:S(2)}) collective-permute-start(f32[96,128]{1,0:T(8,128)S(1)} %bitcast.18), channel_id=1, source_target_pairs={{0,3},{1,2},{2,1},{3,0},{4,7},{5,6},{6,5},{7,4},{8,11},{9,10},{10,... | collective-permute-start | bytes 147464 | tf_op jit(solution)/shard_map/ppermute | solution.py:388
  16.7 1.4 %collective-permute-start.3 = (f32[192,128]{1,0:T(8,128)S(1)}, f32[192,128]{1,0:T(8,128)S(1)}, u32[]{:S(2)}, u32[]{:S(2)}) collective-permute-start(f32[192,128]{1,0:T(8,128)S(1)} %bitcast.15), channel_id=1, source_target_pairs={{0,1},{1,0},{2,3},{3,2},{4,5},{5,4},{6,7},{7,6},{8,9},{9,8},{10,11... | collective-permute-start | bytes 294920 | tf_op jit(solution)/shard_map/ppermute | solution.py:388
  19.5 1.3 %collective-permute-start.4 = (f32[64,128]{1,0:T(8,128)S(1)}, f32[64,128]{1,0:T(8,128)S(1)}, u32[]{:S(2)}, u32[]{:S(2)}) collective-permute-start(f32[64,128]{1,0:T(8,128)S(1)} %get-tuple-element.66), channel_id=1, source_target_pairs={{0,1},{1,0},{2,3},{3,2},{4,5},{5,4},{6,7},{7,6},{8,9},{9,8},{10,11... | collective-permute-start | bytes 98312 | tf_op jit(solution)/shard_map/ppermute | solution.py:388
  20.8 3.3 %collective-permute-start.5 = (f32[64,128]{1,0:T(8,128)S(1)}, f32[64,128]{1,0:T(8,128)S(1)}, u32[]{:S(2)}, u32[]{:S(2)}) collective-permute-start(f32[64,128]{1,0:T(8,128)S(1)} %add.36), channel_id=1, source_target_pairs={{0,3},{1,2},{2,1},{3,0},{4,7},{5,6},{6,5},{7,4},{8,11},{9,10},{10,... | collective-permute-start | bytes 98312 | tf_op jit(solution)/shard_map/ppermute | solution.py:388
  24.1 3.3 %collective-permute-start.6 = (f32[64,128]{1,0:T(8,128)S(1)}, f32[64,128]{1,0:T(8,128)S(1)}, u32[]{:S(2)}, u32[]{:S(2)}) collective-permute-start(f32[64,128]{1,0:T(8,128)S(1)} %add.37), channel_id=1, source_target_pairs={{0,5},{1,4},{2,7},{3,6},{4,1},{5,0},{6,3},{7,2},{8,13},{9,12},{10,... | collective-permute-start | bytes 98312 | tf_op jit(solution)/shard_map/ppermute | solution.py:388
  27.5 4.2 %collective-permute-start.7 = (f32[64,128]{1,0:T(8,128)S(1)}, f32[64,128]{1,0:T(8,128)S(1)}, u32[]{:S(2)}, u32[]{:S(2)}) collective-permute-start(f32[64,128]{1,0:T(8,128)S(1)} %add.38), channel_id=1, source_target_pairs={{0,9},{1,8},{2,11},{3,10},{4,13},{5,12},{6,15},{7,14},{8,1},{9,0},... | collective-permute-start | bytes 98312 | tf_op jit(solution)/shard_map/ppermute | solution.py:388
  31.7 1.2 %collective-permute-start.8 = (f32[64,128]{1,0:T(8,128)S(1)}, f32[64,128]{1,0:T(8,128)S(1)}, u32[]{:S(2)}, u32[]{:S(2)}) collective-permute-start(f32[64,128]{1,0:T(8,128)S(1)} %add.39.sums), channel_id=1, source_target_pairs={{0,1},{1,0},{2,3},{3,2},{4,5},{5,4},{6,7},{7,6},{8,9},{9,8},{10,11... | collective-permute-start | bytes 98312 | tf_op jit(solution)/shard_map/ppermute | solution.py:388
  34.4 1.3 %collective-permute-start.9 = (f32[64,128]{1,0:T(8,128)S(1)}, f32[64,128]{1,0:T(8,128)S(1)}, u32[]{:S(2)}, u32[]{:S(2)}) collective-permute-start(f32[64,128]{1,0:T(8,128)S(1)} %get-tuple-element.75), channel_id=1, source_target_pairs={{0,1},{1,0},{2,3},{3,2},{4,5},{5,4},{6,7},{7,6},{8,9},{9,8},{10,11... | collective-permute-start | bytes 98312 | tf_op jit(solution)/shard_map/ppermute | solution.py:388
  35.6 3.5 %collective-permute-start.10 = (f32[64,128]{1,0:T(8,128)S(1)}, f32[64,128]{1,0:T(8,128)S(1)}, u32[]{:S(2)}, u32[]{:S(2)}) collective-permute-start(f32[64,128]{1,0:T(8,128)S(1)} %add.40), channel_id=1, source_target_pairs={{0,3},{1,2},{2,1},{3,0},{4,7},{5,6},{6,5},{7,4},{8,11},{9,10},{10,... | collective-permute-start | bytes 98312 | tf_op jit(solution)/shard_map/ppermute | solution.py:388
  39.1 3.3 %collective-permute-start.11 = (f32[64,128]{1,0:T(8,128)S(1)}, f32[64,128]{1,0:T(8,128)S(1)}, u32[]{:S(2)}, u32[]{:S(2)}) collective-permute-start(f32[64,128]{1,0:T(8,128)S(1)} %add.41), channel_id=1, source_target_pairs={{0,5},{1,4},{2,7},{3,6},{4,1},{5,0},{6,3},{7,2},{8,13},{9,12},{10,... | collective-permute-start | bytes 98312 | tf_op jit(solution)/shard_map/ppermute | solution.py:388
  42.5 4.2 %collective-permute-start.12 = (f32[64,128]{1,0:T(8,128)S(1)}, f32[64,128]{1,0:T(8,128)S(1)}, u32[]{:S(2)}, u32[]{:S(2)}) collective-permute-start(f32[64,128]{1,0:T(8,128)S(1)} %add.42), channel_id=1, source_target_pairs={{0,9},{1,8},{2,11},{3,10},{4,13},{5,12},{6,15},{7,14},{8,1},{9,0},... | collective-permute-start | bytes 98312 | tf_op jit(solution)/shard_map/ppermute | solution.py:388
  46.7 1.9 %collective-permute-start.13 = (f32[64,128]{1,0:T(8,128)S(1)}, f32[64,128]{1,0:T(8,128)S(1)}, u32[]{:S(2)}, u32[]{:S(2)}) collective-permute-start(f32[64,128]{1,0:T(8,128)S(1)} %add.43.sums), channel_id=1, source_target_pairs={{0,1},{1,0},{2,3},{3,2},{4,5},{5,4},{6,7},{7,6},{8,9},{9,8},{10,11... | collective-permute-start | bytes 98312 | tf_op jit(solution)/shard_map/ppermute | solution.py:388
  50.1 1.3 %collective-permute-start.14 = (f32[64,128]{1,0:T(8,128)S(1)}, f32[64,128]{1,0:T(8,128)S(1)}, u32[]{:S(2)}, u32[]{:S(2)}) collective-permute-start(f32[64,128]{1,0:T(8,128)S(1)} %get-tuple-element.79), channel_id=1, source_target_pairs={{0,1},{1,0},{2,3},{3,2},{4,5},{5,4},{6,7},{7,6},{8,9},{9,8},{10,11... | collective-permute-start | bytes 98312 | tf_op jit(solution)/shard_map/ppermute | solution.py:388
  51.4 3.5 %collective-permute-start.15 = (f32[64,128]{1,0:T(8,128)S(1)}, f32[64,128]{1,0:T(8,128)S(1)}, u32[]{:S(2)}, u32[]{:S(2)}) collective-permute-start(f32[64,128]{1,0:T(8,128)S(1)} %add.44), channel_id=1, source_target_pairs={{0,3},{1,2},{2,1},{3,0},{4,7},{5,6},{6,5},{7,4},{8,11},{9,10},{10,... | collective-permute-start | bytes 98312 | tf_op jit(solution)/shard_map/ppermute | solution.py:388
  55.0 3.3 %collective-permute-start.16 = (f32[64,128]{1,0:T(8,128)S(1)}, f32[64,128]{1,0:T(8,128)S(1)}, u32[]{:S(2)}, u32[]{:S(2)}) collective-permute-start(f32[64,128]{1,0:T(8,128)S(1)} %add.45), channel_id=1, source_target_pairs={{0,5},{1,4},{2,7},{3,6},{4,1},{5,0},{6,3},{7,2},{8,13},{9,12},{10,... | collective-permute-start | bytes 98312 | tf_op jit(solution)/shard_map/ppermute | solution.py:388
  58.3 5.0 %collective-permute-start.17 = (f32[64,128]{1,0:T(8,128)S(1)}, f32[64,128]{1,0:T(8,128)S(1)}, u32[]{:S(2)}, u32[]{:S(2)}) collective-permute-start(f32[64,128]{1,0:T(8,128)S(1)} %add.46), channel_id=1, source_target_pairs={{0,9},{1,8},{2,11},{3,10},{4,13},{5,12},{6,15},{7,14},{8,1},{9,0},... | collective-permute-start | bytes 98312 | tf_op jit(solution)/shard_map/ppermute | solution.py:388
  63.3 1.2 %collective-permute-start.18 = (f32[64,128]{1,0:T(8,128)S(1)}, f32[64,128]{1,0:T(8,128)S(1)}, u32[]{:S(2)}, u32[]{:S(2)}) collective-permute-start(f32[64,128]{1,0:T(8,128)S(1)} %add.47.keep), channel_id=1, source_target_pairs={{0,1},{1,0},{2,3},{3,2},{4,5},{5,4},{6,7},{7,6},{8,9},{9,8},{10,11... | collective-permute-start | bytes 98312 | tf_op jit(solution)/shard_map/ppermute | solution.py:388

commit v9 on v8

--- a/solution.py
+++ b/solution.py
@@ -183,7 +183,7 @@
     return piece, s
 
 
-def add_rows(plan, span, w_ref, k_refs, done):
+def add_rows(plan, span, w_ref, k_refs, out_ref, from_ref=None):
     blocks, block = plan.shape[0] // 2, w_ref.shape[1]
     slots = plan.shape[1] - 2 * STEP
     for s in range(blocks):
@@ -199,7 +199,9 @@
             return acc
 
         first, last = span(s)
-        done(s, lax.fori_loop(first, last, add_row, jnp.zeros((block, block), jnp.float32)))
+        rows = slice(s * block, (s + 1) * block)
+        acc = jnp.zeros((block, block), jnp.float32) if from_ref is None else from_ref[rows, :]
+        out_ref[rows, :] = lax.fori_loop(first, last, add_row, acc)
 
 
 def add_columns(plan, span, u_ref, k_refs, hit, col_ref):
@@ -277,10 +279,10 @@
 
 def finish(plan, hit_ref, shift, acc_ref, w_ref, k_refs, la_refs, send_ref, u_ref, col_ref, sum_ref):
     block = w_ref.shape[1]
-    add_rows(plan, other_span(plan), w_ref, k_refs, keep_rows(sum_ref))
+    add_rows(plan, other_span(plan), w_ref, k_refs, sum_ref, acc_ref)
     for s in range(plan.shape[0] // 2):
         rows = pl.ds(s * block, block)
-        total = jnp.sum(sum_ref[rows, :] + acc_ref[rows, :], axis=1, keepdims=True)
+        total = jnp.sum(sum_ref[rows, :], axis=1, keepdims=True)
         piece, at = place(s)
         la = la_refs[piece][pl.ds(at * block, block), :]
         u_ref[rows, :] = jnp.exp((la - shift) - F * jnp.log(total))
@@ -288,21 +290,12 @@
     send_ref[...] = add_columns(plan, other_span(plan), u_ref, k_refs, hit, col_ref)
 
 
-def keep_rows(acc_ref):
-    block = acc_ref.shape[1]
-
-    def keep(s, acc):
-        acc_ref[s * block : (s + 1) * block, :] = acc
-
-    return keep
-
-
 def first_own(plan, part, *refs):
     k_refs, (acc_ref, fb_ref, et_ref, sums_ref, w_ref) = refs[:-5], refs[-5:]
     am, bm = unpack(part, fb_ref, et_ref)
     sums_ref[:8, :], sums_ref[8:, :] = am, bm
     spread(w_ref, jnp.where(fb_ref[...] > ABSENT, et_ref[...], 0.0), False)
-    add_rows(plan, own_span(plan), w_ref, k_refs, keep_rows(acc_ref))
+    add_rows(plan, own_span(plan), w_ref, k_refs, acc_ref)
 
 
 def first_other(plan, hit_ref, part, sums_ref, acc_ref, *refs):
@@ -323,7 +316,7 @@
     t, mass = half_scale(sums, fb_ref, et_ref)
     mass_ref[...] = jnp.broadcast_to(mass, mass_ref.shape)
     spread(w_ref, t * et_ref[...], False)
-    add_rows(plan, own_span(plan), w_ref, k_refs, keep_rows(acc_ref))
+    add_rows(plan, own_span(plan), w_ref, k_refs, acc_ref)
 
 
 def next_other(plan, hit_ref, sums, fb_ref, et_ref, tot_ref, mass_ref, acc_ref, *refs):
@@ -346,17 +339,22 @@
     keep_ref[...] = add_columns(plan, own_span(plan), u_ref, k_refs, hit, col_ref)
 
 
-def last_kernel(keep, other, fb0, et0, fb1, et1, tot_ref, u_ref, src_ref, tgt_ref, t_ref):
+def last_own(keep, fb_ref, et_ref, u_ref, src_ref, tgt_ref, mass_ref, t_ref):
     local, block = src_ref.shape
-    t, mass = half_scale(keep, fb0, et0)
+    t, mass = half_scale(keep, fb_ref, et_ref)
+    mass_ref[...] = jnp.broadcast_to(mass, mass_ref.shape)
     t_ref[...] = t
-    mass += half_scale(other, fb1, et1)[1]
-    factor = jnp.sqrt(tot_ref[0:1, 0:1] / jnp.sum(mass, axis=1, keepdims=True))
-    own = pl.multiple_of((position() >> 1) * local, local)
-    tgt_ref[...] = t_ref[pl.ds(own, local), :] * factor
+    tgt_ref[...] = t_ref[pl.ds(pl.multiple_of((position() >> 1) * local, local), local), :]
     mask = diag_mask(block)
     for s in range(local):
-        src_ref[s : s + 1, :] = to_row(u_ref[s * block : (s + 1) * block, :] * factor, mask)
+        src_ref[s : s + 1, :] = to_row(u_ref[s * block : (s + 1) * block, :], mask)
+
+
+def last_other(other, fb_ref, et_ref, tot_ref, mass_ref, src, tgt, src_ref, tgt_ref):
+    mass = half_scale(other, fb_ref, et_ref)[1] + mass_ref[0:1, :]
+    factor = jnp.sqrt(tot_ref[0:1, 0:1] / jnp.sum(mass, axis=1, keepdims=True))
+    src_ref[...] = src[...] * factor
+    tgt_ref[...] = tgt[...] * factor
 
 
 def call(kernel, ins, outs, scratch=(), smem=0, hbm=(), vmem_mb=12, **cost):
@@ -505,11 +503,16 @@
                 scratch=[w, col, VMEM((local * block, block), f32)],
                 smem=1,
             )
+    src, tgt, mass = call(
+        last_own,
+        (keep, fb0, et0, u),
+        (shape(local), shape(local), shape(8)),
+        scratch=[VMEM((half, block), f32)],
+    )
     src, tgt = call(
-        last_kernel,
-        (keep, other, fb0, et0, fb1, et1, tot, u),
+        last_other,
+        (other, fb1, et1, tot, mass, src, tgt),
         [jax.ShapeDtypeStruct((local, block), f32)] * 2,
-        scratch=[VMEM((half, block), f32)],
     )
     return (src.reshape(-1), tgt.reshape(-1))
 

time: 66.1 us -> 66.3 us (level)
  waiting for transfers between devices: 27.8 us -> 30 us
  starting transfers between devices: 19.6 us -> 18.5 us
  Pallas kernels: 17.2 us -> 16.3 us
    ppermute x19, waiting for transfers between devices: 27.8 us -> 30 us  [exchange(): return lax.ppermute(x, 'src', [(i, i ^ d) for i in range(n)])]
    ppermute x19, starting transfers between devices: 19.6 us -> 18.5 us  [exchange(): return lax.ppermute(x, 'src', [(i, i ^ d) for i in range(n)])]
    pallas_call x14 -> x15, Pallas kernels: 17.2 us -> 16.3 us  [call(): pl.pallas_call(kernel, out_shape=outs, in_specs=specs, out_specs=[pl.Bloc...]
  transfers between devices with their start and end apart: 19 -> 19, of which waited for: 17 -> 16; matrix products, arithmetic and copies ran while one was open for 0% -> 0% of each run, Pallas kernels for 17% -> 16%
where the time goes in v9:
time: 66.3 us; the launch traced here: 65.6 us
  waiting for transfers between devices  30 us (45%)
  starting transfers between devices  18.5 us (28%)
  Pallas kernels  16.3 us (25%)
  between operations  0.77 us (1%)
    ppermute x19, waiting for transfers between devices, exchange(): return lax.ppermute(x, 'src', [(i, i ^ d) for i in range(n)])  30 us
    ppermute x19, starting transfers between devices, exchange(): return lax.ppermute(x, 'src', [(i, i ^ d) for i in range(n)])  18.5 us
    pallas_call x15, Pallas kernels, call(): pl.pallas_call(kernel, out_shape=outs, in_specs=specs, out_specs=[pl.Bloc...  16.3 us
  transfers between devices with their start and end apart: 19, of which 16 were waited for; matrix products, arithmetic and copies ran while one was open for 0% of the time, Pallas kernels for 16%

profile of v9, /device:TPU:0, one launch (start us, length us, event | category | flops | bytes accessed | tf_op | source)
XLA Modules:
  0.0 65.6 jit_solution(14393549653018302960)
XLA Ops:
  0.6 0.8 %shard_map.105 = f32[24,128]{1,0:T(8,128)S(1)} custom-call(s32[8]{0:T(128)} %count_hbm.1, f32[8,128]{1,0:T(8,128)} %bitcast.28, f32[8,128]{1,0:T(8,128)} %bitcast.29, f32[8,128]{1,0:T(8,128)} %bitcast.24), custom_call_target="tpu_custom_call" | custom-call | tf_op jit(solution)/shard_map/pallas_call | solution.py:368
  1.4 3.5 %collective-permute-start = (f32[24,128]{1,0:T(8,128)S(1)}, f32[24,128]{1,0:T(8,128)S(1)}, u32[]{:S(2)}, u32[]{:S(2)}) collective-permute-start(f32[24,128]{1,0:T(8,128)S(1)} %shard_map.105), channel_id=1, source_target_pairs={{0,9},{1,8},{2,11},{3,10},{4,13},{5,12},{6,15},{7,14},{8,1},{9,0},... | collective-permute-start | bytes 36872 | tf_op jit(solution)/shard_map/ppermute | solution.py:386
  4.9 3.8 %shard_map.104 = (f32[4096,128]{1,0:T(8,128)S(1)}, f32[256,128]{1,0:T(8,128)S(1)}, bf16[3,16,128,256]{3,2,1,0:T(8,128)(2,1)S(1)}, s32[16,24]{1,0:T(8,128)S(4)}, ...) custom-call(s32[8]{0:T(128)} %live_hbm.1, ...), custom_call_target="tpu_custom_call" | custom-call | flops 268435456 | bytes 2097152 | tf_op jit(solution)/shard_map/pallas_call | solution.py:368
  8.8 0.0 collective-permute-done
  8.8 2.2 %collective-permute-start.1 = (f32[48,128]{1,0:T(8,128)S(1)}, f32[48,128]{1,0:T(8,128)S(1)}, u32[]{:S(2)}, u32[]{:S(2)}) collective-permute-start(f32[48,128]{1,0:T(8,128)S(1)} %bitcast.20), channel_id=1, source_target_pairs={{0,5},{1,4},{2,7},{3,6},{4,1},{5,0},{6,3},{7,2},{8,13},{9,12},{10,... | collective-permute-start | bytes 73736 | tf_op jit(solution)/shard_map/ppermute | solution.py:386
  11.0 1.9 %shard_map.106 = (f32[6144,128]{1,0:T(8,128)S(1)}, f32[384,128]{1,0:T(8,128)S(1)}, bf16[3,16,128,256]{3,2,1,0:T(8,128)(2,1)S(1)}) custom-call(s32[16,24]{1,0:T(8,128)S(4)} %get-tuple-element.45.plan, bf16[1024,256]{1,0:T(8,128)(2,1)S(1)} %get-tuple-element.50.x_ref, f32[8,128]{1,0:T(8,128)S(1)} %get-tuple-element.51.lin_ref, ...), custom_call_target="tpu_custom_call" | custom-call | flops 402653184 | bytes 3145728 | tf_op jit(solution)/shard_map/pallas_call | solution.py:368
  12.9 0.0 collective-permute-done.1
  12.9 1.5 %collective-permute-start.2 = (f32[96,128]{1,0:T(8,128)S(1)}, f32[96,128]{1,0:T(8,128)S(1)}, u32[]{:S(2)}, u32[]{:S(2)}) collective-permute-start(f32[96,128]{1,0:T(8,128)S(1)} %bitcast.18), channel_id=1, source_target_pairs={{0,3},{1,2},{2,1},{3,0},{4,7},{5,6},{6,5},{7,4},{8,11},{9,10},{10,... | collective-permute-start | bytes 147464 | tf_op jit(solution)/shard_map/ppermute | solution.py:386
  14.4 2.1 %shard_map.107 = (f32[6144,128]{1,0:T(8,128)S(1)}, f32[384,128]{1,0:T(8,128)S(1)}) custom-call(s32[16,24]{1,0:T(8,128)S(4)} %get-tuple-element.45.plan, bf16[1024,256]{1,0:T(8,128)(2,1)S(1)} %get-tuple-element.50.x_ref, f32[8,128]{1,0:T(8,128)S(1)} %get-tuple-element.51.lin_ref, f32[8,128]{1,0:T(8,128)S(1)} %get-tuple-element.52.mass_ref, ...), custom_call_target="tpu_custom_call" | custom-call | flops 402653184 | bytes 3145728 | tf_op jit(solution)/shard_map/pallas_call | solution.py:368
  16.5 0.0 collective-permute-done.2
  16.5 1.0 %collective-permute-start.3 = (f32[192,128]{1,0:T(8,128)S(1)}, f32[192,128]{1,0:T(8,128)S(1)}, u32[]{:S(2)}, u32[]{:S(2)}) collective-permute-start(f32[192,128]{1,0:T(8,128)S(1)} %bitcast.15), channel_id=1, source_target_pairs={{0,1},{1,0},{2,3},{3,2},{4,5},{5,4},{6,7},{7,6},{8,9},{9,8},{10,11... | collective-permute-start | bytes 294920 | tf_op jit(solution)/shard_map/ppermute | solution.py:386
  17.5 0.4 shard_map.108
  17.9 0.6 collective-permute-done.3.part
  18.4 1.3 %shard_map.109 = (f32[64,128]{1,0:T(8,128)S(1)}, f32[1024,128]{1,0:T(8,128)S(1)}, f32[64,128]{1,0:T(8,128)S(1)}, f32[64,128]{1,0:T(8,128)S(1)}, f32[8,128]{1,0:T(8,128)S(1)}) custom-call(s32[16,24]{1,0:T(8,128)S(4)} %get-tuple-element.45.plan, bf16[128,128]{1,0:T(8,128)(2,1)S(1)} %get-tuple-element.46.hit_ref, f32[192,128]{1,0:T(8,128)S(1)} %collective-permute-done.3.part, ...), custom_call_target="tpu_custom_call" | custom-call | tf_op jit(solution)/shard_map/pallas_call | solution.py:368
  19.8 0.4 collective-permute-start.4
  20.2 0.6 shard_map.110
  20.7 0.3 collective-permute-done.4
  21.0 1.8 %collective-permute-start.5 = (f32[64,128]{1,0:T(8,128)S(1)}, f32[64,128]{1,0:T(8,128)S(1)}, u32[]{:S(2)}, u32[]{:S(2)}) collective-permute-start(f32[64,128]{1,0:T(8,128)S(1)} %add.36), channel_id=1, source_target_pairs={{0,3},{1,2},{2,1},{3,0},{4,7},{5,6},{6,5},{7,4},{8,11},{9,10},{10,... | collective-permute-start | bytes 98312 | tf_op jit(solution)/shard_map/ppermute | solution.py:386
  22.8 1.6 %collective-permute-done.5 = f32[64,128]{1,0:T(8,128)S(1)} collective-permute-done((f32[64,128]{1,0:T(8,128)S(1)}, f32[64,128]{1,0:T(8,128)S(1)}, u32[]{:S(2)}, u32[]{:S(2)}) %collective-permute-start.5) | collective-permute-done | bytes 32800 | tf_op jit(solution)/shard_map/ppermute | solution.py:386
  24.4 0.7 %collective-permute-start.6 = (f32[64,128]{1,0:T(8,128)S(1)}, f32[64,128]{1,0:T(8,128)S(1)}, u32[]{:S(2)}, u32[]{:S(2)}) collective-permute-start(f32[64,128]{1,0:T(8,128)S(1)} %add.37), channel_id=1, source_target_pairs={{0,5},{1,4},{2,7},{3,6},{4,1},{5,0},{6,3},{7,2},{8,13},{9,12},{10,... | collective-permute-start | bytes 98312 | tf_op jit(solution)/shard_map/ppermute | solution.py:386
  25.1 2.7 %collective-permute-done.6 = f32[64,128]{1,0:T(8,128)S(1)} collective-permute-done((f32[64,128]{1,0:T(8,128)S(1)}, f32[64,128]{1,0:T(8,128)S(1)}, u32[]{:S(2)}, u32[]{:S(2)}) %collective-permute-start.6) | collective-permute-done | bytes 32800 | tf_op jit(solution)/shard_map/ppermute | solution.py:386
  27.8 1.2 %collective-permute-start.7 = (f32[64,128]{1,0:T(8,128)S(1)}, f32[64,128]{1,0:T(8,128)S(1)}, u32[]{:S(2)}, u32[]{:S(2)}) collective-permute-start(f32[64,128]{1,0:T(8,128)S(1)} %add.38), channel_id=1, source_target_pairs={{0,9},{1,8},{2,11},{3,10},{4,13},{5,12},{6,15},{7,14},{8,1},{9,0},... | collective-permute-start | bytes 98312 | tf_op jit(solution)/shard_map/ppermute | solution.py:386
  29.0 3.0 %collective-permute-done.7 = f32[64,128]{1,0:T(8,128)S(1)} collective-permute-done((f32[64,128]{1,0:T(8,128)S(1)}, f32[64,128]{1,0:T(8,128)S(1)}, u32[]{:S(2)}, u32[]{:S(2)}) %collective-permute-start.7) | collective-permute-done | bytes 32800 | tf_op jit(solution)/shard_map/ppermute | solution.py:386
  32.0 0.9 %collective-permute-start.8 = (f32[64,128]{1,0:T(8,128)S(1)}, f32[64,128]{1,0:T(8,128)S(1)}, u32[]{:S(2)}, u32[]{:S(2)}) collective-permute-start(f32[64,128]{1,0:T(8,128)S(1)} %add.39.sums), channel_id=1, source_target_pairs={{0,1},{1,0},{2,3},{3,2},{4,5},{5,4},{6,7},{7,6},{8,9},{9,8},{10,11... | collective-permute-start | bytes 98312 | tf_op jit(solution)/shard_map/ppermute | solution.py:386
  32.9 0.4 shard_map.111
  33.3 0.5 collective-permute-done.8.sums
  33.7 1.4 %shard_map.112 = (f32[64,128]{1,0:T(8,128)S(1)}, f32[1024,128]{1,0:T(8,128)S(1)}) custom-call(s32[16,24]{1,0:T(8,128)S(4)} %get-tuple-element.45.plan, bf16[128,128]{1,0:T(8,128)(2,1)S(1)} %get-tuple-element.46.hit_ref, f32[64,128]{1,0:T(8,128)S(1)} %collective-permute-done.8.sums, f32[64,128]{1,0:T(8,128)S(1)} %get-tuple-element.70.fb_ref, ...), custom_call_target="tpu_custom_call" | custom-call | tf_op jit(solution)/shard_map/pallas_call | solution.py:368
  35.1 0.4 collective-permute-start.9
  35.5 0.6 shard_map.113
  36.1 0.3 collective-permute-done.9
  36.4 2.1 %collective-permute-start.10 = (f32[64,128]{1,0:T(8,128)S(1)}, f32[64,128]{1,0:T(8,128)S(1)}, u32[]{:S(2)}, u32[]{:S(2)}) collective-permute-start(f32[64,128]{1,0:T(8,128)S(1)} %add.40), channel_id=1, source_target_pairs={{0,3},{1,2},{2,1},{3,0},{4,7},{5,6},{6,5},{7,4},{8,11},{9,10},{10,... | collective-permute-start | bytes 98312 | tf_op jit(solution)/shard_map/ppermute | solution.py:386
  38.4 1.6 %collective-permute-done.10 = f32[64,128]{1,0:T(8,128)S(1)} collective-permute-done((f32[64,128]{1,0:T(8,128)S(1)}, f32[64,128]{1,0:T(8,128)S(1)}, u32[]{:S(2)}, u32[]{:S(2)}) %collective-permute-start.10) | collective-permute-done | bytes 32800 | tf_op jit(solution)/shard_map/ppermute | solution.py:386
  40.1 0.2 collective-permute-start.11
  40.2 3.2 %collective-permute-done.11 = f32[64,128]{1,0:T(8,128)S(1)} collective-permute-done((f32[64,128]{1,0:T(8,128)S(1)}, f32[64,128]{1,0:T(8,128)S(1)}, u32[]{:S(2)}, u32[]{:S(2)}) %collective-permute-start.11) | collective-permute-done | bytes 32800 | tf_op jit(solution)/shard_map/ppermute | solution.py:386
  43.4 0.5 collective-permute-start.12
  43.9 4.3 %collective-permute-done.12 = f32[64,128]{1,0:T(8,128)S(1)} collective-permute-done((f32[64,128]{1,0:T(8,128)S(1)}, f32[64,128]{1,0:T(8,128)S(1)}, u32[]{:S(2)}, u32[]{:S(2)}) %collective-permute-start.12) | collective-permute-done | bytes 32800 | tf_op jit(solution)/shard_map/ppermute | solution.py:386
  48.2 0.1 collective-permute-start.13
  48.3 0.4 shard_map.114
  48.7 0.7 %collective-permute-done.13.sums = f32[64,128]{1,0:T(8,128)S(1)} collective-permute-done((f32[64,128]{1,0:T(8,128)S(1)}, f32[64,128]{1,0:T(8,128)S(1)}, u32[]{:S(2)}, u32[]{:S(2)}) %collective-permute-start.13) | collective-permute-done | bytes 32800 | tf_op jit(solution)/shard_map/ppermute | solution.py:386
  49.4 1.4 %shard_map.115 = (f32[64,128]{1,0:T(8,128)S(1)}, f32[1024,128]{1,0:T(8,128)S(1)}) custom-call(s32[16,24]{1,0:T(8,128)S(4)} %get-tuple-element.45.plan, bf16[128,128]{1,0:T(8,128)(2,1)S(1)} %get-tuple-element.46.hit_ref, f32[64,128]{1,0:T(8,128)S(1)} %collective-permute-done.13.sums, f32[64,128]{1,0:T(8,128)S(1)} %get-tuple-element.70.fb_ref, ...), custom_call_target="tpu_custom_call" | custom-call | tf_op jit(solution)/shard_map/pallas_call | solution.py:368
  50.8 0.2 collective-permute-start.14
  51.0 0.6 shard_map.116
  51.6 0.5 collective-permute-done.14
  52.1 1.8 %collective-permute-start.15 = (f32[64,128]{1,0:T(8,128)S(1)}, f32[64,128]{1,0:T(8,128)S(1)}, u32[]{:S(2)}, u32[]{:S(2)}) collective-permute-start(f32[64,128]{1,0:T(8,128)S(1)} %add.44), channel_id=1, source_target_pairs={{0,3},{1,2},{2,1},{3,0},{4,7},{5,6},{6,5},{7,4},{8,11},{9,10},{10,... | collective-permute-start | bytes 98312 | tf_op jit(solution)/shard_map/ppermute | solution.py:386
  53.9 1.6 %collective-permute-done.15 = f32[64,128]{1,0:T(8,128)S(1)} collective-permute-done((f32[64,128]{1,0:T(8,128)S(1)}, f32[64,128]{1,0:T(8,128)S(1)}, u32[]{:S(2)}, u32[]{:S(2)}) %collective-permute-start.15) | collective-permute-done | bytes 32800 | tf_op jit(solution)/shard_map/ppermute | solution.py:386
  55.5 0.0 collective-permute-start.16
  55.5 3.3 %collective-permute-done.16 = f32[64,128]{1,0:T(8,128)S(1)} collective-permute-done((f32[64,128]{1,0:T(8,128)S(1)}, f32[64,128]{1,0:T(8,128)S(1)}, u32[]{:S(2)}, u32[]{:S(2)}) %collective-permute-start.16) | collective-permute-done | bytes 32800 | tf_op jit(solution)/shard_map/ppermute | solution.py:386
  58.8 0.0 collective-permute-start.17
  58.8 4.8 %collective-permute-done.17 = f32[64,128]{1,0:T(8,128)S(1)} collective-permute-done((f32[64,128]{1,0:T(8,128)S(1)}, f32[64,128]{1,0:T(8,128)S(1)}, u32[]{:S(2)}, u32[]{:S(2)}) %collective-permute-start.17) | collective-permute-done | bytes 32800 | tf_op jit(solution)/shard_map/ppermute | solution.py:386
  63.7 0.1 collective-permute-start.18
  63.8 0.1 shard_map.117
  63.9 1.0 %collective-permute-done.18.other = f32[64,128]{1,0:T(8,128)S(1)} collective-permute-done((f32[64,128]{1,0:T(8,128)S(1)}, f32[64,128]{1,0:T(8,128)S(1)}, u32[]{:S(2)}, u32[]{:S(2)}) %collective-permute-start.18) | collective-permute-done | bytes 32800 | tf_op jit(solution)/shard_map/ppermute | solution.py:386
  64.9 0.8 %shard_map.118 = (f32[8,128]{1,0:T(8,128)}, f32[8,128]{1,0:T(8,128)}) custom-call(f32[64,128]{1,0:T(8,128)S(1)} %collective-permute-done.18.other, f32[64,128]{1,0:T(8,128)S(1)} %get-tuple-element.70.fb_ref, f32[64,128]{1,0:T(8,128)S(1)} %get-tuple-element.71.et_ref, f32[8,128]{1,0:T(8,128)S(1)} %get-tuple-element.72.tot_ref, ...), custom_call_target="tpu_custom_call" | custom-call | tf_op jit(solution)/shard_map/pallas_call | solution.py:368
  (15 shorter events, 0.1 us)
Async XLA Ops:
  1.4 7.4 %collective-permute-start = (f32[24,128]{1,0:T(8,128)S(1)}, f32[24,128]{1,0:T(8,128)S(1)}, u32[]{:S(2)}, u32[]{:S(2)}) collective-permute-start(f32[24,128]{1,0:T(8,128)S(1)} %shard_map.105), channel_id=1, source_target_pairs={{0,9},{1,8},{2,11},{3,10},{4,13},{5,12},{6,15},{7,14},{8,1},{9,0},... | collective-permute-start | bytes 36872 | tf_op jit(solution)/shard_map/ppermute | solution.py:386
  8.8 4.1 %collective-permute-start.1 = (f32[48,128]{1,0:T(8,128)S(1)}, f32[48,128]{1,0:T(8,128)S(1)}, u32[]{:S(2)}, u32[]{:S(2)}) collective-permute-start(f32[48,128]{1,0:T(8,128)S(1)} %bitcast.20), channel_id=1, source_target_pairs={{0,5},{1,4},{2,7},{3,6},{4,1},{5,0},{6,3},{7,2},{8,13},{9,12},{10,... | collective-permute-start | bytes 73736 | tf_op jit(solution)/shard_map/ppermute | solution.py:386
  12.9 3.6 %collective-permute-start.2 = (f32[96,128]{1,0:T(8,128)S(1)}, f32[96,128]{1,0:T(8,128)S(1)}, u32[]{:S(2)}, u32[]{:S(2)}) collective-permute-start(f32[96,128]{1,0:T(8,128)S(1)} %bitcast.18), channel_id=1, source_target_pairs={{0,3},{1,2},{2,1},{3,0},{4,7},{5,6},{6,5},{7,4},{8,11},{9,10},{10,... | collective-permute-start | bytes 147464 | tf_op jit(solution)/shard_map/ppermute | solution.py:386
  16.5 1.9 %collective-permute-start.3 = (f32[192,128]{1,0:T(8,128)S(1)}, f32[192,128]{1,0:T(8,128)S(1)}, u32[]{:S(2)}, u32[]{:S(2)}) collective-permute-start(f32[192,128]{1,0:T(8,128)S(1)} %bitcast.15), channel_id=1, source_target_pairs={{0,1},{1,0},{2,3},{3,2},{4,5},{5,4},{6,7},{7,6},{8,9},{9,8},{10,11... | collective-permute-start | bytes 294920 | tf_op jit(solution)/shard_map/ppermute | solution.py:386
  19.8 1.3 %collective-permute-start.4 = (f32[64,128]{1,0:T(8,128)S(1)}, f32[64,128]{1,0:T(8,128)S(1)}, u32[]{:S(2)}, u32[]{:S(2)}) collective-permute-start(f32[64,128]{1,0:T(8,128)S(1)} %get-tuple-element.69), channel_id=1, source_target_pairs={{0,1},{1,0},{2,3},{3,2},{4,5},{5,4},{6,7},{7,6},{8,9},{9,8},{10,11... | collective-permute-start | bytes 98312 | tf_op jit(solution)/shard_map/ppermute | solution.py:386
  21.0 3.4 %collective-permute-start.5 = (f32[64,128]{1,0:T(8,128)S(1)}, f32[64,128]{1,0:T(8,128)S(1)}, u32[]{:S(2)}, u32[]{:S(2)}) collective-permute-start(f32[64,128]{1,0:T(8,128)S(1)} %add.36), channel_id=1, source_target_pairs={{0,3},{1,2},{2,1},{3,0},{4,7},{5,6},{6,5},{7,4},{8,11},{9,10},{10,... | collective-permute-start | bytes 98312 | tf_op jit(solution)/shard_map/ppermute | solution.py:386
  24.4 3.3 %collective-permute-start.6 = (f32[64,128]{1,0:T(8,128)S(1)}, f32[64,128]{1,0:T(8,128)S(1)}, u32[]{:S(2)}, u32[]{:S(2)}) collective-permute-start(f32[64,128]{1,0:T(8,128)S(1)} %add.37), channel_id=1, source_target_pairs={{0,5},{1,4},{2,7},{3,6},{4,1},{5,0},{6,3},{7,2},{8,13},{9,12},{10,... | collective-permute-start | bytes 98312 | tf_op jit(solution)/shard_map/ppermute | solution.py:386
  27.8 4.2 %collective-permute-start.7 = (f32[64,128]{1,0:T(8,128)S(1)}, f32[64,128]{1,0:T(8,128)S(1)}, u32[]{:S(2)}, u32[]{:S(2)}) collective-permute-start(f32[64,128]{1,0:T(8,128)S(1)} %add.38), channel_id=1, source_target_pairs={{0,9},{1,8},{2,11},{3,10},{4,13},{5,12},{6,15},{7,14},{8,1},{9,0},... | collective-permute-start | bytes 98312 | tf_op jit(solution)/shard_map/ppermute | solution.py:386
  32.0 1.7 %collective-permute-start.8 = (f32[64,128]{1,0:T(8,128)S(1)}, f32[64,128]{1,0:T(8,128)S(1)}, u32[]{:S(2)}, u32[]{:S(2)}) collective-permute-start(f32[64,128]{1,0:T(8,128)S(1)} %add.39.sums), channel_id=1, source_target_pairs={{0,1},{1,0},{2,3},{3,2},{4,5},{5,4},{6,7},{7,6},{8,9},{9,8},{10,11... | collective-permute-start | bytes 98312 | tf_op jit(solution)/shard_map/ppermute | solution.py:386
  35.1 1.3 %collective-permute-start.9 = (f32[64,128]{1,0:T(8,128)S(1)}, f32[64,128]{1,0:T(8,128)S(1)}, u32[]{:S(2)}, u32[]{:S(2)}) collective-permute-start(f32[64,128]{1,0:T(8,128)S(1)} %get-tuple-element.78), channel_id=1, source_target_pairs={{0,1},{1,0},{2,3},{3,2},{4,5},{5,4},{6,7},{7,6},{8,9},{9,8},{10,11... | collective-permute-start | bytes 98312 | tf_op jit(solution)/shard_map/ppermute | solution.py:386
  36.4 3.7 %collective-permute-start.10 = (f32[64,128]{1,0:T(8,128)S(1)}, f32[64,128]{1,0:T(8,128)S(1)}, u32[]{:S(2)}, u32[]{:S(2)}) collective-permute-start(f32[64,128]{1,0:T(8,128)S(1)} %add.40), channel_id=1, source_target_pairs={{0,3},{1,2},{2,1},{3,0},{4,7},{5,6},{6,5},{7,4},{8,11},{9,10},{10,... | collective-permute-start | bytes 98312 | tf_op jit(solution)/shard_map/ppermute | solution.py:386
  40.1 3.3 %collective-permute-start.11 = (f32[64,128]{1,0:T(8,128)S(1)}, f32[64,128]{1,0:T(8,128)S(1)}, u32[]{:S(2)}, u32[]{:S(2)}) collective-permute-start(f32[64,128]{1,0:T(8,128)S(1)} %add.41), channel_id=1, source_target_pairs={{0,5},{1,4},{2,7},{3,6},{4,1},{5,0},{6,3},{7,2},{8,13},{9,12},{10,... | collective-permute-start | bytes 98312 | tf_op jit(solution)/shard_map/ppermute | solution.py:386
  43.4 4.8 %collective-permute-start.12 = (f32[64,128]{1,0:T(8,128)S(1)}, f32[64,128]{1,0:T(8,128)S(1)}, u32[]{:S(2)}, u32[]{:S(2)}) collective-permute-start(f32[64,128]{1,0:T(8,128)S(1)} %add.42), channel_id=1, source_target_pairs={{0,9},{1,8},{2,11},{3,10},{4,13},{5,12},{6,15},{7,14},{8,1},{9,0},... | collective-permute-start | bytes 98312 | tf_op jit(solution)/shard_map/ppermute | solution.py:386
  48.2 1.2 %collective-permute-start.13 = (f32[64,128]{1,0:T(8,128)S(1)}, f32[64,128]{1,0:T(8,128)S(1)}, u32[]{:S(2)}, u32[]{:S(2)}) collective-permute-start(f32[64,128]{1,0:T(8,128)S(1)} %add.43.sums), channel_id=1, source_target_pairs={{0,1},{1,0},{2,3},{3,2},{4,5},{5,4},{6,7},{7,6},{8,9},{9,8},{10,11... | collective-permute-start | bytes 98312 | tf_op jit(solution)/shard_map/ppermute | solution.py:386
  50.8 1.3 %collective-permute-start.14 = (f32[64,128]{1,0:T(8,128)S(1)}, f32[64,128]{1,0:T(8,128)S(1)}, u32[]{:S(2)}, u32[]{:S(2)}) collective-permute-start(f32[64,128]{1,0:T(8,128)S(1)} %get-tuple-element.82), channel_id=1, source_target_pairs={{0,1},{1,0},{2,3},{3,2},{4,5},{5,4},{6,7},{7,6},{8,9},{9,8},{10,11... | collective-permute-start | bytes 98312 | tf_op jit(solution)/shard_map/ppermute | solution.py:386
  52.1 3.4 %collective-permute-start.15 = (f32[64,128]{1,0:T(8,128)S(1)}, f32[64,128]{1,0:T(8,128)S(1)}, u32[]{:S(2)}, u32[]{:S(2)}) collective-permute-start(f32[64,128]{1,0:T(8,128)S(1)} %add.44), channel_id=1, source_target_pairs={{0,3},{1,2},{2,1},{3,0},{4,7},{5,6},{6,5},{7,4},{8,11},{9,10},{10,... | collective-permute-start | bytes 98312 | tf_op jit(solution)/shard_map/ppermute | solution.py:386
  55.5 3.3 %collective-permute-start.16 = (f32[64,128]{1,0:T(8,128)S(1)}, f32[64,128]{1,0:T(8,128)S(1)}, u32[]{:S(2)}, u32[]{:S(2)}) collective-permute-start(f32[64,128]{1,0:T(8,128)S(1)} %add.45), channel_id=1, source_target_pairs={{0,5},{1,4},{2,7},{3,6},{4,1},{5,0},{6,3},{7,2},{8,13},{9,12},{10,... | collective-permute-start | bytes 98312 | tf_op jit(solution)/shard_map/ppermute | solution.py:386
  58.8 4.8 %collective-permute-start.17 = (f32[64,128]{1,0:T(8,128)S(1)}, f32[64,128]{1,0:T(8,128)S(1)}, u32[]{:S(2)}, u32[]{:S(2)}) collective-permute-start(f32[64,128]{1,0:T(8,128)S(1)} %add.46), channel_id=1, source_target_pairs={{0,9},{1,8},{2,11},{3,10},{4,13},{5,12},{6,15},{7,14},{8,1},{9,0},... | collective-permute-start | bytes 98312 | tf_op jit(solution)/shard_map/ppermute | solution.py:386
  63.7 1.2 %collective-permute-start.18 = (f32[64,128]{1,0:T(8,128)S(1)}, f32[64,128]{1,0:T(8,128)S(1)}, u32[]{:S(2)}, u32[]{:S(2)}) collective-permute-start(f32[64,128]{1,0:T(8,128)S(1)} %add.47.keep), channel_id=1, source_target_pairs={{0,1},{1,0},{2,3},{3,2},{4,5},{5,4},{6,7},{7,6},{8,9},{9,8},{10,11... | collective-permute-start | bytes 98312 | tf_op jit(solution)/shard_map/ppermute | solution.py:386

commit v10 on v9

--- a/solution.py
+++ b/solution.py
@@ -99,7 +99,7 @@
                 cols = slice(q * block, (q + 1) * block)
                 row = to_row(ysq[cols, :], mask)
                 e = (2.0 * scale) * cross[:, cols] + (base - row * scale)
-                start = pl.multiple_of((s * slots + p * STEP + q) * block, block)
+                start = pl.multiple_of((s * (slots + STEP) + p * STEP + q) * block, block)
                 k_ref[pl.ds(start, block), :] = jnp.exp2(e)
             return 0
 
@@ -128,8 +128,11 @@
     slot = lax.broadcasted_iota(jnp.int32, (local, slots), 1)
     key = jnp.where(slot < lives, jnp.where(rows < every // 2, 0, slots), 2 * slots) + slot
     rank = jnp.zeros((local, slots), jnp.int32)
+    own_count = jnp.zeros((local, slots), jnp.int32)
     for k in range(slots):
         rank += jnp.where(key[:, k : k + 1] < key, 1, 0)
+        own_count += jnp.where(key[:, k : k + 1] < slots, 1, 0)
+    rank += (-own_count) & (STEP - 1)
     lanes = plan_ref.shape[1]
     at = lax.broadcasted_iota(jnp.int32, (local, lanes), 1)
     wide_sub = lax.broadcasted_iota(jnp.int32, (local, lanes), 0)
@@ -144,17 +147,19 @@
         slot_at = jnp.where(here, k, slot_at)
         row_at = jnp.where(here, rows[:, k : k + 1], row_at)
         own_count += jnp.where(key[:, k : k + 1] < slots, 1, 0)
-    slot_at = jnp.where(at < lives, slot_at, 0)
-    row_at = jnp.where(at < lives, row_at, every)
+    empty = (-own_count) & (STEP - 1)
+    used = jnp.logical_and(at >= empty, at < empty + lives)
+    slot_at = jnp.where(used, slot_at, 0)
+    row_at = jnp.where(used, row_at, every)
     shift = STEP.bit_length() - 1
-    counts = ((lives + (STEP - 1)) >> shift, (own_count + (STEP - 1)) >> shift, own_count >> shift)
+    counts = ((empty + lives + (STEP - 1)) >> shift, (empty + own_count) >> shift)
     for i, c in enumerate(counts):
         slot_at = jnp.where(at == slots + STEP + i, c, slot_at)
     order_ref[:local, :] = slot_at
     order_ref[local:, :] = row_at
     to_smem = pltpu.make_async_copy(order_ref, plan_ref, sems.at[len(copies)])
     to_smem.start()
-    index = jnp.concatenate([row_at[s : s + 1, :slots] for s in range(local)], axis=1)
+    index = jnp.concatenate([row_at[s : s + 1, : slots + STEP] for s in range(local)], axis=1)
     rows = lax.broadcasted_iota(jnp.int32, hit_ref.shape, 0)
     hit_ref[...] = jnp.where(rows == index, 1.0, 0.0).astype(jnp.bfloat16)
     to_smem.wait()
@@ -185,7 +190,7 @@
 
 def add_rows(plan, span, w_ref, k_refs, out_ref, from_ref=None):
     blocks, block = plan.shape[0] // 2, w_ref.shape[1]
-    slots = plan.shape[1] - 2 * STEP
+    slots = plan.shape[1] - STEP
     for s in range(blocks):
         piece, at = place(s)
         k_ref, base = k_refs[piece], at * slots
@@ -206,7 +211,7 @@
 
 def add_columns(plan, span, u_ref, k_refs, hit, col_ref):
     blocks, block = plan.shape[0] // 2, col_ref.shape[1]
-    slots = plan.shape[1] - 2 * STEP
+    slots = plan.shape[1] - STEP
     col_ref[...] = jnp.zeros_like(col_ref)
     for s in range(blocks):
         piece, at = place(s)
@@ -240,7 +245,7 @@
 
 def other_span(plan):
     at = plan.shape[1] - STEP
-    return lambda s: (plan[s, at + 2], plan[s, at])
+    return lambda s: (plan[s, at + 1], plan[s, at])
 
 
 def spread(w_ref, w, other):
@@ -393,7 +398,8 @@
     local, slots, block, width = tile_feat.shape
     n = lax.axis_size("src")
     every = local * n
-    pairs = local * slots
+    places = slots + STEP
+    pairs = local * places
     lin = src_lin.reshape(local, block)
     amass = src_mass.reshape(local, block)
     def shape(rows, cols=block, dtype=f32):
@@ -417,7 +423,7 @@
         if at < len(PIECES):
             size = PIECES[at]
             ahead = [feats(PIECES[at + 1])] if at + 1 < len(PIECES) else []
-            outs = (shape(size * slots * block), shape(size * block), *ahead)
+            outs = (shape(size * places * block), shape(size * block), *ahead)
             cost = dict(
                 flops=2 * size * slots * block * block * width,
                 bytes_accessed=2 * size * slots * block * width,
@@ -429,7 +435,7 @@
                 (tile_live, tile_tgt, src_feat, lin, amass, tile_feat),
                 (
                     *outs,
-                    SMEM((2 * local, slots + 2 * STEP), jnp.int32),
+                    SMEM((2 * local, places + STEP), jnp.int32),
                     shape(every, pairs, jnp.bfloat16),
                     shape(local * block, width, src_feat.dtype),
                     shape(local),
@@ -438,7 +444,7 @@
                 scratch=[
                     SMEM((local,), jnp.int32),
                     VMEM((local, slots), jnp.int32),
-                    VMEM((2 * local, slots + 2 * STEP), jnp.int32),
+                    VMEM((2 * local, places + STEP), jnp.int32),
                     feats(size),
                     pltpu.SemaphoreType.DMA((7 + size,)),
                 ],

time: 66.3 us -> 66 us (level); the launches traced: 65.6 us -> 66.1 us
  starting transfers between devices: 18.5 us -> 9.13 us
  waiting for transfers between devices: 30 us -> 36.9 us
  Pallas kernels: 16.3 us -> 19.2 us
    ppermute x19, starting transfers between devices: 18.5 us -> 9.13 us  [exchange(): return lax.ppermute(x, 'src', [(i, i ^ d) for i in range(n)])]
    ppermute x19, waiting for transfers between devices: 30 us -> 36.9 us  [exchange(): return lax.ppermute(x, 'src', [(i, i ^ d) for i in range(n)])]
    pallas_call x15, Pallas kernels: 16.3 us -> 19.2 us  [call(): pl.pallas_call(kernel, out_shape=outs, in_specs=specs, out_specs=[pl.Bloc...]
  transfers between devices with their start and end apart: 19 -> 19, of which waited for: 16 -> 17; matrix products, arithmetic and copies ran while one was open for 0% -> 0% of each run, Pallas kernels for 16% -> 20%
where the time goes in v10:
time: 66 us; the launch traced here: 66.1 us
  waiting for transfers between devices  36.9 us (56%)
  Pallas kernels  19.2 us (29%)
  starting transfers between devices  9.13 us (14%)
  between operations  0.8 us (1%)
    ppermute x19, waiting for transfers between devices, exchange(): return lax.ppermute(x, 'src', [(i, i ^ d) for i in range(n)])  36.9 us
    pallas_call x15, Pallas kernels, call(): pl.pallas_call(kernel, out_shape=outs, in_specs=specs, out_specs=[pl.Bloc...  19.2 us
    ppermute x19, starting transfers between devices, exchange(): return lax.ppermute(x, 'src', [(i, i ^ d) for i in range(n)])  9.13 us
  transfers between devices with their start and end apart: 19, of which 17 were waited for; matrix products, arithmetic and copies ran while one was open for 0% of the time, Pallas kernels for 20%

profile of v10, /device:TPU:0, one launch (start us, length us, event | category | flops | bytes accessed | tf_op | source)
XLA Modules:
  0.0 66.1 jit_solution(6463884762291579168)
XLA Ops:
  0.6 0.8 %shard_map.105 = f32[24,128]{1,0:T(8,128)S(1)} custom-call(s32[8]{0:T(128)} %count_hbm.1, f32[8,128]{1,0:T(8,128)} %bitcast.28, f32[8,128]{1,0:T(8,128)} %bitcast.29, f32[8,128]{1,0:T(8,128)} %bitcast.24), custom_call_target="tpu_custom_call" | custom-call | tf_op jit(solution)/shard_map/pallas_call | solution.py:373
  1.4 3.5 %collective-permute-start = (f32[24,128]{1,0:T(8,128)S(1)}, f32[24,128]{1,0:T(8,128)S(1)}, u32[]{:S(2)}, u32[]{:S(2)}) collective-permute-start(f32[24,128]{1,0:T(8,128)S(1)} %shard_map.105), channel_id=1, source_target_pairs={{0,9},{1,8},{2,11},{3,10},{4,13},{5,12},{6,15},{7,14},{8,1},{9,0},... | collective-permute-start | bytes 36872 | tf_op jit(solution)/shard_map/ppermute | solution.py:391
  4.9 4.5 %shard_map.104 = (f32[5120,128]{1,0:T(8,128)S(1)}, f32[256,128]{1,0:T(8,128)S(1)}, bf16[3,16,128,256]{3,2,1,0:T(8,128)(2,1)S(1)}, s32[16,24]{1,0:T(8,128)S(4)}, ...) custom-call(s32[8]{0:T(128)} %live_hbm.1, ...), custom_call_target="tpu_custom_call" | custom-call | flops 268435456 | bytes 2097152 | tf_op jit(solution)/shard_map/pallas_call | solution.py:373
  9.4 0.0 collective-permute-done
  9.5 1.4 %collective-permute-start.1 = (f32[48,128]{1,0:T(8,128)S(1)}, f32[48,128]{1,0:T(8,128)S(1)}, u32[]{:S(2)}, u32[]{:S(2)}) collective-permute-start(f32[48,128]{1,0:T(8,128)S(1)} %bitcast.20), channel_id=1, source_target_pairs={{0,5},{1,4},{2,7},{3,6},{4,1},{5,0},{6,3},{7,2},{8,13},{9,12},{10,... | collective-permute-start | bytes 73736 | tf_op jit(solution)/shard_map/ppermute | solution.py:391
  10.9 2.6 %shard_map.106 = (f32[7680,128]{1,0:T(8,128)S(1)}, f32[384,128]{1,0:T(8,128)S(1)}, bf16[3,16,128,256]{3,2,1,0:T(8,128)(2,1)S(1)}) custom-call(s32[16,24]{1,0:T(8,128)S(4)} %get-tuple-element.45.plan, bf16[1024,256]{1,0:T(8,128)(2,1)S(1)} %get-tuple-element.50.x_ref, f32[8,128]{1,0:T(8,128)S(1)} %get-tuple-element.51.lin_ref, ...), custom_call_target="tpu_custom_call" | custom-call | flops 402653184 | bytes 3145728 | tf_op jit(solution)/shard_map/pallas_call | solution.py:373
  13.5 0.0 collective-permute-done.1
  13.5 0.6 collective-permute-start.2
  14.1 2.8 %shard_map.107 = (f32[7680,128]{1,0:T(8,128)S(1)}, f32[384,128]{1,0:T(8,128)S(1)}) custom-call(s32[16,24]{1,0:T(8,128)S(4)} %get-tuple-element.45.plan, bf16[1024,256]{1,0:T(8,128)(2,1)S(1)} %get-tuple-element.50.x_ref, f32[8,128]{1,0:T(8,128)S(1)} %get-tuple-element.51.lin_ref, f32[8,128]{1,0:T(8,128)S(1)} %get-tuple-element.52.mass_ref, ...), custom_call_target="tpu_custom_call" | custom-call | flops 402653184 | bytes 3145728 | tf_op jit(solution)/shard_map/pallas_call | solution.py:373
  16.9 0.2 collective-permute-done.2
  17.1 0.6 collective-permute-start.3
  17.8 0.4 shard_map.108
  18.2 0.5 collective-permute-done.3.part
  18.7 1.5 %shard_map.109 = (f32[64,128]{1,0:T(8,128)S(1)}, f32[1024,128]{1,0:T(8,128)S(1)}, f32[64,128]{1,0:T(8,128)S(1)}, f32[64,128]{1,0:T(8,128)S(1)}, f32[8,128]{1,0:T(8,128)S(1)}) custom-call(s32[16,24]{1,0:T(8,128)S(4)} %get-tuple-element.45.plan, bf16[128,160]{1,0:T(8,128)(2,1)S(1)} %get-tuple-element.46.hit_ref, f32[192,128]{1,0:T(8,128)S(1)} %collective-permute-done.3.part, ...), custom_call_target="tpu_custom_call" | custom-call | tf_op jit(solution)/shard_map/pallas_call | solution.py:373
  20.2 0.3 collective-permute-start.4
  20.5 0.6 shard_map.110
  21.1 0.3 collective-permute-done.4
  21.5 0.7 %collective-permute-start.5 = (f32[64,128]{1,0:T(8,128)S(1)}, f32[64,128]{1,0:T(8,128)S(1)}, u32[]{:S(2)}, u32[]{:S(2)}) collective-permute-start(f32[64,128]{1,0:T(8,128)S(1)} %add.36), channel_id=1, source_target_pairs={{0,3},{1,2},{2,1},{3,0},{4,7},{5,6},{6,5},{7,4},{8,11},{9,10},{10,... | collective-permute-start | bytes 98312 | tf_op jit(solution)/shard_map/ppermute | solution.py:391
  22.2 2.6 %collective-permute-done.5 = f32[64,128]{1,0:T(8,128)S(1)} collective-permute-done((f32[64,128]{1,0:T(8,128)S(1)}, f32[64,128]{1,0:T(8,128)S(1)}, u32[]{:S(2)}, u32[]{:S(2)}) %collective-permute-start.5) | collective-permute-done | bytes 32800 | tf_op jit(solution)/shard_map/ppermute | solution.py:391
  24.8 0.7 collective-permute-start.6
  25.5 2.7 %collective-permute-done.6 = f32[64,128]{1,0:T(8,128)S(1)} collective-permute-done((f32[64,128]{1,0:T(8,128)S(1)}, f32[64,128]{1,0:T(8,128)S(1)}, u32[]{:S(2)}, u32[]{:S(2)}) %collective-permute-start.6) | collective-permute-done | bytes 32800 | tf_op jit(solution)/shard_map/ppermute | solution.py:391
  28.1 0.5 collective-permute-start.7
  28.6 4.5 %collective-permute-done.7 = f32[64,128]{1,0:T(8,128)S(1)} collective-permute-done((f32[64,128]{1,0:T(8,128)S(1)}, f32[64,128]{1,0:T(8,128)S(1)}, u32[]{:S(2)}, u32[]{:S(2)}) %collective-permute-start.7) | collective-permute-done | bytes 32800 | tf_op jit(solution)/shard_map/ppermute | solution.py:391
  33.1 0.1 collective-permute-start.8
  33.3 0.4 shard_map.111
  33.7 0.6 collective-permute-done.8.sums
  34.3 1.5 %shard_map.112 = (f32[64,128]{1,0:T(8,128)S(1)}, f32[1024,128]{1,0:T(8,128)S(1)}) custom-call(s32[16,24]{1,0:T(8,128)S(4)} %get-tuple-element.45.plan, bf16[128,160]{1,0:T(8,128)(2,1)S(1)} %get-tuple-element.46.hit_ref, f32[64,128]{1,0:T(8,128)S(1)} %collective-permute-done.8.sums, f32[64,128]{1,0:T(8,128)S(1)} %get-tuple-element.70.fb_ref, ...), custom_call_target="tpu_custom_call" | custom-call | tf_op jit(solution)/shard_map/pallas_call | solution.py:373
  35.8 0.1 collective-permute-start.9
  35.9 0.6 shard_map.113
  36.6 0.5 collective-permute-done.9
  37.1 0.2 collective-permute-start.10
  37.3 3.2 %collective-permute-done.10 = f32[64,128]{1,0:T(8,128)S(1)} collective-permute-done((f32[64,128]{1,0:T(8,128)S(1)}, f32[64,128]{1,0:T(8,128)S(1)}, u32[]{:S(2)}, u32[]{:S(2)}) %collective-permute-start.10) | collective-permute-done | bytes 32800 | tf_op jit(solution)/shard_map/ppermute | solution.py:391
  40.5 0.0 collective-permute-start.11
  40.5 3.3 %collective-permute-done.11 = f32[64,128]{1,0:T(8,128)S(1)} collective-permute-done((f32[64,128]{1,0:T(8,128)S(1)}, f32[64,128]{1,0:T(8,128)S(1)}, u32[]{:S(2)}, u32[]{:S(2)}) %collective-permute-start.11) | collective-permute-done | bytes 32800 | tf_op jit(solution)/shard_map/ppermute | solution.py:391
  43.8 0.0 collective-permute-start.12
  43.8 4.8 %collective-permute-done.12 = f32[64,128]{1,0:T(8,128)S(1)} collective-permute-done((f32[64,128]{1,0:T(8,128)S(1)}, f32[64,128]{1,0:T(8,128)S(1)}, u32[]{:S(2)}, u32[]{:S(2)}) %collective-permute-start.12) | collective-permute-done | bytes 32800 | tf_op jit(solution)/shard_map/ppermute | solution.py:391
  48.6 0.1 collective-permute-start.13
  48.8 0.4 shard_map.114
  49.2 0.6 collective-permute-done.13.sums
  49.8 1.5 %shard_map.115 = (f32[64,128]{1,0:T(8,128)S(1)}, f32[1024,128]{1,0:T(8,128)S(1)}) custom-call(s32[16,24]{1,0:T(8,128)S(4)} %get-tuple-element.45.plan, bf16[128,160]{1,0:T(8,128)(2,1)S(1)} %get-tuple-element.46.hit_ref, f32[64,128]{1,0:T(8,128)S(1)} %collective-permute-done.13.sums, f32[64,128]{1,0:T(8,128)S(1)} %get-tuple-element.70.fb_ref, ...), custom_call_target="tpu_custom_call" | custom-call | tf_op jit(solution)/shard_map/pallas_call | solution.py:373
  51.3 0.1 collective-permute-start.14
  51.5 0.6 shard_map.116
  52.1 0.5 collective-permute-done.14
  52.6 0.0 collective-permute-start.15
  52.6 3.3 %collective-permute-done.15 = f32[64,128]{1,0:T(8,128)S(1)} collective-permute-done((f32[64,128]{1,0:T(8,128)S(1)}, f32[64,128]{1,0:T(8,128)S(1)}, u32[]{:S(2)}, u32[]{:S(2)}) %collective-permute-start.15) | collective-permute-done | bytes 32800 | tf_op jit(solution)/shard_map/ppermute | solution.py:391
  56.0 0.0 collective-permute-start.16
  56.0 3.3 %collective-permute-done.16 = f32[64,128]{1,0:T(8,128)S(1)} collective-permute-done((f32[64,128]{1,0:T(8,128)S(1)}, f32[64,128]{1,0:T(8,128)S(1)}, u32[]{:S(2)}, u32[]{:S(2)}) %collective-permute-start.16) | collective-permute-done | bytes 32800 | tf_op jit(solution)/shard_map/ppermute | solution.py:391
  59.3 0.0 collective-permute-start.17
  59.3 4.8 %collective-permute-done.17 = f32[64,128]{1,0:T(8,128)S(1)} collective-permute-done((f32[64,128]{1,0:T(8,128)S(1)}, f32[64,128]{1,0:T(8,128)S(1)}, u32[]{:S(2)}, u32[]{:S(2)}) %collective-permute-start.17) | collective-permute-done | bytes 32800 | tf_op jit(solution)/shard_map/ppermute | solution.py:391
  64.2 0.1 collective-permute-start.18
  64.3 0.1 shard_map.117
  64.3 1.0 %collective-permute-done.18.other = f32[64,128]{1,0:T(8,128)S(1)} collective-permute-done((f32[64,128]{1,0:T(8,128)S(1)}, f32[64,128]{1,0:T(8,128)S(1)}, u32[]{:S(2)}, u32[]{:S(2)}) %collective-permute-start.18) | collective-permute-done | bytes 32800 | tf_op jit(solution)/shard_map/ppermute | solution.py:391
  65.4 0.8 %shard_map.118 = (f32[8,128]{1,0:T(8,128)}, f32[8,128]{1,0:T(8,128)}) custom-call(f32[64,128]{1,0:T(8,128)S(1)} %collective-permute-done.18.other, f32[64,128]{1,0:T(8,128)S(1)} %get-tuple-element.70.fb_ref, f32[64,128]{1,0:T(8,128)S(1)} %get-tuple-element.71.et_ref, f32[8,128]{1,0:T(8,128)S(1)} %get-tuple-element.72.tot_ref, ...), custom_call_target="tpu_custom_call" | custom-call | tf_op jit(solution)/shard_map/pallas_call | solution.py:373
  (15 shorter events, 0.1 us)
Async XLA Ops:
  1.4 8.0 %collective-permute-start = (f32[24,128]{1,0:T(8,128)S(1)}, f32[24,128]{1,0:T(8,128)S(1)}, u32[]{:S(2)}, u32[]{:S(2)}) collective-permute-start(f32[24,128]{1,0:T(8,128)S(1)} %shard_map.105), channel_id=1, source_target_pairs={{0,9},{1,8},{2,11},{3,10},{4,13},{5,12},{6,15},{7,14},{8,1},{9,0},... | collective-permute-start | bytes 36872 | tf_op jit(solution)/shard_map/ppermute | solution.py:391
  9.5 4.0 %collective-permute-start.1 = (f32[48,128]{1,0:T(8,128)S(1)}, f32[48,128]{1,0:T(8,128)S(1)}, u32[]{:S(2)}, u32[]{:S(2)}) collective-permute-start(f32[48,128]{1,0:T(8,128)S(1)} %bitcast.20), channel_id=1, source_target_pairs={{0,5},{1,4},{2,7},{3,6},{4,1},{5,0},{6,3},{7,2},{8,13},{9,12},{10,... | collective-permute-start | bytes 73736 | tf_op jit(solution)/shard_map/ppermute | solution.py:391
  13.5 3.6 %collective-permute-start.2 = (f32[96,128]{1,0:T(8,128)S(1)}, f32[96,128]{1,0:T(8,128)S(1)}, u32[]{:S(2)}, u32[]{:S(2)}) collective-permute-start(f32[96,128]{1,0:T(8,128)S(1)} %bitcast.18), channel_id=1, source_target_pairs={{0,3},{1,2},{2,1},{3,0},{4,7},{5,6},{6,5},{7,4},{8,11},{9,10},{10,... | collective-permute-start | bytes 147464 | tf_op jit(solution)/shard_map/ppermute | solution.py:391
  17.1 1.6 %collective-permute-start.3 = (f32[192,128]{1,0:T(8,128)S(1)}, f32[192,128]{1,0:T(8,128)S(1)}, u32[]{:S(2)}, u32[]{:S(2)}) collective-permute-start(f32[192,128]{1,0:T(8,128)S(1)} %bitcast.15), channel_id=1, source_target_pairs={{0,1},{1,0},{2,3},{3,2},{4,5},{5,4},{6,7},{7,6},{8,9},{9,8},{10,11... | collective-permute-start | bytes 294920 | tf_op jit(solution)/shard_map/ppermute | solution.py:391
  20.2 1.3 %collective-permute-start.4 = (f32[64,128]{1,0:T(8,128)S(1)}, f32[64,128]{1,0:T(8,128)S(1)}, u32[]{:S(2)}, u32[]{:S(2)}) collective-permute-start(f32[64,128]{1,0:T(8,128)S(1)} %get-tuple-element.69), channel_id=1, source_target_pairs={{0,1},{1,0},{2,3},{3,2},{4,5},{5,4},{6,7},{7,6},{8,9},{9,8},{10,11... | collective-permute-start | bytes 98312 | tf_op jit(solution)/shard_map/ppermute | solution.py:391
  21.5 3.3 %collective-permute-start.5 = (f32[64,128]{1,0:T(8,128)S(1)}, f32[64,128]{1,0:T(8,128)S(1)}, u32[]{:S(2)}, u32[]{:S(2)}) collective-permute-start(f32[64,128]{1,0:T(8,128)S(1)} %add.36), channel_id=1, source_target_pairs={{0,3},{1,2},{2,1},{3,0},{4,7},{5,6},{6,5},{7,4},{8,11},{9,10},{10,... | collective-permute-start | bytes 98312 | tf_op jit(solution)/shard_map/ppermute | solution.py:391
  24.8 3.3 %collective-permute-start.6 = (f32[64,128]{1,0:T(8,128)S(1)}, f32[64,128]{1,0:T(8,128)S(1)}, u32[]{:S(2)}, u32[]{:S(2)}) collective-permute-start(f32[64,128]{1,0:T(8,128)S(1)} %add.37), channel_id=1, source_target_pairs={{0,5},{1,4},{2,7},{3,6},{4,1},{5,0},{6,3},{7,2},{8,13},{9,12},{10,... | collective-permute-start | bytes 98312 | tf_op jit(solution)/shard_map/ppermute | solution.py:391
  28.1 5.0 %collective-permute-start.7 = (f32[64,128]{1,0:T(8,128)S(1)}, f32[64,128]{1,0:T(8,128)S(1)}, u32[]{:S(2)}, u32[]{:S(2)}) collective-permute-start(f32[64,128]{1,0:T(8,128)S(1)} %add.38), channel_id=1, source_target_pairs={{0,9},{1,8},{2,11},{3,10},{4,13},{5,12},{6,15},{7,14},{8,1},{9,0},... | collective-permute-start | bytes 98312 | tf_op jit(solution)/shard_map/ppermute | solution.py:391
  33.1 1.2 %collective-permute-start.8 = (f32[64,128]{1,0:T(8,128)S(1)}, f32[64,128]{1,0:T(8,128)S(1)}, u32[]{:S(2)}, u32[]{:S(2)}) collective-permute-start(f32[64,128]{1,0:T(8,128)S(1)} %add.39.sums), channel_id=1, source_target_pairs={{0,1},{1,0},{2,3},{3,2},{4,5},{5,4},{6,7},{7,6},{8,9},{9,8},{10,11... | collective-permute-start | bytes 98312 | tf_op jit(solution)/shard_map/ppermute | solution.py:391
  35.8 1.3 %collective-permute-start.9 = (f32[64,128]{1,0:T(8,128)S(1)}, f32[64,128]{1,0:T(8,128)S(1)}, u32[]{:S(2)}, u32[]{:S(2)}) collective-permute-start(f32[64,128]{1,0:T(8,128)S(1)} %get-tuple-element.78), channel_id=1, source_target_pairs={{0,1},{1,0},{2,3},{3,2},{4,5},{5,4},{6,7},{7,6},{8,9},{9,8},{10,11... | collective-permute-start | bytes 98312 | tf_op jit(solution)/shard_map/ppermute | solution.py:391
  37.1 3.3 %collective-permute-start.10 = (f32[64,128]{1,0:T(8,128)S(1)}, f32[64,128]{1,0:T(8,128)S(1)}, u32[]{:S(2)}, u32[]{:S(2)}) collective-permute-start(f32[64,128]{1,0:T(8,128)S(1)} %add.40), channel_id=1, source_target_pairs={{0,3},{1,2},{2,1},{3,0},{4,7},{5,6},{6,5},{7,4},{8,11},{9,10},{10,... | collective-permute-start | bytes 98312 | tf_op jit(solution)/shard_map/ppermute | solution.py:391
  40.5 3.3 %collective-permute-start.11 = (f32[64,128]{1,0:T(8,128)S(1)}, f32[64,128]{1,0:T(8,128)S(1)}, u32[]{:S(2)}, u32[]{:S(2)}) collective-permute-start(f32[64,128]{1,0:T(8,128)S(1)} %add.41), channel_id=1, source_target_pairs={{0,5},{1,4},{2,7},{3,6},{4,1},{5,0},{6,3},{7,2},{8,13},{9,12},{10,... | collective-permute-start | bytes 98312 | tf_op jit(solution)/shard_map/ppermute | solution.py:391
  43.8 4.8 %collective-permute-start.12 = (f32[64,128]{1,0:T(8,128)S(1)}, f32[64,128]{1,0:T(8,128)S(1)}, u32[]{:S(2)}, u32[]{:S(2)}) collective-permute-start(f32[64,128]{1,0:T(8,128)S(1)} %add.42), channel_id=1, source_target_pairs={{0,9},{1,8},{2,11},{3,10},{4,13},{5,12},{6,15},{7,14},{8,1},{9,0},... | collective-permute-start | bytes 98312 | tf_op jit(solution)/shard_map/ppermute | solution.py:391
  48.6 1.2 %collective-permute-start.13 = (f32[64,128]{1,0:T(8,128)S(1)}, f32[64,128]{1,0:T(8,128)S(1)}, u32[]{:S(2)}, u32[]{:S(2)}) collective-permute-start(f32[64,128]{1,0:T(8,128)S(1)} %add.43.sums), channel_id=1, source_target_pairs={{0,1},{1,0},{2,3},{3,2},{4,5},{5,4},{6,7},{7,6},{8,9},{9,8},{10,11... | collective-permute-start | bytes 98312 | tf_op jit(solution)/shard_map/ppermute | solution.py:391
  51.3 1.3 %collective-permute-start.14 = (f32[64,128]{1,0:T(8,128)S(1)}, f32[64,128]{1,0:T(8,128)S(1)}, u32[]{:S(2)}, u32[]{:S(2)}) collective-permute-start(f32[64,128]{1,0:T(8,128)S(1)} %get-tuple-element.82), channel_id=1, source_target_pairs={{0,1},{1,0},{2,3},{3,2},{4,5},{5,4},{6,7},{7,6},{8,9},{9,8},{10,11... | collective-permute-start | bytes 98312 | tf_op jit(solution)/shard_map/ppermute | solution.py:391
  52.6 3.3 %collective-permute-start.15 = (f32[64,128]{1,0:T(8,128)S(1)}, f32[64,128]{1,0:T(8,128)S(1)}, u32[]{:S(2)}, u32[]{:S(2)}) collective-permute-start(f32[64,128]{1,0:T(8,128)S(1)} %add.44), channel_id=1, source_target_pairs={{0,3},{1,2},{2,1},{3,0},{4,7},{5,6},{6,5},{7,4},{8,11},{9,10},{10,... | collective-permute-start | bytes 98312 | tf_op jit(solution)/shard_map/ppermute | solution.py:391
  56.0 3.3 %collective-permute-start.16 = (f32[64,128]{1,0:T(8,128)S(1)}, f32[64,128]{1,0:T(8,128)S(1)}, u32[]{:S(2)}, u32[]{:S(2)}) collective-permute-start(f32[64,128]{1,0:T(8,128)S(1)} %add.45), channel_id=1, source_target_pairs={{0,5},{1,4},{2,7},{3,6},{4,1},{5,0},{6,3},{7,2},{8,13},{9,12},{10,... | collective-permute-start | bytes 98312 | tf_op jit(solution)/shard_map/ppermute | solution.py:391
  59.3 4.8 %collective-permute-start.17 = (f32[64,128]{1,0:T(8,128)S(1)}, f32[64,128]{1,0:T(8,128)S(1)}, u32[]{:S(2)}, u32[]{:S(2)}) collective-permute-start(f32[64,128]{1,0:T(8,128)S(1)} %add.46), channel_id=1, source_target_pairs={{0,9},{1,8},{2,11},{3,10},{4,13},{5,12},{6,15},{7,14},{8,1},{9,0},... | collective-permute-start | bytes 98312 | tf_op jit(solution)/shard_map/ppermute | solution.py:391
  64.2 1.2 %collective-permute-start.18 = (f32[64,128]{1,0:T(8,128)S(1)}, f32[64,128]{1,0:T(8,128)S(1)}, u32[]{:S(2)}, u32[]{:S(2)}) collective-permute-start(f32[64,128]{1,0:T(8,128)S(1)} %add.47.keep), channel_id=1, source_target_pairs={{0,1},{1,0},{2,3},{3,2},{4,5},{5,4},{6,7},{7,6},{8,9},{9,8},{10,11... | collective-permute-start | bytes 98312 | tf_op jit(solution)/shard_map/ppermute | solution.py:391

commit v11 on v9

--- a/solution.py
+++ b/solution.py
@@ -489,7 +489,7 @@
             own_columns, (plan, hit, u, *kern), (shape(half),), scratch=[col], smem=1
         )
         keep = keep + got
-        for d in order[-2::-1]:
+        for d in order[:-1]:
             keep = keep + exchange(keep, n, d)
         other = exchange(keep, n, order[-1])
         if iteration < ITERS - 1:

time: 66.3 us -> 65.4 us (0.986); the launches traced: 65.6 us -> 65.5 us
  starting transfers between devices: 18.5 us -> 11.8 us
  waiting for transfers between devices: 30 us -> 33.7 us
  Pallas kernels: 16.3 us -> 19 us
    ppermute x19, starting transfers between devices: 18.5 us -> 11.8 us  [exchange(): return lax.ppermute(x, 'src', [(i, i ^ d) for i in range(n)])]
    ppermute x19, waiting for transfers between devices: 30 us -> 33.7 us  [exchange(): return lax.ppermute(x, 'src', [(i, i ^ d) for i in range(n)])]
    pallas_call x15, Pallas kernels: 16.3 us -> 19 us  [call(): pl.pallas_call(kernel, out_shape=outs, in_specs=specs, out_specs=[pl.Bloc...]
  transfers between devices with their start and end apart: 19 -> 19, of which waited for: 16 -> 16; matrix products, arithmetic and copies ran while one was open for 0% -> 0% of each run, Pallas kernels for 16% -> 19%
where the time goes in v11:
time: 65.4 us; the launch traced here: 65.5 us
  waiting for transfers between devices  33.7 us (52%)
  Pallas kernels  19 us (29%)
  starting transfers between devices  11.8 us (18%)
  between operations  0.83 us (1%)
    ppermute x19, waiting for transfers between devices, exchange(): return lax.ppermute(x, 'src', [(i, i ^ d) for i in range(n)])  33.7 us
    pallas_call x15, Pallas kernels, call(): pl.pallas_call(kernel, out_shape=outs, in_specs=specs, out_specs=[pl.Bloc...  19 us
    ppermute x19, starting transfers between devices, exchange(): return lax.ppermute(x, 'src', [(i, i ^ d) for i in range(n)])  11.8 us
  transfers between devices with their start and end apart: 19, of which 16 were waited for; matrix products, arithmetic and copies ran while one was open for 0% of the time, Pallas kernels for 19%

profile of v11, /device:TPU:0, one launch (start us, length us, event | category | flops | bytes accessed | tf_op | source)
XLA Modules:
  0.0 65.5 jit_solution(17434117582990571339)
XLA Ops:
  0.6 0.8 %shard_map.105 = f32[24,128]{1,0:T(8,128)S(1)} custom-call(s32[8]{0:T(128)} %count_hbm.1, f32[8,128]{1,0:T(8,128)} %bitcast.28, f32[8,128]{1,0:T(8,128)} %bitcast.29, f32[8,128]{1,0:T(8,128)} %bitcast.24), custom_call_target="tpu_custom_call" | custom-call | tf_op jit(solution)/shard_map/pallas_call | solution.py:368
  1.4 3.5 %collective-permute-start = (f32[24,128]{1,0:T(8,128)S(1)}, f32[24,128]{1,0:T(8,128)S(1)}, u32[]{:S(2)}, u32[]{:S(2)}) collective-permute-start(f32[24,128]{1,0:T(8,128)S(1)} %shard_map.105), channel_id=1, source_target_pairs={{0,9},{1,8},{2,11},{3,10},{4,13},{5,12},{6,15},{7,14},{8,1},{9,0},... | collective-permute-start | bytes 36872 | tf_op jit(solution)/shard_map/ppermute | solution.py:386
  4.9 4.1 %shard_map.104 = (f32[4096,128]{1,0:T(8,128)S(1)}, f32[256,128]{1,0:T(8,128)S(1)}, bf16[3,16,128,256]{3,2,1,0:T(8,128)(2,1)S(1)}, s32[16,24]{1,0:T(8,128)S(4)}, ...) custom-call(s32[8]{0:T(128)} %live_hbm.1, ...), custom_call_target="tpu_custom_call" | custom-call | flops 268435456 | bytes 2097152 | tf_op jit(solution)/shard_map/pallas_call | solution.py:368
  9.0 0.0 collective-permute-done
  9.0 1.4 %collective-permute-start.1 = (f32[48,128]{1,0:T(8,128)S(1)}, f32[48,128]{1,0:T(8,128)S(1)}, u32[]{:S(2)}, u32[]{:S(2)}) collective-permute-start(f32[48,128]{1,0:T(8,128)S(1)} %bitcast.20), channel_id=1, source_target_pairs={{0,5},{1,4},{2,7},{3,6},{4,1},{5,0},{6,3},{7,2},{8,13},{9,12},{10,... | collective-permute-start | bytes 73736 | tf_op jit(solution)/shard_map/ppermute | solution.py:386
  10.5 2.4 %shard_map.106 = (f32[6144,128]{1,0:T(8,128)S(1)}, f32[384,128]{1,0:T(8,128)S(1)}, bf16[3,16,128,256]{3,2,1,0:T(8,128)(2,1)S(1)}) custom-call(s32[16,24]{1,0:T(8,128)S(4)} %get-tuple-element.45.plan, bf16[1024,256]{1,0:T(8,128)(2,1)S(1)} %get-tuple-element.50.x_ref, f32[8,128]{1,0:T(8,128)S(1)} %get-tuple-element.51.lin_ref, ...), custom_call_target="tpu_custom_call" | custom-call | flops 402653184 | bytes 3145728 | tf_op jit(solution)/shard_map/pallas_call | solution.py:368
  12.8 0.0 collective-permute-done.1
  12.8 2.2 %collective-permute-start.2 = (f32[96,128]{1,0:T(8,128)S(1)}, f32[96,128]{1,0:T(8,128)S(1)}, u32[]{:S(2)}, u32[]{:S(2)}) collective-permute-start(f32[96,128]{1,0:T(8,128)S(1)} %bitcast.18), channel_id=1, source_target_pairs={{0,3},{1,2},{2,1},{3,0},{4,7},{5,6},{6,5},{7,4},{8,11},{9,10},{10,... | collective-permute-start | bytes 147464 | tf_op jit(solution)/shard_map/ppermute | solution.py:386
  15.1 2.8 %shard_map.107 = (f32[6144,128]{1,0:T(8,128)S(1)}, f32[384,128]{1,0:T(8,128)S(1)}) custom-call(s32[16,24]{1,0:T(8,128)S(4)} %get-tuple-element.45.plan, bf16[1024,256]{1,0:T(8,128)(2,1)S(1)} %get-tuple-element.50.x_ref, f32[8,128]{1,0:T(8,128)S(1)} %get-tuple-element.51.lin_ref, f32[8,128]{1,0:T(8,128)S(1)} %get-tuple-element.52.mass_ref, ...), custom_call_target="tpu_custom_call" | custom-call | flops 402653184 | bytes 3145728 | tf_op jit(solution)/shard_map/pallas_call | solution.py:368
  17.9 0.0 collective-permute-done.2
  17.9 0.1 collective-permute-start.3
  18.0 0.5 shard_map.108
  18.5 0.8 %collective-permute-done.3.part = f32[192,128]{1,0:T(8,128)S(1)} collective-permute-done((f32[192,128]{1,0:T(8,128)S(1)}, f32[192,128]{1,0:T(8,128)S(1)}, u32[]{:S(2)}, u32[]{:S(2)}) %collective-permute-start.3) | collective-permute-done | bytes 98336 | tf_op jit(solution)/shard_map/ppermute | solution.py:386
  19.3 1.6 %shard_map.109 = (f32[64,128]{1,0:T(8,128)S(1)}, f32[1024,128]{1,0:T(8,128)S(1)}, f32[64,128]{1,0:T(8,128)S(1)}, f32[64,128]{1,0:T(8,128)S(1)}, f32[8,128]{1,0:T(8,128)S(1)}) custom-call(s32[16,24]{1,0:T(8,128)S(4)} %get-tuple-element.45.plan, bf16[128,128]{1,0:T(8,128)(2,1)S(1)} %get-tuple-element.46.hit_ref, f32[192,128]{1,0:T(8,128)S(1)} %collective-permute-done.3.part, ...), custom_call_target="tpu_custom_call" | custom-call | tf_op jit(solution)/shard_map/pallas_call | solution.py:368
  20.9 0.1 collective-permute-start.4
  21.0 0.7 %shard_map.110 = f32[64,128]{1,0:T(8,128)S(1)} custom-call(s32[16,24]{1,0:T(8,128)S(4)} %get-tuple-element.45.plan, bf16[128,128]{1,0:T(8,128)(2,1)S(1)} %get-tuple-element.46.hit_ref, f32[1024,128]{1,0:T(8,128)S(1)} %get-tuple-element.68.u_ref, f32[4096,128]{1,0:T(8,128)S(1)} %get-tuple-element.60.refs_0_, f32[6144,128]{1,0:T(8,128)S(1)} %get-tuple-element.61.refs_1_, ...), custom_call_target="tpu_custom_call" | custom-call | tf_op jit(solution)/shard_map/pallas_call | solution.py:368
  21.6 0.5 collective-permute-done.4
  22.2 0.0 collective-permute-start.5
  22.2 4.4 %collective-permute-done.5 = f32[64,128]{1,0:T(8,128)S(1)} collective-permute-done((f32[64,128]{1,0:T(8,128)S(1)}, f32[64,128]{1,0:T(8,128)S(1)}, u32[]{:S(2)}, u32[]{:S(2)}) %collective-permute-start.5) | collective-permute-done | bytes 32800 | tf_op jit(solution)/shard_map/ppermute | solution.py:386
  26.6 0.0 collective-permute-start.6
  26.6 3.4 %collective-permute-done.6 = f32[64,128]{1,0:T(8,128)S(1)} collective-permute-done((f32[64,128]{1,0:T(8,128)S(1)}, f32[64,128]{1,0:T(8,128)S(1)}, u32[]{:S(2)}, u32[]{:S(2)}) %collective-permute-start.6) | collective-permute-done | bytes 32800 | tf_op jit(solution)/shard_map/ppermute | solution.py:386
  30.0 1.1 %collective-permute-start.7 = (f32[64,128]{1,0:T(8,128)S(1)}, f32[64,128]{1,0:T(8,128)S(1)}, u32[]{:S(2)}, u32[]{:S(2)}) collective-permute-start(f32[64,128]{1,0:T(8,128)S(1)} %add.38), channel_id=1, source_target_pairs={{0,3},{1,2},{2,1},{3,0},{4,7},{5,6},{6,5},{7,4},{8,11},{9,10},{10,... | collective-permute-start | bytes 98312 | tf_op jit(solution)/shard_map/ppermute | solution.py:386
  31.1 2.3 %collective-permute-done.7 = f32[64,128]{1,0:T(8,128)S(1)} collective-permute-done((f32[64,128]{1,0:T(8,128)S(1)}, f32[64,128]{1,0:T(8,128)S(1)}, u32[]{:S(2)}, u32[]{:S(2)}) %collective-permute-start.7) | collective-permute-done | bytes 32800 | tf_op jit(solution)/shard_map/ppermute | solution.py:386
  33.4 0.1 collective-permute-start.8
  33.5 0.5 shard_map.111
  34.0 0.6 collective-permute-done.8.sums
  34.6 1.6 %shard_map.112 = (f32[64,128]{1,0:T(8,128)S(1)}, f32[1024,128]{1,0:T(8,128)S(1)}) custom-call(s32[16,24]{1,0:T(8,128)S(4)} %get-tuple-element.45.plan, bf16[128,128]{1,0:T(8,128)(2,1)S(1)} %get-tuple-element.46.hit_ref, f32[64,128]{1,0:T(8,128)S(1)} %collective-permute-done.8.sums, f32[64,128]{1,0:T(8,128)S(1)} %get-tuple-element.70.fb_ref, ...), custom_call_target="tpu_custom_call" | custom-call | tf_op jit(solution)/shard_map/pallas_call | solution.py:368
  36.2 0.1 collective-permute-start.9
  36.3 0.7 %shard_map.113 = f32[64,128]{1,0:T(8,128)S(1)} custom-call(s32[16,24]{1,0:T(8,128)S(4)} %get-tuple-element.45.plan, bf16[128,128]{1,0:T(8,128)(2,1)S(1)} %get-tuple-element.46.hit_ref, f32[1024,128]{1,0:T(8,128)S(1)} %get-tuple-element.77.u_ref, f32[4096,128]{1,0:T(8,128)S(1)} %get-tuple-element.60.refs_0_, f32[6144,128]{1,0:T(8,128)S(1)} %get-tuple-element.61.refs_1_, ...), custom_call_target="tpu_custom_call" | custom-call | tf_op jit(solution)/shard_map/pallas_call | solution.py:368
  36.9 0.5 collective-permute-done.9
  37.5 0.0 collective-permute-start.10
  37.5 4.2 %collective-permute-done.10 = f32[64,128]{1,0:T(8,128)S(1)} collective-permute-done((f32[64,128]{1,0:T(8,128)S(1)}, f32[64,128]{1,0:T(8,128)S(1)}, u32[]{:S(2)}, u32[]{:S(2)}) %collective-permute-start.10) | collective-permute-done | bytes 32800 | tf_op jit(solution)/shard_map/ppermute | solution.py:386
  41.7 0.0 collective-permute-start.11
  41.7 3.3 %collective-permute-done.11 = f32[64,128]{1,0:T(8,128)S(1)} collective-permute-done((f32[64,128]{1,0:T(8,128)S(1)}, f32[64,128]{1,0:T(8,128)S(1)}, u32[]{:S(2)}, u32[]{:S(2)}) %collective-permute-start.11) | collective-permute-done | bytes 32800 | tf_op jit(solution)/shard_map/ppermute | solution.py:386
  45.1 1.3 %collective-permute-start.12 = (f32[64,128]{1,0:T(8,128)S(1)}, f32[64,128]{1,0:T(8,128)S(1)}, u32[]{:S(2)}, u32[]{:S(2)}) collective-permute-start(f32[64,128]{1,0:T(8,128)S(1)} %add.42), channel_id=1, source_target_pairs={{0,3},{1,2},{2,1},{3,0},{4,7},{5,6},{6,5},{7,4},{8,11},{9,10},{10,... | collective-permute-start | bytes 98312 | tf_op jit(solution)/shard_map/ppermute | solution.py:386
  46.3 2.1 %collective-permute-done.12 = f32[64,128]{1,0:T(8,128)S(1)} collective-permute-done((f32[64,128]{1,0:T(8,128)S(1)}, f32[64,128]{1,0:T(8,128)S(1)}, u32[]{:S(2)}, u32[]{:S(2)}) %collective-permute-start.12) | collective-permute-done | bytes 32800 | tf_op jit(solution)/shard_map/ppermute | solution.py:386
  48.4 0.2 collective-permute-start.13
  48.6 0.5 shard_map.114
  49.1 0.6 collective-permute-done.13.sums
  49.6 1.6 %shard_map.115 = (f32[64,128]{1,0:T(8,128)S(1)}, f32[1024,128]{1,0:T(8,128)S(1)}) custom-call(s32[16,24]{1,0:T(8,128)S(4)} %get-tuple-element.45.plan, bf16[128,128]{1,0:T(8,128)(2,1)S(1)} %get-tuple-element.46.hit_ref, f32[64,128]{1,0:T(8,128)S(1)} %collective-permute-done.13.sums, f32[64,128]{1,0:T(8,128)S(1)} %get-tuple-element.70.fb_ref, ...), custom_call_target="tpu_custom_call" | custom-call | tf_op jit(solution)/shard_map/pallas_call | solution.py:368
  51.2 0.1 collective-permute-start.14
  51.3 0.7 %shard_map.116 = f32[64,128]{1,0:T(8,128)S(1)} custom-call(s32[16,24]{1,0:T(8,128)S(4)} %get-tuple-element.45.plan, bf16[128,128]{1,0:T(8,128)(2,1)S(1)} %get-tuple-element.46.hit_ref, f32[1024,128]{1,0:T(8,128)S(1)} %get-tuple-element.81.u_ref, f32[4096,128]{1,0:T(8,128)S(1)} %get-tuple-element.60.refs_0_, f32[6144,128]{1,0:T(8,128)S(1)} %get-tuple-element.61.refs_1_, ...), custom_call_target="tpu_custom_call" | custom-call | tf_op jit(solution)/shard_map/pallas_call | solution.py:368
  52.0 0.5 collective-permute-done.14
  52.5 0.0 collective-permute-start.15
  52.5 4.3 %collective-permute-done.15 = f32[64,128]{1,0:T(8,128)S(1)} collective-permute-done((f32[64,128]{1,0:T(8,128)S(1)}, f32[64,128]{1,0:T(8,128)S(1)}, u32[]{:S(2)}, u32[]{:S(2)}) %collective-permute-start.15) | collective-permute-done | bytes 32800 | tf_op jit(solution)/shard_map/ppermute | solution.py:386
  56.8 0.0 collective-permute-start.16
  56.8 3.3 %collective-permute-done.16 = f32[64,128]{1,0:T(8,128)S(1)} collective-permute-done((f32[64,128]{1,0:T(8,128)S(1)}, f32[64,128]{1,0:T(8,128)S(1)}, u32[]{:S(2)}, u32[]{:S(2)}) %collective-permute-start.16) | collective-permute-done | bytes 32800 | tf_op jit(solution)/shard_map/ppermute | solution.py:386
  60.1 1.4 %collective-permute-start.17 = (f32[64,128]{1,0:T(8,128)S(1)}, f32[64,128]{1,0:T(8,128)S(1)}, u32[]{:S(2)}, u32[]{:S(2)}) collective-permute-start(f32[64,128]{1,0:T(8,128)S(1)} %add.46), channel_id=1, source_target_pairs={{0,3},{1,2},{2,1},{3,0},{4,7},{5,6},{6,5},{7,4},{8,11},{9,10},{10,... | collective-permute-start | bytes 98312 | tf_op jit(solution)/shard_map/ppermute | solution.py:386
  61.6 1.9 %collective-permute-done.17 = f32[64,128]{1,0:T(8,128)S(1)} collective-permute-done((f32[64,128]{1,0:T(8,128)S(1)}, f32[64,128]{1,0:T(8,128)S(1)}, u32[]{:S(2)}, u32[]{:S(2)}) %collective-permute-start.17) | collective-permute-done | bytes 32800 | tf_op jit(solution)/shard_map/ppermute | solution.py:386
  63.5 0.2 collective-permute-start.18
  63.7 0.1 shard_map.117
  63.7 1.0 %collective-permute-done.18.other = f32[64,128]{1,0:T(8,128)S(1)} collective-permute-done((f32[64,128]{1,0:T(8,128)S(1)}, f32[64,128]{1,0:T(8,128)S(1)}, u32[]{:S(2)}, u32[]{:S(2)}) %collective-permute-start.18) | collective-permute-done | bytes 32800 | tf_op jit(solution)/shard_map/ppermute | solution.py:386
  64.7 0.8 %shard_map.118 = (f32[8,128]{1,0:T(8,128)}, f32[8,128]{1,0:T(8,128)}) custom-call(f32[64,128]{1,0:T(8,128)S(1)} %collective-permute-done.18.other, f32[64,128]{1,0:T(8,128)S(1)} %get-tuple-element.70.fb_ref, f32[64,128]{1,0:T(8,128)S(1)} %get-tuple-element.71.et_ref, f32[8,128]{1,0:T(8,128)S(1)} %get-tuple-element.72.tot_ref, ...), custom_call_target="tpu_custom_call" | custom-call | tf_op jit(solution)/shard_map/pallas_call | solution.py:368
  (15 shorter events, 0.1 us)
Async XLA Ops:
  1.4 7.6 %collective-permute-start = (f32[24,128]{1,0:T(8,128)S(1)}, f32[24,128]{1,0:T(8,128)S(1)}, u32[]{:S(2)}, u32[]{:S(2)}) collective-permute-start(f32[24,128]{1,0:T(8,128)S(1)} %shard_map.105), channel_id=1, source_target_pairs={{0,9},{1,8},{2,11},{3,10},{4,13},{5,12},{6,15},{7,14},{8,1},{9,0},... | collective-permute-start | bytes 36872 | tf_op jit(solution)/shard_map/ppermute | solution.py:386
  9.0 3.8 %collective-permute-start.1 = (f32[48,128]{1,0:T(8,128)S(1)}, f32[48,128]{1,0:T(8,128)S(1)}, u32[]{:S(2)}, u32[]{:S(2)}) collective-permute-start(f32[48,128]{1,0:T(8,128)S(1)} %bitcast.20), channel_id=1, source_target_pairs={{0,5},{1,4},{2,7},{3,6},{4,1},{5,0},{6,3},{7,2},{8,13},{9,12},{10,... | collective-permute-start | bytes 73736 | tf_op jit(solution)/shard_map/ppermute | solution.py:386
  12.8 5.1 %collective-permute-start.2 = (f32[96,128]{1,0:T(8,128)S(1)}, f32[96,128]{1,0:T(8,128)S(1)}, u32[]{:S(2)}, u32[]{:S(2)}) collective-permute-start(f32[96,128]{1,0:T(8,128)S(1)} %bitcast.18), channel_id=1, source_target_pairs={{0,3},{1,2},{2,1},{3,0},{4,7},{5,6},{6,5},{7,4},{8,11},{9,10},{10,... | collective-permute-start | bytes 147464 | tf_op jit(solution)/shard_map/ppermute | solution.py:386
  17.9 1.4 %collective-permute-start.3 = (f32[192,128]{1,0:T(8,128)S(1)}, f32[192,128]{1,0:T(8,128)S(1)}, u32[]{:S(2)}, u32[]{:S(2)}) collective-permute-start(f32[192,128]{1,0:T(8,128)S(1)} %bitcast.15), channel_id=1, source_target_pairs={{0,1},{1,0},{2,3},{3,2},{4,5},{5,4},{6,7},{7,6},{8,9},{9,8},{10,11... | collective-permute-start | bytes 294920 | tf_op jit(solution)/shard_map/ppermute | solution.py:386
  20.9 1.3 %collective-permute-start.4 = (f32[64,128]{1,0:T(8,128)S(1)}, f32[64,128]{1,0:T(8,128)S(1)}, u32[]{:S(2)}, u32[]{:S(2)}) collective-permute-start(f32[64,128]{1,0:T(8,128)S(1)} %get-tuple-element.69), channel_id=1, source_target_pairs={{0,1},{1,0},{2,3},{3,2},{4,5},{5,4},{6,7},{7,6},{8,9},{9,8},{10,11... | collective-permute-start | bytes 98312 | tf_op jit(solution)/shard_map/ppermute | solution.py:386
  22.2 4.4 %collective-permute-start.5 = (f32[64,128]{1,0:T(8,128)S(1)}, f32[64,128]{1,0:T(8,128)S(1)}, u32[]{:S(2)}, u32[]{:S(2)}) collective-permute-start(f32[64,128]{1,0:T(8,128)S(1)} %add.36), channel_id=1, source_target_pairs={{0,9},{1,8},{2,11},{3,10},{4,13},{5,12},{6,15},{7,14},{8,1},{9,0},... | collective-permute-start | bytes 98312 | tf_op jit(solution)/shard_map/ppermute | solution.py:386
  26.6 3.4 %collective-permute-start.6 = (f32[64,128]{1,0:T(8,128)S(1)}, f32[64,128]{1,0:T(8,128)S(1)}, u32[]{:S(2)}, u32[]{:S(2)}) collective-permute-start(f32[64,128]{1,0:T(8,128)S(1)} %add.37), channel_id=1, source_target_pairs={{0,5},{1,4},{2,7},{3,6},{4,1},{5,0},{6,3},{7,2},{8,13},{9,12},{10,... | collective-permute-start | bytes 98312 | tf_op jit(solution)/shard_map/ppermute | solution.py:386
  30.0 3.4 %collective-permute-start.7 = (f32[64,128]{1,0:T(8,128)S(1)}, f32[64,128]{1,0:T(8,128)S(1)}, u32[]{:S(2)}, u32[]{:S(2)}) collective-permute-start(f32[64,128]{1,0:T(8,128)S(1)} %add.38), channel_id=1, source_target_pairs={{0,3},{1,2},{2,1},{3,0},{4,7},{5,6},{6,5},{7,4},{8,11},{9,10},{10,... | collective-permute-start | bytes 98312 | tf_op jit(solution)/shard_map/ppermute | solution.py:386
  33.4 1.2 %collective-permute-start.8 = (f32[64,128]{1,0:T(8,128)S(1)}, f32[64,128]{1,0:T(8,128)S(1)}, u32[]{:S(2)}, u32[]{:S(2)}) collective-permute-start(f32[64,128]{1,0:T(8,128)S(1)} %add.39.sums), channel_id=1, source_target_pairs={{0,1},{1,0},{2,3},{3,2},{4,5},{5,4},{6,7},{7,6},{8,9},{9,8},{10,11... | collective-permute-start | bytes 98312 | tf_op jit(solution)/shard_map/ppermute | solution.py:386
  36.2 1.3 %collective-permute-start.9 = (f32[64,128]{1,0:T(8,128)S(1)}, f32[64,128]{1,0:T(8,128)S(1)}, u32[]{:S(2)}, u32[]{:S(2)}) collective-permute-start(f32[64,128]{1,0:T(8,128)S(1)} %get-tuple-element.78), channel_id=1, source_target_pairs={{0,1},{1,0},{2,3},{3,2},{4,5},{5,4},{6,7},{7,6},{8,9},{9,8},{10,11... | collective-permute-start | bytes 98312 | tf_op jit(solution)/shard_map/ppermute | solution.py:386
  37.5 4.2 %collective-permute-start.10 = (f32[64,128]{1,0:T(8,128)S(1)}, f32[64,128]{1,0:T(8,128)S(1)}, u32[]{:S(2)}, u32[]{:S(2)}) collective-permute-start(f32[64,128]{1,0:T(8,128)S(1)} %add.40), channel_id=1, source_target_pairs={{0,9},{1,8},{2,11},{3,10},{4,13},{5,12},{6,15},{7,14},{8,1},{9,0},... | collective-permute-start | bytes 98312 | tf_op jit(solution)/shard_map/ppermute | solution.py:386
  41.7 3.3 %collective-permute-start.11 = (f32[64,128]{1,0:T(8,128)S(1)}, f32[64,128]{1,0:T(8,128)S(1)}, u32[]{:S(2)}, u32[]{:S(2)}) collective-permute-start(f32[64,128]{1,0:T(8,128)S(1)} %add.41), channel_id=1, source_target_pairs={{0,5},{1,4},{2,7},{3,6},{4,1},{5,0},{6,3},{7,2},{8,13},{9,12},{10,... | collective-permute-start | bytes 98312 | tf_op jit(solution)/shard_map/ppermute | solution.py:386
  45.1 3.3 %collective-permute-start.12 = (f32[64,128]{1,0:T(8,128)S(1)}, f32[64,128]{1,0:T(8,128)S(1)}, u32[]{:S(2)}, u32[]{:S(2)}) collective-permute-start(f32[64,128]{1,0:T(8,128)S(1)} %add.42), channel_id=1, source_target_pairs={{0,3},{1,2},{2,1},{3,0},{4,7},{5,6},{6,5},{7,4},{8,11},{9,10},{10,... | collective-permute-start | bytes 98312 | tf_op jit(solution)/shard_map/ppermute | solution.py:386
  48.4 1.2 %collective-permute-start.13 = (f32[64,128]{1,0:T(8,128)S(1)}, f32[64,128]{1,0:T(8,128)S(1)}, u32[]{:S(2)}, u32[]{:S(2)}) collective-permute-start(f32[64,128]{1,0:T(8,128)S(1)} %add.43.sums), channel_id=1, source_target_pairs={{0,1},{1,0},{2,3},{3,2},{4,5},{5,4},{6,7},{7,6},{8,9},{9,8},{10,11... | collective-permute-start | bytes 98312 | tf_op jit(solution)/shard_map/ppermute | solution.py:386
  51.2 1.3 %collective-permute-start.14 = (f32[64,128]{1,0:T(8,128)S(1)}, f32[64,128]{1,0:T(8,128)S(1)}, u32[]{:S(2)}, u32[]{:S(2)}) collective-permute-start(f32[64,128]{1,0:T(8,128)S(1)} %get-tuple-element.82), channel_id=1, source_target_pairs={{0,1},{1,0},{2,3},{3,2},{4,5},{5,4},{6,7},{7,6},{8,9},{9,8},{10,11... | collective-permute-start | bytes 98312 | tf_op jit(solution)/shard_map/ppermute | solution.py:386
  52.5 4.3 %collective-permute-start.15 = (f32[64,128]{1,0:T(8,128)S(1)}, f32[64,128]{1,0:T(8,128)S(1)}, u32[]{:S(2)}, u32[]{:S(2)}) collective-permute-start(f32[64,128]{1,0:T(8,128)S(1)} %add.44), channel_id=1, source_target_pairs={{0,9},{1,8},{2,11},{3,10},{4,13},{5,12},{6,15},{7,14},{8,1},{9,0},... | collective-permute-start | bytes 98312 | tf_op jit(solution)/shard_map/ppermute | solution.py:386
  56.8 3.4 %collective-permute-start.16 = (f32[64,128]{1,0:T(8,128)S(1)}, f32[64,128]{1,0:T(8,128)S(1)}, u32[]{:S(2)}, u32[]{:S(2)}) collective-permute-start(f32[64,128]{1,0:T(8,128)S(1)} %add.45), channel_id=1, source_target_pairs={{0,5},{1,4},{2,7},{3,6},{4,1},{5,0},{6,3},{7,2},{8,13},{9,12},{10,... | collective-permute-start | bytes 98312 | tf_op jit(solution)/shard_map/ppermute | solution.py:386
  60.1 3.4 %collective-permute-start.17 = (f32[64,128]{1,0:T(8,128)S(1)}, f32[64,128]{1,0:T(8,128)S(1)}, u32[]{:S(2)}, u32[]{:S(2)}) collective-permute-start(f32[64,128]{1,0:T(8,128)S(1)} %add.46), channel_id=1, source_target_pairs={{0,3},{1,2},{2,1},{3,0},{4,7},{5,6},{6,5},{7,4},{8,11},{9,10},{10,... | collective-permute-start | bytes 98312 | tf_op jit(solution)/shard_map/ppermute | solution.py:386
  63.5 1.2 %collective-permute-start.18 = (f32[64,128]{1,0:T(8,128)S(1)}, f32[64,128]{1,0:T(8,128)S(1)}, u32[]{:S(2)}, u32[]{:S(2)}) collective-permute-start(f32[64,128]{1,0:T(8,128)S(1)} %add.47.keep), channel_id=1, source_target_pairs={{0,1},{1,0},{2,3},{3,2},{4,5},{5,4},{6,7},{7,6},{8,9},{9,8},{10,11... | collective-permute-start | bytes 98312 | tf_op jit(solution)/shard_map/ppermute | solution.py:386

commit v12 on v11

--- a/solution.py
+++ b/solution.py
@@ -15,7 +15,7 @@
 LOG2E = 1.4426950408889634
 STEP = 4
 ABSENT = -1e30
-PIECES = (2, 3, 3)
+PIECES = (2, 3, 2, 1)
 
 VMEM = pltpu.VMEM
 SMEM = pltpu.SMEM

time: 65.4 us -> 66 us (level)
  the two profiles are of different devices: /device:TPU:0 before, /device:TPU:3 now
where the time goes in v12:
time: 66 us; the launch traced here: 65.8 us
  waiting for transfers between devices  38.6 us (58%)
  Pallas kernels  18.2 us (28%)
  starting transfers between devices  8.1 us (12%)
  between operations  0.79 us (1%)
    ppermute x19, waiting for transfers between devices, exchange(): return lax.ppermute(x, 'src', [(i, i ^ d) for i in range(n)])  38.6 us
    pallas_call x16, Pallas kernels, call(): pl.pallas_call(kernel, out_shape=outs, in_specs=specs, out_specs=[pl.Bloc...  18.2 us
    ppermute x19, starting transfers between devices, exchange(): return lax.ppermute(x, 'src', [(i, i ^ d) for i in range(n)])  8.1 us
  transfers between devices with their start and end apart: 19, of which 17 were waited for; matrix products, arithmetic and copies ran while one was open for 0% of the time, Pallas kernels for 19%

profile of v12, /device:TPU:3, one launch (start us, length us, event | category | flops | bytes accessed | tf_op | source)
XLA Modules:
  0.0 65.8 jit_solution(6197858332219758958)
XLA Ops:
  0.6 0.8 %shard_map.105 = f32[24,128]{1,0:T(8,128)S(1)} custom-call(s32[8]{0:T(128)} %count_hbm.1, f32[8,128]{1,0:T(8,128)} %bitcast.28, f32[8,128]{1,0:T(8,128)} %bitcast.29, f32[8,128]{1,0:T(8,128)} %bitcast.24), custom_call_target="tpu_custom_call" | custom-call | tf_op jit(solution)/shard_map/pallas_call | solution.py:368
  1.4 2.9 %collective-permute-start = (f32[24,128]{1,0:T(8,128)S(1)}, f32[24,128]{1,0:T(8,128)S(1)}, u32[]{:S(2)}, u32[]{:S(2)}) collective-permute-start(f32[24,128]{1,0:T(8,128)S(1)} %shard_map.105), channel_id=1, source_target_pairs={{0,9},{1,8},{2,11},{3,10},{4,13},{5,12},{6,15},{7,14},{8,1},{9,0},... | collective-permute-start | bytes 36872 | tf_op jit(solution)/shard_map/ppermute | solution.py:386
  4.3 4.3 %shard_map.104 = (f32[4096,128]{1,0:T(8,128)S(1)}, f32[256,128]{1,0:T(8,128)S(1)}, bf16[3,16,128,256]{3,2,1,0:T(8,128)(2,1)S(1)}, s32[16,24]{1,0:T(8,128)S(4)}, ...) custom-call(s32[8]{0:T(128)} %live_hbm.1, ...), custom_call_target="tpu_custom_call" | custom-call | flops 268435456 | bytes 2097152 | tf_op jit(solution)/shard_map/pallas_call | solution.py:368
  8.6 0.0 collective-permute-done
  8.7 0.4 collective-permute-start.1
  9.0 1.9 %shard_map.106 = (f32[6144,128]{1,0:T(8,128)S(1)}, f32[384,128]{1,0:T(8,128)S(1)}, bf16[2,16,128,256]{3,2,1,0:T(8,128)(2,1)S(1)}) custom-call(s32[16,24]{1,0:T(8,128)S(4)} %get-tuple-element.49.plan, bf16[1024,256]{1,0:T(8,128)(2,1)S(1)} %get-tuple-element.54.x_ref, f32[8,128]{1,0:T(8,128)S(1)} %get-tuple-element.55.lin_ref, ...), custom_call_target="tpu_custom_call" | custom-call | flops 402653184 | bytes 3145728 | tf_op jit(solution)/shard_map/pallas_call | solution.py:368
  10.9 1.1 %collective-permute-done.1 = f32[48,128]{1,0:T(8,128)S(1)} collective-permute-done((f32[48,128]{1,0:T(8,128)S(1)}, f32[48,128]{1,0:T(8,128)S(1)}, u32[]{:S(2)}, u32[]{:S(2)}) %collective-permute-start.1) | collective-permute-done | bytes 24608 | tf_op jit(solution)/shard_map/ppermute | solution.py:386
  12.0 1.0 %collective-permute-start.2 = (f32[96,128]{1,0:T(8,128)S(1)}, f32[96,128]{1,0:T(8,128)S(1)}, u32[]{:S(2)}, u32[]{:S(2)}) collective-permute-start(f32[96,128]{1,0:T(8,128)S(1)} %bitcast.18), channel_id=1, source_target_pairs={{0,3},{1,2},{2,1},{3,0},{4,7},{5,6},{6,5},{7,4},{8,11},{9,10},{10,... | collective-permute-start | bytes 147464 | tf_op jit(solution)/shard_map/ppermute | solution.py:386
  13.0 2.0 %shard_map.107 = (f32[4096,128]{1,0:T(8,128)S(1)}, f32[256,128]{1,0:T(8,128)S(1)}, bf16[1,16,128,256]{3,2,1,0:T(8,128)(2,1)S(1)}) custom-call(s32[16,24]{1,0:T(8,128)S(4)} %get-tuple-element.49.plan, bf16[1024,256]{1,0:T(8,128)(2,1)S(1)} %get-tuple-element.54.x_ref, f32[8,128]{1,0:T(8,128)S(1)} %get-tuple-element.55.lin_ref, ...), custom_call_target="tpu_custom_call" | custom-call | flops 268435456 | bytes 2097152 | tf_op jit(solution)/shard_map/pallas_call | solution.py:368
  15.0 1.1 %collective-permute-done.2 = f32[96,128]{1,0:T(8,128)S(1)} collective-permute-done((f32[96,128]{1,0:T(8,128)S(1)}, f32[96,128]{1,0:T(8,128)S(1)}, u32[]{:S(2)}, u32[]{:S(2)}) %collective-permute-start.2) | collective-permute-done | bytes 49184 | tf_op jit(solution)/shard_map/ppermute | solution.py:386
  16.1 0.7 collective-permute-start.3
  16.8 0.6 shard_map.108
  17.4 0.5 shard_map.109
  17.9 0.0 collective-permute-done.3.part
  18.0 1.3 %shard_map.110 = (f32[64,128]{1,0:T(8,128)S(1)}, f32[1024,128]{1,0:T(8,128)S(1)}, f32[64,128]{1,0:T(8,128)S(1)}, f32[64,128]{1,0:T(8,128)S(1)}, f32[8,128]{1,0:T(8,128)S(1)}) custom-call(s32[16,24]{1,0:T(8,128)S(4)} %get-tuple-element.49.plan, bf16[128,128]{1,0:T(8,128)(2,1)S(1)} %get-tuple-element.50.hit_ref, f32[192,128]{1,0:T(8,128)S(1)} %collective-permute-done.3.part, ...), custom_call_target="tpu_custom_call" | custom-call | tf_op jit(solution)/shard_map/pallas_call | solution.py:368
  19.3 0.5 collective-permute-start.4
  19.8 0.7 %shard_map.111 = f32[64,128]{1,0:T(8,128)S(1)} custom-call(s32[16,24]{1,0:T(8,128)S(4)} %get-tuple-element.49.plan, bf16[128,128]{1,0:T(8,128)(2,1)S(1)} %get-tuple-element.50.hit_ref, f32[1024,128]{1,0:T(8,128)S(1)} %get-tuple-element.76.u_ref, f32[4096,128]{1,0:T(8,128)S(1)} %get-tuple-element.65.refs_0_, f32[6144,128]{1,0:T(8,128)S(1)} %get-tuple-element.66.refs_1_, ...), custom_call_target="tpu_custom_call" | custom-call | tf_op jit(solution)/shard_map/pallas_call | solution.py:368
  20.5 0.1 collective-permute-done.4
  20.6 0.5 collective-permute-start.5
  21.1 4.5 %collective-permute-done.5 = f32[64,128]{1,0:T(8,128)S(1)} collective-permute-done((f32[64,128]{1,0:T(8,128)S(1)}, f32[64,128]{1,0:T(8,128)S(1)}, u32[]{:S(2)}, u32[]{:S(2)}) %collective-permute-start.5) | collective-permute-done | bytes 32800 | tf_op jit(solution)/shard_map/ppermute | solution.py:386
  25.6 0.3 collective-permute-start.6
  25.9 3.1 %collective-permute-done.6 = f32[64,128]{1,0:T(8,128)S(1)} collective-permute-done((f32[64,128]{1,0:T(8,128)S(1)}, f32[64,128]{1,0:T(8,128)S(1)}, u32[]{:S(2)}, u32[]{:S(2)}) %collective-permute-start.6) | collective-permute-done | bytes 32800 | tf_op jit(solution)/shard_map/ppermute | solution.py:386
  28.9 0.0 collective-permute-start.7
  28.9 3.3 %collective-permute-done.7 = f32[64,128]{1,0:T(8,128)S(1)} collective-permute-done((f32[64,128]{1,0:T(8,128)S(1)}, f32[64,128]{1,0:T(8,128)S(1)}, u32[]{:S(2)}, u32[]{:S(2)}) %collective-permute-start.7) | collective-permute-done | bytes 32800 | tf_op jit(solution)/shard_map/ppermute | solution.py:386
  32.3 0.0 collective-permute-start.8
  32.3 0.5 shard_map.112
  32.8 0.7 %collective-permute-done.8.sums = f32[64,128]{1,0:T(8,128)S(1)} collective-permute-done((f32[64,128]{1,0:T(8,128)S(1)}, f32[64,128]{1,0:T(8,128)S(1)}, u32[]{:S(2)}, u32[]{:S(2)}) %collective-permute-start.8) | collective-permute-done | bytes 32800 | tf_op jit(solution)/shard_map/ppermute | solution.py:386
  33.5 1.4 %shard_map.113 = (f32[64,128]{1,0:T(8,128)S(1)}, f32[1024,128]{1,0:T(8,128)S(1)}) custom-call(s32[16,24]{1,0:T(8,128)S(4)} %get-tuple-element.49.plan, bf16[128,128]{1,0:T(8,128)(2,1)S(1)} %get-tuple-element.50.hit_ref, f32[64,128]{1,0:T(8,128)S(1)} %collective-permute-done.8.sums, f32[64,128]{1,0:T(8,128)S(1)} %get-tuple-element.78.fb_ref, ...), custom_call_target="tpu_custom_call" | custom-call | tf_op jit(solution)/shard_map/pallas_call | solution.py:368
  34.9 0.4 collective-permute-start.9
  35.3 0.7 %shard_map.114 = f32[64,128]{1,0:T(8,128)S(1)} custom-call(s32[16,24]{1,0:T(8,128)S(4)} %get-tuple-element.49.plan, bf16[128,128]{1,0:T(8,128)(2,1)S(1)} %get-tuple-element.50.hit_ref, f32[1024,128]{1,0:T(8,128)S(1)} %get-tuple-element.85.u_ref, f32[4096,128]{1,0:T(8,128)S(1)} %get-tuple-element.65.refs_0_, f32[6144,128]{1,0:T(8,128)S(1)} %get-tuple-element.66.refs_1_, ...), custom_call_target="tpu_custom_call" | custom-call | tf_op jit(solution)/shard_map/pallas_call | solution.py:368
  36.0 0.1 collective-permute-done.9
  36.1 0.0 collective-permute-start.10
  36.1 5.1 %collective-permute-done.10 = f32[64,128]{1,0:T(8,128)S(1)} collective-permute-done((f32[64,128]{1,0:T(8,128)S(1)}, f32[64,128]{1,0:T(8,128)S(1)}, u32[]{:S(2)}, u32[]{:S(2)}) %collective-permute-start.10) | collective-permute-done | bytes 32800 | tf_op jit(solution)/shard_map/ppermute | solution.py:386
  41.3 0.0 collective-permute-start.11
  41.3 3.4 %collective-permute-done.11 = f32[64,128]{1,0:T(8,128)S(1)} collective-permute-done((f32[64,128]{1,0:T(8,128)S(1)}, f32[64,128]{1,0:T(8,128)S(1)}, u32[]{:S(2)}, u32[]{:S(2)}) %collective-permute-start.11) | collective-permute-done | bytes 32800 | tf_op jit(solution)/shard_map/ppermute | solution.py:386
  44.7 0.1 collective-permute-start.12
  44.8 3.3 %collective-permute-done.12 = f32[64,128]{1,0:T(8,128)S(1)} collective-permute-done((f32[64,128]{1,0:T(8,128)S(1)}, f32[64,128]{1,0:T(8,128)S(1)}, u32[]{:S(2)}, u32[]{:S(2)}) %collective-permute-start.12) | collective-permute-done | bytes 32800 | tf_op jit(solution)/shard_map/ppermute | solution.py:386
  48.1 0.4 collective-permute-start.13
  48.5 0.5 shard_map.115
  49.0 0.3 collective-permute-done.13.sums
  49.3 1.4 %shard_map.116 = (f32[64,128]{1,0:T(8,128)S(1)}, f32[1024,128]{1,0:T(8,128)S(1)}) custom-call(s32[16,24]{1,0:T(8,128)S(4)} %get-tuple-element.49.plan, bf16[128,128]{1,0:T(8,128)(2,1)S(1)} %get-tuple-element.50.hit_ref, f32[64,128]{1,0:T(8,128)S(1)} %collective-permute-done.13.sums, f32[64,128]{1,0:T(8,128)S(1)} %get-tuple-element.78.fb_ref, ...), custom_call_target="tpu_custom_call" | custom-call | tf_op jit(solution)/shard_map/pallas_call | solution.py:368
  50.7 0.6 collective-permute-start.14
  51.3 0.7 %shard_map.117 = f32[64,128]{1,0:T(8,128)S(1)} custom-call(s32[16,24]{1,0:T(8,128)S(4)} %get-tuple-element.49.plan, bf16[128,128]{1,0:T(8,128)(2,1)S(1)} %get-tuple-element.50.hit_ref, f32[1024,128]{1,0:T(8,128)S(1)} %get-tuple-element.89.u_ref, f32[4096,128]{1,0:T(8,128)S(1)} %get-tuple-element.65.refs_0_, f32[6144,128]{1,0:T(8,128)S(1)} %get-tuple-element.66.refs_1_, ...), custom_call_target="tpu_custom_call" | custom-call | tf_op jit(solution)/shard_map/pallas_call | solution.py:368
  52.0 0.1 collective-permute-done.14
  52.2 0.0 collective-permute-start.15
  52.2 4.8 %collective-permute-done.15 = f32[64,128]{1,0:T(8,128)S(1)} collective-permute-done((f32[64,128]{1,0:T(8,128)S(1)}, f32[64,128]{1,0:T(8,128)S(1)}, u32[]{:S(2)}, u32[]{:S(2)}) %collective-permute-start.15) | collective-permute-done | bytes 32800 | tf_op jit(solution)/shard_map/ppermute | solution.py:386
  56.9 0.0 collective-permute-start.16
  57.0 3.4 %collective-permute-done.16 = f32[64,128]{1,0:T(8,128)S(1)} collective-permute-done((f32[64,128]{1,0:T(8,128)S(1)}, f32[64,128]{1,0:T(8,128)S(1)}, u32[]{:S(2)}, u32[]{:S(2)}) %collective-permute-start.16) | collective-permute-done | bytes 32800 | tf_op jit(solution)/shard_map/ppermute | solution.py:386
  60.3 0.0 collective-permute-start.17
  60.4 3.4 %collective-permute-done.17 = f32[64,128]{1,0:T(8,128)S(1)} collective-permute-done((f32[64,128]{1,0:T(8,128)S(1)}, f32[64,128]{1,0:T(8,128)S(1)}, u32[]{:S(2)}, u32[]{:S(2)}) %collective-permute-start.17) | collective-permute-done | bytes 32800 | tf_op jit(solution)/shard_map/ppermute | solution.py:386
  63.7 0.4 collective-permute-start.18
  64.1 0.1 shard_map.118
  64.2 0.8 %collective-permute-done.18.other = f32[64,128]{1,0:T(8,128)S(1)} collective-permute-done((f32[64,128]{1,0:T(8,128)S(1)}, f32[64,128]{1,0:T(8,128)S(1)}, u32[]{:S(2)}, u32[]{:S(2)}) %collective-permute-start.18) | collective-permute-done | bytes 32800 | tf_op jit(solution)/shard_map/ppermute | solution.py:386
  65.0 0.8 %shard_map.119 = (f32[8,128]{1,0:T(8,128)}, f32[8,128]{1,0:T(8,128)}) custom-call(f32[64,128]{1,0:T(8,128)S(1)} %collective-permute-done.18.other, f32[64,128]{1,0:T(8,128)S(1)} %get-tuple-element.78.fb_ref, f32[64,128]{1,0:T(8,128)S(1)} %get-tuple-element.79.et_ref, f32[8,128]{1,0:T(8,128)S(1)} %get-tuple-element.80.tot_ref, ...), custom_call_target="tpu_custom_call" | custom-call | tf_op jit(solution)/shard_map/pallas_call | solution.py:368
  (15 shorter events, 0.1 us)
Async XLA Ops:
  1.4 7.2 %collective-permute-start = (f32[24,128]{1,0:T(8,128)S(1)}, f32[24,128]{1,0:T(8,128)S(1)}, u32[]{:S(2)}, u32[]{:S(2)}) collective-permute-start(f32[24,128]{1,0:T(8,128)S(1)} %shard_map.105), channel_id=1, source_target_pairs={{0,9},{1,8},{2,11},{3,10},{4,13},{5,12},{6,15},{7,14},{8,1},{9,0},... | collective-permute-start | bytes 36872 | tf_op jit(solution)/shard_map/ppermute | solution.py:386
  8.7 3.3 %collective-permute-start.1 = (f32[48,128]{1,0:T(8,128)S(1)}, f32[48,128]{1,0:T(8,128)S(1)}, u32[]{:S(2)}, u32[]{:S(2)}) collective-permute-start(f32[48,128]{1,0:T(8,128)S(1)} %bitcast.20), channel_id=1, source_target_pairs={{0,5},{1,4},{2,7},{3,6},{4,1},{5,0},{6,3},{7,2},{8,13},{9,12},{10,... | collective-permute-start | bytes 73736 | tf_op jit(solution)/shard_map/ppermute | solution.py:386
  12.0 4.1 %collective-permute-start.2 = (f32[96,128]{1,0:T(8,128)S(1)}, f32[96,128]{1,0:T(8,128)S(1)}, u32[]{:S(2)}, u32[]{:S(2)}) collective-permute-start(f32[96,128]{1,0:T(8,128)S(1)} %bitcast.18), channel_id=1, source_target_pairs={{0,3},{1,2},{2,1},{3,0},{4,7},{5,6},{6,5},{7,4},{8,11},{9,10},{10,... | collective-permute-start | bytes 147464 | tf_op jit(solution)/shard_map/ppermute | solution.py:386
  16.1 1.8 %collective-permute-start.3 = (f32[192,128]{1,0:T(8,128)S(1)}, f32[192,128]{1,0:T(8,128)S(1)}, u32[]{:S(2)}, u32[]{:S(2)}) collective-permute-start(f32[192,128]{1,0:T(8,128)S(1)} %bitcast.15), channel_id=1, source_target_pairs={{0,1},{1,0},{2,3},{3,2},{4,5},{5,4},{6,7},{7,6},{8,9},{9,8},{10,11... | collective-permute-start | bytes 294920 | tf_op jit(solution)/shard_map/ppermute | solution.py:386
  19.3 1.3 %collective-permute-start.4 = (f32[64,128]{1,0:T(8,128)S(1)}, f32[64,128]{1,0:T(8,128)S(1)}, u32[]{:S(2)}, u32[]{:S(2)}) collective-permute-start(f32[64,128]{1,0:T(8,128)S(1)} %get-tuple-element.77), channel_id=1, source_target_pairs={{0,1},{1,0},{2,3},{3,2},{4,5},{5,4},{6,7},{7,6},{8,9},{9,8},{10,11... | collective-permute-start | bytes 98312 | tf_op jit(solution)/shard_map/ppermute | solution.py:386
  20.6 5.0 %collective-permute-start.5 = (f32[64,128]{1,0:T(8,128)S(1)}, f32[64,128]{1,0:T(8,128)S(1)}, u32[]{:S(2)}, u32[]{:S(2)}) collective-permute-start(f32[64,128]{1,0:T(8,128)S(1)} %add.36), channel_id=1, source_target_pairs={{0,9},{1,8},{2,11},{3,10},{4,13},{5,12},{6,15},{7,14},{8,1},{9,0},... | collective-permute-start | bytes 98312 | tf_op jit(solution)/shard_map/ppermute | solution.py:386
  25.6 3.3 %collective-permute-start.6 = (f32[64,128]{1,0:T(8,128)S(1)}, f32[64,128]{1,0:T(8,128)S(1)}, u32[]{:S(2)}, u32[]{:S(2)}) collective-permute-start(f32[64,128]{1,0:T(8,128)S(1)} %add.37), channel_id=1, source_target_pairs={{0,5},{1,4},{2,7},{3,6},{4,1},{5,0},{6,3},{7,2},{8,13},{9,12},{10,... | collective-permute-start | bytes 98312 | tf_op jit(solution)/shard_map/ppermute | solution.py:386
  28.9 3.3 %collective-permute-start.7 = (f32[64,128]{1,0:T(8,128)S(1)}, f32[64,128]{1,0:T(8,128)S(1)}, u32[]{:S(2)}, u32[]{:S(2)}) collective-permute-start(f32[64,128]{1,0:T(8,128)S(1)} %add.38), channel_id=1, source_target_pairs={{0,3},{1,2},{2,1},{3,0},{4,7},{5,6},{6,5},{7,4},{8,11},{9,10},{10,... | collective-permute-start | bytes 98312 | tf_op jit(solution)/shard_map/ppermute | solution.py:386
  32.3 1.2 %collective-permute-start.8 = (f32[64,128]{1,0:T(8,128)S(1)}, f32[64,128]{1,0:T(8,128)S(1)}, u32[]{:S(2)}, u32[]{:S(2)}) collective-permute-start(f32[64,128]{1,0:T(8,128)S(1)} %add.39.sums), channel_id=1, source_target_pairs={{0,1},{1,0},{2,3},{3,2},{4,5},{5,4},{6,7},{7,6},{8,9},{9,8},{10,11... | collective-permute-start | bytes 98312 | tf_op jit(solution)/shard_map/ppermute | solution.py:386
  34.9 1.3 %collective-permute-start.9 = (f32[64,128]{1,0:T(8,128)S(1)}, f32[64,128]{1,0:T(8,128)S(1)}, u32[]{:S(2)}, u32[]{:S(2)}) collective-permute-start(f32[64,128]{1,0:T(8,128)S(1)} %get-tuple-element.86), channel_id=1, source_target_pairs={{0,1},{1,0},{2,3},{3,2},{4,5},{5,4},{6,7},{7,6},{8,9},{9,8},{10,11... | collective-permute-start | bytes 98312 | tf_op jit(solution)/shard_map/ppermute | solution.py:386
  36.1 5.1 %collective-permute-start.10 = (f32[64,128]{1,0:T(8,128)S(1)}, f32[64,128]{1,0:T(8,128)S(1)}, u32[]{:S(2)}, u32[]{:S(2)}) collective-permute-start(f32[64,128]{1,0:T(8,128)S(1)} %add.40), channel_id=1, source_target_pairs={{0,9},{1,8},{2,11},{3,10},{4,13},{5,12},{6,15},{7,14},{8,1},{9,0},... | collective-permute-start | bytes 98312 | tf_op jit(solution)/shard_map/ppermute | solution.py:386
  41.3 3.4 %collective-permute-start.11 = (f32[64,128]{1,0:T(8,128)S(1)}, f32[64,128]{1,0:T(8,128)S(1)}, u32[]{:S(2)}, u32[]{:S(2)}) collective-permute-start(f32[64,128]{1,0:T(8,128)S(1)} %add.41), channel_id=1, source_target_pairs={{0,5},{1,4},{2,7},{3,6},{4,1},{5,0},{6,3},{7,2},{8,13},{9,12},{10,... | collective-permute-start | bytes 98312 | tf_op jit(solution)/shard_map/ppermute | solution.py:386
  44.7 3.4 %collective-permute-start.12 = (f32[64,128]{1,0:T(8,128)S(1)}, f32[64,128]{1,0:T(8,128)S(1)}, u32[]{:S(2)}, u32[]{:S(2)}) collective-permute-start(f32[64,128]{1,0:T(8,128)S(1)} %add.42), channel_id=1, source_target_pairs={{0,3},{1,2},{2,1},{3,0},{4,7},{5,6},{6,5},{7,4},{8,11},{9,10},{10,... | collective-permute-start | bytes 98312 | tf_op jit(solution)/shard_map/ppermute | solution.py:386
  48.1 1.2 %collective-permute-start.13 = (f32[64,128]{1,0:T(8,128)S(1)}, f32[64,128]{1,0:T(8,128)S(1)}, u32[]{:S(2)}, u32[]{:S(2)}) collective-permute-start(f32[64,128]{1,0:T(8,128)S(1)} %add.43.sums), channel_id=1, source_target_pairs={{0,1},{1,0},{2,3},{3,2},{4,5},{5,4},{6,7},{7,6},{8,9},{9,8},{10,11... | collective-permute-start | bytes 98312 | tf_op jit(solution)/shard_map/ppermute | solution.py:386
  50.7 1.5 %collective-permute-start.14 = (f32[64,128]{1,0:T(8,128)S(1)}, f32[64,128]{1,0:T(8,128)S(1)}, u32[]{:S(2)}, u32[]{:S(2)}) collective-permute-start(f32[64,128]{1,0:T(8,128)S(1)} %get-tuple-element.90), channel_id=1, source_target_pairs={{0,1},{1,0},{2,3},{3,2},{4,5},{5,4},{6,7},{7,6},{8,9},{9,8},{10,11... | collective-permute-start | bytes 98312 | tf_op jit(solution)/shard_map/ppermute | solution.py:386
  52.2 4.8 %collective-permute-start.15 = (f32[64,128]{1,0:T(8,128)S(1)}, f32[64,128]{1,0:T(8,128)S(1)}, u32[]{:S(2)}, u32[]{:S(2)}) collective-permute-start(f32[64,128]{1,0:T(8,128)S(1)} %add.44), channel_id=1, source_target_pairs={{0,9},{1,8},{2,11},{3,10},{4,13},{5,12},{6,15},{7,14},{8,1},{9,0},... | collective-permute-start | bytes 98312 | tf_op jit(solution)/shard_map/ppermute | solution.py:386
  56.9 3.4 %collective-permute-start.16 = (f32[64,128]{1,0:T(8,128)S(1)}, f32[64,128]{1,0:T(8,128)S(1)}, u32[]{:S(2)}, u32[]{:S(2)}) collective-permute-start(f32[64,128]{1,0:T(8,128)S(1)} %add.45), channel_id=1, source_target_pairs={{0,5},{1,4},{2,7},{3,6},{4,1},{5,0},{6,3},{7,2},{8,13},{9,12},{10,... | collective-permute-start | bytes 98312 | tf_op jit(solution)/shard_map/ppermute | solution.py:386
  60.3 3.4 %collective-permute-start.17 = (f32[64,128]{1,0:T(8,128)S(1)}, f32[64,128]{1,0:T(8,128)S(1)}, u32[]{:S(2)}, u32[]{:S(2)}) collective-permute-start(f32[64,128]{1,0:T(8,128)S(1)} %add.46), channel_id=1, source_target_pairs={{0,3},{1,2},{2,1},{3,0},{4,7},{5,6},{6,5},{7,4},{8,11},{9,10},{10,... | collective-permute-start | bytes 98312 | tf_op jit(solution)/shard_map/ppermute | solution.py:386
  63.7 1.2 %collective-permute-start.18 = (f32[64,128]{1,0:T(8,128)S(1)}, f32[64,128]{1,0:T(8,128)S(1)}, u32[]{:S(2)}, u32[]{:S(2)}) collective-permute-start(f32[64,128]{1,0:T(8,128)S(1)} %add.47.keep), channel_id=1, source_target_pairs={{0,1},{1,0},{2,3},{3,2},{4,5},{5,4},{6,7},{7,6},{8,9},{9,8},{10,11... | collective-permute-start | bytes 98312 | tf_op jit(solution)/shard_map/ppermute | solution.py:386
